TPU v7x, 32 devices: a whole 2x2x4 slice. The times are simulated.
32 devices in a mesh: shot: 8 (over y, x, core), slab: 4 (over z).
Axes of the slice: x: 2, y: 2, z: 4, core: 2. Of those that a mesh axis runs over, the one named last changes fastest.
Arguments:
- state_before: float32 [8, 64, 128, 128], P('shot', 'slab'), may hold values from -6 to 6
- state_now: float32 [8, 64, 128, 128], P('shot', 'slab'), may hold values from -6 to 6
- adjoint_after: float32 [8, 64, 128, 128], P('shot', 'slab'), may hold values from -6 to 6
- adjoint_now: float32 [8, 64, 128, 128], P('shot', 'slab'), may hold values from -6 to 6
- speed_term: float32 [64, 128, 128], P('slab'), may hold values from 0.04 to 0.18
- wavelet: float32 [8, 8], P('shot'), may hold values from -180 to 180
- source: int32 [8, 3], P('shot'), may hold values from 0 to 127, as said below
- receivers: int32 [8, 3, 1024], P('shot'), may hold values from 0 to 127, as said below
- traces: float32 [8, 8, 1024], P('shot', None, 'slab'), may hold values from -6 to 6
Outputs:
- adj_first: float32 [8, 64, 128, 128], P('shot', 'slab')
- adj_second: float32 [8, 64, 128, 128], P('shot', 'slab')
- gradient: float32 [64, 128, 128], P('slab', 'shot')
Inputs may be any that keep to these rules, and one draw needn't show every extreme that they name: `source`: row 0 is a depth row below 64, row 1 a cell below 128, row 2 a cell below 128. `receivers`: row 0 is a depth row below 64, row 1 a cell below 128, row 2 a cell below 128; several receivers may share a cell.
All inputs are finite; a program needn't handle non-finite values.
Results may differ from a plain program's by a relative error of at most 0.0003.
Values sent between devices are 32-bit elements; how exact they have to be, the bound alone decides.
No kernel may reach another device: no remote copies, remote signals or barrier semaphores. Data moves between devices by JAX's collectives and lax.ppermute only.
A program may use at most 128 MiB of HBM per device.

v0:
```python
import jax
import jax.numpy as jnp
from jax import lax
from jax.sharding import PartitionSpec as P

stencil_weights = (-205.0 / 72.0, 8.0 / 5.0, -1.0 / 5.0, 8.0 / 315.0, -1.0 / 560.0)


def extended_2(block, sides, width):
    for axis, dim in sides:
        count = lax.axis_size(axis)
        forward = [(i, i + 1) for i in range(count - 1)]
        backward = [(target, source) for source, target in forward]
        low = lax.ppermute(
            lax.slice_in_dim(block, block.shape[dim] - width, None, axis=dim), axis, forward
        )
        high = lax.ppermute(lax.slice_in_dim(block, 0, width, axis=dim), axis, backward)
        block = jnp.concatenate([low, block, high], axis=dim)
    return block


def laplace(extended):
    count = extended.shape[0] - 8
    width_y = extended.shape[1]
    width_z = extended.shape[2]
    centre = extended[4 : 4 + count]
    sided = jnp.pad(centre, ((0, 0), (4, 4), (4, 4)))
    total = 3.0 * stencil_weights[0] * centre
    for step in range(1, 5):
        near = extended[4 + step : 4 + step + count] + extended[4 - step : 4 - step + count]
        near = (
            near
            + sided[:, 4 + step : 4 + step + width_y, 4 : 4 + width_z]
            + sided[:, 4 - step : 4 - step + width_y, 4 : 4 + width_z]
        )
        near = (
            near
            + sided[:, 4 : 4 + width_y, 4 + step : 4 + step + width_z]
            + sided[:, 4 : 4 + width_y, 4 - step : 4 - step + width_z]
        )
        total = total + stencil_weights[step] * near
    return total


def cell_index(coords, anchor, count, width_y, width_z):
    depth = coords[0] - anchor
    valid = (depth >= 0) & (depth < count)
    flat = depth * (width_y * width_z) + coords[1] * width_z + coords[2]
    return jnp.where(valid, flat, count * width_y * width_z)


def spot_field(coords, anchor, count, width_y, width_z):
    shape = (count, width_y, width_z)
    rows = lax.broadcasted_iota(jnp.int32, shape, 0) + anchor
    cols = lax.broadcasted_iota(jnp.int32, shape, 1)
    lanes = lax.broadcasted_iota(jnp.int32, shape, 2)
    hit = (rows == coords[0]) & (cols == coords[1]) & (lanes == coords[2])
    return jnp.where(hit, 1.0, 0.0).astype(jnp.float32)


def injections(listen, values, anchor, count, width_y, width_z):
    steps = values.shape[0]
    cells = count * width_y * width_z
    flat = cell_index(listen, anchor, count, width_y, width_z)
    offsets = lax.broadcasted_iota(jnp.int32, values.shape, 0) * cells
    where_to = jnp.where(flat[None, :] < cells, offsets + flat[None, :], steps * cells)
    buffer = jnp.zeros((steps * cells,), jnp.float32)
    buffer = buffer.at[where_to.reshape(-1)].add(values.reshape(-1), mode="drop")
    return buffer.reshape(steps, count, width_y, width_z)


def body(
    state_before,
    state_now,
    adjoint_after,
    adjoint_now,
    speed_term,
    wavelet,
    source,
    receivers,
    traces,
):
    count, width_y, width_z = speed_term.shape
    steps = wavelet.shape[1]
    anchor = lax.axis_index("slab") * count
    scale = 1.0 / (8.0 * steps)
    all_traces = lax.all_gather(traces[0], "slab", axis=1, tiled=True)
    spot = source[0]
    listen = receivers[0]
    wave = wavelet[0]
    zero = jnp.zeros(speed_term.shape, jnp.float32)
    core_mark = spot_field(spot, anchor, count, width_y, width_z)
    inject = injections(listen, all_traces, anchor, count, width_y, width_z)

    def advance(prev, cur):
        extended = extended_2(cur, (("slab", 0),), 4)
        lapl = laplace(extended)
        return (2.0 * cur - prev + speed_term * lapl, lapl)

    def forward(carry, amount):
        prev, cur = carry
        nxt, lapl = advance(prev, cur)
        return ((cur, nxt + amount * core_mark), lapl)

    _, stored = lax.scan(forward, (state_before[0], state_now[0]), wave)

    def backward(carry, inputs):
        later, cur, total = carry
        lapl_t, added = inputs
        nxt, _ = advance(later, cur)
        return ((cur, nxt + added, total + cur * lapl_t), None)

    (second, opening, total), _ = lax.scan(
        backward, (adjoint_after[0], adjoint_now[0], zero), (stored, inject), reverse=True
    )
    gradient = lax.psum_scatter(total * scale, "shot", scatter_dimension=1, tiled=True)
    return (opening[None], second[None], gradient)


def solution(mesh):
    return jax.shard_map(
        body,
        mesh=mesh,
        in_specs=(
            P("shot", "slab", None, None),
            P("shot", "slab", None, None),
            P("shot", "slab", None, None),
            P("shot", "slab", None, None),
            P("slab", None, None),
            P("shot", None),
            P("shot", None),
            P("shot", None, None),
            P("shot", None, "slab"),
        ),
        out_specs=(
            P("shot", "slab", None, None),
            P("shot", "slab", None, None),
            P("slab", "shot", None),
        ),
        check_vma=False,
    )
```

profile of v0, /device:TPU:0, one launch (start us, length us, event | category | flops | bytes accessed | tf_op | source)
XLA Modules:
  0.0 402.0 jit_solution(4855447956908505319)
XLA Ops:
  13.8 14.8 %all-gather = f32[1,8,1024]{2,1,0:T(8,128)S(1)} all-gather(f32[1,8,256]{2,1,0:T(8,128)S(1)} %copy-done.10), channel_id=2, replica_groups=mesh['shot'=8,'slab'=4] {'slab'}, dimensions={2}, use_global_device_ids=true | all-gather | bytes 40960 | tf_op jit(solution)/shard_map/all_gather | solution.py:87
  29.9 46.9 %scatter_custom_fusion = f32[2097152]{0:T(1024)} fusion(s32[8192]{0:T(1024)S(1)} %bitcast.48, f32[8192]{0:T(1024)S(1)} %bitcast.49, f32[]{:T(128)} %constant.160.clone.1), kind=kCustom, calls=%fused_computation.106 | custom fusion | flops 8192 | bytes 8388612 | tf_op jit(solution)/shard_map/scatter-add | solution.py:68
  76.9 143.5 %while.36 = (s32[]{:T(128)}, f32[16,128,128]{2,1,0:T(8,128)}, f32[16,128,128]{2,1,0:T(8,128)S(1)}, f32[8,16,128,128]{3,2,1,0:T(8,128)}, f32[16,128,128]{2,1,0:T(...) while((s32[]{:T(128)}, f32[16,128,128]{2,1,0:T(8,128)}, ...), condition=%wide.region_1.2_spmd.clone, body=%wide.region_0.1_spmd.clone.sunk | while | flops 9961474 | bytes 32506364 | solution.py:105
  77.8 4.1 %collective-permute-start = (f32[4,128,128]{2,1,0:T(8,128)}, f32[4,128,128]{2,1,0:T(8,128)}, u32[]{:S(2)}, u32[]{:S(2)}) collective-permute-start(f32[4,128,128]{2,1,0:T(8,128)} %get-tuple-element.439), channel_id=1, source_target_pairs={{0,1},{1,2},{2,3},{4,5},{5,6},{6,7},{8,9},{9,10},{10,11},{12,13},{... | collective-permute-start | bytes 786440 | tf_op jit(solution)/shard_map/while/body/eval_jaxpr/ppermute | solution.py:14
  86.7 3.7 collective-permute-done.1
  115.1 3.9 collective-permute-start
  123.8 3.7 collective-permute-done.1
  141.2 3.7 collective-permute-done.1
  158.6 3.7 collective-permute-done.1
  193.4 3.7 collective-permute-done.1
  210.9 3.7 collective-permute-done.1
  220.5 137.6 %while.37 = (s32[]{:T(128)}, f32[16,128,128]{2,1,0:T(8,128)}, f32[16,128,128]{2,1,0:T(8,128)S(1)}, f32[16,128,128]{2,1,0:T(8,128)}, f32[16,128,128]{2,1,0:T(8,12...) while((s32[]{:T(128)}, f32[16,128,128]{2,1,0:T(8,128)}, ...), condition=%wide.region_4.5_spmd.clone, body=%wide.region_3.4_spmd.clone.sunk | while | flops 9699332 | bytes 40894752 | solution.py:113
  227.8 4.6 %collective-permute-done.3 = f32[4,128,128]{2,1,0:T(8,128)S(1)} collective-permute-done((f32[4,128,128]{2,1,0:T(8,128)}, f32[4,128,128]{2,1,0:T(8,128)S(1)}, u32[]{:S(2)}, u32[]{:S(2)}) %collective-permute-start.3) | collective-permute-done | bytes 262176 | tf_op jit(solution)/shard_map/while/body/eval_jaxpr/ppermute | solution.py:17
  232.5 3.7 fusion.68
  241.2 4.6 %collective-permute-done.2 = f32[4,128,128]{2,1,0:T(8,128)S(1)} collective-permute-done((f32[4,128,128]{2,1,0:T(8,128)S(1)}, f32[4,128,128]{2,1,0:T(8,128)S(1)}, u32[]{:S(2)}, u32[]{:S(2)}) %collective-permute-start.2) | collective-permute-done | bytes 262176 | tf_op jit(solution)/shard_map/while/body/eval_jaxpr/ppermute | solution.py:14
  246.1 4.7 %collective-permute-done.3 = f32[4,128,128]{2,1,0:T(8,128)S(1)} collective-permute-done((f32[4,128,128]{2,1,0:T(8,128)}, f32[4,128,128]{2,1,0:T(8,128)S(1)}, u32[]{:S(2)}, u32[]{:S(2)}) %collective-permute-start.3) | collective-permute-done | bytes 262176 | tf_op jit(solution)/shard_map/while/body/eval_jaxpr/ppermute | solution.py:17
  250.9 3.7 fusion.68
  259.6 4.9 %collective-permute-done.2 = f32[4,128,128]{2,1,0:T(8,128)S(1)} collective-permute-done((f32[4,128,128]{2,1,0:T(8,128)S(1)}, f32[4,128,128]{2,1,0:T(8,128)S(1)}, u32[]{:S(2)}, u32[]{:S(2)}) %collective-permute-start.2) | collective-permute-done | bytes 262176 | tf_op jit(solution)/shard_map/while/body/eval_jaxpr/ppermute | solution.py:14
  264.8 4.1 %collective-permute-done.3 = f32[4,128,128]{2,1,0:T(8,128)S(1)} collective-permute-done((f32[4,128,128]{2,1,0:T(8,128)}, f32[4,128,128]{2,1,0:T(8,128)S(1)}, u32[]{:S(2)}, u32[]{:S(2)}) %collective-permute-start.3) | collective-permute-done | bytes 262176 | tf_op jit(solution)/shard_map/while/body/eval_jaxpr/ppermute | solution.py:17
  268.9 3.7 fusion.68
  278.2 4.1 %collective-permute-done.2 = f32[4,128,128]{2,1,0:T(8,128)S(1)} collective-permute-done((f32[4,128,128]{2,1,0:T(8,128)S(1)}, f32[4,128,128]{2,1,0:T(8,128)S(1)}, u32[]{:S(2)}, u32[]{:S(2)}) %collective-permute-start.2) | collective-permute-done | bytes 262176 | tf_op jit(solution)/shard_map/while/body/eval_jaxpr/ppermute | solution.py:14
  282.6 4.1 %collective-permute-done.3 = f32[4,128,128]{2,1,0:T(8,128)S(1)} collective-permute-done((f32[4,128,128]{2,1,0:T(8,128)}, f32[4,128,128]{2,1,0:T(8,128)S(1)}, u32[]{:S(2)}, u32[]{:S(2)}) %collective-permute-start.3) | collective-permute-done | bytes 262176 | tf_op jit(solution)/shard_map/while/body/eval_jaxpr/ppermute | solution.py:17
  286.7 3.7 fusion.68
  299.5 4.1 %collective-permute-done.3 = f32[4,128,128]{2,1,0:T(8,128)S(1)} collective-permute-done((f32[4,128,128]{2,1,0:T(8,128)}, f32[4,128,128]{2,1,0:T(8,128)S(1)}, u32[]{:S(2)}, u32[]{:S(2)}) %collective-permute-start.3) | collective-permute-done | bytes 262176 | tf_op jit(solution)/shard_map/while/body/eval_jaxpr/ppermute | solution.py:17
  303.6 3.7 fusion.68
  315.9 4.3 %collective-permute-done.3 = f32[4,128,128]{2,1,0:T(8,128)S(1)} collective-permute-done((f32[4,128,128]{2,1,0:T(8,128)}, f32[4,128,128]{2,1,0:T(8,128)S(1)}, u32[]{:S(2)}, u32[]{:S(2)}) %collective-permute-start.3) | collective-permute-done | bytes 262176 | tf_op jit(solution)/shard_map/while/body/eval_jaxpr/ppermute | solution.py:17
  320.3 3.7 fusion.68
  332.4 4.3 %collective-permute-done.3 = f32[4,128,128]{2,1,0:T(8,128)S(1)} collective-permute-done((f32[4,128,128]{2,1,0:T(8,128)}, f32[4,128,128]{2,1,0:T(8,128)S(1)}, u32[]{:S(2)}, u32[]{:S(2)}) %collective-permute-start.3) | collective-permute-done | bytes 262176 | tf_op jit(solution)/shard_map/while/body/eval_jaxpr/ppermute | solution.py:17
  336.8 3.7 fusion.68
  348.6 4.3 %collective-permute-done.3 = f32[4,128,128]{2,1,0:T(8,128)S(1)} collective-permute-done((f32[4,128,128]{2,1,0:T(8,128)}, f32[4,128,128]{2,1,0:T(8,128)S(1)}, u32[]{:S(2)}, u32[]{:S(2)}) %collective-permute-start.3) | collective-permute-done | bytes 262176 | tf_op jit(solution)/shard_map/while/body/eval_jaxpr/ppermute | solution.py:17
  353.0 3.7 fusion.68
  360.8 34.4 %reduce-scatter.2.cloned.1.call-done = f32[16,16,128]{2,1,0:T(8,128)} async-done(((f32[16,128,128]{2,1,0:T(8,128)}), f32[16,16,128]{2,1,0:T(8,128)}) %reduce-scatter.2.cloned.1.call-update) | async-done | bytes 131088 | tf_op jit(solution)/shard_map/reduce_scatter | solution.py:116
  (264 shorter events, 182.1 us)
Async XLA Ops:
  7.2 388.0 %reduce-scatter.2.cloned.1.call-start = ((), (), s32[]{:S(2)}) async-start(), calls=%async_computation.1 | async-start | bytes 1179648 | tf_op jit(solution)/shard_map/reduce_scatter | solution.py:116
  77.8 7.6 %collective-permute-start = (f32[4,128,128]{2,1,0:T(8,128)}, f32[4,128,128]{2,1,0:T(8,128)}, u32[]{:S(2)}, u32[]{:S(2)}) collective-permute-start(f32[4,128,128]{2,1,0:T(8,128)} %get-tuple-element.439), channel_id=1, source_target_pairs={{0,1},{1,2},{2,3},{4,5},{5,6},{6,7},{8,9},{9,10},{10,11},{12,13},{... | collective-permute-start | bytes 786440 | tf_op jit(solution)/shard_map/while/body/eval_jaxpr/ppermute | solution.py:14
  81.9 8.5 %collective-permute-start.1 = (f32[4,128,128]{2,1,0:T(8,128)}, f32[4,128,128]{2,1,0:T(8,128)S(1)}, u32[]{:S(2)}, u32[]{:S(2)}) collective-permute-start(f32[4,128,128]{2,1,0:T(8,128)} %get-tuple-element.442), channel_id=1, source_target_pairs={{1,0},{2,1},{3,2},{5,4},{6,5},{7,6},{9,8},{10,9},{11,10},{13,12},{... | collective-permute-start | bytes 786440 | tf_op jit(solution)/shard_map/while/body/eval_jaxpr/ppermute | solution.py:17
  97.1 6.3 %collective-permute-start = (f32[4,128,128]{2,1,0:T(8,128)}, f32[4,128,128]{2,1,0:T(8,128)}, u32[]{:S(2)}, u32[]{:S(2)}) collective-permute-start(f32[4,128,128]{2,1,0:T(8,128)} %get-tuple-element.439), channel_id=1, source_target_pairs={{0,1},{1,2},{2,3},{4,5},{5,6},{6,7},{8,9},{9,10},{10,11},{12,13},{... | collective-permute-start | bytes 786440 | tf_op jit(solution)/shard_map/while/body/eval_jaxpr/ppermute | solution.py:14
  99.9 8.5 %collective-permute-start.1 = (f32[4,128,128]{2,1,0:T(8,128)}, f32[4,128,128]{2,1,0:T(8,128)S(1)}, u32[]{:S(2)}, u32[]{:S(2)}) collective-permute-start(f32[4,128,128]{2,1,0:T(8,128)} %get-tuple-element.442), channel_id=1, source_target_pairs={{1,0},{2,1},{3,2},{5,4},{6,5},{7,6},{9,8},{10,9},{11,10},{13,12},{... | collective-permute-start | bytes 786440 | tf_op jit(solution)/shard_map/while/body/eval_jaxpr/ppermute | solution.py:17
  115.1 7.4 %collective-permute-start = (f32[4,128,128]{2,1,0:T(8,128)}, f32[4,128,128]{2,1,0:T(8,128)}, u32[]{:S(2)}, u32[]{:S(2)}) collective-permute-start(f32[4,128,128]{2,1,0:T(8,128)} %get-tuple-element.439), channel_id=1, source_target_pairs={{0,1},{1,2},{2,3},{4,5},{5,6},{6,7},{8,9},{9,10},{10,11},{12,13},{... | collective-permute-start | bytes 786440 | tf_op jit(solution)/shard_map/while/body/eval_jaxpr/ppermute | solution.py:14
  119.0 8.5 %collective-permute-start.1 = (f32[4,128,128]{2,1,0:T(8,128)}, f32[4,128,128]{2,1,0:T(8,128)S(1)}, u32[]{:S(2)}, u32[]{:S(2)}) collective-permute-start(f32[4,128,128]{2,1,0:T(8,128)} %get-tuple-element.442), channel_id=1, source_target_pairs={{1,0},{2,1},{3,2},{5,4},{6,5},{7,6},{9,8},{10,9},{11,10},{13,12},{... | collective-permute-start | bytes 786440 | tf_op jit(solution)/shard_map/while/body/eval_jaxpr/ppermute | solution.py:17
  134.2 5.7 %collective-permute-start = (f32[4,128,128]{2,1,0:T(8,128)}, f32[4,128,128]{2,1,0:T(8,128)}, u32[]{:S(2)}, u32[]{:S(2)}) collective-permute-start(f32[4,128,128]{2,1,0:T(8,128)} %get-tuple-element.439), channel_id=1, source_target_pairs={{0,1},{1,2},{2,3},{4,5},{5,6},{6,7},{8,9},{9,10},{10,11},{12,13},{... | collective-permute-start | bytes 786440 | tf_op jit(solution)/shard_map/while/body/eval_jaxpr/ppermute | solution.py:14
  136.4 8.5 %collective-permute-start.1 = (f32[4,128,128]{2,1,0:T(8,128)}, f32[4,128,128]{2,1,0:T(8,128)S(1)}, u32[]{:S(2)}, u32[]{:S(2)}) collective-permute-start(f32[4,128,128]{2,1,0:T(8,128)} %get-tuple-element.442), channel_id=1, source_target_pairs={{1,0},{2,1},{3,2},{5,4},{6,5},{7,6},{9,8},{10,9},{11,10},{13,12},{... | collective-permute-start | bytes 786440 | tf_op jit(solution)/shard_map/while/body/eval_jaxpr/ppermute | solution.py:17
  151.6 5.7 %collective-permute-start = (f32[4,128,128]{2,1,0:T(8,128)}, f32[4,128,128]{2,1,0:T(8,128)}, u32[]{:S(2)}, u32[]{:S(2)}) collective-permute-start(f32[4,128,128]{2,1,0:T(8,128)} %get-tuple-element.439), channel_id=1, source_target_pairs={{0,1},{1,2},{2,3},{4,5},{5,6},{6,7},{8,9},{9,10},{10,11},{12,13},{... | collective-permute-start | bytes 786440 | tf_op jit(solution)/shard_map/while/body/eval_jaxpr/ppermute | solution.py:14
  153.9 8.5 %collective-permute-start.1 = (f32[4,128,128]{2,1,0:T(8,128)}, f32[4,128,128]{2,1,0:T(8,128)S(1)}, u32[]{:S(2)}, u32[]{:S(2)}) collective-permute-start(f32[4,128,128]{2,1,0:T(8,128)} %get-tuple-element.442), channel_id=1, source_target_pairs={{1,0},{2,1},{3,2},{5,4},{6,5},{7,6},{9,8},{10,9},{11,10},{13,12},{... | collective-permute-start | bytes 786440 | tf_op jit(solution)/shard_map/while/body/eval_jaxpr/ppermute | solution.py:17
  169.0 5.7 %collective-permute-start = (f32[4,128,128]{2,1,0:T(8,128)}, f32[4,128,128]{2,1,0:T(8,128)}, u32[]{:S(2)}, u32[]{:S(2)}) collective-permute-start(f32[4,128,128]{2,1,0:T(8,128)} %get-tuple-element.439), channel_id=1, source_target_pairs={{0,1},{1,2},{2,3},{4,5},{5,6},{6,7},{8,9},{9,10},{10,11},{12,13},{... | collective-permute-start | bytes 786440 | tf_op jit(solution)/shard_map/while/body/eval_jaxpr/ppermute | solution.py:14
  171.3 8.5 %collective-permute-start.1 = (f32[4,128,128]{2,1,0:T(8,128)}, f32[4,128,128]{2,1,0:T(8,128)S(1)}, u32[]{:S(2)}, u32[]{:S(2)}) collective-permute-start(f32[4,128,128]{2,1,0:T(8,128)} %get-tuple-element.442), channel_id=1, source_target_pairs={{1,0},{2,1},{3,2},{5,4},{6,5},{7,6},{9,8},{10,9},{11,10},{13,12},{... | collective-permute-start | bytes 786440 | tf_op jit(solution)/shard_map/while/body/eval_jaxpr/ppermute | solution.py:17
  186.5 5.7 %collective-permute-start = (f32[4,128,128]{2,1,0:T(8,128)}, f32[4,128,128]{2,1,0:T(8,128)}, u32[]{:S(2)}, u32[]{:S(2)}) collective-permute-start(f32[4,128,128]{2,1,0:T(8,128)} %get-tuple-element.439), channel_id=1, source_target_pairs={{0,1},{1,2},{2,3},{4,5},{5,6},{6,7},{8,9},{9,10},{10,11},{12,13},{... | collective-permute-start | bytes 786440 | tf_op jit(solution)/shard_map/while/body/eval_jaxpr/ppermute | solution.py:14
  188.7 8.5 %collective-permute-start.1 = (f32[4,128,128]{2,1,0:T(8,128)}, f32[4,128,128]{2,1,0:T(8,128)S(1)}, u32[]{:S(2)}, u32[]{:S(2)}) collective-permute-start(f32[4,128,128]{2,1,0:T(8,128)} %get-tuple-element.442), channel_id=1, source_target_pairs={{1,0},{2,1},{3,2},{5,4},{6,5},{7,6},{9,8},{10,9},{11,10},{13,12},{... | collective-permute-start | bytes 786440 | tf_op jit(solution)/shard_map/while/body/eval_jaxpr/ppermute | solution.py:17
  206.1 8.5 %collective-permute-start.1 = (f32[4,128,128]{2,1,0:T(8,128)}, f32[4,128,128]{2,1,0:T(8,128)S(1)}, u32[]{:S(2)}, u32[]{:S(2)}) collective-permute-start(f32[4,128,128]{2,1,0:T(8,128)} %get-tuple-element.442), channel_id=1, source_target_pairs={{1,0},{2,1},{3,2},{5,4},{6,5},{7,6},{9,8},{10,9},{11,10},{13,12},{... | collective-permute-start | bytes 786440 | tf_op jit(solution)/shard_map/while/body/eval_jaxpr/ppermute | solution.py:17
  221.2 6.3 %collective-permute-start.2 = (f32[4,128,128]{2,1,0:T(8,128)S(1)}, f32[4,128,128]{2,1,0:T(8,128)S(1)}, u32[]{:S(2)}, u32[]{:S(2)}) collective-permute-start(f32[4,128,128]{2,1,0:T(8,128)S(1)} %get-tuple-element.452), channel_id=1, source_target_pairs={{0,1},{1,2},{2,3},{4,5},{5,6},{6,7},{8,9},{9,10},{10,11},{12,13},{... | collective-permute-start | bytes 786440 | tf_op jit(solution)/shard_map/while/body/eval_jaxpr/ppermute | solution.py:14
  222.8 9.7 %collective-permute-start.3 = (f32[4,128,128]{2,1,0:T(8,128)}, f32[4,128,128]{2,1,0:T(8,128)S(1)}, u32[]{:S(2)}, u32[]{:S(2)}) collective-permute-start(f32[4,128,128]{2,1,0:T(8,128)} %get-tuple-element.455), channel_id=1, source_target_pairs={{1,0},{2,1},{3,2},{5,4},{6,5},{7,6},{9,8},{10,9},{11,10},{13,12},{... | collective-permute-start | bytes 786440 | tf_op jit(solution)/shard_map/while/body/eval_jaxpr/ppermute | solution.py:17
  238.3 7.6 %collective-permute-start.2 = (f32[4,128,128]{2,1,0:T(8,128)S(1)}, f32[4,128,128]{2,1,0:T(8,128)S(1)}, u32[]{:S(2)}, u32[]{:S(2)}) collective-permute-start(f32[4,128,128]{2,1,0:T(8,128)S(1)} %get-tuple-element.452), channel_id=1, source_target_pairs={{0,1},{1,2},{2,3},{4,5},{5,6},{6,7},{8,9},{9,10},{10,11},{12,13},{... | collective-permute-start | bytes 786440 | tf_op jit(solution)/shard_map/while/body/eval_jaxpr/ppermute | solution.py:14
  239.9 10.9 %collective-permute-start.3 = (f32[4,128,128]{2,1,0:T(8,128)}, f32[4,128,128]{2,1,0:T(8,128)S(1)}, u32[]{:S(2)}, u32[]{:S(2)}) collective-permute-start(f32[4,128,128]{2,1,0:T(8,128)} %get-tuple-element.455), channel_id=1, source_target_pairs={{1,0},{2,1},{3,2},{5,4},{6,5},{7,6},{9,8},{10,9},{11,10},{13,12},{... | collective-permute-start | bytes 786440 | tf_op jit(solution)/shard_map/while/body/eval_jaxpr/ppermute | solution.py:17
  256.6 7.8 %collective-permute-start.2 = (f32[4,128,128]{2,1,0:T(8,128)S(1)}, f32[4,128,128]{2,1,0:T(8,128)S(1)}, u32[]{:S(2)}, u32[]{:S(2)}) collective-permute-start(f32[4,128,128]{2,1,0:T(8,128)S(1)} %get-tuple-element.452), channel_id=1, source_target_pairs={{0,1},{1,2},{2,3},{4,5},{5,6},{6,7},{8,9},{9,10},{10,11},{12,13},{... | collective-permute-start | bytes 786440 | tf_op jit(solution)/shard_map/while/body/eval_jaxpr/ppermute | solution.py:14
  258.2 10.6 %collective-permute-start.3 = (f32[4,128,128]{2,1,0:T(8,128)}, f32[4,128,128]{2,1,0:T(8,128)S(1)}, u32[]{:S(2)}, u32[]{:S(2)}) collective-permute-start(f32[4,128,128]{2,1,0:T(8,128)} %get-tuple-element.455), channel_id=1, source_target_pairs={{1,0},{2,1},{3,2},{5,4},{6,5},{7,6},{9,8},{10,9},{11,10},{13,12},{... | collective-permute-start | bytes 786440 | tf_op jit(solution)/shard_map/while/body/eval_jaxpr/ppermute | solution.py:17
  274.7 7.7 %collective-permute-start.2 = (f32[4,128,128]{2,1,0:T(8,128)S(1)}, f32[4,128,128]{2,1,0:T(8,128)S(1)}, u32[]{:S(2)}, u32[]{:S(2)}) collective-permute-start(f32[4,128,128]{2,1,0:T(8,128)S(1)} %get-tuple-element.452), channel_id=1, source_target_pairs={{0,1},{1,2},{2,3},{4,5},{5,6},{6,7},{8,9},{9,10},{10,11},{12,13},{... | collective-permute-start | bytes 786440 | tf_op jit(solution)/shard_map/while/body/eval_jaxpr/ppermute | solution.py:14
  276.8 9.8 %collective-permute-start.3 = (f32[4,128,128]{2,1,0:T(8,128)}, f32[4,128,128]{2,1,0:T(8,128)S(1)}, u32[]{:S(2)}, u32[]{:S(2)}) collective-permute-start(f32[4,128,128]{2,1,0:T(8,128)} %get-tuple-element.455), channel_id=1, source_target_pairs={{1,0},{2,1},{3,2},{5,4},{6,5},{7,6},{9,8},{10,9},{11,10},{13,12},{... | collective-permute-start | bytes 786440 | tf_op jit(solution)/shard_map/while/body/eval_jaxpr/ppermute | solution.py:17
  292.5 6.8 %collective-permute-start.2 = (f32[4,128,128]{2,1,0:T(8,128)S(1)}, f32[4,128,128]{2,1,0:T(8,128)S(1)}, u32[]{:S(2)}, u32[]{:S(2)}) collective-permute-start(f32[4,128,128]{2,1,0:T(8,128)S(1)} %get-tuple-element.452), channel_id=1, source_target_pairs={{0,1},{1,2},{2,3},{4,5},{5,6},{6,7},{8,9},{9,10},{10,11},{12,13},{... | collective-permute-start | bytes 786440 | tf_op jit(solution)/shard_map/while/body/eval_jaxpr/ppermute | solution.py:14
  294.7 8.9 %collective-permute-start.3 = (f32[4,128,128]{2,1,0:T(8,128)}, f32[4,128,128]{2,1,0:T(8,128)S(1)}, u32[]{:S(2)}, u32[]{:S(2)}) collective-permute-start(f32[4,128,128]{2,1,0:T(8,128)} %get-tuple-element.455), channel_id=1, source_target_pairs={{1,0},{2,1},{3,2},{5,4},{6,5},{7,6},{9,8},{10,9},{11,10},{13,12},{... | collective-permute-start | bytes 786440 | tf_op jit(solution)/shard_map/while/body/eval_jaxpr/ppermute | solution.py:17
  309.4 6.2 %collective-permute-start.2 = (f32[4,128,128]{2,1,0:T(8,128)S(1)}, f32[4,128,128]{2,1,0:T(8,128)S(1)}, u32[]{:S(2)}, u32[]{:S(2)}) collective-permute-start(f32[4,128,128]{2,1,0:T(8,128)S(1)} %get-tuple-element.452), channel_id=1, source_target_pairs={{0,1},{1,2},{2,3},{4,5},{5,6},{6,7},{8,9},{9,10},{10,11},{12,13},{... | collective-permute-start | bytes 786440 | tf_op jit(solution)/shard_map/while/body/eval_jaxpr/ppermute | solution.py:14
  311.7 8.5 %collective-permute-start.3 = (f32[4,128,128]{2,1,0:T(8,128)}, f32[4,128,128]{2,1,0:T(8,128)S(1)}, u32[]{:S(2)}, u32[]{:S(2)}) collective-permute-start(f32[4,128,128]{2,1,0:T(8,128)} %get-tuple-element.455), channel_id=1, source_target_pairs={{1,0},{2,1},{3,2},{5,4},{6,5},{7,6},{9,8},{10,9},{11,10},{13,12},{... | collective-permute-start | bytes 786440 | tf_op jit(solution)/shard_map/while/body/eval_jaxpr/ppermute | solution.py:17
  326.0 6.1 %collective-permute-start.2 = (f32[4,128,128]{2,1,0:T(8,128)S(1)}, f32[4,128,128]{2,1,0:T(8,128)S(1)}, u32[]{:S(2)}, u32[]{:S(2)}) collective-permute-start(f32[4,128,128]{2,1,0:T(8,128)S(1)} %get-tuple-element.452), channel_id=1, source_target_pairs={{0,1},{1,2},{2,3},{4,5},{5,6},{6,7},{8,9},{9,10},{10,11},{12,13},{... | collective-permute-start | bytes 786440 | tf_op jit(solution)/shard_map/while/body/eval_jaxpr/ppermute | solution.py:14
  328.2 8.5 %collective-permute-start.3 = (f32[4,128,128]{2,1,0:T(8,128)}, f32[4,128,128]{2,1,0:T(8,128)S(1)}, u32[]{:S(2)}, u32[]{:S(2)}) collective-permute-start(f32[4,128,128]{2,1,0:T(8,128)} %get-tuple-element.455), channel_id=1, source_target_pairs={{1,0},{2,1},{3,2},{5,4},{6,5},{7,6},{9,8},{10,9},{11,10},{13,12},{... | collective-permute-start | bytes 786440 | tf_op jit(solution)/shard_map/while/body/eval_jaxpr/ppermute | solution.py:17
  342.6 5.8 %collective-permute-start.2 = (f32[4,128,128]{2,1,0:T(8,128)S(1)}, f32[4,128,128]{2,1,0:T(8,128)S(1)}, u32[]{:S(2)}, u32[]{:S(2)}) collective-permute-start(f32[4,128,128]{2,1,0:T(8,128)S(1)} %get-tuple-element.452), channel_id=1, source_target_pairs={{0,1},{1,2},{2,3},{4,5},{5,6},{6,7},{8,9},{9,10},{10,11},{12,13},{... | collective-permute-start | bytes 786440 | tf_op jit(solution)/shard_map/while/body/eval_jaxpr/ppermute | solution.py:14
  344.5 8.5 %collective-permute-start.3 = (f32[4,128,128]{2,1,0:T(8,128)}, f32[4,128,128]{2,1,0:T(8,128)S(1)}, u32[]{:S(2)}, u32[]{:S(2)}) collective-permute-start(f32[4,128,128]{2,1,0:T(8,128)} %get-tuple-element.455), channel_id=1, source_target_pairs={{1,0},{2,1},{3,2},{5,4},{6,5},{7,6},{9,8},{10,9},{11,10},{13,12},{... | collective-permute-start | bytes 786440 | tf_op jit(solution)/shard_map/while/body/eval_jaxpr/ppermute | solution.py:17
  (42 other events, 409.3 us)
Sparse Core Ops, SparseCore 0:
  360.9 34.2 reduce-scatter.1
where the time goes:
time: 404 us; the launch traced here: 402 us
  waiting for transfers between devices  139 us (34%)
  other arithmetic  120 us (30%)
  starting transfers between devices  58.4 us (14%)
  local copies, waits for them, and re-layouts  54.8 us (14%)
  blocking collectives  14.8 us (4%)
  between operations  14.2 us (4%)
    ppermute x16, waiting for transfers between devices, extended_2(): lax.ppermute(lax.slice_in_dim(block, 0, width, axis=dim), axis, backward)  64.2 us
    scatter-add x1, other arithmetic, injections(): buffer.at[where_to.reshape(-1)].add(values.reshape(-1), mode='drop')  46.9 us
    ppermute x16, waiting for transfers between devices, extended_2(): lax.ppermute(lax.slice_in_dim(block, block.shape[dim] - width, None, axis...  40.5 us
    ppermute x16, starting transfers between devices, extended_2(): lax.ppermute(lax.slice_in_dim(block, block.shape[dim] - width, None, axis...  37.7 us
    reduce_scatter x1, waiting for transfers between devices, body(): lax.psum_scatter(total * scale, 'shot', scatter_dimension=1, tiled=True)  34.4 us
    while x128, local copies, waits for them, and re-layouts  30.9 us
    add x8, other arithmetic, backward(): return ((cur, nxt + added, total + cur * lapl_t), None)  29.8 us
    dynamic_update_slice x8, other arithmetic, body(): _, stored = lax.scan(forward, (state_before[0], state_now[0]), wave)  26.3 us
  transfers between devices with their start and end apart: 33, of which 33 were waited for; matrix products, arithmetic and copies ran while one was open for 4% of the time, Pallas kernels for 0%

commit v1 on v0

v1 whole, which is shorter than its diff:
```python
import functools

import jax
import jax.numpy as jnp
import ml_dtypes
import numpy as np
from jax import lax
from jax.experimental import pallas as pl
from jax.experimental.pallas import tpu as pltpu
from jax.sharding import PartitionSpec as P

weights = (-205.0 / 72.0, 8.0 / 5.0, -1.0 / 5.0, 8.0 / 315.0, -1.0 / 560.0)
reach = 4
VMEM = pltpu.VMEM
SMEM = pltpu.SMEM
limit = 20 * 1024 * 1024


def band(width, centre):
    out = np.zeros((width, width), np.float64)
    for k in range(1, reach + 1):
        out += weights[k] * (np.eye(width, k=k) + np.eye(width, k=-k))
    out += centre * np.eye(width)
    high = out.astype(np.float32).astype(ml_dtypes.bfloat16)
    low = (out - high.astype(np.float64)).astype(np.float32).astype(ml_dtypes.bfloat16)
    return high, low


def band_right(width):
    high, low = band(width, 3.0 * weights[0])
    return np.block([[high, low], [high, np.zeros_like(low)]])


def band_left(width):
    high, low = band(width, 0.0)
    return np.block([[high, high], [low, np.zeros_like(low)]])


def split(v):
    high = v.astype(jnp.bfloat16)
    low = (v - high.astype(jnp.float32)).astype(jnp.bfloat16)
    return high, low


def fill_halo(parity, even, odd, halo):
    @pl.when(parity == 0)
    def _():
        halo[:reach] = odd[...]
        halo[reach:] = even[...]

    @pl.when(parity != 0)
    def _():
        halo[:reach] = even[...]
        halo[reach:] = odd[...]


def emit_edges(parity, field, even, odd):
    count = field.shape[0]

    @pl.when(parity == 0)
    def _():
        even[...] = field[count - reach :]
        odd[...] = field[:reach]

    @pl.when(parity != 0)
    def _():
        even[...] = field[:reach]
        odd[...] = field[count - reach :]


def laplace_planes(cur, halo, right, left, put):
    count, width_y, width_z = cur.shape

    def plane(i):
        if i < 0:
            return halo[reach + i]
        if i >= count:
            return halo[reach + i - count]
        return cur[i]

    for x in range(0, count, 2):
        v = [cur[x], cur[x + 1]]
        (h0, l0), (h1, l1) = split(v[0]), split(v[1])
        rows = jnp.concatenate(
            [jnp.concatenate([h0, l0], axis=1), jnp.concatenate([h1, l1], axis=1)], axis=0
        )
        along = jnp.dot(rows, right[...], preferred_element_type=jnp.float32)
        cols = jnp.concatenate(
            [jnp.concatenate([h0, h1], axis=1), jnp.concatenate([l0, l1], axis=1)], axis=0
        )
        across = jnp.dot(left[...], cols, preferred_element_type=jnp.float32)
        for j in range(2):
            rows_j = slice(j * width_y, (j + 1) * width_y)
            lanes_j = slice(j * width_z, (j + 1) * width_z)
            lap = along[rows_j, :width_z] + along[rows_j, width_z:]
            lap = lap + (across[:width_y, lanes_j] + across[width_y:, lanes_j])
            for k in range(1, reach + 1):
                lap = lap + weights[k] * (plane(x + j + k) + plane(x + j - k))
            put(x + j, v[j], lap)


def forward_kernel(parts, *refs):
    it = iter(refs)
    meta, wave, cur, even, odd, right, left = [next(it) for _ in range(7)]
    moves, stores, adds, opens = parts["moves"], parts["stores"], parts["adds"], parts["opens"]
    prev, speed = (next(it), next(it)) if moves else (None, None)
    late = next(it) if adds else None
    acc_in = next(it) if adds and not opens else None
    first, lap_first = (next(it), next(it)) if not moves else (None, None)
    nxt, even_out, odd_out = [next(it) for _ in range(3)] if moves else (None,) * 3
    lap_out = next(it) if stores else None
    acc_out = next(it) if adds and moves else None
    send, keep = (next(it), next(it)) if not moves else (None, None)
    halo = next(it)
    total = next(it) if not moves else None
    fill_halo(meta[0], even, odd, halo)

    def put(x, v, lap):
        if moves:
            nxt[x] = 2.0 * v - prev[x] + speed[x] * lap
        if stores:
            lap_out[x] = lap
        if adds:
            value = lap * late[x]
            if not opens:
                value = value + acc_in[x]
            if moves:
                acc_out[x] = value
            else:
                total[x] = (value + first[x] * lap_first[x]) * parts["scale"]

    laplace_planes(cur, halo, right, left, put)
    if moves:
        row, col, lane = meta[1], meta[2], meta[3]

        @pl.when((row >= 0) & (row < cur.shape[0]))
        def _():
            tile = pl.ds(pl.multiple_of((col // 8) * 8, 8), 8)
            shape = (8, cur.shape[2])
            hit = (lax.broadcasted_iota(jnp.int32, shape, 0) == col % 8) & (
                lax.broadcasted_iota(jnp.int32, shape, 1) == lane
            )
            nxt[row, tile, :] = nxt[row, tile, :] + jnp.where(hit, wave[parts["step"]], 0.0)

        emit_edges(meta[0], nxt, even_out, odd_out)
    else:
        chunk = send.shape[2]
        mine = meta[4] % 2
        for j in range(send.shape[0]):
            away = pl.multiple_of((2 * j + 1 - mine) * chunk, 8)
            here = pl.multiple_of((2 * j + mine) * chunk, 8)
            send[j] = total[:, pl.ds(away, chunk), :]
            keep[j] = total[:, pl.ds(here, chunk), :]


def adjoint_kernel(parts, *refs):
    it = iter(refs)
    meta, cur, later, speed, even, odd, inject, right, left = [next(it) for _ in range(9)]
    adds, edges = parts["adds"], parts["edges"]
    lap_of, acc_in = (next(it), next(it)) if adds else (None, None)
    nxt = next(it)
    even_out, odd_out = (next(it), next(it)) if edges else (None, None)
    acc_out = next(it) if adds else None
    halo = next(it)
    fill_halo(meta[0], even, odd, halo)
    width_y = cur.shape[1]

    def put(x, v, lap):
        added = inject[pl.ds(x * width_y * 8 + parts["time"], width_y, stride=8), :]
        nxt[x] = 2.0 * v - later[x] + speed[x] * lap + added
        if adds:
            acc_out[x] = acc_in[x] + v * lap_of[x]

    laplace_planes(cur, halo, right, left, put)
    if edges:
        emit_edges(meta[0], nxt, even_out, odd_out)


def scatter_kernel(meta, where_to, blocks, out):
    slabs, steps, per = blocks.shape
    group = 4
    zero_rows = 64 * 8

    @pl.loop(0, out.shape[0] // zero_rows)
    def _(i):
        out[pl.ds(pl.multiple_of(i * zero_rows, 8), zero_rows), :] = jnp.zeros(
            (zero_rows, 128), jnp.float32
        )

    rest = out.shape[0] % zero_rows
    if rest:
        out[out.shape[0] - rest :, :] = jnp.zeros((rest, 128), jnp.float32)
    lanes = lax.broadcasted_iota(jnp.int32, (8, 128), 1)
    for d in range(slabs):
        base = (meta[5] ^ d) * per
        for part in range(per // 128):
            block = blocks[d, :, part * 128 : (part + 1) * 128]

            @pl.loop(0, 128 // group)
            def _(i):
                tiles, terms, slots = [], [], []
                for u in range(group):
                    j = i * group + u
                    flat = where_to[base + part * 128 + j]
                    lane = flat & 127
                    tile = flat >> 7
                    moved = pltpu.roll(block, (lane - j) & 127, 1)
                    tiles.append(tile)
                    terms.append(jnp.where(lanes == lane, moved, 0.0))
                    slots.append(pl.ds(pl.multiple_of(tile * 8, 8), 8))
                held = [out[slot, :] for slot in slots]
                for u in range(group):
                    value = held[u] + terms[u]
                    for w in range(u):
                        same = (tiles[w] == tiles[u]).astype(jnp.float32)
                        value = value + terms[w] * same
                    held[u] = value
                for u in range(group):
                    out[slots[u], :] = held[u]


def vmem(*shape):
    return VMEM(shape, jnp.float32)


def vmem_spec():
    return pl.BlockSpec(memory_space=VMEM)


def smem_spec():
    return pl.BlockSpec(memory_space=SMEM)


def call(kernel, specs, outs, scratch, name, cycles):
    return pl.pallas_call(
        kernel,
        out_shape=outs,
        in_specs=specs,
        out_specs=jax.tree.map(lambda _: vmem_spec(), outs),
        scratch_shapes=scratch,
        compiler_params=pltpu.CompilerParams(vmem_limit_bytes=limit),
        cost_estimate=pl.CostEstimate(flops=cycles, bytes_accessed=4 << 20, transcendentals=0),
        name=name,
    )


def pair_swap(count, start):
    pairs = []
    for i in range(start, count - 1, 2):
        pairs += [(i, i + 1), (i + 1, i)]
    return pairs


def body(
    state_before,
    state_now,
    adjoint_after,
    adjoint_now,
    speed_term,
    wavelet,
    source,
    receivers,
    traces,
):
    count, width_y, width_z = speed_term.shape
    steps = wavelet.shape[1]
    slabs = lax.axis_size("slab")
    shots = lax.axis_size("shot")
    slab = lax.axis_index("slab")
    shot = lax.axis_index("shot")
    half = steps // 2
    scale = 1.0 / (8.0 * steps)
    parity = slab % 2
    even_pairs, odd_pairs = pair_swap(slabs, 0), pair_swap(slabs, 1)

    def swap(edges):
        return (
            lax.ppermute(edges[0], "slab", even_pairs),
            lax.ppermute(edges[1], "slab", odd_pairs),
        )

    def first_edges(field):
        top = count - reach
        return (
            lax.dynamic_slice_in_dim(field, jnp.where(parity == 0, top, 0), reach, 0),
            lax.dynamic_slice_in_dim(field, jnp.where(parity == 0, 0, top), reach, 0),
        )

    right = jnp.asarray(band_right(width_z))
    left = jnp.asarray(band_left(width_y))
    spot = source[0]
    meta = jnp.stack([parity, spot[0] - slab * count, spot[1], spot[2], shot, slab]).astype(jnp.int32)
    wave = wavelet[0]
    listen = receivers[0]
    depth = listen[0] - slab * count
    inside = (depth >= 0) & (depth < count)
    flat = depth * (width_y * width_z) + listen[1] * width_z + listen[2]
    where_to = jnp.where(inside, flat, count * width_y * width_z)

    blocks = traces[0][None]
    bit = 1
    while bit < slabs:
        other = lax.ppermute(blocks, "slab", [(i, i ^ bit) for i in range(slabs)])
        blocks = jnp.concatenate([blocks, other], axis=0)
        bit *= 2

    field = vmem(count, width_y, width_z)
    edge = vmem(reach, width_y, width_z)
    halo = vmem(2 * reach, width_y, width_z)
    p = {-1: state_before[0], 0: state_now[0]}
    q = {steps + 1: adjoint_after[0], steps: adjoint_now[0]}
    laps = {}
    acc = None
    p_halo = swap(first_edges(p[0]))
    q_halo = swap(first_edges(q[steps]))
    inject = call(
        scatter_kernel,
        [smem_spec(), smem_spec(), vmem_spec()],
        vmem((count * width_y + 1) * 8, width_z),
        [],
        "receivers",
        1000,
    )(meta, where_to, blocks)

    for k in range(steps):
        last = k == steps - 1
        parts = dict(moves=not last, stores=k < half, adds=k >= half, opens=k == half, step=k, scale=scale)
        args = [meta, wave, p[k], *p_halo, right, left]
        outs, scratch = [], [halo]
        if not last:
            args += [p[k - 1], speed_term]
            outs += [field, edge, edge]
        if parts["stores"]:
            outs += [field]
        if parts["adds"]:
            args += [q[k + 1]]
            if not parts["opens"]:
                args += [acc]
            if not last:
                outs += [field]
        if last:
            args += [q[1], laps[0]]
            piece = jax.ShapeDtypeStruct((shots // 2, count, width_y // shots, width_z), jnp.float32)
            outs += [piece, piece]
            scratch = scratch + [field]
        specs = [smem_spec(), smem_spec()] + [vmem_spec()] * (len(args) - 2)
        got = call(functools.partial(forward_kernel, parts), specs, outs, scratch, "forward", 1000)(*args)
        if not last:
            p[k + 1] = got[0]
            p_halo = swap(got[1:3])
            if parts["stores"]:
                laps[k] = got[3]
            else:
                acc = got[3]
        else:
            send, kept = got
            arrived = lax.ppermute(send, "shot", [(i, i ^ 1) for i in range(shots)])
            paired = kept + arrived
            mine = shot // 2
            gradient = lax.dynamic_index_in_dim(paired, mine, 0, keepdims=False)
            for m in range(1, shots // 2):
                piece = lax.dynamic_index_in_dim(paired, mine ^ m, 0, keepdims=False)
                gradient = gradient + lax.ppermute(
                    piece, "shot", [(i, i ^ (2 * m)) for i in range(shots)]
                )

        t = steps - 1 - k
        parts = dict(adds=k >= half and not last, edges=not last, time=t)
        args = [meta, q[t + 1], q[t + 2], speed_term, *q_halo, inject, right, left]
        outs = [jax.ShapeDtypeStruct((count, width_y, width_z), jnp.float32) if last else field]
        if parts["adds"]:
            args += [laps[t], acc]
        if not last:
            outs += [edge, edge]
        if parts["adds"]:
            outs += [field]
        specs = [smem_spec()] + [vmem_spec()] * (len(args) - 1)
        got = call(functools.partial(adjoint_kernel, parts), specs, outs, [halo], "adjoint", 1000)(*args)
        q[t] = got[0]
        if not last:
            q_halo = swap(got[1:3])
        if parts["adds"]:
            acc = got[3]

    return (q[0][None], q[1][None], gradient)


def solution(mesh):
    return jax.shard_map(
        body,
        mesh=mesh,
        in_specs=(
            P("shot", "slab", None, None),
            P("shot", "slab", None, None),
            P("shot", "slab", None, None),
            P("shot", "slab", None, None),
            P("slab", None, None),
            P("shot", None),
            P("shot", None),
            P("shot", None, None),
            P("shot", None, "slab"),
        ),
        out_specs=(
            P("shot", "slab", None, None),
            P("shot", "slab", None, None),
            P("slab", "shot", None),
        ),
        check_vma=False,
    )
```

time: 404 us -> 158 us (0.39)
  waiting for transfers between devices: 139 us -> 2.63 us
  other arithmetic: 120 us -> 5.13 us
  Pallas kernels: 0 us -> 57.3 us
  local copies, waits for them, and re-layouts: 54.8 us -> 20.6 us
  blocking collectives: 14.8 us -> 0 us
  between operations: 14.2 us -> 1.85 us
  starting transfers between devices: 58.4 us -> 69.5 us
    ppermute x32 -> x38, waiting for transfers between devices: 105 us -> 2.63 us  [the longest x16 1.82 us: swap(): lax.ppermute(edges[0], 'slab', even_pairs)]
    pallas_call x0 -> x17, Pallas kernels: none -> 57.3 us  [the longest x1 20.6 us: body(): call(scatter_kernel, [smem_spec(), smem_spec(), vmem_spec()], vmem((count...]
    scatter-add x1 -> x0, other arithmetic: 46.9 us -> none  [injections(): buffer.at[where_to.reshape(-1)].add(values.reshape(-1), mode='drop')]
    add x16 -> x2, other arithmetic: 41.6 us -> 2.99 us  [the longest x1 1.72 us: body(): gradient + lax.ppermute(piece, 'shot', [(i, i ^ 2 * m) for i in range(sho...]
    reduce_scatter x1 -> x0, waiting for transfers between devices: 34.4 us -> none  [body(): lax.psum_scatter(total * scale, 'shot', scatter_dimension=1, tiled=True)]
    while x128 -> x0, local copies, waits for them, and re-layouts: 30.9 us -> none
    dynamic_update_slice x8 -> x0, other arithmetic: 26.3 us -> none  [body(): _, stored = lax.scan(forward, (state_before[0], state_now[0]), wave)]
    all_gather x1 -> x0, blocking collectives: 14.8 us -> none  [body(): all_traces = lax.all_gather(traces[0], 'slab', axis=1, tiled=True)]
  transfers between devices with their start and end apart: 33 -> 38, of which waited for: 33 -> 6; matrix products, arithmetic and copies ran while one was open for 4% -> 6% of each run, Pallas kernels for 0% -> 35%
where the time goes in v1:
time: 158 us; the launch traced here: 157 us
  starting transfers between devices  69.5 us (44%)
  Pallas kernels  57.3 us (36%)
  local copies, waits for them, and re-layouts  20.6 us (13%)
  other arithmetic  5.13 us (3%)
  waiting for transfers between devices  2.63 us (2%)
  between operations  1.85 us (1%)
    ppermute x16, starting transfers between devices, swap(): lax.ppermute(edges[0], 'slab', even_pairs)  52 us
    pallas_call x1, Pallas kernels, body(): call(scatter_kernel, [smem_spec(), smem_spec(), vmem_spec()], vmem((count...  20.6 us
    pallas_call x8, Pallas kernels, body(): call(functools.partial(adjoint_kernel, parts), specs, outs, [halo], 'adjo...  19.5 us
    pallas_call x8, Pallas kernels, body(): call(functools.partial(forward_kernel, parts), specs, outs, scratch, 'for...  17.2 us
    unnamed x35, local copies, waits for them, and re-layouts  13.3 us
    ppermute x16, starting transfers between devices, swap(): lax.ppermute(edges[1], 'slab', odd_pairs)  10.6 us
    dynamic_slice x2, local copies, waits for them, and re-layouts, first_edges(): lax.dynamic_slice_in_dim(field, jnp.where(parity == 0, 0, top), reach, 0)  3.78 us
    ppermute x3, starting transfers between devices, body(): lax.ppermute(piece, 'shot', [(i, i ^ 2 * m) for i in range(shots)])  3.49 us
  transfers between devices with their start and end apart: 38, of which 6 were waited for; matrix products, arithmetic and copies ran while one was open for 6% of the time, Pallas kernels for 35%

profile of v1, /device:TPU:0, one launch (start us, length us, event | category | flops | bytes accessed | tf_op | source)
XLA Modules:
  0.0 157.0 jit_solution(18244128388353761233)
XLA Ops:
  0.7 2.0 %dynamic-slice_bitcast_fusion = (f32[4,128,128]{2,1,0:T(8,128)}, f32[4,128,128]{2,1,0:T(8,128)}) fusion(f32[1,16,128,128]{3,2,1,0:T(8,128)} %param.12, s32[]{:T(128)S(6)} %select_n.43, s32[]{:T(128)S(6)} %select_n.42), kind=kLoop, calls=%fused_computation | loop fusion | bytes 1048584 | tf_op jit(solution)/shard_map/dynamic_slice | solution.py:286
  2.7 3.0 %collective-permute-start.12 = (f32[4,128,128]{2,1,0:T(8,128)}, f32[4,128,128]{2,1,0:T(8,128)S(1)}, u32[]{:S(2)}, u32[]{:S(2)}) collective-permute-start(f32[4,128,128]{2,1,0:T(8,128)} %get-tuple-element.112), channel_id=1, source_target_pairs={{0,1},{1,0},{2,3},{3,2},{4,5},{5,4},{6,7},{7,6},{8,9},{9,8},{10,11... | collective-permute-start | bytes 786440 | tf_op jit(solution)/shard_map/ppermute | solution.py:278
  8.2 4.4 %collective-permute-start = (f32[4,128,128]{2,1,0:T(8,128)}, f32[4,128,128]{2,1,0:T(8,128)S(1)}, u32[]{:S(2)}, u32[]{:S(2)}) collective-permute-start(f32[4,128,128]{2,1,0:T(8,128)} %get-tuple-element.114), channel_id=1, source_target_pairs={{0,1},{1,0},{2,3},{3,2},{4,5},{5,4},{6,7},{7,6},{8,9},{9,8},{10,11... | collective-permute-start | bytes 786440 | tf_op jit(solution)/shard_map/ppermute | solution.py:278
  19.4 2.1 %collective-permute-start.3 = (f32[2,8,256]{2,1,0:T(8,128)S(1)}, f32[2,8,256]{2,1,0:T(8,128)S(1)}, u32[]{:S(2)}, u32[]{:S(2)}) collective-permute-start(f32[2,8,256]{2,1,0:T(8,128)S(1)} %pad_maximum_fusion.1), channel_id=1, source_target_pairs={{0,2},{1,3},{2,0},{3,1},{4,6},{5,7},{6,4},{7,5},{8,10},{9,11},{10,... | collective-permute-start | bytes 49160 | tf_op jit(solution)/shard_map/ppermute | solution.py:303
  33.3 20.6 %receivers.1.refs_6_ = f32[16392,128]{1,0:T(8,128)S(1)} custom-call(s32[6]{0:T(128)S(1)} %stack.19.meta.refs_0_, s32[1024]{0:T(1024)S(1)} %bitcast.51, f32[4,8,256]{2,1,0:T(8,128)S(1)} %pad_maximum_fusion.blocks), custom_call_target="tpu_custom_call" | custom-call | flops 1000 | bytes 4194304 | tf_op jit(solution)/shard_map/receivers/pallas_call | solution.py:316
  54.0 2.0 %adjoint.8 = (f32[16,128,128]{2,1,0:T(8,128)S(1)}, f32[4,128,128]{2,1,0:T(8,128)S(1)}, f32[4,128,128]{2,1,0:T(8,128)S(1)}) custom-call(s32[6]{0:T(128)S(1)} %stack.19.meta.refs_0_, f32[16,128,128]{2,1,0:T(8,128)S(1)} %bitcast.36, f32[16,128,128]{2,1,0:T(8,128)S(1)} %bitcast.42, f32[16,128,128]{2,1,0:T(8,128)S(1)} %copy-done.3, ...), custom_call_target="tpu_custom_call" | custom-call | flops 1000 | bytes 4194304 | tf_op jit(solution)/shard_map/adjoint/pallas_call | solution.py:378
  56.0 2.8 %collective-permute-start.4 = (f32[4,128,128]{2,1,0:T(8,128)S(1)}, f32[4,128,128]{2,1,0:T(8,128)S(1)}, u32[]{:S(2)}, u32[]{:S(2)}) collective-permute-start(f32[4,128,128]{2,1,0:T(8,128)S(1)} %get-tuple-element.58), channel_id=1, source_target_pairs={{0,1},{1,0},{2,3},{3,2},{4,5},{5,4},{6,7},{7,6},{8,9},{9,8},{10,11... | collective-permute-start | bytes 786440 | tf_op jit(solution)/shard_map/ppermute | solution.py:278
  59.5 2.0 %forward.9 = (f32[16,128,128]{2,1,0:T(8,128)S(1)}, f32[4,128,128]{2,1,0:T(8,128)S(1)}, f32[4,128,128]{2,1,0:T(8,128)S(1)}, f32[16,128,128]{2,1,0:T(8,128)S(1)}) custom-call(s32[6]{0:T(128)S(1)} %stack.19.meta.refs_0_, f32[8]{0:T(128)S(1)} %bitcast.44, f32[16,128,128]{2,1,0:T(8,128)S(1)} %get-tuple-element.69.refs_2_.refs_7_, ...), custom_call_target="tpu_custom_call" | custom-call | flops 1000 | bytes 4194304 | tf_op jit(solution)/shard_map/forward/pallas_call | solution.py:347
  61.5 2.2 %collective-permute-start.16 = (f32[4,128,128]{2,1,0:T(8,128)S(1)}, f32[4,128,128]{2,1,0:T(8,128)S(1)}, u32[]{:S(2)}, u32[]{:S(2)}) collective-permute-start(f32[4,128,128]{2,1,0:T(8,128)S(1)} %get-tuple-element.73), channel_id=1, source_target_pairs={{0,1},{1,0},{2,3},{3,2},{4,5},{5,4},{6,7},{7,6},{8,9},{9,8},{10,11... | collective-permute-start | bytes 786440 | tf_op jit(solution)/shard_map/ppermute | solution.py:278
  64.5 2.3 %adjoint.9 = (f32[16,128,128]{2,1,0:T(8,128)S(1)}, f32[4,128,128]{2,1,0:T(8,128)S(1)}, f32[4,128,128]{2,1,0:T(8,128)S(1)}) custom-call(s32[6]{0:T(128)S(1)} %stack.19.meta.refs_0_, f32[16,128,128]{2,1,0:T(8,128)S(1)} %get-tuple-element.57.refs_1_.refs_2_.refs_9_, f32[16,128,128]{2,1,0:T(8,128)S(1)} %bitcast.37, f32[16,128,128]{2,1,0:T(8,128)S(1)} %copy-done.3, ...), custom_call_target="tpu_custom_call" | custom-call | flops 1000 | bytes 4194304 | tf_op jit(solution)/shard_map/adjoint/pallas_call | solution.py:378
  66.7 3.4 %collective-permute-start.6 = (f32[4,128,128]{2,1,0:T(8,128)S(1)}, f32[4,128,128]{2,1,0:T(8,128)S(1)}, u32[]{:S(2)}, u32[]{:S(2)}) collective-permute-start(f32[4,128,128]{2,1,0:T(8,128)S(1)} %get-tuple-element.61), channel_id=1, source_target_pairs={{0,1},{1,0},{2,3},{3,2},{4,5},{5,4},{6,7},{7,6},{8,9},{9,8},{10,11... | collective-permute-start | bytes 786440 | tf_op jit(solution)/shard_map/ppermute | solution.py:278
  72.7 3.8 %collective-permute-start.18 = (f32[4,128,128]{2,1,0:T(8,128)S(1)}, f32[4,128,128]{2,1,0:T(8,128)S(1)}, u32[]{:S(2)}, u32[]{:S(2)}) collective-permute-start(f32[4,128,128]{2,1,0:T(8,128)S(1)} %get-tuple-element.76), channel_id=1, source_target_pairs={{0,1},{1,0},{2,3},{3,2},{4,5},{5,4},{6,7},{7,6},{8,9},{9,8},{10,11... | collective-permute-start | bytes 786440 | tf_op jit(solution)/shard_map/ppermute | solution.py:278
  77.2 2.2 %adjoint.10 = (f32[16,128,128]{2,1,0:T(8,128)S(1)}, f32[4,128,128]{2,1,0:T(8,128)S(1)}, f32[4,128,128]{2,1,0:T(8,128)S(1)}) custom-call(s32[6]{0:T(128)S(1)} %stack.19.meta.refs_0_, f32[16,128,128]{2,1,0:T(8,128)S(1)} %get-tuple-element.60.refs_1_.refs_2_.refs_9_, f32[16,128,128]{2,1,0:T(8,128)S(1)} %get-tuple-element.57.refs_1_.refs_2_.refs_9_, ...), custom_call_target="tpu_custom_call" | custom-call | flops 1000 | bytes 4194304 | tf_op jit(solution)/shard_map/adjoint/pallas_call | solution.py:378
  79.4 2.4 %collective-permute-start.8 = (f32[4,128,128]{2,1,0:T(8,128)S(1)}, f32[4,128,128]{2,1,0:T(8,128)S(1)}, u32[]{:S(2)}, u32[]{:S(2)}) collective-permute-start(f32[4,128,128]{2,1,0:T(8,128)S(1)} %get-tuple-element.64), channel_id=1, source_target_pairs={{0,1},{1,0},{2,3},{3,2},{4,5},{5,4},{6,7},{7,6},{8,9},{9,8},{10,11... | collective-permute-start | bytes 786440 | tf_op jit(solution)/shard_map/ppermute | solution.py:278
  85.0 4.3 %collective-permute-start.20 = (f32[4,128,128]{2,1,0:T(8,128)S(1)}, f32[4,128,128]{2,1,0:T(8,128)S(1)}, u32[]{:S(2)}, u32[]{:S(2)}) collective-permute-start(f32[4,128,128]{2,1,0:T(8,128)S(1)} %get-tuple-element.80), channel_id=1, source_target_pairs={{0,1},{1,0},{2,3},{3,2},{4,5},{5,4},{6,7},{7,6},{8,9},{9,8},{10,11... | collective-permute-start | bytes 786440 | tf_op jit(solution)/shard_map/ppermute | solution.py:278
  90.0 2.4 %adjoint.11 = (f32[16,128,128]{2,1,0:T(8,128)S(1)}, f32[4,128,128]{2,1,0:T(8,128)S(1)}, f32[4,128,128]{2,1,0:T(8,128)S(1)}) custom-call(s32[6]{0:T(128)S(1)} %stack.19.meta.refs_0_, f32[16,128,128]{2,1,0:T(8,128)S(1)} %get-tuple-element.63.refs_1_.refs_9_.refs_2_, f32[16,128,128]{2,1,0:T(8,128)S(1)} %get-tuple-element.60.refs_1_.refs_2_.refs_9_, ...), custom_call_target="tpu_custom_call" | custom-call | flops 1000 | bytes 4194304 | tf_op jit(solution)/shard_map/adjoint/pallas_call | solution.py:378
  92.4 3.0 %collective-permute-start.10 = (f32[4,128,128]{2,1,0:T(8,128)S(1)}, f32[4,128,128]{2,1,0:T(8,128)S(1)}, u32[]{:S(2)}, u32[]{:S(2)}) collective-permute-start(f32[4,128,128]{2,1,0:T(8,128)S(1)} %get-tuple-element.67), channel_id=1, source_target_pairs={{0,1},{1,0},{2,3},{3,2},{4,5},{5,4},{6,7},{7,6},{8,9},{9,8},{10,11... | collective-permute-start | bytes 786440 | tf_op jit(solution)/shard_map/ppermute | solution.py:278
  96.2 2.0 %forward.12 = (f32[16,128,128]{2,1,0:T(8,128)S(1)}, f32[4,128,128]{2,1,0:T(8,128)S(1)}, f32[4,128,128]{2,1,0:T(8,128)S(1)}, f32[16,128,128]{2,1,0:T(8,128)S(1)}) custom-call(s32[6]{0:T(128)S(1)} %stack.19.meta.refs_0_, f32[8]{0:T(128)S(1)} %bitcast.47, f32[16,128,128]{2,1,0:T(8,128)S(1)} %get-tuple-element.79.refs_2_.refs_7_, ...), custom_call_target="tpu_custom_call" | custom-call | flops 1000 | bytes 4194304 | tf_op jit(solution)/shard_map/forward/pallas_call | solution.py:347
  98.2 4.2 %collective-permute-start.24 = (f32[4,128,128]{2,1,0:T(8,128)S(1)}, f32[4,128,128]{2,1,0:T(8,128)S(1)}, u32[]{:S(2)}, u32[]{:S(2)}) collective-permute-start(f32[4,128,128]{2,1,0:T(8,128)S(1)} %get-tuple-element.88), channel_id=1, source_target_pairs={{0,1},{1,0},{2,3},{3,2},{4,5},{5,4},{6,7},{7,6},{8,9},{9,8},{10,11... | collective-permute-start | bytes 786440 | tf_op jit(solution)/shard_map/ppermute | solution.py:278
  103.1 2.3 %adjoint.12 = (f32[16,128,128]{2,1,0:T(8,128)S(1)}, f32[4,128,128]{2,1,0:T(8,128)S(1)}, f32[4,128,128]{2,1,0:T(8,128)S(1)}, f32[16,128,128]{2,1,0:T(8,128)S(1)}) custom-call(s32[6]{0:T(128)S(1)} %stack.19.meta.refs_0_, f32[16,128,128]{2,1,0:T(8,128)S(1)} %get-tuple-element.66.refs_1_.refs_2_, f32[16,128,128]{2,1,0:T(8,128)S(1)} %get-tuple-element.63.refs_1_.refs_9_.refs_2_, ...), custom_call_target="tpu_custom_call" | custom-call | flops 1000 | bytes 4194304 | tf_op jit(solution)/shard_map/adjoint/pallas_call | solution.py:378
  105.4 3.0 %collective-permute-start.22 = (f32[4,128,128]{2,1,0:T(8,128)S(1)}, f32[4,128,128]{2,1,0:T(8,128)S(1)}, u32[]{:S(2)}, u32[]{:S(2)}) collective-permute-start(f32[4,128,128]{2,1,0:T(8,128)S(1)} %get-tuple-element.84), channel_id=1, source_target_pairs={{0,1},{1,0},{2,3},{3,2},{4,5},{5,4},{6,7},{7,6},{8,9},{9,8},{10,11... | collective-permute-start | bytes 786440 | tf_op jit(solution)/shard_map/ppermute | solution.py:278
  109.5 2.1 %forward.13 = (f32[16,128,128]{2,1,0:T(8,128)S(1)}, f32[4,128,128]{2,1,0:T(8,128)S(1)}, f32[4,128,128]{2,1,0:T(8,128)S(1)}, f32[16,128,128]{2,1,0:T(8,128)S(1)}) custom-call(s32[6]{0:T(128)S(1)} %stack.19.meta.refs_0_, f32[8]{0:T(128)S(1)} %bitcast.48, f32[16,128,128]{2,1,0:T(8,128)S(1)} %get-tuple-element.87.refs_2_.refs_7_, ...), custom_call_target="tpu_custom_call" | custom-call | flops 1000 | bytes 4194304 | tf_op jit(solution)/shard_map/forward/pallas_call | solution.py:347
  111.6 3.9 %collective-permute-start.28 = (f32[4,128,128]{2,1,0:T(8,128)S(1)}, f32[4,128,128]{2,1,0:T(8,128)S(1)}, u32[]{:S(2)}, u32[]{:S(2)}) collective-permute-start(f32[4,128,128]{2,1,0:T(8,128)S(1)} %get-tuple-element.97), channel_id=1, source_target_pairs={{0,1},{1,0},{2,3},{3,2},{4,5},{5,4},{6,7},{7,6},{8,9},{9,8},{10,11... | collective-permute-start | bytes 786440 | tf_op jit(solution)/shard_map/ppermute | solution.py:278
  116.2 2.3 %adjoint.13 = (f32[16,128,128]{2,1,0:T(8,128)S(1)}, f32[4,128,128]{2,1,0:T(8,128)S(1)}, f32[4,128,128]{2,1,0:T(8,128)S(1)}, f32[16,128,128]{2,1,0:T(8,128)S(1)}) custom-call(s32[6]{0:T(128)S(1)} %stack.19.meta.refs_0_, f32[16,128,128]{2,1,0:T(8,128)S(1)} %get-tuple-element.83.refs_1_.refs_2_, f32[16,128,128]{2,1,0:T(8,128)S(1)} %get-tuple-element.66.refs_1_.refs_2_, ...), custom_call_target="tpu_custom_call" | custom-call | flops 1000 | bytes 4194304 | tf_op jit(solution)/shard_map/adjoint/pallas_call | solution.py:378
  118.5 2.3 %collective-permute-start.26 = (f32[4,128,128]{2,1,0:T(8,128)S(1)}, f32[4,128,128]{2,1,0:T(8,128)S(1)}, u32[]{:S(2)}, u32[]{:S(2)}) collective-permute-start(f32[4,128,128]{2,1,0:T(8,128)S(1)} %get-tuple-element.93), channel_id=1, source_target_pairs={{0,1},{1,0},{2,3},{3,2},{4,5},{5,4},{6,7},{7,6},{8,9},{9,8},{10,11... | collective-permute-start | bytes 786440 | tf_op jit(solution)/shard_map/ppermute | solution.py:278
  121.6 2.1 %forward.14 = (f32[16,128,128]{2,1,0:T(8,128)S(1)}, f32[4,128,128]{2,1,0:T(8,128)S(1)}, f32[4,128,128]{2,1,0:T(8,128)S(1)}, f32[16,128,128]{2,1,0:T(8,128)S(1)}) custom-call(s32[6]{0:T(128)S(1)} %stack.19.meta.refs_0_, f32[8]{0:T(128)S(1)} %bitcast.49, f32[16,128,128]{2,1,0:T(8,128)S(1)} %get-tuple-element.96.refs_2_, ...), custom_call_target="tpu_custom_call" | custom-call | flops 1000 | bytes 4194304 | tf_op jit(solution)/shard_map/forward/pallas_call | solution.py:347
  123.7 3.7 %collective-permute-start.32 = (f32[4,128,128]{2,1,0:T(8,128)S(1)}, f32[4,128,128]{2,1,0:T(8,128)S(1)}, u32[]{:S(2)}, u32[]{:S(2)}) collective-permute-start(f32[4,128,128]{2,1,0:T(8,128)S(1)} %get-tuple-element.105), channel_id=1, source_target_pairs={{0,1},{1,0},{2,3},{3,2},{4,5},{5,4},{6,7},{7,6},{8,9},{9,8},{10,11... | collective-permute-start | bytes 786440 | tf_op jit(solution)/shard_map/ppermute | solution.py:278
  128.1 3.1 %adjoint.14 = (f32[16,128,128]{2,1,0:T(8,128)S(1)}, f32[4,128,128]{2,1,0:T(8,128)}, f32[4,128,128]{2,1,0:T(8,128)}, f32[16,128,128]{2,1,0:T(8,128)S(1)}) custom-call(s32[6]{0:T(128)S(1)} %stack.19.meta.refs_0_, f32[16,128,128]{2,1,0:T(8,128)S(1)} %get-tuple-element.92.refs_1_.refs_2_, f32[16,128,128]{2,1,0:T(8,128)S(1)} %get-tuple-element.83.refs_1_.refs_2_, ...), custom_call_target="tpu_custom_call" | custom-call | flops 1000 | bytes 4194304 | tf_op jit(solution)/shard_map/adjoint/pallas_call | solution.py:378
  131.8 3.1 %forward.15 = (f32[4,16,16,128]{3,2,1,0:T(8,128)}, f32[4,16,16,128]{3,2,1,0:T(8,128)S(1)}) custom-call(s32[6]{0:T(128)S(1)} %stack.19.meta.refs_0_, f32[8]{0:T(128)S(1)} %bitcast.50, f32[16,128,128]{2,1,0:T(8,128)S(1)} %get-tuple-element.104.refs_2_, f32[4,128,128]{2,1,0:T(8,128)S(1)} %collective-permute-done.32.refs_3_, ...), custom_call_target="tpu_custom_call" | custom-call | flops 1000 | bytes 4194304 | tf_op jit(solution)/shard_map/forward/pallas_call | solution.py:347
  135.7 3.9 %collective-permute-start.30 = (f32[4,128,128]{2,1,0:T(8,128)}, f32[4,128,128]{2,1,0:T(8,128)S(1)}, u32[]{:S(2)}, u32[]{:S(2)}) collective-permute-start(f32[4,128,128]{2,1,0:T(8,128)} %get-tuple-element.102), channel_id=1, source_target_pairs={{0,1},{1,0},{2,3},{3,2},{4,5},{5,4},{6,7},{7,6},{8,9},{9,8},{10,11... | collective-permute-start | bytes 786440 | tf_op jit(solution)/shard_map/ppermute | solution.py:278
  147.6 3.4 %copy-done.1 = f32[16392,128]{1,0:T(8,128)S(1)} copy-done((f32[16392,128]{1,0:T(8,128)S(1)}, f32[16392,128]{1,0:T(8,128)}, u32[]{:S(2)}) %copy-start.1) | copy-done | bytes 8392728
  152.2 3.1 %adjoint.15 = f32[16,128,128]{2,1,0:T(8,128)} custom-call(s32[6]{0:T(128)S(1)} %stack.19.meta.refs_0_, f32[16,128,128]{2,1,0:T(8,128)S(1)} %get-tuple-element.101.refs_1_.refs_9_, f32[16,128,128]{2,1,0:T(8,128)S(1)} %copy-done.11, f32[16,128,128]{2,1,0:T(8,128)S(1)} %copy-done.3, f32[4,128,128]{2,1,0:T(8,128)S(1)} %collective-permute-done.30.refs_4_, ...), custom_call_target="tpu_custom_call" | custom-call | flops 1000 | bytes 4194304 | tf_op jit(solution)/shard_map/adjoint/pallas_call | solution.py:378
  (106 shorter events, 45.9 us)
Async XLA Ops:
  2.7 18.8 %collective-permute-start.12 = (f32[4,128,128]{2,1,0:T(8,128)}, f32[4,128,128]{2,1,0:T(8,128)S(1)}, u32[]{:S(2)}, u32[]{:S(2)}) collective-permute-start(f32[4,128,128]{2,1,0:T(8,128)} %get-tuple-element.112), channel_id=1, source_target_pairs={{0,1},{1,0},{2,3},{3,2},{4,5},{5,4},{6,7},{7,6},{8,9},{9,8},{10,11... | collective-permute-start | bytes 786440 | tf_op jit(solution)/shard_map/ppermute | solution.py:278
  5.7 15.8 %collective-permute-start.13 = (f32[4,128,128]{2,1,0:T(8,128)}, f32[4,128,128]{2,1,0:T(8,128)S(1)}, u32[]{:S(2)}, u32[]{:S(2)}) collective-permute-start(f32[4,128,128]{2,1,0:T(8,128)} %get-tuple-element.111), channel_id=1, source_target_pairs={{1,2},{2,1},{5,6},{6,5},{9,10},{10,9},{13,14},{14,13},{17,18},{18,... | collective-permute-start | bytes 786440 | tf_op jit(solution)/shard_map/ppermute | solution.py:279
  8.2 45.8 %collective-permute-start = (f32[4,128,128]{2,1,0:T(8,128)}, f32[4,128,128]{2,1,0:T(8,128)S(1)}, u32[]{:S(2)}, u32[]{:S(2)}) collective-permute-start(f32[4,128,128]{2,1,0:T(8,128)} %get-tuple-element.114), channel_id=1, source_target_pairs={{0,1},{1,0},{2,3},{3,2},{4,5},{5,4},{6,7},{7,6},{8,9},{9,8},{10,11... | collective-permute-start | bytes 786440 | tf_op jit(solution)/shard_map/ppermute | solution.py:278
  12.5 41.4 %collective-permute-start.1 = (f32[4,128,128]{2,1,0:T(8,128)S(1)}, f32[4,128,128]{2,1,0:T(8,128)S(1)}, u32[]{:S(2)}, u32[]{:S(2)}) collective-permute-start(f32[4,128,128]{2,1,0:T(8,128)S(1)} %get-tuple-element.113), channel_id=1, source_target_pairs={{1,2},{2,1},{5,6},{6,5},{9,10},{10,9},{13,14},{14,13},{17,18},{18,... | collective-permute-start | bytes 786440 | tf_op jit(solution)/shard_map/ppermute | solution.py:279
  19.4 13.3 %collective-permute-start.3 = (f32[2,8,256]{2,1,0:T(8,128)S(1)}, f32[2,8,256]{2,1,0:T(8,128)S(1)}, u32[]{:S(2)}, u32[]{:S(2)}) collective-permute-start(f32[2,8,256]{2,1,0:T(8,128)S(1)} %pad_maximum_fusion.1), channel_id=1, source_target_pairs={{0,2},{1,3},{2,0},{3,1},{4,6},{5,7},{6,4},{7,5},{8,10},{9,11},{10,... | collective-permute-start | bytes 49160 | tf_op jit(solution)/shard_map/ppermute | solution.py:303
  29.6 30.0 %collective-permute-start.14 = (f32[4,128,128]{2,1,0:T(8,128)S(1)}, f32[4,128,128]{2,1,0:T(8,128)S(1)}, u32[]{:S(2)}, u32[]{:S(2)}) collective-permute-start(f32[4,128,128]{2,1,0:T(8,128)S(1)} %get-tuple-element.70), channel_id=1, source_target_pairs={{0,1},{1,0},{2,3},{3,2},{4,5},{5,4},{6,7},{7,6},{8,9},{9,8},{10,11... | collective-permute-start | bytes 786440 | tf_op jit(solution)/shard_map/ppermute | solution.py:278
  31.2 28.3 %collective-permute-start.15 = (f32[4,128,128]{2,1,0:T(8,128)S(1)}, f32[4,128,128]{2,1,0:T(8,128)S(1)}, u32[]{:S(2)}, u32[]{:S(2)}) collective-permute-start(f32[4,128,128]{2,1,0:T(8,128)S(1)} %get-tuple-element.71), channel_id=1, source_target_pairs={{1,2},{2,1},{5,6},{6,5},{9,10},{10,9},{13,14},{14,13},{17,18},{18,... | collective-permute-start | bytes 786440 | tf_op jit(solution)/shard_map/ppermute | solution.py:279
  56.0 8.4 %collective-permute-start.4 = (f32[4,128,128]{2,1,0:T(8,128)S(1)}, f32[4,128,128]{2,1,0:T(8,128)S(1)}, u32[]{:S(2)}, u32[]{:S(2)}) collective-permute-start(f32[4,128,128]{2,1,0:T(8,128)S(1)} %get-tuple-element.58), channel_id=1, source_target_pairs={{0,1},{1,0},{2,3},{3,2},{4,5},{5,4},{6,7},{7,6},{8,9},{9,8},{10,11... | collective-permute-start | bytes 786440 | tf_op jit(solution)/shard_map/ppermute | solution.py:278
  61.5 9.2 %collective-permute-start.16 = (f32[4,128,128]{2,1,0:T(8,128)S(1)}, f32[4,128,128]{2,1,0:T(8,128)S(1)}, u32[]{:S(2)}, u32[]{:S(2)}) collective-permute-start(f32[4,128,128]{2,1,0:T(8,128)S(1)} %get-tuple-element.73), channel_id=1, source_target_pairs={{0,1},{1,0},{2,3},{3,2},{4,5},{5,4},{6,7},{7,6},{8,9},{9,8},{10,11... | collective-permute-start | bytes 786440 | tf_op jit(solution)/shard_map/ppermute | solution.py:278
  63.8 7.0 %collective-permute-start.17 = (f32[4,128,128]{2,1,0:T(8,128)S(1)}, f32[4,128,128]{2,1,0:T(8,128)S(1)}, u32[]{:S(2)}, u32[]{:S(2)}) collective-permute-start(f32[4,128,128]{2,1,0:T(8,128)S(1)} %get-tuple-element.74), channel_id=1, source_target_pairs={{1,2},{2,1},{5,6},{6,5},{9,10},{10,9},{13,14},{14,13},{17,18},{18,... | collective-permute-start | bytes 786440 | tf_op jit(solution)/shard_map/ppermute | solution.py:279
  66.7 10.5 %collective-permute-start.6 = (f32[4,128,128]{2,1,0:T(8,128)S(1)}, f32[4,128,128]{2,1,0:T(8,128)S(1)}, u32[]{:S(2)}, u32[]{:S(2)}) collective-permute-start(f32[4,128,128]{2,1,0:T(8,128)S(1)} %get-tuple-element.61), channel_id=1, source_target_pairs={{0,1},{1,0},{2,3},{3,2},{4,5},{5,4},{6,7},{7,6},{8,9},{9,8},{10,11... | collective-permute-start | bytes 786440 | tf_op jit(solution)/shard_map/ppermute | solution.py:278
  70.1 7.1 %collective-permute-start.7 = (f32[4,128,128]{2,1,0:T(8,128)S(1)}, f32[4,128,128]{2,1,0:T(8,128)S(1)}, u32[]{:S(2)}, u32[]{:S(2)}) collective-permute-start(f32[4,128,128]{2,1,0:T(8,128)S(1)} %get-tuple-element.62), channel_id=1, source_target_pairs={{1,2},{2,1},{5,6},{6,5},{9,10},{10,9},{13,14},{14,13},{17,18},{18,... | collective-permute-start | bytes 786440 | tf_op jit(solution)/shard_map/ppermute | solution.py:279
  72.7 10.2 %collective-permute-start.18 = (f32[4,128,128]{2,1,0:T(8,128)S(1)}, f32[4,128,128]{2,1,0:T(8,128)S(1)}, u32[]{:S(2)}, u32[]{:S(2)}) collective-permute-start(f32[4,128,128]{2,1,0:T(8,128)S(1)} %get-tuple-element.76), channel_id=1, source_target_pairs={{0,1},{1,0},{2,3},{3,2},{4,5},{5,4},{6,7},{7,6},{8,9},{9,8},{10,11... | collective-permute-start | bytes 786440 | tf_op jit(solution)/shard_map/ppermute | solution.py:278
  79.4 10.5 %collective-permute-start.8 = (f32[4,128,128]{2,1,0:T(8,128)S(1)}, f32[4,128,128]{2,1,0:T(8,128)S(1)}, u32[]{:S(2)}, u32[]{:S(2)}) collective-permute-start(f32[4,128,128]{2,1,0:T(8,128)S(1)} %get-tuple-element.64), channel_id=1, source_target_pairs={{0,1},{1,0},{2,3},{3,2},{4,5},{5,4},{6,7},{7,6},{8,9},{9,8},{10,11... | collective-permute-start | bytes 786440 | tf_op jit(solution)/shard_map/ppermute | solution.py:278
  81.9 8.1 %collective-permute-start.9 = (f32[4,128,128]{2,1,0:T(8,128)S(1)}, f32[4,128,128]{2,1,0:T(8,128)S(1)}, u32[]{:S(2)}, u32[]{:S(2)}) collective-permute-start(f32[4,128,128]{2,1,0:T(8,128)S(1)} %get-tuple-element.65), channel_id=1, source_target_pairs={{1,2},{2,1},{5,6},{6,5},{9,10},{10,9},{13,14},{14,13},{17,18},{18,... | collective-permute-start | bytes 786440 | tf_op jit(solution)/shard_map/ppermute | solution.py:279
  85.0 11.2 %collective-permute-start.20 = (f32[4,128,128]{2,1,0:T(8,128)S(1)}, f32[4,128,128]{2,1,0:T(8,128)S(1)}, u32[]{:S(2)}, u32[]{:S(2)}) collective-permute-start(f32[4,128,128]{2,1,0:T(8,128)S(1)} %get-tuple-element.80), channel_id=1, source_target_pairs={{0,1},{1,0},{2,3},{3,2},{4,5},{5,4},{6,7},{7,6},{8,9},{9,8},{10,11... | collective-permute-start | bytes 786440 | tf_op jit(solution)/shard_map/ppermute | solution.py:278
  89.3 6.9 %collective-permute-start.21 = (f32[4,128,128]{2,1,0:T(8,128)S(1)}, f32[4,128,128]{2,1,0:T(8,128)S(1)}, u32[]{:S(2)}, u32[]{:S(2)}) collective-permute-start(f32[4,128,128]{2,1,0:T(8,128)S(1)} %get-tuple-element.81), channel_id=1, source_target_pairs={{1,2},{2,1},{5,6},{6,5},{9,10},{10,9},{13,14},{14,13},{17,18},{18,... | collective-permute-start | bytes 786440 | tf_op jit(solution)/shard_map/ppermute | solution.py:279
  92.4 10.7 %collective-permute-start.10 = (f32[4,128,128]{2,1,0:T(8,128)S(1)}, f32[4,128,128]{2,1,0:T(8,128)S(1)}, u32[]{:S(2)}, u32[]{:S(2)}) collective-permute-start(f32[4,128,128]{2,1,0:T(8,128)S(1)} %get-tuple-element.67), channel_id=1, source_target_pairs={{0,1},{1,0},{2,3},{3,2},{4,5},{5,4},{6,7},{7,6},{8,9},{9,8},{10,11... | collective-permute-start | bytes 786440 | tf_op jit(solution)/shard_map/ppermute | solution.py:278
  95.3 7.8 %collective-permute-start.11 = (f32[4,128,128]{2,1,0:T(8,128)S(1)}, f32[4,128,128]{2,1,0:T(8,128)S(1)}, u32[]{:S(2)}, u32[]{:S(2)}) collective-permute-start(f32[4,128,128]{2,1,0:T(8,128)S(1)} %get-tuple-element.68), channel_id=1, source_target_pairs={{1,2},{2,1},{5,6},{6,5},{9,10},{10,9},{13,14},{14,13},{17,18},{18,... | collective-permute-start | bytes 786440 | tf_op jit(solution)/shard_map/ppermute | solution.py:279
  98.2 11.3 %collective-permute-start.24 = (f32[4,128,128]{2,1,0:T(8,128)S(1)}, f32[4,128,128]{2,1,0:T(8,128)S(1)}, u32[]{:S(2)}, u32[]{:S(2)}) collective-permute-start(f32[4,128,128]{2,1,0:T(8,128)S(1)} %get-tuple-element.88), channel_id=1, source_target_pairs={{0,1},{1,0},{2,3},{3,2},{4,5},{5,4},{6,7},{7,6},{8,9},{9,8},{10,11... | collective-permute-start | bytes 786440 | tf_op jit(solution)/shard_map/ppermute | solution.py:278
  102.4 7.1 %collective-permute-start.25 = (f32[4,128,128]{2,1,0:T(8,128)S(1)}, f32[4,128,128]{2,1,0:T(8,128)S(1)}, u32[]{:S(2)}, u32[]{:S(2)}) collective-permute-start(f32[4,128,128]{2,1,0:T(8,128)S(1)} %get-tuple-element.89), channel_id=1, source_target_pairs={{1,2},{2,1},{5,6},{6,5},{9,10},{10,9},{13,14},{14,13},{17,18},{18,... | collective-permute-start | bytes 786440 | tf_op jit(solution)/shard_map/ppermute | solution.py:279
  105.4 10.8 %collective-permute-start.22 = (f32[4,128,128]{2,1,0:T(8,128)S(1)}, f32[4,128,128]{2,1,0:T(8,128)S(1)}, u32[]{:S(2)}, u32[]{:S(2)}) collective-permute-start(f32[4,128,128]{2,1,0:T(8,128)S(1)} %get-tuple-element.84), channel_id=1, source_target_pairs={{0,1},{1,0},{2,3},{3,2},{4,5},{5,4},{6,7},{7,6},{8,9},{9,8},{10,11... | collective-permute-start | bytes 786440 | tf_op jit(solution)/shard_map/ppermute | solution.py:278
  108.4 7.8 %collective-permute-start.23 = (f32[4,128,128]{2,1,0:T(8,128)S(1)}, f32[4,128,128]{2,1,0:T(8,128)S(1)}, u32[]{:S(2)}, u32[]{:S(2)}) collective-permute-start(f32[4,128,128]{2,1,0:T(8,128)S(1)} %get-tuple-element.85), channel_id=1, source_target_pairs={{1,2},{2,1},{5,6},{6,5},{9,10},{10,9},{13,14},{14,13},{17,18},{18,... | collective-permute-start | bytes 786440 | tf_op jit(solution)/shard_map/ppermute | solution.py:279
  111.6 10.0 %collective-permute-start.28 = (f32[4,128,128]{2,1,0:T(8,128)S(1)}, f32[4,128,128]{2,1,0:T(8,128)S(1)}, u32[]{:S(2)}, u32[]{:S(2)}) collective-permute-start(f32[4,128,128]{2,1,0:T(8,128)S(1)} %get-tuple-element.97), channel_id=1, source_target_pairs={{0,1},{1,0},{2,3},{3,2},{4,5},{5,4},{6,7},{7,6},{8,9},{9,8},{10,11... | collective-permute-start | bytes 786440 | tf_op jit(solution)/shard_map/ppermute | solution.py:278
  118.5 9.6 %collective-permute-start.26 = (f32[4,128,128]{2,1,0:T(8,128)S(1)}, f32[4,128,128]{2,1,0:T(8,128)S(1)}, u32[]{:S(2)}, u32[]{:S(2)}) collective-permute-start(f32[4,128,128]{2,1,0:T(8,128)S(1)} %get-tuple-element.93), channel_id=1, source_target_pairs={{0,1},{1,0},{2,3},{3,2},{4,5},{5,4},{6,7},{7,6},{8,9},{9,8},{10,11... | collective-permute-start | bytes 786440 | tf_op jit(solution)/shard_map/ppermute | solution.py:278
  120.8 7.3 %collective-permute-start.27 = (f32[4,128,128]{2,1,0:T(8,128)S(1)}, f32[4,128,128]{2,1,0:T(8,128)S(1)}, u32[]{:S(2)}, u32[]{:S(2)}) collective-permute-start(f32[4,128,128]{2,1,0:T(8,128)S(1)} %get-tuple-element.94), channel_id=1, source_target_pairs={{1,2},{2,1},{5,6},{6,5},{9,10},{10,9},{13,14},{14,13},{17,18},{18,... | collective-permute-start | bytes 786440 | tf_op jit(solution)/shard_map/ppermute | solution.py:279
  123.7 8.1 %collective-permute-start.32 = (f32[4,128,128]{2,1,0:T(8,128)S(1)}, f32[4,128,128]{2,1,0:T(8,128)S(1)}, u32[]{:S(2)}, u32[]{:S(2)}) collective-permute-start(f32[4,128,128]{2,1,0:T(8,128)S(1)} %get-tuple-element.105), channel_id=1, source_target_pairs={{0,1},{1,0},{2,3},{3,2},{4,5},{5,4},{6,7},{7,6},{8,9},{9,8},{10,11... | collective-permute-start | bytes 786440 | tf_op jit(solution)/shard_map/ppermute | solution.py:278
  135.7 11.9 %collective-permute-start.30 = (f32[4,128,128]{2,1,0:T(8,128)}, f32[4,128,128]{2,1,0:T(8,128)S(1)}, u32[]{:S(2)}, u32[]{:S(2)}) collective-permute-start(f32[4,128,128]{2,1,0:T(8,128)} %get-tuple-element.102), channel_id=1, source_target_pairs={{0,1},{1,0},{2,3},{3,2},{4,5},{5,4},{6,7},{7,6},{8,9},{9,8},{10,11... | collective-permute-start | bytes 786440 | tf_op jit(solution)/shard_map/ppermute | solution.py:278
  139.6 8.0 %collective-permute-start.31 = (f32[4,128,128]{2,1,0:T(8,128)}, f32[4,128,128]{2,1,0:T(8,128)S(1)}, u32[]{:S(2)}, u32[]{:S(2)}) collective-permute-start(f32[4,128,128]{2,1,0:T(8,128)} %get-tuple-element.103), channel_id=1, source_target_pairs={{1,2},{2,1},{5,6},{6,5},{9,10},{10,9},{13,14},{14,13},{17,18},{18,... | collective-permute-start | bytes 786440 | tf_op jit(solution)/shard_map/ppermute | solution.py:279
  143.1 12.2 %collective-permute-start.35 = (f32[16,16,128]{2,1,0:T(8,128)}, f32[16,16,128]{2,1,0:T(8,128)}, u32[]{:S(2)}, u32[]{:S(2)}) collective-permute-start(f32[16,16,128]{2,1,0:T(8,128)} %get-tuple-element.115), channel_id=1, source_target_pairs={{0,8},{4,12},{8,0},{12,4},{16,24},{20,28},{24,16},{28,20},{1,9},{5... | collective-permute-start | bytes 393224 | tf_op jit(solution)/shard_map/ppermute | solution.py:363
  144.5 10.7 %collective-permute-start.36 = (f32[16,16,128]{2,1,0:T(8,128)}, f32[16,16,128]{2,1,0:T(8,128)}, u32[]{:S(2)}, u32[]{:S(2)}) collective-permute-start(f32[16,16,128]{2,1,0:T(8,128)} %get-tuple-element.117), channel_id=1, source_target_pairs={{0,16},{4,20},{8,24},{12,28},{16,0},{20,4},{24,8},{28,12},{1,17},{... | collective-permute-start | bytes 393224 | tf_op jit(solution)/shard_map/ppermute | solution.py:363
  146.2 9.1 %collective-permute-start.37 = (f32[16,16,128]{2,1,0:T(8,128)S(1)}, f32[16,16,128]{2,1,0:T(8,128)}, u32[]{:S(2)}, u32[]{:S(2)}) collective-permute-start(f32[16,16,128]{2,1,0:T(8,128)S(1)} %get-tuple-element.116), channel_id=1, source_target_pairs={{0,24},{4,28},{8,16},{12,20},{16,8},{20,12},{24,0},{28,4},{1,25},{... | collective-permute-start | bytes 393224 | tf_op jit(solution)/shard_map/ppermute | solution.py:363
  (23 other events, 297.8 us)

commit v2 on v1

v2 whole, which is shorter than its diff:
```python
import functools

import jax
import jax.numpy as jnp
import ml_dtypes
import numpy as np
from jax import lax
from jax.experimental import pallas as pl
from jax.experimental.pallas import tpu as pltpu
from jax.sharding import PartitionSpec as P

weights = (-205.0 / 72.0, 8.0 / 5.0, -1.0 / 5.0, 8.0 / 315.0, -1.0 / 560.0)
reach = 4
VMEM = pltpu.VMEM
SMEM = pltpu.SMEM
HBM = pltpu.HBM
limit = 12 * 1024 * 1024


def band(width, centre):
    out = np.zeros((width, width), np.float64)
    for k in range(1, reach + 1):
        out += weights[k] * (np.eye(width, k=k) + np.eye(width, k=-k))
    out += centre * np.eye(width)
    high = out.astype(np.float32).astype(ml_dtypes.bfloat16)
    low = (out - high.astype(np.float64)).astype(np.float32).astype(ml_dtypes.bfloat16)
    return high, low


def band_right(width):
    high, low = band(width, 3.0 * weights[0])
    return np.block([[high, low], [high, np.zeros_like(low)]])


def band_left(width):
    high, low = band(width, 0.0)
    return np.block([[high, high], [low, np.zeros_like(low)]])


def split(v):
    high = v.astype(jnp.bfloat16)
    low = (v - high.astype(jnp.float32)).astype(jnp.bfloat16)
    return high, low


def fill_halo(parity, even, odd, halo):
    @pl.when(parity == 0)
    def _():
        halo[:reach] = odd[...]
        halo[reach:] = even[...]

    @pl.when(parity != 0)
    def _():
        halo[:reach] = even[...]
        halo[reach:] = odd[...]


def emit_edges(parity, field, even, odd):
    count = field.shape[0]

    @pl.when(parity == 0)
    def _():
        even[...] = field[count - reach :]
        odd[...] = field[:reach]

    @pl.when(parity != 0)
    def _():
        even[...] = field[:reach]
        odd[...] = field[count - reach :]


def laplace_planes(cur, halo, right, left, put):
    count, width_y, width_z = cur.shape

    def plane(i):
        if i < 0:
            return halo[reach + i]
        if i >= count:
            return halo[reach + i - count]
        return cur[i]

    for x in range(0, count, 2):
        v = [cur[x], cur[x + 1]]
        (h0, l0), (h1, l1) = split(v[0]), split(v[1])
        rows = jnp.concatenate(
            [jnp.concatenate([h0, l0], axis=1), jnp.concatenate([h1, l1], axis=1)], axis=0
        )
        along = jnp.dot(rows, right[...], preferred_element_type=jnp.float32)
        cols = jnp.concatenate(
            [jnp.concatenate([h0, h1], axis=1), jnp.concatenate([l0, l1], axis=1)], axis=0
        )
        across = jnp.dot(left[...], cols, preferred_element_type=jnp.float32)
        for j in range(2):
            rows_j = slice(j * width_y, (j + 1) * width_y)
            lanes_j = slice(j * width_z, (j + 1) * width_z)
            lap = along[rows_j, :width_z] + along[rows_j, width_z:]
            lap = lap + (across[:width_y, lanes_j] + across[width_y:, lanes_j])
            for k in range(1, reach + 1):
                lap = lap + weights[k] * (plane(x + j + k) + plane(x + j - k))
            put(x + j, v[j], lap)


def forward_kernel(parts, *refs):
    it = iter(refs)
    cur, even, odd, right, left = [next(it) for _ in range(5)]
    moves, stores, adds, opens = parts["moves"], parts["stores"], parts["adds"], parts["opens"]
    prev, speed, source, wave = [next(it) for _ in range(4)] if moves else (None,) * 4
    late = next(it) if adds else None
    acc_in = next(it) if adds and not opens else None
    first, lap_first = (next(it), next(it)) if not moves else (None, None)
    nxt, even_out, odd_out = [next(it) for _ in range(3)] if moves else (None,) * 3
    lap_out = next(it) if stores else None
    acc_out = next(it) if adds and moves else None
    send, keep = (next(it), next(it)) if not moves else (None, None)
    halo = next(it)
    if moves:
        spot_smem, wave_smem, spot_sem, wave_sem = [next(it) for _ in range(4)]
        spot_copy = pltpu.make_async_copy(source, spot_smem, spot_sem)
        wave_copy = pltpu.make_async_copy(wave, wave_smem, wave_sem)
        spot_copy.start()
        wave_copy.start()
    total = next(it) if not moves else None
    slab = lax.axis_index("slab")
    parity = slab % 2
    fill_halo(parity, even, odd, halo)

    def put(x, v, lap):
        if moves:
            nxt[x] = 2.0 * v - prev[x] + speed[x] * lap
        if stores:
            lap_out[x] = lap
        if adds:
            value = lap * late[x]
            if not opens:
                value = value + acc_in[x]
            if moves:
                acc_out[x] = value
            else:
                total[x] = (value + first[x] * lap_first[x]) * parts["scale"]

    laplace_planes(cur, halo, right, left, put)
    if moves:
        spot_copy.wait()
        wave_copy.wait()
        row = spot_smem[0, 0] - slab * cur.shape[0]
        col, lane = spot_smem[0, 1], spot_smem[0, 2]

        @pl.when((row >= 0) & (row < cur.shape[0]))
        def _():
            tile = pl.ds(pl.multiple_of((col // 8) * 8, 8), 8)
            shape = (8, cur.shape[2])
            hit = (lax.broadcasted_iota(jnp.int32, shape, 0) == col % 8) & (
                lax.broadcasted_iota(jnp.int32, shape, 1) == lane
            )
            nxt[row, tile, :] = nxt[row, tile, :] + jnp.where(hit, wave_smem[0, parts["step"]], 0.0)

        emit_edges(parity, nxt, even_out, odd_out)
    else:
        chunk = send.shape[2]
        mine = lax.axis_index("shot") % 2
        for j in range(send.shape[0]):
            away = pl.multiple_of((2 * j + 1 - mine) * chunk, 8)
            here = pl.multiple_of((2 * j + mine) * chunk, 8)
            send[j] = total[:, pl.ds(away, chunk), :]
            keep[j] = total[:, pl.ds(here, chunk), :]


def adjoint_kernel(parts, *refs):
    it = iter(refs)
    cur, later, speed, even, odd, inject, right, left = [next(it) for _ in range(8)]
    adds, last = parts["adds"], parts["last"]
    lap_of, acc_in = (next(it), next(it)) if adds else (None, None)
    nxt = next(it)
    even_out, odd_out = (next(it), next(it)) if not last else (None, None)
    cur_out = next(it) if last else None
    acc_out = next(it) if adds else None
    halo = next(it)
    parity = lax.axis_index("slab") % 2
    fill_halo(parity, even, odd, halo)
    width_y = cur.shape[1]
    field, copies = nxt, []
    if last:
        field, sems, cur_sem = next(it), next(it), next(it)
        copies.append(pltpu.make_async_copy(cur, cur_out, cur_sem))
        copies[0].start()

    def put(x, v, lap):
        added = inject[pl.ds(x * width_y * 8 + parts["time"], width_y, stride=8), :]
        field[x] = 2.0 * v - later[x] + speed[x] * lap + added
        if adds:
            acc_out[x] = acc_in[x] + v * lap_of[x]
        if last and x % 2:
            both = pl.ds(x - 1, 2)
            copy = pltpu.make_async_copy(field.at[both], nxt.at[both], sems.at[x // 2])
            copy.start()
            copies.append(copy)

    laplace_planes(cur, halo, right, left, put)
    if not last:
        emit_edges(parity, field, even_out, odd_out)
    for copy in copies:
        copy.wait()


def edges_kernel(*refs):
    fields, outs, sems = refs[:2], refs[2:6], refs[6]
    parity = lax.axis_index("slab") % 2
    top = fields[0].shape[0] - reach
    starts = (top * (1 - parity), top * parity)
    copies = []
    for i in range(4):
        rows = pl.ds(starts[i % 2], reach)
        copies.append(pltpu.make_async_copy(fields[i // 2].at[rows], outs[i], sems.at[i]))
        copies[-1].start()
    for copy in copies:
        copy.wait()


def load_kernel(listen, *refs):
    fields, outs, where_to, sems = refs[:5], refs[5:10], refs[10], refs[11]
    copies = [pltpu.make_async_copy(fields[i], outs[i], sems.at[i]) for i in range(5)]
    for copy in copies:
        copy.start()
    count, width_y, width_z = fields[0].shape
    depth = listen[0:1, :] - lax.axis_index("slab") * count
    inside = (depth >= 0) & (depth < count)
    flat = depth * (width_y * width_z) + listen[1:2, :] * width_z + listen[2:3, :]
    where_to[...] = jnp.where(inside, flat, count * width_y * width_z)
    for copy in copies:
        copy.wait()


def scatter_kernel(where_to, *refs):
    blocks, out = refs[:-1], refs[-1]
    steps, per = blocks[0].shape[-2:]
    group, groups = 4, 8
    zero_rows = 64 * 8
    slab = lax.axis_index("slab")

    @pl.loop(0, out.shape[0] // zero_rows)
    def _(i):
        out[pl.ds(pl.multiple_of(i * zero_rows, 8), zero_rows), :] = jnp.zeros(
            (zero_rows, 128), jnp.float32
        )

    rest = out.shape[0] % zero_rows
    if rest:
        out[out.shape[0] - rest :, :] = jnp.zeros((rest, 128), jnp.float32)
    lanes = lax.broadcasted_iota(jnp.int32, (8, 128), 1)
    d = 0
    for held_blocks in blocks:
        for e in range(held_blocks.shape[0]):
            base = (slab ^ d) * per
            d += 1
            for part in range(per // 128):
                block = held_blocks[e, :, part * 128 : (part + 1) * 128]

                @pl.loop(0, 128 // (group * groups))
                def _(i):
                    tiles, terms, slots = [], [], []
                    for u in range(group * groups):
                        j = i * (group * groups) + u
                        flat = where_to[0, base + part * 128 + j]
                        lane = flat & 127
                        tile = flat >> 7
                        moved = pltpu.roll(block, (lane - j) & 127, 1)
                        tiles.append(tile)
                        terms.append(jnp.where(lanes == lane, moved, 0.0))
                        slots.append(pl.ds(pl.multiple_of(tile * 8, 8), 8))
                    for g in range(groups):
                        own = range(g * group, (g + 1) * group)
                        held = {u: out[slots[u], :] for u in own}
                        for u in own:
                            value = held[u] + terms[u]
                            for w in range(g * group, u):
                                same = (tiles[w] == tiles[u]).astype(jnp.float32)
                                value = value + terms[w] * same
                            held[u] = value
                        for u in own:
                            out[slots[u], :] = held[u]


def pair_kernel(keep, arrived, *outs):
    mine = lax.axis_index("shot") // 2
    for m in range(len(outs)):
        outs[m][...] = keep[mine ^ m] + arrived[mine ^ m]


def sum_kernel(*refs):
    total = refs[0][...]
    for ref in refs[1:-1]:
        total = total + ref[...]
    refs[-1][...] = total


def vmem(*shape):
    return VMEM(shape, jnp.float32)


def plain(*shape):
    return jax.ShapeDtypeStruct(shape, jnp.float32)


def call(name, kernel, args, outs, scratch=(), spaces=None, out_spaces=None, micros=2):
    spec = lambda space: pl.BlockSpec(memory_space=space)
    spaces = spaces or {}
    args = [
        pltpu.with_memory_space_constraint(arg, HBM) if spaces.get(i) is HBM else arg
        for i, arg in enumerate(args)
    ]
    out_spaces = out_spaces or {}
    return pl.pallas_call(
        kernel,
        out_shape=outs,
        in_specs=[spec(spaces.get(i, VMEM)) for i in range(len(args))],
        out_specs=[spec(out_spaces.get(i, VMEM)) for i in range(len(outs))],
        scratch_shapes=scratch,
        compiler_params=pltpu.CompilerParams(vmem_limit_bytes=limit),
        cost_estimate=pl.CostEstimate(
            flops=micros * 1000000000, bytes_accessed=micros << 16, transcendentals=0
        ),
        name=name,
    )(*args)


def pair_swap(count, start):
    pairs = []
    for i in range(start, count - 1, 2):
        pairs += [(i, i + 1), (i + 1, i)]
    return pairs


def body(
    state_before,
    state_now,
    adjoint_after,
    adjoint_now,
    speed_term,
    wavelet,
    source,
    receivers,
    traces,
):
    count, width_y, width_z = speed_term.shape
    steps = wavelet.shape[1]
    slabs = lax.axis_size("slab")
    shots = lax.axis_size("shot")
    half = steps // 2
    scale = 1.0 / (8.0 * steps)
    even_pairs, odd_pairs = pair_swap(slabs, 0), pair_swap(slabs, 1)
    field = vmem(count, width_y, width_z)
    edge = vmem(reach, width_y, width_z)
    halo = vmem(2 * reach, width_y, width_z)
    dma = pltpu.SemaphoreType.DMA

    def swap(even, odd):
        return lax.ppermute(even, "slab", even_pairs), lax.ppermute(odd, "slab", odd_pairs)

    right = jnp.asarray(band_right(width_z))
    left = jnp.asarray(band_left(width_y))
    listen = receivers[0]

    blocks = [traces]
    bit = 1
    while bit < slabs:
        held = blocks[0] if len(blocks) == 1 else jnp.concatenate(blocks, axis=0)
        blocks.append(lax.ppermute(held, "slab", [(i, i ^ bit) for i in range(slabs)]))
        bit *= 2

    p0_even, p0_odd, q8_even, q8_odd = call(
        "edges", edges_kernel, [state_now[0], adjoint_now[0]], [edge] * 4, [dma((4,))], {0: HBM, 1: HBM}
    )
    p_halo = swap(p0_even, p0_odd)
    q_halo = swap(q8_even, q8_odd)
    fields = [state_before[0], state_now[0], adjoint_after[0], adjoint_now[0], speed_term]
    *loaded, where_to = call(
        "load",
        load_kernel,
        [listen, *fields],
        [field] * 5 + [VMEM((1, listen.shape[1]), jnp.int32)],
        [dma((5,))],
        {1 + i: HBM for i in range(5)},
        micros=1,
    )
    (inject,) = call(
        "receivers",
        scatter_kernel,
        [where_to, *blocks],
        [vmem((count * width_y + 1) * 8, width_z)],
        (),
        {0: SMEM},
        micros=1,
    )
    p = {-1: loaded[0], 0: loaded[1]}
    q = {steps + 1: loaded[2], steps: loaded[3]}
    speed = loaded[4]
    laps = {}
    acc = None

    for k in range(steps):
        last = k == steps - 1
        parts = dict(moves=not last, stores=k < half, adds=k >= half, opens=k == half, step=k, scale=scale)
        args = [p[k], *p_halo, right, left]
        outs, scratch, spaces = [], [halo], {}
        if not last:
            spaces = {len(args) + 2: HBM, len(args) + 3: HBM}
            args += [p[k - 1], speed, source, wavelet]
            outs += [field, edge, edge]
            scratch += [SMEM(source.shape, jnp.int32), SMEM(wavelet.shape, jnp.float32), dma, dma]
        if parts["stores"]:
            outs += [field]
        if parts["adds"]:
            args += [q[k + 1]]
            if not parts["opens"]:
                args += [acc]
            if not last:
                outs += [field]
        if last:
            args += [q[1], laps[0]]
            piece = vmem(shots // 2, count, width_y // shots, width_z)
            outs += [piece, piece]
            scratch += [field]
        got = call(
            "forward", functools.partial(forward_kernel, parts), args, outs, scratch, spaces,
            micros=0 if last else 2,
        )
        if not last:
            p[k + 1] = got[0]
            p_halo = swap(*got[1:3])
            if parts["stores"]:
                laps[k] = got[3]
            else:
                acc = got[3]
        else:
            send, kept = got
            arrived = lax.ppermute(send, "shot", [(i, i ^ 1) for i in range(shots)])
            piece = vmem(count, width_y // shots, width_z)
            pieces = call("pair", pair_kernel, [kept, arrived], [piece] * (shots // 2), micros=0)
            terms = [pieces[0]] + [
                lax.ppermute(pieces[m], "shot", [(i, i ^ (2 * m)) for i in range(shots)])
                for m in range(1, shots // 2)
            ]
            (gradient,) = call("sum", sum_kernel, terms, [plain(count, width_y // shots, width_z)], micros=0)

        t = steps - 1 - k
        parts = dict(adds=k >= half and not last, last=last, time=t)
        args = [q[t + 1], q[t + 2], speed, *q_halo, inject, right, left]
        outs, scratch, out_spaces = [field, edge, edge], [halo], {}
        if last:
            outs = [plain(count, width_y, width_z)] * 2
            scratch += [field, dma((count // 2,)), dma]
            out_spaces = {0: HBM, 1: HBM}
        if parts["adds"]:
            args += [laps[t], acc]
            outs += [field]
        got = call(
            "adjoint", functools.partial(adjoint_kernel, parts), args, outs, scratch, None, out_spaces,
            micros=30 if last else 2,
        )
        q[t] = got[0]
        if last:
            opening, second = got
        else:
            q_halo = swap(*got[1:3])
        if parts["adds"]:
            acc = got[3]

    return (opening[None], second[None], gradient)


def solution(mesh):
    return jax.shard_map(
        body,
        mesh=mesh,
        in_specs=(
            P("shot", "slab", None, None),
            P("shot", "slab", None, None),
            P("shot", "slab", None, None),
            P("shot", "slab", None, None),
            P("slab", None, None),
            P("shot", None),
            P("shot", None),
            P("shot", None, None),
            P("shot", None, "slab"),
        ),
        out_specs=(
            P("shot", "slab", None, None),
            P("shot", "slab", None, None),
            P("slab", "shot", None),
        ),
        check_vma=False,
    )
```

time: 158 us -> 121 us (0.77)
  Pallas kernels: 57.3 us -> 36.6 us
  local copies, waits for them, and re-layouts: 20.6 us -> 0.73 us
  waiting for transfers between devices: 2.63 us -> 8.21 us
  other arithmetic: 5.13 us -> 0.01 us
  starting transfers between devices: 69.5 us -> 73.2 us
    pallas_call x17 -> x21, Pallas kernels: 57.3 us -> 36.6 us  [call(): pl.pallas_call(kernel, out_shape=outs, in_specs=[spec(spaces.get(i, VMEM)...]
    unnamed x35 -> x7, local copies, waits for them, and re-layouts: 13.3 us -> 0.73 us
    ppermute x37, waiting for transfers between devices: 2.63 us -> 8.21 us  [the longest x16 6.01 us: swap(): lax.ppermute(even, 'slab', even_pairs)]
    dynamic_slice x2 -> x0, local copies, waits for them, and re-layouts: 3.78 us -> none  [first_edges(): lax.dynamic_slice_in_dim(field, jnp.where(parity == 0, 0, top), reach, 0)]
    ppermute x37, starting transfers between devices: 69.5 us -> 73.1 us  [the longest x16 49.8 us: swap(): lax.ppermute(even, 'slab', even_pairs)]
    add x2 -> x0, other arithmetic: 2.99 us -> none  [the longest x1 1.72 us: body(): gradient + lax.ppermute(piece, 'shot', [(i, i ^ 2 * m) for i in range(sho...]
  transfers between devices with their start and end apart: 38 -> 38, of which waited for: 6 -> 8; matrix products, arithmetic and copies ran while one was open for 6% -> 1% of each run, Pallas kernels for 35% -> 28%
where the time goes in v2:
time: 121 us; the launch traced here: 120 us
  starting transfers between devices  73.2 us (60%)
  Pallas kernels  36.6 us (30%)
  waiting for transfers between devices  8.21 us (7%)
    ppermute x16, starting transfers between devices, swap(): lax.ppermute(even, 'slab', even_pairs)  49.8 us
    pallas_call x21, Pallas kernels, call(): pl.pallas_call(kernel, out_shape=outs, in_specs=[spec(spaces.get(i, VMEM)...  36.6 us
    ppermute x16, starting transfers between devices, swap(): lax.ppermute(odd, 'slab', odd_pairs)  10.7 us
    ppermute x2, starting transfers between devices, body(): lax.ppermute(held, 'slab', [(i, i ^ bit) for i in range(slabs)])  9.15 us
    ppermute x16, waiting for transfers between devices, swap(): lax.ppermute(even, 'slab', even_pairs)  6.01 us
    ppermute x3, starting transfers between devices, body(): lax.ppermute(pieces[m], 'shot', [(i, i ^ 2 * m) for i in range(shots)])  3.55 us
  transfers between devices with their start and end apart: 38, of which 8 were waited for; matrix products, arithmetic and copies ran while one was open for 1% of the time, Pallas kernels for 28%

profile of v2, /device:TPU:0, one launch (start us, length us, event | category | flops | bytes accessed | tf_op | source)
XLA Modules:
  0.0 119.9 jit_solution(11453495999618786438)
XLA Ops:
  2.0 3.1 %collective-permute-start.12 = (f32[4,128,128]{2,1,0:T(8,128)S(1)}, f32[4,128,128]{2,1,0:T(8,128)S(1)}, u32[]{:S(2)}, u32[]{:S(2)}) collective-permute-start(f32[4,128,128]{2,1,0:T(8,128)S(1)} %get-tuple-element.92), channel_id=1, source_target_pairs={{0,1},{1,0},{2,3},{3,2},{4,5},{5,4},{6,7},{7,6},{8,9},{9,8},{10,11... | collective-permute-start | bytes 786440 | tf_op jit(solution)/shard_map/ppermute | solution.py:357
  5.7 4.4 %collective-permute-start.2 = (f32[1,8,256]{2,1,0:T(8,128)}, f32[1,8,256]{2,1,0:T(8,128)S(1)}, u32[]{:S(2)}, u32[]{:S(2)}) collective-permute-start(f32[1,8,256]{2,1,0:T(8,128)} %refs_0_.1), channel_id=1, source_target_pairs={{0,1},{1,0},{2,3},{3,2},{4,5},{5,4},{6,7},{7,6},{8,9},{9,8},{10,11... | collective-permute-start | bytes 24584 | tf_op jit(solution)/shard_map/ppermute | solution.py:367
  11.7 2.5 %load.1 = (f32[16,128,128]{2,1,0:T(8,128)S(1)}, f32[16,128,128]{2,1,0:T(8,128)S(1)}, f32[16,128,128]{2,1,0:T(8,128)S(1)}, f32[16,128,128]{2,1,0:T(8,128)S(1)}, f...) custom-call(s32[3,1024]{1,0:T(4,128)S(1)} %bitcast.9, f32[16,128,128]{2,1,0:T(8,128)} %bitcast.10, ...), custom_call_target="tpu_custom_call" | custom-call | flops 1000000000 | bytes 65536 | tf_op jit(solution)/shard_map/load/pallas_call | solution.py:312
  14.2 4.7 %collective-permute-start.3 = (f32[2,8,256]{2,1,0:T(8,128)S(1)}, f32[2,8,256]{2,1,0:T(8,128)S(1)}, u32[]{:S(2)}, u32[]{:S(2)}) collective-permute-start(f32[2,8,256]{2,1,0:T(8,128)S(1)} %pad_maximum_fusion), channel_id=1, source_target_pairs={{0,2},{1,3},{2,0},{3,1},{4,6},{5,7},{6,4},{7,5},{8,10},{9,11},{10,... | collective-permute-start | bytes 49160 | tf_op jit(solution)/shard_map/ppermute | solution.py:367
  22.0 7.0 %receivers.1.refs_5_ = f32[16392,128]{1,0:T(8,128)S(1)} custom-call(s32[1,1024]{1,0:T(1,128)S(1)} %get-tuple-element.78.where_to, f32[1,8,256]{2,1,0:T(8,128)S(1)} %copy-done.2, f32[1,8,256]{2,1,0:T(8,128)S(1)} %collective-permute-done.2.refs_1_, f32[2,8,256]{2,1,0:T(8,128)S(1)} %collective-permute-done.3.refs_2_), custom_call_target="tpu_custom_call" | custom-call | flops 1000000000 | bytes 65536 | tf_op jit(solution)/shard_map/receivers/pallas_call | solution.py:312
  29.0 1.6 %adjoint.8 = (f32[16,128,128]{2,1,0:T(8,128)S(1)}, f32[4,128,128]{2,1,0:T(8,128)S(1)}, f32[4,128,128]{2,1,0:T(8,128)S(1)}) custom-call(f32[16,128,128]{2,1,0:T(8,128)S(1)} %get-tuple-element.73.refs_0_.refs_1_.refs_5_, f32[16,128,128]{2,1,0:T(8,128)S(1)} %get-tuple-element.74.refs_1_, f32[16,128,128]{2,1,0:T(8,128)S(1)} %get-tuple-element.75.refs_2_.refs_6_, ...), custom_call_target="tpu_custom_call" | custom-call | flops 2000000000 | bytes 131072 | tf_op jit(solution)/shard_map/adjoint/pallas_call | solution.py:312
  30.6 2.4 %collective-permute-start.4 = (f32[4,128,128]{2,1,0:T(8,128)S(1)}, f32[4,128,128]{2,1,0:T(8,128)S(1)}, u32[]{:S(2)}, u32[]{:S(2)}) collective-permute-start(f32[4,128,128]{2,1,0:T(8,128)S(1)} %get-tuple-element.80), channel_id=1, source_target_pairs={{0,1},{1,0},{2,3},{3,2},{4,5},{5,4},{6,7},{7,6},{8,9},{9,8},{10,11... | collective-permute-start | bytes 786440 | tf_op jit(solution)/shard_map/ppermute | solution.py:357
  35.1 3.4 %collective-permute-start.16 = (f32[4,128,128]{2,1,0:T(8,128)S(1)}, f32[4,128,128]{2,1,0:T(8,128)S(1)}, u32[]{:S(2)}, u32[]{:S(2)}) collective-permute-start(f32[4,128,128]{2,1,0:T(8,128)S(1)} %get-tuple-element.99), channel_id=1, source_target_pairs={{0,1},{1,0},{2,3},{3,2},{4,5},{5,4},{6,7},{7,6},{8,9},{9,8},{10,11... | collective-permute-start | bytes 786440 | tf_op jit(solution)/shard_map/ppermute | solution.py:357
  39.2 1.6 %adjoint.9 = (f32[16,128,128]{2,1,0:T(8,128)S(1)}, f32[4,128,128]{2,1,0:T(8,128)S(1)}, f32[4,128,128]{2,1,0:T(8,128)S(1)}) custom-call(f32[16,128,128]{2,1,0:T(8,128)S(1)} %get-tuple-element.79.refs_0_.refs_1_.refs_9_, f32[16,128,128]{2,1,0:T(8,128)S(1)} %get-tuple-element.73.refs_0_.refs_1_.refs_5_, f32[16,128,128]{2,1,0:T(8,128)S(1)} %get-tuple-element.75.refs_2_.refs_6_, ...), custom_call_target="tpu_custom_call" | custom-call | flops 2000000000 | bytes 131072 | tf_op jit(solution)/shard_map/adjoint/pallas_call | solution.py:312
  40.8 4.2 %collective-permute-start.6 = (f32[4,128,128]{2,1,0:T(8,128)S(1)}, f32[4,128,128]{2,1,0:T(8,128)S(1)}, u32[]{:S(2)}, u32[]{:S(2)}) collective-permute-start(f32[4,128,128]{2,1,0:T(8,128)S(1)} %get-tuple-element.83), channel_id=1, source_target_pairs={{0,1},{1,0},{2,3},{3,2},{4,5},{5,4},{6,7},{7,6},{8,9},{9,8},{10,11... | collective-permute-start | bytes 786440 | tf_op jit(solution)/shard_map/ppermute | solution.py:357
  47.1 3.8 %collective-permute-start.18 = (f32[4,128,128]{2,1,0:T(8,128)S(1)}, f32[4,128,128]{2,1,0:T(8,128)S(1)}, u32[]{:S(2)}, u32[]{:S(2)}) collective-permute-start(f32[4,128,128]{2,1,0:T(8,128)S(1)} %get-tuple-element.102), channel_id=1, source_target_pairs={{0,1},{1,0},{2,3},{3,2},{4,5},{5,4},{6,7},{7,6},{8,9},{9,8},{10,11... | collective-permute-start | bytes 786440 | tf_op jit(solution)/shard_map/ppermute | solution.py:357
  52.1 1.5 %adjoint.10 = (f32[16,128,128]{2,1,0:T(8,128)S(1)}, f32[4,128,128]{2,1,0:T(8,128)S(1)}, f32[4,128,128]{2,1,0:T(8,128)S(1)}) custom-call(f32[16,128,128]{2,1,0:T(8,128)S(1)} %get-tuple-element.82.refs_0_.refs_1_.refs_9_, f32[16,128,128]{2,1,0:T(8,128)S(1)} %get-tuple-element.79.refs_0_.refs_1_.refs_9_, f32[16,128,128]{2,1,0:T(8,128)S(1)} %get-tuple-element.75.refs_2_.refs_6_, ...), custom_call_target="tpu_custom_call" | custom-call | flops 2000000000 | bytes 131072 | tf_op jit(solution)/shard_map/adjoint/pallas_call | solution.py:312
  53.6 4.4 %collective-permute-start.8 = (f32[4,128,128]{2,1,0:T(8,128)S(1)}, f32[4,128,128]{2,1,0:T(8,128)S(1)}, u32[]{:S(2)}, u32[]{:S(2)}) collective-permute-start(f32[4,128,128]{2,1,0:T(8,128)S(1)} %get-tuple-element.86), channel_id=1, source_target_pairs={{0,1},{1,0},{2,3},{3,2},{4,5},{5,4},{6,7},{7,6},{8,9},{9,8},{10,11... | collective-permute-start | bytes 786440 | tf_op jit(solution)/shard_map/ppermute | solution.py:357
  58.7 1.5 %forward.11 = (f32[16,128,128]{2,1,0:T(8,128)S(1)}, f32[4,128,128]{2,1,0:T(8,128)S(1)}, f32[4,128,128]{2,1,0:T(8,128)S(1)}, f32[16,128,128]{2,1,0:T(8,128)S(1)}) custom-call(f32[16,128,128]{2,1,0:T(8,128)S(1)} %get-tuple-element.101.refs_0_.refs_5_, f32[4,128,128]{2,1,0:T(8,128)S(1)} %collective-permute-done.18.refs_1_, ...), custom_call_target="tpu_custom_call" | custom-call | flops 2000000000 | bytes 131072 | tf_op jit(solution)/shard_map/forward/pallas_call | solution.py:312
  60.1 3.3 %collective-permute-start.20 = (f32[4,128,128]{2,1,0:T(8,128)S(1)}, f32[4,128,128]{2,1,0:T(8,128)S(1)}, u32[]{:S(2)}, u32[]{:S(2)}) collective-permute-start(f32[4,128,128]{2,1,0:T(8,128)S(1)} %get-tuple-element.106), channel_id=1, source_target_pairs={{0,1},{1,0},{2,3},{3,2},{4,5},{5,4},{6,7},{7,6},{8,9},{9,8},{10,11... | collective-permute-start | bytes 786440 | tf_op jit(solution)/shard_map/ppermute | solution.py:357
  65.6 3.7 %collective-permute-start.10 = (f32[4,128,128]{2,1,0:T(8,128)S(1)}, f32[4,128,128]{2,1,0:T(8,128)S(1)}, u32[]{:S(2)}, u32[]{:S(2)}) collective-permute-start(f32[4,128,128]{2,1,0:T(8,128)S(1)} %get-tuple-element.89), channel_id=1, source_target_pairs={{0,1},{1,0},{2,3},{3,2},{4,5},{5,4},{6,7},{7,6},{8,9},{9,8},{10,11... | collective-permute-start | bytes 786440 | tf_op jit(solution)/shard_map/ppermute | solution.py:357
  72.0 3.8 %collective-permute-start.24 = (f32[4,128,128]{2,1,0:T(8,128)S(1)}, f32[4,128,128]{2,1,0:T(8,128)S(1)}, u32[]{:S(2)}, u32[]{:S(2)}) collective-permute-start(f32[4,128,128]{2,1,0:T(8,128)S(1)} %get-tuple-element.114), channel_id=1, source_target_pairs={{0,1},{1,0},{2,3},{3,2},{4,5},{5,4},{6,7},{7,6},{8,9},{9,8},{10,11... | collective-permute-start | bytes 786440 | tf_op jit(solution)/shard_map/ppermute | solution.py:357
  76.5 1.7 %adjoint.12 = (f32[16,128,128]{2,1,0:T(8,128)S(1)}, f32[4,128,128]{2,1,0:T(8,128)S(1)}, f32[4,128,128]{2,1,0:T(8,128)S(1)}, f32[16,128,128]{2,1,0:T(8,128)S(1)}) custom-call(f32[16,128,128]{2,1,0:T(8,128)S(1)} %get-tuple-element.88.refs_0_.refs_1_, f32[16,128,128]{2,1,0:T(8,128)S(1)} %get-tuple-element.85.refs_0_.refs_9_.refs_1_, ...), custom_call_target="tpu_custom_call" | custom-call | flops 2000000000 | bytes 131072 | tf_op jit(solution)/shard_map/adjoint/pallas_call | solution.py:312
  78.2 3.1 %collective-permute-start.22 = (f32[4,128,128]{2,1,0:T(8,128)S(1)}, f32[4,128,128]{2,1,0:T(8,128)S(1)}, u32[]{:S(2)}, u32[]{:S(2)}) collective-permute-start(f32[4,128,128]{2,1,0:T(8,128)S(1)} %get-tuple-element.110), channel_id=1, source_target_pairs={{0,1},{1,0},{2,3},{3,2},{4,5},{5,4},{6,7},{7,6},{8,9},{9,8},{10,11... | collective-permute-start | bytes 786440 | tf_op jit(solution)/shard_map/ppermute | solution.py:357
  82.0 1.5 %forward.13 = (f32[16,128,128]{2,1,0:T(8,128)S(1)}, f32[4,128,128]{2,1,0:T(8,128)S(1)}, f32[4,128,128]{2,1,0:T(8,128)S(1)}, f32[16,128,128]{2,1,0:T(8,128)S(1)}) custom-call(f32[16,128,128]{2,1,0:T(8,128)S(1)} %get-tuple-element.113.refs_0_.refs_5_, f32[4,128,128]{2,1,0:T(8,128)S(1)} %collective-permute-done.24.refs_1_, ...), custom_call_target="tpu_custom_call" | custom-call | flops 2000000000 | bytes 131072 | tf_op jit(solution)/shard_map/forward/pallas_call | solution.py:312
  83.5 3.5 %collective-permute-start.28 = (f32[4,128,128]{2,1,0:T(8,128)S(1)}, f32[4,128,128]{2,1,0:T(8,128)S(1)}, u32[]{:S(2)}, u32[]{:S(2)}) collective-permute-start(f32[4,128,128]{2,1,0:T(8,128)S(1)} %get-tuple-element.123), channel_id=1, source_target_pairs={{0,1},{1,0},{2,3},{3,2},{4,5},{5,4},{6,7},{7,6},{8,9},{9,8},{10,11... | collective-permute-start | bytes 786440 | tf_op jit(solution)/shard_map/ppermute | solution.py:357
  88.2 1.6 %adjoint.13 = (f32[16,128,128]{2,1,0:T(8,128)S(1)}, f32[4,128,128]{2,1,0:T(8,128)S(1)}, f32[4,128,128]{2,1,0:T(8,128)S(1)}, f32[16,128,128]{2,1,0:T(8,128)S(1)}) custom-call(f32[16,128,128]{2,1,0:T(8,128)S(1)} %get-tuple-element.109.refs_0_.refs_1_, f32[16,128,128]{2,1,0:T(8,128)S(1)} %get-tuple-element.88.refs_0_.refs_1_, ...), custom_call_target="tpu_custom_call" | custom-call | flops 2000000000 | bytes 131072 | tf_op jit(solution)/shard_map/adjoint/pallas_call | solution.py:312
  89.7 3.7 %collective-permute-start.26 = (f32[4,128,128]{2,1,0:T(8,128)S(1)}, f32[4,128,128]{2,1,0:T(8,128)S(1)}, u32[]{:S(2)}, u32[]{:S(2)}) collective-permute-start(f32[4,128,128]{2,1,0:T(8,128)S(1)} %get-tuple-element.119), channel_id=1, source_target_pairs={{0,1},{1,0},{2,3},{3,2},{4,5},{5,4},{6,7},{7,6},{8,9},{9,8},{10,11... | collective-permute-start | bytes 786440 | tf_op jit(solution)/shard_map/ppermute | solution.py:357
  94.1 1.6 %forward.14 = (f32[16,128,128]{2,1,0:T(8,128)S(1)}, f32[4,128,128]{2,1,0:T(8,128)S(1)}, f32[4,128,128]{2,1,0:T(8,128)S(1)}, f32[16,128,128]{2,1,0:T(8,128)S(1)}) custom-call(f32[16,128,128]{2,1,0:T(8,128)S(1)} %get-tuple-element.122.refs_0_, f32[4,128,128]{2,1,0:T(8,128)S(1)} %collective-permute-done.28.refs_1_, ...), custom_call_target="tpu_custom_call" | custom-call | flops 2000000000 | bytes 131072 | tf_op jit(solution)/shard_map/forward/pallas_call | solution.py:312
  95.8 3.3 %collective-permute-start.32 = (f32[4,128,128]{2,1,0:T(8,128)S(1)}, f32[4,128,128]{2,1,0:T(8,128)S(1)}, u32[]{:S(2)}, u32[]{:S(2)}) collective-permute-start(f32[4,128,128]{2,1,0:T(8,128)S(1)} %get-tuple-element.133), channel_id=1, source_target_pairs={{0,1},{1,0},{2,3},{3,2},{4,5},{5,4},{6,7},{7,6},{8,9},{9,8},{10,11... | collective-permute-start | bytes 786440 | tf_op jit(solution)/shard_map/ppermute | solution.py:357
  99.7 1.9 %adjoint.14 = (f32[16,128,128]{2,1,0:T(8,128)S(1)}, f32[4,128,128]{2,1,0:T(8,128)S(1)}, f32[4,128,128]{2,1,0:T(8,128)S(1)}, f32[16,128,128]{2,1,0:T(8,128)S(1)}) custom-call(f32[16,128,128]{2,1,0:T(8,128)S(1)} %get-tuple-element.118.refs_0_.refs_1_, f32[16,128,128]{2,1,0:T(8,128)S(1)} %get-tuple-element.109.refs_0_.refs_1_, ...), custom_call_target="tpu_custom_call" | custom-call | flops 2000000000 | bytes 131072 | tf_op jit(solution)/shard_map/adjoint/pallas_call | solution.py:312
  101.7 1.7 %collective-permute-done.32.refs_1_ = f32[4,128,128]{2,1,0:T(8,128)S(1)} collective-permute-done((f32[4,128,128]{2,1,0:T(8,128)S(1)}, f32[4,128,128]{2,1,0:T(8,128)S(1)}, u32[]{:S(2)}, u32[]{:S(2)}) %collective-permute-start.32) | collective-permute-done | bytes 262176 | tf_op jit(solution)/shard_map/ppermute | solution.py:357
  104.8 4.0 %collective-permute-start.30 = (f32[4,128,128]{2,1,0:T(8,128)S(1)}, f32[4,128,128]{2,1,0:T(8,128)S(1)}, u32[]{:S(2)}, u32[]{:S(2)}) collective-permute-start(f32[4,128,128]{2,1,0:T(8,128)S(1)} %get-tuple-element.128), channel_id=1, source_target_pairs={{0,1},{1,0},{2,3},{3,2},{4,5},{5,4},{6,7},{7,6},{8,9},{9,8},{10,11... | collective-permute-start | bytes 786440 | tf_op jit(solution)/shard_map/ppermute | solution.py:357
  109.6 1.6 %collective-permute-start.35 = (f32[16,16,128]{2,1,0:T(8,128)S(1)}, f32[16,16,128]{2,1,0:T(8,128)S(1)}, u32[]{:S(2)}, u32[]{:S(2)}) collective-permute-start(f32[16,16,128]{2,1,0:T(8,128)S(1)} %get-tuple-element.140), channel_id=1, source_target_pairs={{0,8},{4,12},{8,0},{12,4},{16,24},{20,28},{24,16},{28,20},{1,9},{5... | collective-permute-start | bytes 393224 | tf_op jit(solution)/shard_map/ppermute | solution.py:440
  111.1 1.5 %collective-permute-start.36 = (f32[16,16,128]{2,1,0:T(8,128)S(1)}, f32[16,16,128]{2,1,0:T(8,128)S(1)}, u32[]{:S(2)}, u32[]{:S(2)}) collective-permute-start(f32[16,16,128]{2,1,0:T(8,128)S(1)} %get-tuple-element.141), channel_id=1, source_target_pairs={{0,16},{4,20},{8,24},{12,28},{16,0},{20,4},{24,8},{28,12},{1,17},{... | collective-permute-start | bytes 393224 | tf_op jit(solution)/shard_map/ppermute | solution.py:440
  113.1 2.6 %collective-permute-done.30.refs_3_ = f32[4,128,128]{2,1,0:T(8,128)S(1)} collective-permute-done((f32[4,128,128]{2,1,0:T(8,128)S(1)}, f32[4,128,128]{2,1,0:T(8,128)S(1)}, u32[]{:S(2)}, u32[]{:S(2)}) %collective-permute-start.30) | collective-permute-done | bytes 262176 | tf_op jit(solution)/shard_map/ppermute | solution.py:357
  115.7 2.3 %adjoint.15 = (f32[16,128,128]{2,1,0:T(8,128)}, f32[16,128,128]{2,1,0:T(8,128)}) custom-call(f32[16,128,128]{2,1,0:T(8,128)S(1)} %get-tuple-element.127.refs_0_.refs_7_, f32[16,128,128]{2,1,0:T(8,128)S(1)} %get-tuple-element.118.refs_0_.refs_1_, f32[16,128,128]{2,1,0:T(8,128)S(1)} %get-tuple-element.75.refs_2_.refs_6_, ...), custom_call_target="tpu_custom_call" | custom-call | flops 30000001024 | bytes 1966080 | tf_op jit(solution)/shard_map/adjoint/pallas_call | solution.py:312
  (73 shorter events, 26.4 us)
Async XLA Ops:
  2.0 17.0 %collective-permute-start.12 = (f32[4,128,128]{2,1,0:T(8,128)S(1)}, f32[4,128,128]{2,1,0:T(8,128)S(1)}, u32[]{:S(2)}, u32[]{:S(2)}) collective-permute-start(f32[4,128,128]{2,1,0:T(8,128)S(1)} %get-tuple-element.92), channel_id=1, source_target_pairs={{0,1},{1,0},{2,3},{3,2},{4,5},{5,4},{6,7},{7,6},{8,9},{9,8},{10,11... | collective-permute-start | bytes 786440 | tf_op jit(solution)/shard_map/ppermute | solution.py:357
  5.1 13.9 %collective-permute-start.13 = (f32[4,128,128]{2,1,0:T(8,128)S(1)}, f32[4,128,128]{2,1,0:T(8,128)S(1)}, u32[]{:S(2)}, u32[]{:S(2)}) collective-permute-start(f32[4,128,128]{2,1,0:T(8,128)S(1)} %get-tuple-element.93), channel_id=1, source_target_pairs={{1,2},{2,1},{5,6},{6,5},{9,10},{10,9},{13,14},{14,13},{17,18},{18,... | collective-permute-start | bytes 786440 | tf_op jit(solution)/shard_map/ppermute | solution.py:357
  5.7 8.5 %collective-permute-start.2 = (f32[1,8,256]{2,1,0:T(8,128)}, f32[1,8,256]{2,1,0:T(8,128)S(1)}, u32[]{:S(2)}, u32[]{:S(2)}) collective-permute-start(f32[1,8,256]{2,1,0:T(8,128)} %refs_0_.1), channel_id=1, source_target_pairs={{0,1},{1,0},{2,3},{3,2},{4,5},{5,4},{6,7},{7,6},{8,9},{9,8},{10,11... | collective-permute-start | bytes 24584 | tf_op jit(solution)/shard_map/ppermute | solution.py:367
  10.2 18.8 %collective-permute-start = (f32[4,128,128]{2,1,0:T(8,128)S(1)}, f32[4,128,128]{2,1,0:T(8,128)S(1)}, u32[]{:S(2)}, u32[]{:S(2)}) collective-permute-start(f32[4,128,128]{2,1,0:T(8,128)S(1)} %get-tuple-element.76), channel_id=1, source_target_pairs={{0,1},{1,0},{2,3},{3,2},{4,5},{5,4},{6,7},{7,6},{8,9},{9,8},{10,11... | collective-permute-start | bytes 786440 | tf_op jit(solution)/shard_map/ppermute | solution.py:357
  10.3 18.8 %collective-permute-start.1 = (f32[4,128,128]{2,1,0:T(8,128)S(1)}, f32[4,128,128]{2,1,0:T(8,128)S(1)}, u32[]{:S(2)}, u32[]{:S(2)}) collective-permute-start(f32[4,128,128]{2,1,0:T(8,128)S(1)} %get-tuple-element.77), channel_id=1, source_target_pairs={{1,2},{2,1},{5,6},{6,5},{9,10},{10,9},{13,14},{14,13},{17,18},{18,... | collective-permute-start | bytes 786440 | tf_op jit(solution)/shard_map/ppermute | solution.py:357
  14.2 7.8 %collective-permute-start.3 = (f32[2,8,256]{2,1,0:T(8,128)S(1)}, f32[2,8,256]{2,1,0:T(8,128)S(1)}, u32[]{:S(2)}, u32[]{:S(2)}) collective-permute-start(f32[2,8,256]{2,1,0:T(8,128)S(1)} %pad_maximum_fusion), channel_id=1, source_target_pairs={{0,2},{1,3},{2,0},{3,1},{4,6},{5,7},{6,4},{7,5},{8,10},{9,11},{10,... | collective-permute-start | bytes 49160 | tf_op jit(solution)/shard_map/ppermute | solution.py:367
  20.3 13.4 %collective-permute-start.14 = (f32[4,128,128]{2,1,0:T(8,128)S(1)}, f32[4,128,128]{2,1,0:T(8,128)S(1)}, u32[]{:S(2)}, u32[]{:S(2)}) collective-permute-start(f32[4,128,128]{2,1,0:T(8,128)S(1)} %get-tuple-element.96), channel_id=1, source_target_pairs={{0,1},{1,0},{2,3},{3,2},{4,5},{5,4},{6,7},{7,6},{8,9},{9,8},{10,11... | collective-permute-start | bytes 786440 | tf_op jit(solution)/shard_map/ppermute | solution.py:357
  20.3 13.3 %collective-permute-start.15 = (f32[4,128,128]{2,1,0:T(8,128)S(1)}, f32[4,128,128]{2,1,0:T(8,128)S(1)}, u32[]{:S(2)}, u32[]{:S(2)}) collective-permute-start(f32[4,128,128]{2,1,0:T(8,128)S(1)} %get-tuple-element.97), channel_id=1, source_target_pairs={{1,2},{2,1},{5,6},{6,5},{9,10},{10,9},{13,14},{14,13},{17,18},{18,... | collective-permute-start | bytes 786440 | tf_op jit(solution)/shard_map/ppermute | solution.py:357
  30.6 8.5 %collective-permute-start.4 = (f32[4,128,128]{2,1,0:T(8,128)S(1)}, f32[4,128,128]{2,1,0:T(8,128)S(1)}, u32[]{:S(2)}, u32[]{:S(2)}) collective-permute-start(f32[4,128,128]{2,1,0:T(8,128)S(1)} %get-tuple-element.80), channel_id=1, source_target_pairs={{0,1},{1,0},{2,3},{3,2},{4,5},{5,4},{6,7},{7,6},{8,9},{9,8},{10,11... | collective-permute-start | bytes 786440 | tf_op jit(solution)/shard_map/ppermute | solution.py:357
  35.1 10.5 %collective-permute-start.16 = (f32[4,128,128]{2,1,0:T(8,128)S(1)}, f32[4,128,128]{2,1,0:T(8,128)S(1)}, u32[]{:S(2)}, u32[]{:S(2)}) collective-permute-start(f32[4,128,128]{2,1,0:T(8,128)S(1)} %get-tuple-element.99), channel_id=1, source_target_pairs={{0,1},{1,0},{2,3},{3,2},{4,5},{5,4},{6,7},{7,6},{8,9},{9,8},{10,11... | collective-permute-start | bytes 786440 | tf_op jit(solution)/shard_map/ppermute | solution.py:357
  38.5 7.2 %collective-permute-start.17 = (f32[4,128,128]{2,1,0:T(8,128)S(1)}, f32[4,128,128]{2,1,0:T(8,128)S(1)}, u32[]{:S(2)}, u32[]{:S(2)}) collective-permute-start(f32[4,128,128]{2,1,0:T(8,128)S(1)} %get-tuple-element.100), channel_id=1, source_target_pairs={{1,2},{2,1},{5,6},{6,5},{9,10},{10,9},{13,14},{14,13},{17,18},{18,... | collective-permute-start | bytes 786440 | tf_op jit(solution)/shard_map/ppermute | solution.py:357
  40.8 11.3 %collective-permute-start.6 = (f32[4,128,128]{2,1,0:T(8,128)S(1)}, f32[4,128,128]{2,1,0:T(8,128)S(1)}, u32[]{:S(2)}, u32[]{:S(2)}) collective-permute-start(f32[4,128,128]{2,1,0:T(8,128)S(1)} %get-tuple-element.83), channel_id=1, source_target_pairs={{0,1},{1,0},{2,3},{3,2},{4,5},{5,4},{6,7},{7,6},{8,9},{9,8},{10,11... | collective-permute-start | bytes 786440 | tf_op jit(solution)/shard_map/ppermute | solution.py:357
  45.0 7.1 %collective-permute-start.7 = (f32[4,128,128]{2,1,0:T(8,128)S(1)}, f32[4,128,128]{2,1,0:T(8,128)S(1)}, u32[]{:S(2)}, u32[]{:S(2)}) collective-permute-start(f32[4,128,128]{2,1,0:T(8,128)S(1)} %get-tuple-element.84), channel_id=1, source_target_pairs={{1,2},{2,1},{5,6},{6,5},{9,10},{10,9},{13,14},{14,13},{17,18},{18,... | collective-permute-start | bytes 786440 | tf_op jit(solution)/shard_map/ppermute | solution.py:357
  47.1 11.6 %collective-permute-start.18 = (f32[4,128,128]{2,1,0:T(8,128)S(1)}, f32[4,128,128]{2,1,0:T(8,128)S(1)}, u32[]{:S(2)}, u32[]{:S(2)}) collective-permute-start(f32[4,128,128]{2,1,0:T(8,128)S(1)} %get-tuple-element.102), channel_id=1, source_target_pairs={{0,1},{1,0},{2,3},{3,2},{4,5},{5,4},{6,7},{7,6},{8,9},{9,8},{10,11... | collective-permute-start | bytes 786440 | tf_op jit(solution)/shard_map/ppermute | solution.py:357
  50.9 7.8 %collective-permute-start.19 = (f32[4,128,128]{2,1,0:T(8,128)S(1)}, f32[4,128,128]{2,1,0:T(8,128)S(1)}, u32[]{:S(2)}, u32[]{:S(2)}) collective-permute-start(f32[4,128,128]{2,1,0:T(8,128)S(1)} %get-tuple-element.103), channel_id=1, source_target_pairs={{1,2},{2,1},{5,6},{6,5},{9,10},{10,9},{13,14},{14,13},{17,18},{18,... | collective-permute-start | bytes 786440 | tf_op jit(solution)/shard_map/ppermute | solution.py:357
  53.6 10.6 %collective-permute-start.8 = (f32[4,128,128]{2,1,0:T(8,128)S(1)}, f32[4,128,128]{2,1,0:T(8,128)S(1)}, u32[]{:S(2)}, u32[]{:S(2)}) collective-permute-start(f32[4,128,128]{2,1,0:T(8,128)S(1)} %get-tuple-element.86), channel_id=1, source_target_pairs={{0,1},{1,0},{2,3},{3,2},{4,5},{5,4},{6,7},{7,6},{8,9},{9,8},{10,11... | collective-permute-start | bytes 786440 | tf_op jit(solution)/shard_map/ppermute | solution.py:357
  60.1 10.4 %collective-permute-start.20 = (f32[4,128,128]{2,1,0:T(8,128)S(1)}, f32[4,128,128]{2,1,0:T(8,128)S(1)}, u32[]{:S(2)}, u32[]{:S(2)}) collective-permute-start(f32[4,128,128]{2,1,0:T(8,128)S(1)} %get-tuple-element.106), channel_id=1, source_target_pairs={{0,1},{1,0},{2,3},{3,2},{4,5},{5,4},{6,7},{7,6},{8,9},{9,8},{10,11... | collective-permute-start | bytes 786440 | tf_op jit(solution)/shard_map/ppermute | solution.py:357
  63.5 7.1 %collective-permute-start.21 = (f32[4,128,128]{2,1,0:T(8,128)S(1)}, f32[4,128,128]{2,1,0:T(8,128)S(1)}, u32[]{:S(2)}, u32[]{:S(2)}) collective-permute-start(f32[4,128,128]{2,1,0:T(8,128)S(1)} %get-tuple-element.107), channel_id=1, source_target_pairs={{1,2},{2,1},{5,6},{6,5},{9,10},{10,9},{13,14},{14,13},{17,18},{18,... | collective-permute-start | bytes 786440 | tf_op jit(solution)/shard_map/ppermute | solution.py:357
  65.6 10.8 %collective-permute-start.10 = (f32[4,128,128]{2,1,0:T(8,128)S(1)}, f32[4,128,128]{2,1,0:T(8,128)S(1)}, u32[]{:S(2)}, u32[]{:S(2)}) collective-permute-start(f32[4,128,128]{2,1,0:T(8,128)S(1)} %get-tuple-element.89), channel_id=1, source_target_pairs={{0,1},{1,0},{2,3},{3,2},{4,5},{5,4},{6,7},{7,6},{8,9},{9,8},{10,11... | collective-permute-start | bytes 786440 | tf_op jit(solution)/shard_map/ppermute | solution.py:357
  69.3 7.1 %collective-permute-start.11 = (f32[4,128,128]{2,1,0:T(8,128)S(1)}, f32[4,128,128]{2,1,0:T(8,128)S(1)}, u32[]{:S(2)}, u32[]{:S(2)}) collective-permute-start(f32[4,128,128]{2,1,0:T(8,128)S(1)} %get-tuple-element.90), channel_id=1, source_target_pairs={{1,2},{2,1},{5,6},{6,5},{9,10},{10,9},{13,14},{14,13},{17,18},{18,... | collective-permute-start | bytes 786440 | tf_op jit(solution)/shard_map/ppermute | solution.py:357
  72.0 10.0 %collective-permute-start.24 = (f32[4,128,128]{2,1,0:T(8,128)S(1)}, f32[4,128,128]{2,1,0:T(8,128)S(1)}, u32[]{:S(2)}, u32[]{:S(2)}) collective-permute-start(f32[4,128,128]{2,1,0:T(8,128)S(1)} %get-tuple-element.114), channel_id=1, source_target_pairs={{0,1},{1,0},{2,3},{3,2},{4,5},{5,4},{6,7},{7,6},{8,9},{9,8},{10,11... | collective-permute-start | bytes 786440 | tf_op jit(solution)/shard_map/ppermute | solution.py:357
  78.2 10.0 %collective-permute-start.22 = (f32[4,128,128]{2,1,0:T(8,128)S(1)}, f32[4,128,128]{2,1,0:T(8,128)S(1)}, u32[]{:S(2)}, u32[]{:S(2)}) collective-permute-start(f32[4,128,128]{2,1,0:T(8,128)S(1)} %get-tuple-element.110), channel_id=1, source_target_pairs={{0,1},{1,0},{2,3},{3,2},{4,5},{5,4},{6,7},{7,6},{8,9},{9,8},{10,11... | collective-permute-start | bytes 786440 | tf_op jit(solution)/shard_map/ppermute | solution.py:357
  81.3 6.8 %collective-permute-start.23 = (f32[4,128,128]{2,1,0:T(8,128)S(1)}, f32[4,128,128]{2,1,0:T(8,128)S(1)}, u32[]{:S(2)}, u32[]{:S(2)}) collective-permute-start(f32[4,128,128]{2,1,0:T(8,128)S(1)} %get-tuple-element.111), channel_id=1, source_target_pairs={{1,2},{2,1},{5,6},{6,5},{9,10},{10,9},{13,14},{14,13},{17,18},{18,... | collective-permute-start | bytes 786440 | tf_op jit(solution)/shard_map/ppermute | solution.py:357
  83.5 10.6 %collective-permute-start.28 = (f32[4,128,128]{2,1,0:T(8,128)S(1)}, f32[4,128,128]{2,1,0:T(8,128)S(1)}, u32[]{:S(2)}, u32[]{:S(2)}) collective-permute-start(f32[4,128,128]{2,1,0:T(8,128)S(1)} %get-tuple-element.123), channel_id=1, source_target_pairs={{0,1},{1,0},{2,3},{3,2},{4,5},{5,4},{6,7},{7,6},{8,9},{9,8},{10,11... | collective-permute-start | bytes 786440 | tf_op jit(solution)/shard_map/ppermute | solution.py:357
  87.1 7.1 %collective-permute-start.29 = (f32[4,128,128]{2,1,0:T(8,128)S(1)}, f32[4,128,128]{2,1,0:T(8,128)S(1)}, u32[]{:S(2)}, u32[]{:S(2)}) collective-permute-start(f32[4,128,128]{2,1,0:T(8,128)S(1)} %get-tuple-element.124), channel_id=1, source_target_pairs={{1,2},{2,1},{5,6},{6,5},{9,10},{10,9},{13,14},{14,13},{17,18},{18,... | collective-permute-start | bytes 786440 | tf_op jit(solution)/shard_map/ppermute | solution.py:357
  89.7 10.0 %collective-permute-start.26 = (f32[4,128,128]{2,1,0:T(8,128)S(1)}, f32[4,128,128]{2,1,0:T(8,128)S(1)}, u32[]{:S(2)}, u32[]{:S(2)}) collective-permute-start(f32[4,128,128]{2,1,0:T(8,128)S(1)} %get-tuple-element.119), channel_id=1, source_target_pairs={{0,1},{1,0},{2,3},{3,2},{4,5},{5,4},{6,7},{7,6},{8,9},{9,8},{10,11... | collective-permute-start | bytes 786440 | tf_op jit(solution)/shard_map/ppermute | solution.py:357
  95.8 7.6 %collective-permute-start.32 = (f32[4,128,128]{2,1,0:T(8,128)S(1)}, f32[4,128,128]{2,1,0:T(8,128)S(1)}, u32[]{:S(2)}, u32[]{:S(2)}) collective-permute-start(f32[4,128,128]{2,1,0:T(8,128)S(1)} %get-tuple-element.133), channel_id=1, source_target_pairs={{0,1},{1,0},{2,3},{3,2},{4,5},{5,4},{6,7},{7,6},{8,9},{9,8},{10,11... | collective-permute-start | bytes 786440 | tf_op jit(solution)/shard_map/ppermute | solution.py:357
  104.8 10.9 %collective-permute-start.30 = (f32[4,128,128]{2,1,0:T(8,128)S(1)}, f32[4,128,128]{2,1,0:T(8,128)S(1)}, u32[]{:S(2)}, u32[]{:S(2)}) collective-permute-start(f32[4,128,128]{2,1,0:T(8,128)S(1)} %get-tuple-element.128), channel_id=1, source_target_pairs={{0,1},{1,0},{2,3},{3,2},{4,5},{5,4},{6,7},{7,6},{8,9},{9,8},{10,11... | collective-permute-start | bytes 786440 | tf_op jit(solution)/shard_map/ppermute | solution.py:357
  108.8 6.9 %collective-permute-start.31 = (f32[4,128,128]{2,1,0:T(8,128)S(1)}, f32[4,128,128]{2,1,0:T(8,128)S(1)}, u32[]{:S(2)}, u32[]{:S(2)}) collective-permute-start(f32[4,128,128]{2,1,0:T(8,128)S(1)} %get-tuple-element.129), channel_id=1, source_target_pairs={{1,2},{2,1},{5,6},{6,5},{9,10},{10,9},{13,14},{14,13},{17,18},{18,... | collective-permute-start | bytes 786440 | tf_op jit(solution)/shard_map/ppermute | solution.py:357
  109.6 8.5 %collective-permute-start.35 = (f32[16,16,128]{2,1,0:T(8,128)S(1)}, f32[16,16,128]{2,1,0:T(8,128)S(1)}, u32[]{:S(2)}, u32[]{:S(2)}) collective-permute-start(f32[16,16,128]{2,1,0:T(8,128)S(1)} %get-tuple-element.140), channel_id=1, source_target_pairs={{0,8},{4,12},{8,0},{12,4},{16,24},{20,28},{24,16},{28,20},{1,9},{5... | collective-permute-start | bytes 393224 | tf_op jit(solution)/shard_map/ppermute | solution.py:440
  111.1 8.1 %collective-permute-start.36 = (f32[16,16,128]{2,1,0:T(8,128)S(1)}, f32[16,16,128]{2,1,0:T(8,128)S(1)}, u32[]{:S(2)}, u32[]{:S(2)}) collective-permute-start(f32[16,16,128]{2,1,0:T(8,128)S(1)} %get-tuple-element.141), channel_id=1, source_target_pairs={{0,16},{4,20},{8,24},{12,28},{16,0},{20,4},{24,8},{28,12},{1,17},{... | collective-permute-start | bytes 393224 | tf_op jit(solution)/shard_map/ppermute | solution.py:440
  112.6 6.6 %collective-permute-start.37 = (f32[16,16,128]{2,1,0:T(8,128)S(1)}, f32[16,16,128]{2,1,0:T(8,128)S(1)}, u32[]{:S(2)}, u32[]{:S(2)}) collective-permute-start(f32[16,16,128]{2,1,0:T(8,128)S(1)} %get-tuple-element.142), channel_id=1, source_target_pairs={{0,24},{4,28},{8,16},{12,20},{16,8},{20,12},{24,0},{28,4},{1,25},{... | collective-permute-start | bytes 393224 | tf_op jit(solution)/shard_map/ppermute | solution.py:440
  (9 other events, 84.2 us)

commit v3 on v2

v3 whole, which is shorter than its diff:
```python
import functools

import jax
import jax.numpy as jnp
import ml_dtypes
import numpy as np
from jax import lax
from jax.experimental import pallas as pl
from jax.experimental.pallas import tpu as pltpu
from jax.sharding import PartitionSpec as P

weights = (-205.0 / 72.0, 8.0 / 5.0, -1.0 / 5.0, 8.0 / 315.0, -1.0 / 560.0)
reach = 4
VMEM = pltpu.VMEM
SMEM = pltpu.SMEM
HBM = pltpu.HBM
limit = 12 * 1024 * 1024


def band(width, centre):
    out = np.zeros((width, width), np.float64)
    for k in range(1, reach + 1):
        out += weights[k] * (np.eye(width, k=k) + np.eye(width, k=-k))
    out += centre * np.eye(width)
    high = out.astype(np.float32).astype(ml_dtypes.bfloat16)
    low = (out - high.astype(np.float64)).astype(np.float32).astype(ml_dtypes.bfloat16)
    return high, low


def band_right(width):
    high, low = band(width, 3.0 * weights[0])
    return np.block([[high, low], [high, np.zeros_like(low)]])


def band_left(width):
    high, low = band(width, 0.0)
    return np.block([[high, high], [low, np.zeros_like(low)]])


def split(v):
    high = v.astype(jnp.bfloat16)
    low = (v - high.astype(jnp.float32)).astype(jnp.bfloat16)
    return high, low


def fill_halo(parity, even, odd, halo):
    @pl.when(parity == 0)
    def _():
        halo[:reach] = odd[...]
        halo[reach:] = even[...]

    @pl.when(parity != 0)
    def _():
        halo[:reach] = even[...]
        halo[reach:] = odd[...]


def emit_edge(upper, outer, out):
    @pl.when(upper)
    def _():
        out[...] = outer[reach:]

    @pl.when(jnp.logical_not(upper))
    def _():
        out[...] = outer[:reach]


def rows_of(count, border):
    if border:
        return list(range(reach)) + list(range(count - reach, count))
    return list(range(reach, count - reach))


def laplace_rows(border, inner, outer, halo, right, left, put):
    count, width_y, width_z = inner.shape[0] + 2 * reach, inner.shape[1], inner.shape[2]

    def plane(i):
        if i < 0:
            return halo[reach + i]
        if i < reach:
            return outer[i]
        if i < count - reach:
            return inner[i - reach]
        if i < count:
            return outer[i - count + 2 * reach]
        return halo[reach + i - count]

    rows = rows_of(count, border)
    for i in range(0, len(rows), 2):
        x = rows[i]
        v = [plane(x), plane(x + 1)]
        (h0, l0), (h1, l1) = split(v[0]), split(v[1])
        flat = jnp.concatenate(
            [jnp.concatenate([h0, l0], axis=1), jnp.concatenate([h1, l1], axis=1)], axis=0
        )
        along = jnp.dot(flat, right[...], preferred_element_type=jnp.float32)
        cols = jnp.concatenate(
            [jnp.concatenate([h0, h1], axis=1), jnp.concatenate([l0, l1], axis=1)], axis=0
        )
        across = jnp.dot(left[...], cols, preferred_element_type=jnp.float32)
        for j in range(2):
            rows_j = slice(j * width_y, (j + 1) * width_y)
            lanes_j = slice(j * width_z, (j + 1) * width_z)
            lap = along[rows_j, :width_z] + along[rows_j, width_z:]
            lap = lap + (across[:width_y, lanes_j] + across[width_y:, lanes_j])
            for k in range(1, reach + 1):
                lap = lap + weights[k] * (plane(x + j + k) + plane(x + j - k))
            put(i + j, x + j, v[j], lap)


def forward_kernel(parts, *refs):
    it = iter(refs)
    border, moves, stores = parts["border"], parts["moves"], parts["stores"]
    adds, opens = parts["adds"], parts["opens"]
    inner, outer = next(it), next(it)
    even, odd = (next(it), next(it)) if border else (None, None)
    right, left = next(it), next(it)
    prev, speed, source, wave = [next(it) for _ in range(4)] if moves else (None,) * 4
    late = next(it) if adds else None
    acc_in = next(it) if adds and not opens else None
    first, lap_first = (next(it), next(it)) if not moves else (None, None)
    nxt = next(it) if moves else None
    edge_out = next(it) if moves or not border else None
    lap_out = next(it) if stores else None
    acc_out = next(it) if adds and moves else None
    send, keep = (next(it), next(it)) if not moves else (None, None)
    halo = next(it) if border else None
    if moves:
        spot_smem, wave_smem, spot_sem, wave_sem = [next(it) for _ in range(4)]
        spot_copy = pltpu.make_async_copy(source, spot_smem, spot_sem)
        wave_copy = pltpu.make_async_copy(wave, wave_smem, wave_sem)
        spot_copy.start()
        wave_copy.start()
    total = next(it) if not moves else None
    slab = lax.axis_index("slab")
    parity = slab % 2
    count = inner.shape[0] + 2 * reach
    if border:
        fill_halo(parity, even, odd, halo)
    else:
        emit_edge(parity != 0, outer, edge_out)

    def put(i, x, v, lap):
        if moves:
            nxt[i] = 2.0 * v - prev[i] + speed[x] * lap
        if stores:
            lap_out[i] = lap
        if adds:
            value = lap * late[i]
            if not opens:
                value = value + acc_in[i]
            if moves:
                acc_out[i] = value
            else:
                total[i] = (value + first[i] * lap_first[i]) * parts["scale"]

    laplace_rows(border, inner, outer, halo, right, left, put)
    if moves:
        spot_copy.wait()
        wave_copy.wait()
        row = spot_smem[0, 0] - slab * count
        col, lane = spot_smem[0, 1], spot_smem[0, 2]
        within = (row >= reach) & (row < count - reach)
        place = row - reach
        if border:
            within = (row >= 0) & (row < count) & jnp.logical_not(within)
            place = jnp.where(row < reach, row, row - count + 2 * reach)

        @pl.when(within)
        def _():
            tile = pl.ds(pl.multiple_of((col // 8) * 8, 8), 8)
            shape = (8, inner.shape[2])
            hit = (lax.broadcasted_iota(jnp.int32, shape, 0) == col % 8) & (
                lax.broadcasted_iota(jnp.int32, shape, 1) == lane
            )
            added = jnp.where(hit, wave_smem[0, parts["step"]], 0.0)
            nxt[place, tile, :] = nxt[place, tile, :] + added

        if border:
            emit_edge(parity == 0, nxt, edge_out)
    else:
        chunk = send.shape[2]
        mine = lax.axis_index("shot") % 2
        for j in range(send.shape[0]):
            away = pl.multiple_of((2 * j + 1 - mine) * chunk, 8)
            here = pl.multiple_of((2 * j + mine) * chunk, 8)
            send[j] = total[:, pl.ds(away, chunk), :]
            keep[j] = total[:, pl.ds(here, chunk), :]


def part_copies(border, part, whole, sems, to_whole):
    count = whole.shape[0]
    if border:
        pieces = [(0, 0, reach), (reach, count - reach, reach)]
    else:
        pieces = [(0, reach, count - 2 * reach)]
    copies = []
    for n, (i, x, rows) in enumerate(pieces):
        near, far = part.at[pl.ds(i, rows)], whole.at[pl.ds(x, rows)]
        ends = (near, far) if to_whole else (far, near)
        copies.append(pltpu.make_async_copy(*ends, sems.at[n]))
    return copies


def adjoint_kernel(parts, *refs):
    it = iter(refs)
    border, adds, last = parts["border"], parts["adds"], parts["last"]
    inner, outer = next(it), next(it)
    even, odd = (next(it), next(it)) if border else (None, None)
    right, left, later, speed, inject = [next(it) for _ in range(5)]
    lap_of, acc_in = (next(it), next(it)) if adds else (None, None)
    if last and border:
        next(it)
    nxt = next(it)
    second = next(it) if last and not border else None
    edge_out = next(it) if parts["sends"] else None
    acc_out = next(it) if adds else None
    halo = next(it) if border else None
    part, copies = nxt, []
    if last:
        part, sems = next(it), next(it)
    parity = lax.axis_index("slab") % 2
    width_y = inner.shape[1]
    if border:
        fill_halo(parity, even, odd, halo)
    else:
        if parts["sends"]:
            emit_edge(parity != 0, outer, edge_out)
        if last:
            copies += part_copies(True, outer, second, sems.at[pl.ds(2, 2)], True)
            copies += part_copies(False, inner, second, sems.at[pl.ds(4, 1)], True)
            for copy in copies:
                copy.start()

    def put(i, x, v, lap):
        added = inject[pl.ds(x * width_y * 8 + parts["time"], width_y, stride=8), :]
        part[i] = 2.0 * v - later[i] + speed[x] * lap + added
        if adds:
            acc_out[i] = acc_in[i] + v * lap_of[i]

    laplace_rows(border, inner, outer, halo, right, left, put)
    if last:
        for copy in part_copies(border, part, nxt, sems, True):
            copy.start()
            copies.append(copy)
    elif border:
        emit_edge(parity == 0, part, edge_out)
    for copy in copies:
        copy.wait()


def edges_kernel(*refs):
    fields, outs, sems = refs[:2], refs[2:4], refs[4]
    parity = lax.axis_index("slab") % 2
    top = fields[0].shape[0] - reach
    rows = pl.ds(top * (1 - parity), reach)
    copies = [pltpu.make_async_copy(fields[i].at[rows], outs[i], sems.at[i]) for i in range(2)]
    for copy in copies:
        copy.start()
    for copy in copies:
        copy.wait()


def load_kernel(listen, *refs):
    fields, speed, refs = refs[:4], refs[4], refs[5:]
    parts, speed_out, where_to, tiles, edge, sems = refs[:8], *refs[8:13]
    top = fields[3].shape[0] - reach
    rows = pl.ds(top * (lax.axis_index("slab") % 2), reach)
    copies = [
        pltpu.make_async_copy(speed, speed_out, sems.at[12]),
        pltpu.make_async_copy(fields[3].at[rows], edge, sems.at[13]),
    ]
    for i in range(4):
        copies += part_copies(False, parts[2 * i], fields[i], sems.at[pl.ds(3 * i, 1)], False)
        copies += part_copies(True, parts[2 * i + 1], fields[i], sems.at[pl.ds(3 * i + 1, 2)], False)
    for copy in copies:
        copy.start()
    count, width_y, width_z = fields[0].shape
    depth = listen[0:1, :] - lax.axis_index("slab") * count
    inside = (depth >= 0) & (depth < count)
    flat = depth * (width_y * width_z) + listen[1:2, :] * width_z + listen[2:3, :]
    where_to[...] = jnp.where(inside, flat, count * width_y * width_z)
    zero_rows = 64 * 8

    @pl.loop(0, tiles.shape[0] // zero_rows)
    def _(i):
        tiles[pl.ds(pl.multiple_of(i * zero_rows, 8), zero_rows), :] = jnp.zeros(
            (zero_rows, 128), jnp.float32
        )

    rest = tiles.shape[0] % zero_rows
    if rest:
        tiles[tiles.shape[0] - rest :, :] = jnp.zeros((rest, 128), jnp.float32)
    for copy in copies:
        copy.wait()


def scatter_kernel(where_to, *refs):
    blocks, out = refs[:-3], refs[-1]
    steps, per = blocks[0].shape[-2:]
    group, groups = 4, 8
    slab = lax.axis_index("slab")
    lanes = lax.broadcasted_iota(jnp.int32, (8, 128), 1)
    d = 0
    for held_blocks in blocks:
        for e in range(held_blocks.shape[0]):
            base = (slab ^ d) * per
            d += 1
            for part in range(per // 128):
                block = held_blocks[e, :, part * 128 : (part + 1) * 128]

                @pl.loop(0, 128 // (group * groups))
                def _(i):
                    tiles, terms, slots = [], [], []
                    for u in range(group * groups):
                        j = i * (group * groups) + u
                        flat = where_to[0, base + part * 128 + j]
                        lane = flat & 127
                        tile = flat >> 7
                        moved = pltpu.roll(block, (lane - j) & 127, 1)
                        tiles.append(tile)
                        terms.append(jnp.where(lanes == lane, moved, 0.0))
                        slots.append(pl.ds(pl.multiple_of(tile * 8, 8), 8))
                    for g in range(groups):
                        own = range(g * group, (g + 1) * group)
                        held = {u: out[slots[u], :] for u in own}
                        for u in own:
                            value = held[u] + terms[u]
                            for w in range(g * group, u):
                                same = (tiles[w] == tiles[u]).astype(jnp.float32)
                                value = value + terms[w] * same
                            held[u] = value
                        for u in own:
                            out[slots[u], :] = held[u]


def pair_kernel(keep, arrived, *outs):
    mine = lax.axis_index("shot") // 2
    for m in range(len(outs)):
        outs[m][...] = keep[mine ^ m] + arrived[mine ^ m]


def sum_kernel(*refs):
    out = refs[-1]
    half = len(refs) // 2
    for border, terms in ((False, refs[:half]), (True, refs[half:-1])):
        total = terms[0][...]
        for term in terms[1:]:
            total = total + term[...]
        if border:
            out[:reach] = total[:reach]
            out[out.shape[0] - reach :] = total[reach:]
        else:
            out[reach : out.shape[0] - reach] = total


def vmem(*shape):
    return VMEM(shape, jnp.float32)


def plain(*shape):
    return jax.ShapeDtypeStruct(shape, jnp.float32)


def call(name, kernel, args, outs, scratch=(), spaces=None, out_spaces=None, micros=1, aliases=None):
    spec = lambda space: pl.BlockSpec(memory_space=space)
    spaces = spaces or {}
    args = [
        pltpu.with_memory_space_constraint(arg, HBM) if spaces.get(i) is HBM else arg
        for i, arg in enumerate(args)
    ]
    out_spaces = out_spaces or {}
    return pl.pallas_call(
        kernel,
        out_shape=outs,
        in_specs=[spec(spaces.get(i, VMEM)) for i in range(len(args))],
        out_specs=[spec(out_spaces.get(i, VMEM)) for i in range(len(outs))],
        scratch_shapes=scratch,
        input_output_aliases=aliases or {},
        compiler_params=pltpu.CompilerParams(vmem_limit_bytes=limit),
        cost_estimate=pl.CostEstimate(
            flops=micros * 1000000000, bytes_accessed=micros << 16, transcendentals=0
        ),
        name=name,
    )(*args)


def pair_swap(count, start):
    pairs = []
    for i in range(start, count - 1, 2):
        pairs += [(i, i + 1), (i + 1, i)]
    return pairs


def body(
    state_before,
    state_now,
    adjoint_after,
    adjoint_now,
    speed_term,
    wavelet,
    source,
    receivers,
    traces,
):
    count, width_y, width_z = speed_term.shape
    steps = wavelet.shape[1]
    slabs = lax.axis_size("slab")
    shots = lax.axis_size("shot")
    half = steps // 2
    scale = 1.0 / (8.0 * steps)
    even_pairs, odd_pairs = pair_swap(slabs, 0), pair_swap(slabs, 1)
    inner = count - 2 * reach
    field = vmem(count, width_y, width_z)
    part = {False: vmem(inner, width_y, width_z), True: vmem(2 * reach, width_y, width_z)}
    edge = vmem(reach, width_y, width_z)
    dma = pltpu.SemaphoreType.DMA

    def by_even(edges):
        return lax.ppermute(edges, "slab", even_pairs)

    def by_odd(edges):
        return lax.ppermute(edges, "slab", odd_pairs)

    right = jnp.asarray(band_right(width_z))
    left = jnp.asarray(band_left(width_y))
    listen = receivers[0]

    blocks = [traces]
    bit = 1
    while bit < slabs:
        held = blocks[0] if len(blocks) == 1 else jnp.concatenate(blocks, axis=0)
        blocks.append(lax.ppermute(held, "slab", [(i, i ^ bit) for i in range(slabs)]))
        bit *= 2

    p_even, q_even = call(
        "edges", edges_kernel, [state_now[0], adjoint_now[0]], [edge] * 2, [dma((2,))], {0: HBM, 1: HBM}
    )
    p_even, q_even = by_even(p_even), by_even(q_even)
    fields = [state_before[0], state_now[0], adjoint_after[0], adjoint_now[0], speed_term]
    tiles = vmem((count * width_y + 1) * 8, width_z)
    *loaded, speed, where_to, zeros, q_odd = call(
        "load",
        load_kernel,
        [listen, *fields],
        [part[False], part[True]] * 4 + [field, VMEM((1, listen.shape[1]), jnp.int32), tiles, edge],
        [dma((14,))],
        {1 + i: HBM for i in range(5)},
    )
    p = {-1: loaded[0:2], 0: loaded[2:4]}
    q = {steps + 1: loaded[4:6], steps: loaded[6:8]}
    laps, acc = {}, {False: None, True: None}

    def forward(k, border, halos):
        last = k == steps - 1
        parts = dict(
            border=border, moves=not last, stores=k < half, adds=k >= half, opens=k == half, step=k, scale=scale
        )
        args = [*p[k], *halos, right, left]
        outs, scratch, spaces = [], [part[True]] if border else [], {}
        if not last:
            spaces = {len(args) + 2: HBM, len(args) + 3: HBM}
            args += [p[k - 1][border], speed, source, wavelet]
            outs += [part[border]]
            scratch += [SMEM(source.shape, jnp.int32), SMEM(wavelet.shape, jnp.float32), dma, dma]
        if not last or not border:
            outs += [edge]
        if parts["stores"]:
            outs += [part[border]]
        if parts["adds"]:
            args += [q[k + 1][border]]
            if not parts["opens"]:
                args += [acc[border]]
            if not last:
                outs += [part[border]]
        if last:
            args += [q[1][border], laps[0][border]]
            piece = vmem(shots // 2, part[border].shape[0], width_y // shots, width_z)
            outs += [piece, piece]
            scratch += [part[border]]
        name = "forward_border" if border else "forward_inner"
        got = list(call(name, functools.partial(forward_kernel, parts), args, outs, scratch, spaces))
        nxt = None if last else got.pop(0)
        sides = None if last and border else got.pop(0)
        if last:
            return sides, got
        if parts["stores"]:
            laps.setdefault(k, [None, None])[border] = got[0]
        else:
            acc[border] = got[0]
        p.setdefault(k + 1, [None, None])[border] = nxt
        return sides

    def adjoint(k, border, halos, opening=None):
        last = k == steps - 1
        t = steps - 1 - k
        sends = not last if border else k > 0
        parts = dict(border=border, adds=k >= half and not last, last=last, time=t, sends=sends)
        args = [*q[t + 1], *halos, right, left, q[t + 2][border], speed, inject]
        outs, scratch, out_spaces, aliases = [part[border]], [part[True]] if border else [], {}, {}
        spaces = {}
        if parts["adds"]:
            args += [laps[t][border], acc[border]]
        if last:
            whole = plain(count, width_y, width_z)
            outs = [whole] if border else [whole, whole]
            out_spaces = {i: HBM for i in range(len(outs))}
            scratch += [part[border], dma((5,))]
            if border:
                spaces, aliases = {len(args): HBM}, {len(args): 0}
                args += [opening]
        if sends:
            outs += [edge]
        if parts["adds"]:
            outs += [part[border]]
        name = "adjoint_border" if border else "adjoint_inner"
        got = call(
            name, functools.partial(adjoint_kernel, parts), args, outs, scratch, spaces, out_spaces,
            micros=30 if last and border else 1, aliases=aliases,
        )
        if last:
            return got
        q.setdefault(t, [None, None])[border] = got[0]
        if parts["adds"]:
            acc[border] = got[2]
        return got[1] if sends else None

    def spread(send, kept):
        arrived = lax.ppermute(send, "shot", [(i, i ^ 1) for i in range(shots)])
        piece = vmem(*send.shape[1:])
        pieces = call("pair", pair_kernel, [kept, arrived], [piece] * (shots // 2), micros=0)
        return [pieces[0]] + [
            lax.ppermute(pieces[m], "shot", [(i, i ^ (2 * m)) for i in range(shots)])
            for m in range(1, shots // 2)
        ]

    p_odd = by_odd(forward(0, False, ()))
    q_odd = by_odd(q_odd)
    for k in range(steps - 1):
        p_even = by_even(forward(k, True, (p_even, p_odd)))
        if k == 0:
            (inject,) = call(
                "receivers",
                scatter_kernel,
                [where_to, *blocks, p[1][True], zeros],
                [tiles],
                (),
                {0: SMEM},
                aliases={2 + len(blocks): 0},
            )
            adjoint(0, False, ())
        if k + 1 < steps - 1:
            p_odd = by_odd(forward(k + 1, False, ()))
        else:
            sides, halves = forward(k + 1, False, ())
            p_odd = by_odd(sides)
            terms = spread(*halves)
        q_even = by_even(adjoint(k, True, (q_even, q_odd)))
        if k + 1 < steps - 1:
            q_odd = by_odd(adjoint(k + 1, False, ()))
        else:
            opening, second, sides = adjoint(k + 1, False, ())
            q_odd = by_odd(sides)
    _, halves = forward(steps - 1, True, (p_even, p_odd))
    terms += spread(*halves)
    (opening,) = adjoint(steps - 1, True, (q_even, q_odd), opening)
    (gradient,) = call("sum", sum_kernel, terms, [plain(count, width_y // shots, width_z)], micros=0)
    return (opening[None], second[None], gradient)


def solution(mesh):
    return jax.shard_map(
        body,
        mesh=mesh,
        in_specs=(
            P("shot", "slab", None, None),
            P("shot", "slab", None, None),
            P("shot", "slab", None, None),
            P("shot", "slab", None, None),
            P("slab", None, None),
            P("shot", None),
            P("shot", None),
            P("shot", None, None),
            P("shot", None, "slab"),
        ),
        out_specs=(
            P("shot", "slab", None, None),
            P("shot", "slab", None, None),
            P("slab", "shot", None),
        ),
        check_vma=False,
    )
```

time: 121 us -> 132 us (1.091)
  the two profiles are of different devices: /device:TPU:0 before, /device:TPU:10 now
where the time goes in v3:
time: 132 us
  starting transfers between devices  63.3 us (48%)
  Pallas kernels  37.8 us (29%)
  waiting for transfers between devices  28.5 us (22%)
  between operations  1.36 us (1%)
    ppermute x16, starting transfers between devices, by_odd(): return lax.ppermute(edges, 'slab', odd_pairs)  49.8 us
    pallas_call x38, Pallas kernels, call(): pl.pallas_call(kernel, out_shape=outs, in_specs=[spec(spaces.get(i, VMEM)...  37.8 us
    ppermute x16, waiting for transfers between devices, by_odd(): return lax.ppermute(edges, 'slab', odd_pairs)  18.6 us
    ppermute x16, starting transfers between devices, by_even(): return lax.ppermute(edges, 'slab', even_pairs)  7.05 us
    ppermute x16, waiting for transfers between devices, by_even(): return lax.ppermute(edges, 'slab', even_pairs)  6.65 us
    ppermute x6, starting transfers between devices, spread(): lax.ppermute(pieces[m], 'shot', [(i, i ^ 2 * m) for i in range(shots)])  6.16 us
    ppermute x6, waiting for transfers between devices, spread(): lax.ppermute(pieces[m], 'shot', [(i, i ^ 2 * m) for i in range(shots)])  3.08 us
  transfers between devices with their start and end apart: 42, of which 19 were waited for; matrix products, arithmetic and copies ran while one was open for 1% of the time, Pallas kernels for 27%

profile of v3, /device:TPU:10, one launch (start us, length us, event | category | flops | bytes accessed | tf_op | source)
XLA Modules:
  0.0 131.7 jit_solution(11440597778729267109)
XLA Ops:
  3.0 2.6 %load.1 = (f32[8,128,128]{2,1,0:T(8,128)S(1)}, f32[8,128,128]{2,1,0:T(8,128)S(1)}, f32[8,128,128]{2,1,0:T(8,128)S(1)}, f32[8,128,128]{2,1,0:T(8,128)S(1)}, f32[8...) custom-call(s32[3,1024]{1,0:T(4,128)S(1)} %bitcast.9, ...), custom_call_target="tpu_custom_call" | custom-call | flops 1000000000 | bytes 65536 | tf_op jit(solution)/shard_map/load/pallas_call | solution.py:373
  6.4 4.6 %collective-permute-start.3 = (f32[4,128,128]{2,1,0:T(8,128)S(1)}, f32[4,128,128]{2,1,0:T(8,128)S(1)}, u32[]{:S(2)}, u32[]{:S(2)}) collective-permute-start(f32[4,128,128]{2,1,0:T(8,128)S(1)} %get-tuple-element.116), channel_id=1, source_target_pairs={{1,2},{2,1},{5,6},{6,5},{9,10},{10,9},{13,14},{14,13},{17,18},{18,... | collective-permute-start | bytes 786440 | tf_op jit(solution)/shard_map/ppermute | solution.py:423
  11.1 2.0 %collective-permute-start.4 = (f32[4,128,128]{2,1,0:T(8,128)S(1)}, f32[4,128,128]{2,1,0:T(8,128)S(1)}, u32[]{:S(2)}, u32[]{:S(2)}) collective-permute-start(f32[4,128,128]{2,1,0:T(8,128)S(1)} %get-tuple-element.120), channel_id=1, source_target_pairs={{0,1},{1,0},{2,3},{3,2},{4,5},{5,4},{6,7},{7,6},{8,9},{9,8},{10,11... | collective-permute-start | bytes 786440 | tf_op jit(solution)/shard_map/ppermute | solution.py:420
  13.2 1.9 %collective-permute-start.5 = (f32[4,128,128]{2,1,0:T(8,128)S(1)}, f32[4,128,128]{2,1,0:T(8,128)S(1)}, u32[]{:S(2)}, u32[]{:S(2)}) collective-permute-start(f32[4,128,128]{2,1,0:T(8,128)S(1)} %get-tuple-element.121), channel_id=1, source_target_pairs={{1,2},{2,1},{5,6},{6,5},{9,10},{10,9},{13,14},{14,13},{17,18},{18,... | collective-permute-start | bytes 786440 | tf_op jit(solution)/shard_map/ppermute | solution.py:423
  15.2 2.8 %collective-permute-done.3.refs_3_ = f32[4,128,128]{2,1,0:T(8,128)S(1)} collective-permute-done((f32[4,128,128]{2,1,0:T(8,128)S(1)}, f32[4,128,128]{2,1,0:T(8,128)S(1)}, u32[]{:S(2)}, u32[]{:S(2)}) %collective-permute-start.3) | collective-permute-done | bytes 262176 | tf_op jit(solution)/shard_map/ppermute | solution.py:423
  20.2 3.8 %collective-permute-start.13 = (f32[4,128,128]{2,1,0:T(8,128)S(1)}, f32[4,128,128]{2,1,0:T(8,128)S(1)}, u32[]{:S(2)}, u32[]{:S(2)}) collective-permute-start(f32[4,128,128]{2,1,0:T(8,128)S(1)} %get-tuple-element.139), channel_id=1, source_target_pairs={{1,2},{2,1},{5,6},{6,5},{9,10},{10,9},{13,14},{14,13},{17,18},{18,... | collective-permute-start | bytes 786440 | tf_op jit(solution)/shard_map/ppermute | solution.py:423
  24.1 6.4 %receivers.1.refs_6_.refs_8_ = f32[16392,128]{1,0:T(8,128)S(1)} custom-call(s32[1,1024]{1,0:T(1,128)S(1)} %get-tuple-element.111.where_to, f32[1,8,256]{2,1,0:T(8,128)S(1)} %copy-done.2, f32[1,8,256]{2,1,0:T(8,128)S(1)} %collective-permute-done.refs_1_, f32[2,8,256]{2,1,0:T(8,128)S(1)} %collective-permute-done.1.refs_2_, ...), custom_call_target="tpu_custom_call", output_to_operand_aliasing={{}: (5, {})} | custom-call | flops 1000000000 | bytes 65536 | tf_op jit(solution)/shard_map/receivers/pallas_call | solution.py:373
  31.4 1.5 %collective-permute-start.6 = (f32[4,128,128]{2,1,0:T(8,128)S(1)}, f32[4,128,128]{2,1,0:T(8,128)S(1)}, u32[]{:S(2)}, u32[]{:S(2)}) collective-permute-start(f32[4,128,128]{2,1,0:T(8,128)S(1)} %get-tuple-element.125), channel_id=1, source_target_pairs={{0,1},{1,0},{2,3},{3,2},{4,5},{5,4},{6,7},{7,6},{8,9},{9,8},{10,11... | collective-permute-start | bytes 786440 | tf_op jit(solution)/shard_map/ppermute | solution.py:420
  34.4 4.4 %collective-permute-start.7 = (f32[4,128,128]{2,1,0:T(8,128)S(1)}, f32[4,128,128]{2,1,0:T(8,128)S(1)}, u32[]{:S(2)}, u32[]{:S(2)}) collective-permute-start(f32[4,128,128]{2,1,0:T(8,128)S(1)} %get-tuple-element.126), channel_id=1, source_target_pairs={{1,2},{2,1},{5,6},{6,5},{9,10},{10,9},{13,14},{14,13},{17,18},{18,... | collective-permute-start | bytes 786440 | tf_op jit(solution)/shard_map/ppermute | solution.py:423
  40.6 1.9 %collective-permute-start.15 = (f32[4,128,128]{2,1,0:T(8,128)S(1)}, f32[4,128,128]{2,1,0:T(8,128)S(1)}, u32[]{:S(2)}, u32[]{:S(2)}) collective-permute-start(f32[4,128,128]{2,1,0:T(8,128)S(1)} %get-tuple-element.143), channel_id=1, source_target_pairs={{1,2},{2,1},{5,6},{6,5},{9,10},{10,9},{13,14},{14,13},{17,18},{18,... | collective-permute-start | bytes 786440 | tf_op jit(solution)/shard_map/ppermute | solution.py:423
  42.5 2.7 %collective-permute-done.7.refs_3_ = f32[4,128,128]{2,1,0:T(8,128)S(1)} collective-permute-done((f32[4,128,128]{2,1,0:T(8,128)S(1)}, f32[4,128,128]{2,1,0:T(8,128)S(1)}, u32[]{:S(2)}, u32[]{:S(2)}) %collective-permute-start.7) | collective-permute-done | bytes 262176 | tf_op jit(solution)/shard_map/ppermute | solution.py:423
  46.9 4.4 %collective-permute-start.9 = (f32[4,128,128]{2,1,0:T(8,128)S(1)}, f32[4,128,128]{2,1,0:T(8,128)S(1)}, u32[]{:S(2)}, u32[]{:S(2)}) collective-permute-start(f32[4,128,128]{2,1,0:T(8,128)S(1)} %get-tuple-element.130), channel_id=1, source_target_pairs={{1,2},{2,1},{5,6},{6,5},{9,10},{10,9},{13,14},{14,13},{17,18},{18,... | collective-permute-start | bytes 786440 | tf_op jit(solution)/shard_map/ppermute | solution.py:423
  53.2 3.2 %collective-permute-start.17 = (f32[4,128,128]{2,1,0:T(8,128)S(1)}, f32[4,128,128]{2,1,0:T(8,128)S(1)}, u32[]{:S(2)}, u32[]{:S(2)}) collective-permute-start(f32[4,128,128]{2,1,0:T(8,128)S(1)} %get-tuple-element.148), channel_id=1, source_target_pairs={{1,2},{2,1},{5,6},{6,5},{9,10},{10,9},{13,14},{14,13},{17,18},{18,... | collective-permute-start | bytes 786440 | tf_op jit(solution)/shard_map/ppermute | solution.py:423
  59.6 2.6 %collective-permute-start.11 = (f32[4,128,128]{2,1,0:T(8,128)S(1)}, f32[4,128,128]{2,1,0:T(8,128)S(1)}, u32[]{:S(2)}, u32[]{:S(2)}) collective-permute-start(f32[4,128,128]{2,1,0:T(8,128)S(1)} %get-tuple-element.134), channel_id=1, source_target_pairs={{1,2},{2,1},{5,6},{6,5},{9,10},{10,9},{13,14},{14,13},{17,18},{18,... | collective-permute-start | bytes 786440 | tf_op jit(solution)/shard_map/ppermute | solution.py:423
  65.2 3.4 %collective-permute-start.21 = (f32[4,128,128]{2,1,0:T(8,128)S(1)}, f32[4,128,128]{2,1,0:T(8,128)S(1)}, u32[]{:S(2)}, u32[]{:S(2)}) collective-permute-start(f32[4,128,128]{2,1,0:T(8,128)S(1)} %get-tuple-element.156), channel_id=1, source_target_pairs={{1,2},{2,1},{5,6},{6,5},{9,10},{10,9},{13,14},{14,13},{17,18},{18,... | collective-permute-start | bytes 786440 | tf_op jit(solution)/shard_map/ppermute | solution.py:423
  70.9 3.3 %collective-permute-start.19 = (f32[4,128,128]{2,1,0:T(8,128)S(1)}, f32[4,128,128]{2,1,0:T(8,128)S(1)}, u32[]{:S(2)}, u32[]{:S(2)}) collective-permute-start(f32[4,128,128]{2,1,0:T(8,128)S(1)} %get-tuple-element.153), channel_id=1, source_target_pairs={{1,2},{2,1},{5,6},{6,5},{9,10},{10,9},{13,14},{14,13},{17,18},{18,... | collective-permute-start | bytes 786440 | tf_op jit(solution)/shard_map/ppermute | solution.py:423
  77.9 2.6 %collective-permute-start.25 = (f32[4,128,128]{2,1,0:T(8,128)S(1)}, f32[4,128,128]{2,1,0:T(8,128)S(1)}, u32[]{:S(2)}, u32[]{:S(2)}) collective-permute-start(f32[4,128,128]{2,1,0:T(8,128)S(1)} %get-tuple-element.169), channel_id=1, source_target_pairs={{1,2},{2,1},{5,6},{6,5},{9,10},{10,9},{13,14},{14,13},{17,18},{18,... | collective-permute-start | bytes 786440 | tf_op jit(solution)/shard_map/ppermute | solution.py:423
  80.9 2.3 %collective-permute-done.18.refs_2_ = f32[4,128,128]{2,1,0:T(8,128)S(1)} collective-permute-done((f32[4,128,128]{2,1,0:T(8,128)S(1)}, f32[4,128,128]{2,1,0:T(8,128)S(1)}, u32[]{:S(2)}, u32[]{:S(2)}) %collective-permute-start.18) | collective-permute-done | bytes 262176 | tf_op jit(solution)/shard_map/ppermute | solution.py:420
  85.1 2.3 %collective-permute-start.23 = (f32[4,128,128]{2,1,0:T(8,128)S(1)}, f32[4,128,128]{2,1,0:T(8,128)S(1)}, u32[]{:S(2)}, u32[]{:S(2)}) collective-permute-start(f32[4,128,128]{2,1,0:T(8,128)S(1)} %get-tuple-element.166), channel_id=1, source_target_pairs={{1,2},{2,1},{5,6},{6,5},{9,10},{10,9},{13,14},{14,13},{17,18},{18,... | collective-permute-start | bytes 786440 | tf_op jit(solution)/shard_map/ppermute | solution.py:423
  90.7 2.4 %collective-permute-start.29 = (f32[4,128,128]{2,1,0:T(8,128)S(1)}, f32[4,128,128]{2,1,0:T(8,128)S(1)}, u32[]{:S(2)}, u32[]{:S(2)}) collective-permute-start(f32[4,128,128]{2,1,0:T(8,128)S(1)} %get-tuple-element.183), channel_id=1, source_target_pairs={{1,2},{2,1},{5,6},{6,5},{9,10},{10,9},{13,14},{14,13},{17,18},{18,... | collective-permute-start | bytes 786440 | tf_op jit(solution)/shard_map/ppermute | solution.py:423
  96.8 3.2 %collective-permute-start.27 = (f32[4,128,128]{2,1,0:T(8,128)S(1)}, f32[4,128,128]{2,1,0:T(8,128)S(1)}, u32[]{:S(2)}, u32[]{:S(2)}) collective-permute-start(f32[4,128,128]{2,1,0:T(8,128)S(1)} %get-tuple-element.180), channel_id=1, source_target_pairs={{1,2},{2,1},{5,6},{6,5},{9,10},{10,9},{13,14},{14,13},{17,18},{18,... | collective-permute-start | bytes 786440 | tf_op jit(solution)/shard_map/ppermute | solution.py:423
  103.0 2.9 %collective-permute-start.37 = (f32[4,128,128]{2,1,0:T(8,128)S(1)}, f32[4,128,128]{2,1,0:T(8,128)S(1)}, u32[]{:S(2)}, u32[]{:S(2)}) collective-permute-start(f32[4,128,128]{2,1,0:T(8,128)S(1)} %get-tuple-element.202), channel_id=1, source_target_pairs={{1,2},{2,1},{5,6},{6,5},{9,10},{10,9},{13,14},{14,13},{17,18},{18,... | collective-permute-start | bytes 786440 | tf_op jit(solution)/shard_map/ppermute | solution.py:423
  106.9 1.6 %collective-permute-done.36.refs_2_ = f32[4,128,128]{2,1,0:T(8,128)S(1)} collective-permute-done((f32[4,128,128]{2,1,0:T(8,128)S(1)}, f32[4,128,128]{2,1,0:T(8,128)S(1)}, u32[]{:S(2)}, u32[]{:S(2)}) %collective-permute-start.36) | collective-permute-done | bytes 262176 | tf_op jit(solution)/shard_map/ppermute | solution.py:420
  108.5 2.7 %collective-permute-done.37.refs_3_ = f32[4,128,128]{2,1,0:T(8,128)S(1)} collective-permute-done((f32[4,128,128]{2,1,0:T(8,128)S(1)}, f32[4,128,128]{2,1,0:T(8,128)S(1)}, u32[]{:S(2)}, u32[]{:S(2)}) %collective-permute-start.37) | collective-permute-done | bytes 262176 | tf_op jit(solution)/shard_map/ppermute | solution.py:423
  112.1 1.7 %adjoint_inner.15 = (f32[16,128,128]{2,1,0:T(8,128)}, f32[16,128,128]{2,1,0:T(8,128)}, f32[4,128,128]{2,1,0:T(8,128)S(1)}) custom-call(f32[8,128,128]{2,1,0:T(8,128)S(1)} %get-tuple-element.178.refs_0_.refs_6_, f32[8,128,128]{2,1,0:T(8,128)S(1)} %get-tuple-element.186.refs_1_.refs_8_, bf16[256,256]{1,0:T(8,128)(2,1)S(1)} %copy-done.1, ...), custom_call_target="tpu_custom_call" | custom-call | flops 1000000000 | bytes 65536 | tf_op jit(solution)/shard_map/adjoint_inner/pallas_call | solution.py:373
  113.7 2.9 %collective-permute-start.31 = (f32[4,128,128]{2,1,0:T(8,128)S(1)}, f32[4,128,128]{2,1,0:T(8,128)S(1)}, u32[]{:S(2)}, u32[]{:S(2)}) collective-permute-start(f32[4,128,128]{2,1,0:T(8,128)S(1)} %get-tuple-element.188), channel_id=1, source_target_pairs={{1,2},{2,1},{5,6},{6,5},{9,10},{10,9},{13,14},{14,13},{17,18},{18,... | collective-permute-start | bytes 786440 | tf_op jit(solution)/shard_map/ppermute | solution.py:423
  117.4 1.5 %collective-permute-start.34 = (f32[8,16,128]{2,1,0:T(8,128)S(1)}, f32[8,16,128]{2,1,0:T(8,128)S(1)}, u32[]{:S(2)}, u32[]{:S(2)}) collective-permute-start(f32[8,16,128]{2,1,0:T(8,128)S(1)} %get-tuple-element.199), channel_id=1, source_target_pairs={{0,16},{4,20},{8,24},{12,28},{16,0},{20,4},{24,8},{28,12},{1,17},{... | collective-permute-start | bytes 196616 | tf_op jit(solution)/shard_map/ppermute | solution.py:533
  118.9 1.4 %collective-permute-start.35 = (f32[8,16,128]{2,1,0:T(8,128)S(1)}, f32[8,16,128]{2,1,0:T(8,128)S(1)}, u32[]{:S(2)}, u32[]{:S(2)}) collective-permute-start(f32[8,16,128]{2,1,0:T(8,128)S(1)} %get-tuple-element.200), channel_id=1, source_target_pairs={{0,24},{4,28},{8,16},{12,20},{16,8},{20,12},{24,0},{28,4},{1,25},{... | collective-permute-start | bytes 196616 | tf_op jit(solution)/shard_map/ppermute | solution.py:533
  121.0 3.4 %collective-permute-done.31.refs_3_ = f32[4,128,128]{2,1,0:T(8,128)S(1)} collective-permute-done((f32[4,128,128]{2,1,0:T(8,128)S(1)}, f32[4,128,128]{2,1,0:T(8,128)S(1)}, u32[]{:S(2)}, u32[]{:S(2)}) %collective-permute-start.31) | collective-permute-done | bytes 262176 | tf_op jit(solution)/shard_map/ppermute | solution.py:423
  124.3 1.5 %collective-permute-start.40 = (f32[8,16,128]{2,1,0:T(8,128)S(1)}, f32[8,16,128]{2,1,0:T(8,128)S(1)}, u32[]{:S(2)}, u32[]{:S(2)}) collective-permute-start(f32[8,16,128]{2,1,0:T(8,128)S(1)} %get-tuple-element.209), channel_id=1, source_target_pairs={{0,16},{4,20},{8,24},{12,28},{16,0},{20,4},{24,8},{28,12},{1,17},{... | collective-permute-start | bytes 196616 | tf_op jit(solution)/shard_map/ppermute | solution.py:533
  126.3 1.6 %adjoint_border.15 = f32[16,128,128]{2,1,0:T(8,128)} custom-call(f32[8,128,128]{2,1,0:T(8,128)S(1)} %get-tuple-element.178.refs_0_.refs_6_, f32[8,128,128]{2,1,0:T(8,128)S(1)} %get-tuple-element.186.refs_1_.refs_8_, f32[4,128,128]{2,1,0:T(8,128)S(1)} %collective-permute-done.30.refs_2_, ...), custom_call_target="tpu_custom_call", output_to_operand_aliasing={{}: (9, {})} | custom-call | flops 30000001024 | bytes 1966080 | tf_op jit(solution)/shard_map/adjoint_border/pallas_call | solution.py:373
  128.6 2.4 %collective-permute-done.41.refs_7_ = f32[8,16,128]{2,1,0:T(8,128)S(1)} collective-permute-done((f32[8,16,128]{2,1,0:T(8,128)S(1)}, f32[8,16,128]{2,1,0:T(8,128)S(1)}, u32[]{:S(2)}, u32[]{:S(2)}) %collective-permute-start.41) | collective-permute-done | bytes 65568 | tf_op jit(solution)/shard_map/ppermute | solution.py:533
  (98 shorter events, 42.2 us)
Async XLA Ops:
  1.8 13.4 %collective-permute-start.2 = (f32[4,128,128]{2,1,0:T(8,128)S(1)}, f32[4,128,128]{2,1,0:T(8,128)S(1)}, u32[]{:S(2)}, u32[]{:S(2)}) collective-permute-start(f32[4,128,128]{2,1,0:T(8,128)S(1)} %get-tuple-element.114), channel_id=1, source_target_pairs={{0,1},{1,0},{2,3},{3,2},{4,5},{5,4},{6,7},{7,6},{8,9},{9,8},{10,11... | collective-permute-start | bytes 786440 | tf_op jit(solution)/shard_map/ppermute | solution.py:420
  6.4 11.5 %collective-permute-start.3 = (f32[4,128,128]{2,1,0:T(8,128)S(1)}, f32[4,128,128]{2,1,0:T(8,128)S(1)}, u32[]{:S(2)}, u32[]{:S(2)}) collective-permute-start(f32[4,128,128]{2,1,0:T(8,128)S(1)} %get-tuple-element.116), channel_id=1, source_target_pairs={{1,2},{2,1},{5,6},{6,5},{9,10},{10,9},{13,14},{14,13},{17,18},{18,... | collective-permute-start | bytes 786440 | tf_op jit(solution)/shard_map/ppermute | solution.py:423
  11.1 19.4 %collective-permute-start.4 = (f32[4,128,128]{2,1,0:T(8,128)S(1)}, f32[4,128,128]{2,1,0:T(8,128)S(1)}, u32[]{:S(2)}, u32[]{:S(2)}) collective-permute-start(f32[4,128,128]{2,1,0:T(8,128)S(1)} %get-tuple-element.120), channel_id=1, source_target_pairs={{0,1},{1,0},{2,3},{3,2},{4,5},{5,4},{6,7},{7,6},{8,9},{9,8},{10,11... | collective-permute-start | bytes 786440 | tf_op jit(solution)/shard_map/ppermute | solution.py:420
  13.2 17.4 %collective-permute-start.5 = (f32[4,128,128]{2,1,0:T(8,128)S(1)}, f32[4,128,128]{2,1,0:T(8,128)S(1)}, u32[]{:S(2)}, u32[]{:S(2)}) collective-permute-start(f32[4,128,128]{2,1,0:T(8,128)S(1)} %get-tuple-element.121), channel_id=1, source_target_pairs={{1,2},{2,1},{5,6},{6,5},{9,10},{10,9},{13,14},{14,13},{17,18},{18,... | collective-permute-start | bytes 786440 | tf_op jit(solution)/shard_map/ppermute | solution.py:423
  18.7 20.2 %collective-permute-start.12 = (f32[4,128,128]{2,1,0:T(8,128)S(1)}, f32[4,128,128]{2,1,0:T(8,128)S(1)}, u32[]{:S(2)}, u32[]{:S(2)}) collective-permute-start(f32[4,128,128]{2,1,0:T(8,128)S(1)} %get-tuple-element.138), channel_id=1, source_target_pairs={{0,1},{1,0},{2,3},{3,2},{4,5},{5,4},{6,7},{7,6},{8,9},{9,8},{10,11... | collective-permute-start | bytes 786440 | tf_op jit(solution)/shard_map/ppermute | solution.py:420
  20.2 18.7 %collective-permute-start.13 = (f32[4,128,128]{2,1,0:T(8,128)S(1)}, f32[4,128,128]{2,1,0:T(8,128)S(1)}, u32[]{:S(2)}, u32[]{:S(2)}) collective-permute-start(f32[4,128,128]{2,1,0:T(8,128)S(1)} %get-tuple-element.139), channel_id=1, source_target_pairs={{1,2},{2,1},{5,6},{6,5},{9,10},{10,9},{13,14},{14,13},{17,18},{18,... | collective-permute-start | bytes 786440 | tf_op jit(solution)/shard_map/ppermute | solution.py:423
  31.4 11.1 %collective-permute-start.6 = (f32[4,128,128]{2,1,0:T(8,128)S(1)}, f32[4,128,128]{2,1,0:T(8,128)S(1)}, u32[]{:S(2)}, u32[]{:S(2)}) collective-permute-start(f32[4,128,128]{2,1,0:T(8,128)S(1)} %get-tuple-element.125), channel_id=1, source_target_pairs={{0,1},{1,0},{2,3},{3,2},{4,5},{5,4},{6,7},{7,6},{8,9},{9,8},{10,11... | collective-permute-start | bytes 786440 | tf_op jit(solution)/shard_map/ppermute | solution.py:420
  34.4 10.8 %collective-permute-start.7 = (f32[4,128,128]{2,1,0:T(8,128)S(1)}, f32[4,128,128]{2,1,0:T(8,128)S(1)}, u32[]{:S(2)}, u32[]{:S(2)}) collective-permute-start(f32[4,128,128]{2,1,0:T(8,128)S(1)} %get-tuple-element.126), channel_id=1, source_target_pairs={{1,2},{2,1},{5,6},{6,5},{9,10},{10,9},{13,14},{14,13},{17,18},{18,... | collective-permute-start | bytes 786440 | tf_op jit(solution)/shard_map/ppermute | solution.py:423
  39.7 11.6 %collective-permute-start.14 = (f32[4,128,128]{2,1,0:T(8,128)S(1)}, f32[4,128,128]{2,1,0:T(8,128)S(1)}, u32[]{:S(2)}, u32[]{:S(2)}) collective-permute-start(f32[4,128,128]{2,1,0:T(8,128)S(1)} %get-tuple-element.142), channel_id=1, source_target_pairs={{0,1},{1,0},{2,3},{3,2},{4,5},{5,4},{6,7},{7,6},{8,9},{9,8},{10,11... | collective-permute-start | bytes 786440 | tf_op jit(solution)/shard_map/ppermute | solution.py:420
  40.6 11.1 %collective-permute-start.15 = (f32[4,128,128]{2,1,0:T(8,128)S(1)}, f32[4,128,128]{2,1,0:T(8,128)S(1)}, u32[]{:S(2)}, u32[]{:S(2)}) collective-permute-start(f32[4,128,128]{2,1,0:T(8,128)S(1)} %get-tuple-element.143), channel_id=1, source_target_pairs={{1,2},{2,1},{5,6},{6,5},{9,10},{10,9},{13,14},{14,13},{17,18},{18,... | collective-permute-start | bytes 786440 | tf_op jit(solution)/shard_map/ppermute | solution.py:423
  46.0 10.5 %collective-permute-start.8 = (f32[4,128,128]{2,1,0:T(8,128)S(1)}, f32[4,128,128]{2,1,0:T(8,128)S(1)}, u32[]{:S(2)}, u32[]{:S(2)}) collective-permute-start(f32[4,128,128]{2,1,0:T(8,128)S(1)} %get-tuple-element.129), channel_id=1, source_target_pairs={{0,1},{1,0},{2,3},{3,2},{4,5},{5,4},{6,7},{7,6},{8,9},{9,8},{10,11... | collective-permute-start | bytes 786440 | tf_op jit(solution)/shard_map/ppermute | solution.py:420
  46.9 11.0 %collective-permute-start.9 = (f32[4,128,128]{2,1,0:T(8,128)S(1)}, f32[4,128,128]{2,1,0:T(8,128)S(1)}, u32[]{:S(2)}, u32[]{:S(2)}) collective-permute-start(f32[4,128,128]{2,1,0:T(8,128)S(1)} %get-tuple-element.130), channel_id=1, source_target_pairs={{1,2},{2,1},{5,6},{6,5},{9,10},{10,9},{13,14},{14,13},{17,18},{18,... | collective-permute-start | bytes 786440 | tf_op jit(solution)/shard_map/ppermute | solution.py:423
  52.4 9.8 %collective-permute-start.16 = (f32[4,128,128]{2,1,0:T(8,128)S(1)}, f32[4,128,128]{2,1,0:T(8,128)S(1)}, u32[]{:S(2)}, u32[]{:S(2)}) collective-permute-start(f32[4,128,128]{2,1,0:T(8,128)S(1)} %get-tuple-element.147), channel_id=1, source_target_pairs={{0,1},{1,0},{2,3},{3,2},{4,5},{5,4},{6,7},{7,6},{8,9},{9,8},{10,11... | collective-permute-start | bytes 786440 | tf_op jit(solution)/shard_map/ppermute | solution.py:420
  53.2 10.3 %collective-permute-start.17 = (f32[4,128,128]{2,1,0:T(8,128)S(1)}, f32[4,128,128]{2,1,0:T(8,128)S(1)}, u32[]{:S(2)}, u32[]{:S(2)}) collective-permute-start(f32[4,128,128]{2,1,0:T(8,128)S(1)} %get-tuple-element.148), channel_id=1, source_target_pairs={{1,2},{2,1},{5,6},{6,5},{9,10},{10,9},{13,14},{14,13},{17,18},{18,... | collective-permute-start | bytes 786440 | tf_op jit(solution)/shard_map/ppermute | solution.py:423
  58.8 9.7 %collective-permute-start.10 = (f32[4,128,128]{2,1,0:T(8,128)S(1)}, f32[4,128,128]{2,1,0:T(8,128)S(1)}, u32[]{:S(2)}, u32[]{:S(2)}) collective-permute-start(f32[4,128,128]{2,1,0:T(8,128)S(1)} %get-tuple-element.133), channel_id=1, source_target_pairs={{0,1},{1,0},{2,3},{3,2},{4,5},{5,4},{6,7},{7,6},{8,9},{9,8},{10,11... | collective-permute-start | bytes 786440 | tf_op jit(solution)/shard_map/ppermute | solution.py:420
  59.6 9.6 %collective-permute-start.11 = (f32[4,128,128]{2,1,0:T(8,128)S(1)}, f32[4,128,128]{2,1,0:T(8,128)S(1)}, u32[]{:S(2)}, u32[]{:S(2)}) collective-permute-start(f32[4,128,128]{2,1,0:T(8,128)S(1)} %get-tuple-element.134), channel_id=1, source_target_pairs={{1,2},{2,1},{5,6},{6,5},{9,10},{10,9},{13,14},{14,13},{17,18},{18,... | collective-permute-start | bytes 786440 | tf_op jit(solution)/shard_map/ppermute | solution.py:423
  64.4 9.9 %collective-permute-start.20 = (f32[4,128,128]{2,1,0:T(8,128)S(1)}, f32[4,128,128]{2,1,0:T(8,128)S(1)}, u32[]{:S(2)}, u32[]{:S(2)}) collective-permute-start(f32[4,128,128]{2,1,0:T(8,128)S(1)} %get-tuple-element.155), channel_id=1, source_target_pairs={{0,1},{1,0},{2,3},{3,2},{4,5},{5,4},{6,7},{7,6},{8,9},{9,8},{10,11... | collective-permute-start | bytes 786440 | tf_op jit(solution)/shard_map/ppermute | solution.py:420
  65.2 10.1 %collective-permute-start.21 = (f32[4,128,128]{2,1,0:T(8,128)S(1)}, f32[4,128,128]{2,1,0:T(8,128)S(1)}, u32[]{:S(2)}, u32[]{:S(2)}) collective-permute-start(f32[4,128,128]{2,1,0:T(8,128)S(1)} %get-tuple-element.156), channel_id=1, source_target_pairs={{1,2},{2,1},{5,6},{6,5},{9,10},{10,9},{13,14},{14,13},{17,18},{18,... | collective-permute-start | bytes 786440 | tf_op jit(solution)/shard_map/ppermute | solution.py:423
  70.9 10.0 %collective-permute-start.19 = (f32[4,128,128]{2,1,0:T(8,128)S(1)}, f32[4,128,128]{2,1,0:T(8,128)S(1)}, u32[]{:S(2)}, u32[]{:S(2)}) collective-permute-start(f32[4,128,128]{2,1,0:T(8,128)S(1)} %get-tuple-element.153), channel_id=1, source_target_pairs={{1,2},{2,1},{5,6},{6,5},{9,10},{10,9},{13,14},{14,13},{17,18},{18,... | collective-permute-start | bytes 786440 | tf_op jit(solution)/shard_map/ppermute | solution.py:423
  76.1 12.7 %collective-permute-start.24 = (f32[4,128,128]{2,1,0:T(8,128)S(1)}, f32[4,128,128]{2,1,0:T(8,128)S(1)}, u32[]{:S(2)}, u32[]{:S(2)}) collective-permute-start(f32[4,128,128]{2,1,0:T(8,128)S(1)} %get-tuple-element.168), channel_id=1, source_target_pairs={{0,1},{1,0},{2,3},{3,2},{4,5},{5,4},{6,7},{7,6},{8,9},{9,8},{10,11... | collective-permute-start | bytes 786440 | tf_op jit(solution)/shard_map/ppermute | solution.py:420
  77.9 10.9 %collective-permute-start.25 = (f32[4,128,128]{2,1,0:T(8,128)S(1)}, f32[4,128,128]{2,1,0:T(8,128)S(1)}, u32[]{:S(2)}, u32[]{:S(2)}) collective-permute-start(f32[4,128,128]{2,1,0:T(8,128)S(1)} %get-tuple-element.169), channel_id=1, source_target_pairs={{1,2},{2,1},{5,6},{6,5},{9,10},{10,9},{13,14},{14,13},{17,18},{18,... | collective-permute-start | bytes 786440 | tf_op jit(solution)/shard_map/ppermute | solution.py:423
  84.0 10.4 %collective-permute-start.22 = (f32[4,128,128]{2,1,0:T(8,128)S(1)}, f32[4,128,128]{2,1,0:T(8,128)S(1)}, u32[]{:S(2)}, u32[]{:S(2)}) collective-permute-start(f32[4,128,128]{2,1,0:T(8,128)S(1)} %get-tuple-element.165), channel_id=1, source_target_pairs={{0,1},{1,0},{2,3},{3,2},{4,5},{5,4},{6,7},{7,6},{8,9},{9,8},{10,11... | collective-permute-start | bytes 786440 | tf_op jit(solution)/shard_map/ppermute | solution.py:420
  85.1 10.1 %collective-permute-start.23 = (f32[4,128,128]{2,1,0:T(8,128)S(1)}, f32[4,128,128]{2,1,0:T(8,128)S(1)}, u32[]{:S(2)}, u32[]{:S(2)}) collective-permute-start(f32[4,128,128]{2,1,0:T(8,128)S(1)} %get-tuple-element.166), channel_id=1, source_target_pairs={{1,2},{2,1},{5,6},{6,5},{9,10},{10,9},{13,14},{14,13},{17,18},{18,... | collective-permute-start | bytes 786440 | tf_op jit(solution)/shard_map/ppermute | solution.py:423
  89.6 10.4 %collective-permute-start.28 = (f32[4,128,128]{2,1,0:T(8,128)S(1)}, f32[4,128,128]{2,1,0:T(8,128)S(1)}, u32[]{:S(2)}, u32[]{:S(2)}) collective-permute-start(f32[4,128,128]{2,1,0:T(8,128)S(1)} %get-tuple-element.182), channel_id=1, source_target_pairs={{0,1},{1,0},{2,3},{3,2},{4,5},{5,4},{6,7},{7,6},{8,9},{9,8},{10,11... | collective-permute-start | bytes 786440 | tf_op jit(solution)/shard_map/ppermute | solution.py:420
  90.7 10.4 %collective-permute-start.29 = (f32[4,128,128]{2,1,0:T(8,128)S(1)}, f32[4,128,128]{2,1,0:T(8,128)S(1)}, u32[]{:S(2)}, u32[]{:S(2)}) collective-permute-start(f32[4,128,128]{2,1,0:T(8,128)S(1)} %get-tuple-element.183), channel_id=1, source_target_pairs={{1,2},{2,1},{5,6},{6,5},{9,10},{10,9},{13,14},{14,13},{17,18},{18,... | collective-permute-start | bytes 786440 | tf_op jit(solution)/shard_map/ppermute | solution.py:423
  96.0 10.0 %collective-permute-start.26 = (f32[4,128,128]{2,1,0:T(8,128)S(1)}, f32[4,128,128]{2,1,0:T(8,128)S(1)}, u32[]{:S(2)}, u32[]{:S(2)}) collective-permute-start(f32[4,128,128]{2,1,0:T(8,128)S(1)} %get-tuple-element.179), channel_id=1, source_target_pairs={{0,1},{1,0},{2,3},{3,2},{4,5},{5,4},{6,7},{7,6},{8,9},{9,8},{10,11... | collective-permute-start | bytes 786440 | tf_op jit(solution)/shard_map/ppermute | solution.py:420
  96.8 9.2 %collective-permute-start.27 = (f32[4,128,128]{2,1,0:T(8,128)S(1)}, f32[4,128,128]{2,1,0:T(8,128)S(1)}, u32[]{:S(2)}, u32[]{:S(2)}) collective-permute-start(f32[4,128,128]{2,1,0:T(8,128)S(1)} %get-tuple-element.180), channel_id=1, source_target_pairs={{1,2},{2,1},{5,6},{6,5},{9,10},{10,9},{13,14},{14,13},{17,18},{18,... | collective-permute-start | bytes 786440 | tf_op jit(solution)/shard_map/ppermute | solution.py:423
  105.9 10.8 %collective-permute-start.32 = (f32[4,8,16,128]{3,2,1,0:T(8,128)S(1)}, f32[4,8,16,128]{3,2,1,0:T(8,128)S(1)}, u32[]{:S(2)}, u32[]{:S(2)}) collective-permute-start(f32[4,8,16,128]{3,2,1,0:T(8,128)S(1)} %get-tuple-element.196), channel_id=1, source_target_pairs={{0,4},{4,0},{8,12},{12,8},{16,20},{20,16},{24,28},{28,24},{1,5},{5... | collective-permute-start | bytes 786440 | tf_op jit(solution)/shard_map/ppermute | solution.py:529
  106.8 13.5 %collective-permute-start.30 = (f32[4,128,128]{2,1,0:T(8,128)S(1)}, f32[4,128,128]{2,1,0:T(8,128)S(1)}, u32[]{:S(2)}, u32[]{:S(2)}) collective-permute-start(f32[4,128,128]{2,1,0:T(8,128)S(1)} %get-tuple-element.187), channel_id=1, source_target_pairs={{0,1},{1,0},{2,3},{3,2},{4,5},{5,4},{6,7},{7,6},{8,9},{9,8},{10,11... | collective-permute-start | bytes 786440 | tf_op jit(solution)/shard_map/ppermute | solution.py:420
  113.7 10.6 %collective-permute-start.31 = (f32[4,128,128]{2,1,0:T(8,128)S(1)}, f32[4,128,128]{2,1,0:T(8,128)S(1)}, u32[]{:S(2)}, u32[]{:S(2)}) collective-permute-start(f32[4,128,128]{2,1,0:T(8,128)S(1)} %get-tuple-element.188), channel_id=1, source_target_pairs={{1,2},{2,1},{5,6},{6,5},{9,10},{10,9},{13,14},{14,13},{17,18},{18,... | collective-permute-start | bytes 786440 | tf_op jit(solution)/shard_map/ppermute | solution.py:423
  116.7 9.1 %collective-permute-start.33 = (f32[8,16,128]{2,1,0:T(8,128)S(1)}, f32[8,16,128]{2,1,0:T(8,128)S(1)}, u32[]{:S(2)}, u32[]{:S(2)}) collective-permute-start(f32[8,16,128]{2,1,0:T(8,128)S(1)} %get-tuple-element.198), channel_id=1, source_target_pairs={{0,8},{4,12},{8,0},{12,4},{16,24},{20,28},{24,16},{28,20},{1,9},{5... | collective-permute-start | bytes 196616 | tf_op jit(solution)/shard_map/ppermute | solution.py:533
  117.4 10.6 %collective-permute-start.34 = (f32[8,16,128]{2,1,0:T(8,128)S(1)}, f32[8,16,128]{2,1,0:T(8,128)S(1)}, u32[]{:S(2)}, u32[]{:S(2)}) collective-permute-start(f32[8,16,128]{2,1,0:T(8,128)S(1)} %get-tuple-element.199), channel_id=1, source_target_pairs={{0,16},{4,20},{8,24},{12,28},{16,0},{20,4},{24,8},{28,12},{1,17},{... | collective-permute-start | bytes 196616 | tf_op jit(solution)/shard_map/ppermute | solution.py:533
  (13 other events, 90.2 us)

commit v4 on v2

--- a/solution.py
+++ b/solution.py
@@ -69,7 +69,7 @@
         odd[...] = field[count - reach :]
 
 
-def laplace_planes(cur, halo, right, left, put):
+def laplace_planes(cur, halo, right, left, put, rows=None):
     count, width_y, width_z = cur.shape
 
     def plane(i):
@@ -79,7 +79,7 @@
             return halo[reach + i - count]
         return cur[i]
 
-    for x in range(0, count, 2):
+    for x in (range(0, count, 2) if rows is None else rows):
         v = [cur[x], cur[x + 1]]
         (h0, l0), (h1, l1) = split(v[0]), split(v[1])
         rows = jnp.concatenate(
@@ -108,7 +108,8 @@
     late = next(it) if adds else None
     acc_in = next(it) if adds and not opens else None
     first, lap_first = (next(it), next(it)) if not moves else (None, None)
-    nxt, even_out, odd_out = [next(it) for _ in range(3)] if moves else (None,) * 3
+    nxt = next(it) if moves else None
+    even_out, odd_out = (next(it), next(it)) if parts["sends"] else (None, None)
     lap_out = next(it) if stores else None
     acc_out = next(it) if adds and moves else None
     send, keep = (next(it), next(it)) if not moves else (None, None)
@@ -154,7 +155,8 @@
             )
             nxt[row, tile, :] = nxt[row, tile, :] + jnp.where(hit, wave_smem[0, parts["step"]], 0.0)
 
-        emit_edges(parity, nxt, even_out, odd_out)
+        if parts["sends"]:
+            emit_edges(parity, nxt, even_out, odd_out)
     else:
         chunk = send.shape[2]
         mine = lax.axis_index("shot") % 2
@@ -168,36 +170,59 @@
 def adjoint_kernel(parts, *refs):
     it = iter(refs)
     cur, later, speed, even, odd, inject, right, left = [next(it) for _ in range(8)]
-    adds, last = parts["adds"], parts["last"]
+    adds = parts["adds"]
     lap_of, acc_in = (next(it), next(it)) if adds else (None, None)
-    nxt = next(it)
-    even_out, odd_out = (next(it), next(it)) if not last else (None, None)
-    cur_out = next(it) if last else None
+    nxt, even_out, odd_out = [next(it) for _ in range(3)]
     acc_out = next(it) if adds else None
     halo = next(it)
     parity = lax.axis_index("slab") % 2
     fill_halo(parity, even, odd, halo)
     width_y = cur.shape[1]
-    field, copies = nxt, []
-    if last:
-        field, sems, cur_sem = next(it), next(it), next(it)
-        copies.append(pltpu.make_async_copy(cur, cur_out, cur_sem))
-        copies[0].start()
 
     def put(x, v, lap):
         added = inject[pl.ds(x * width_y * 8 + parts["time"], width_y, stride=8), :]
-        field[x] = 2.0 * v - later[x] + speed[x] * lap + added
+        nxt[x] = 2.0 * v - later[x] + speed[x] * lap + added
         if adds:
             acc_out[x] = acc_in[x] + v * lap_of[x]
-        if last and x % 2:
-            both = pl.ds(x - 1, 2)
-            copy = pltpu.make_async_copy(field.at[both], nxt.at[both], sems.at[x // 2])
-            copy.start()
-            copies.append(copy)
 
     laplace_planes(cur, halo, right, left, put)
-    if not last:
-        emit_edges(parity, field, even_out, odd_out)
+    emit_edges(parity, nxt, even_out, odd_out)
+
+
+def last_inner_kernel(cur, later, speed, inject, right, left, opening, second, field, sems):
+    count, width_y = cur.shape[:2]
+    copies = [pltpu.make_async_copy(cur, second, sems.at[0])]
+    copies[0].start()
+
+    def put(x, v, lap):
+        added = inject[pl.ds(x * width_y * 8, width_y, stride=8), :]
+        field[x - reach] = 2.0 * v - later[x] + speed[x] * lap + added
+
+    laplace_planes(cur, None, right, left, put, range(reach, count - reach, 2))
+    inner = opening.at[pl.ds(reach, count - 2 * reach)]
+    copies.append(pltpu.make_async_copy(field, inner, sems.at[1]))
+    copies[1].start()
+    for copy in copies:
+        copy.wait()
+
+
+def last_border_kernel(
+    cur, later, speed, even, odd, inject, right, left, opening_in, opening, halo, field, sems
+):
+    count, width_y = cur.shape[:2]
+    fill_halo(lax.axis_index("slab") % 2, even, odd, halo)
+    top = count - reach
+    copies = []
+    for n, first in enumerate((0, top)):
+
+        def put(x, v, lap):
+            added = inject[pl.ds(x * width_y * 8, width_y, stride=8), :]
+            field[n * reach + x - first] = 2.0 * v - later[x] + speed[x] * lap + added
+
+        laplace_planes(cur, halo, right, left, put, range(first, first + reach, 2))
+        rows = opening.at[pl.ds(first, reach)]
+        copies.append(pltpu.make_async_copy(field.at[pl.ds(n * reach, reach)], rows, sems.at[n]))
+        copies[n].start()
     for copy in copies:
         copy.wait()
 
@@ -216,11 +241,32 @@
         copy.wait()
 
 
-def load_kernel(listen, *refs):
-    fields, outs, where_to, sems = refs[:5], refs[5:10], refs[10], refs[11]
-    copies = [pltpu.make_async_copy(fields[i], outs[i], sems.at[i]) for i in range(5)]
+def stack_kernel(*refs):
+    first = 0
+    for ref in refs[:-1]:
+        refs[-1][first : first + ref.shape[0]] = ref[...]
+        first += ref.shape[0]
+
+
+def load_kernel(listen_hbm, *refs):
+    fields, outs, where_to, tiles, listen, sems = refs[:3], refs[4:7], *refs[7:]
+    listen_copy = pltpu.make_async_copy(listen_hbm.at[0], listen, sems.at[3])
+    listen_copy.start()
+    copies = [pltpu.make_async_copy(fields[i], outs[i], sems.at[i]) for i in range(3)]
     for copy in copies:
         copy.start()
+    zero_rows = 64 * 8
+
+    @pl.loop(0, tiles.shape[0] // zero_rows)
+    def _(i):
+        tiles[pl.ds(pl.multiple_of(i * zero_rows, 8), zero_rows), :] = jnp.zeros(
+            (zero_rows, 128), jnp.float32
+        )
+
+    rest = tiles.shape[0] % zero_rows
+    if rest:
+        tiles[tiles.shape[0] - rest :, :] = jnp.zeros((rest, 128), jnp.float32)
+    listen_copy.wait()
     count, width_y, width_z = fields[0].shape
     depth = listen[0:1, :] - lax.axis_index("slab") * count
     inside = (depth >= 0) & (depth < count)
@@ -230,22 +276,16 @@
         copy.wait()
 
 
-def scatter_kernel(where_to, *refs):
-    blocks, out = refs[:-1], refs[-1]
-    steps, per = blocks[0].shape[-2:]
+def scatter_kernel(levels, where_to, *refs):
+    blocks, refs = refs[:levels], refs[levels:]
+    fields, stepped, _, out, outs, even_out, odd_out, sems = refs[:2], *refs[2:5], refs[5:7], *refs[7:]
+    copies = [pltpu.make_async_copy(fields[i], outs[i], sems.at[i]) for i in range(2)]
+    for copy in copies:
+        copy.start()
+    emit_edges(lax.axis_index("slab") % 2, stepped, even_out, odd_out)
+    per = blocks[0].shape[-1]
     group, groups = 4, 8
-    zero_rows = 64 * 8
     slab = lax.axis_index("slab")
-
-    @pl.loop(0, out.shape[0] // zero_rows)
-    def _(i):
-        out[pl.ds(pl.multiple_of(i * zero_rows, 8), zero_rows), :] = jnp.zeros(
-            (zero_rows, 128), jnp.float32
-        )
-
-    rest = out.shape[0] % zero_rows
-    if rest:
-        out[out.shape[0] - rest :, :] = jnp.zeros((rest, 128), jnp.float32)
     lanes = lax.broadcasted_iota(jnp.int32, (8, 128), 1)
     d = 0
     for held_blocks in blocks:
@@ -264,7 +304,7 @@
                         lane = flat & 127
                         tile = flat >> 7
                         moved = pltpu.roll(block, (lane - j) & 127, 1)
-                        tiles.append(tile)
+                        tiles.append(jnp.full((8, 128), tile, jnp.int32))
                         terms.append(jnp.where(lanes == lane, moved, 0.0))
                         slots.append(pl.ds(pl.multiple_of(tile * 8, 8), 8))
                     for g in range(groups):
@@ -273,14 +313,15 @@
                         for u in own:
                             value = held[u] + terms[u]
                             for w in range(g * group, u):
-                                same = (tiles[w] == tiles[u]).astype(jnp.float32)
-                                value = value + terms[w] * same
+                                value = value + jnp.where(tiles[w] == tiles[u], terms[w], 0.0)
                             held[u] = value
                         for u in own:
                             out[slots[u], :] = held[u]
-
-
-def pair_kernel(keep, arrived, *outs):
+    for copy in copies:
+        copy.wait()
+
+
+def pair_kernel(keep, arrived, _, *outs):
     mine = lax.axis_index("shot") // 2
     for m in range(len(outs)):
         outs[m][...] = keep[mine ^ m] + arrived[mine ^ m]
@@ -301,7 +342,7 @@
     return jax.ShapeDtypeStruct(shape, jnp.float32)
 
 
-def call(name, kernel, args, outs, scratch=(), spaces=None, out_spaces=None, micros=2):
+def call(name, kernel, args, outs, scratch=(), spaces=None, out_spaces=None, micros=2, aliases=None):
     spec = lambda space: pl.BlockSpec(memory_space=space)
     spaces = spaces or {}
     args = [
@@ -315,6 +356,7 @@
         in_specs=[spec(spaces.get(i, VMEM)) for i in range(len(args))],
         out_specs=[spec(out_spaces.get(i, VMEM)) for i in range(len(outs))],
         scratch_shapes=scratch,
+        input_output_aliases=aliases or {},
         compiler_params=pltpu.CompilerParams(vmem_limit_bytes=limit),
         cost_estimate=pl.CostEstimate(
             flops=micros * 1000000000, bytes_accessed=micros << 16, transcendentals=0
@@ -358,12 +400,13 @@
 
     right = jnp.asarray(band_right(width_z))
     left = jnp.asarray(band_left(width_y))
-    listen = receivers[0]
 
     blocks = [traces]
     bit = 1
     while bit < slabs:
-        held = blocks[0] if len(blocks) == 1 else jnp.concatenate(blocks, axis=0)
+        held = blocks[0]
+        if len(blocks) > 1:
+            (held,) = call("stack", stack_kernel, blocks, [vmem(bit, *traces.shape[1:])], micros=0)
         blocks.append(lax.ppermute(held, "slab", [(i, i ^ bit) for i in range(slabs)]))
         bit *= 2
 
@@ -372,41 +415,35 @@
     )
     p_halo = swap(p0_even, p0_odd)
     q_halo = swap(q8_even, q8_odd)
-    fields = [state_before[0], state_now[0], adjoint_after[0], adjoint_now[0], speed_term]
-    *loaded, where_to = call(
+    tiles = vmem((count * width_y + 1) * 8, width_z)
+    before, now, speed, where_to, zeros = call(
         "load",
         load_kernel,
-        [listen, *fields],
-        [field] * 5 + [VMEM((1, listen.shape[1]), jnp.int32)],
-        [dma((5,))],
-        {1 + i: HBM for i in range(5)},
+        [receivers, state_before[0], state_now[0], speed_term, held],
+        [field] * 3 + [VMEM((1, receivers.shape[2]), jnp.int32), tiles],
+        [VMEM(receivers.shape[1:], jnp.int32), dma((4,))],
+        {i: HBM for i in range(4)},
         micros=1,
     )
-    (inject,) = call(
-        "receivers",
-        scatter_kernel,
-        [where_to, *blocks],
-        [vmem((count * width_y + 1) * 8, width_z)],
-        (),
-        {0: SMEM},
-        micros=1,
-    )
-    p = {-1: loaded[0], 0: loaded[1]}
-    q = {steps + 1: loaded[2], steps: loaded[3]}
-    speed = loaded[4]
+    p, q = {-1: before, 0: now}, {}
     laps = {}
     acc = None
 
     for k in range(steps):
         last = k == steps - 1
-        parts = dict(moves=not last, stores=k < half, adds=k >= half, opens=k == half, step=k, scale=scale)
+        parts = dict(
+            moves=not last, stores=k < half, adds=k >= half, opens=k == half, step=k, scale=scale,
+            sends=0 < k < steps - 1,
+        )
         args = [p[k], *p_halo, right, left]
         outs, scratch, spaces = [], [halo], {}
         if not last:
             spaces = {len(args) + 2: HBM, len(args) + 3: HBM}
             args += [p[k - 1], speed, source, wavelet]
-            outs += [field, edge, edge]
+            outs += [field]
             scratch += [SMEM(source.shape, jnp.int32), SMEM(wavelet.shape, jnp.float32), dma, dma]
+        if parts["sends"]:
+            outs += [edge, edge]
         if parts["stores"]:
             outs += [field]
         if parts["adds"]:
@@ -420,48 +457,78 @@
             piece = vmem(shots // 2, count, width_y // shots, width_z)
             outs += [piece, piece]
             scratch += [field]
-        got = call(
-            "forward", functools.partial(forward_kernel, parts), args, outs, scratch, spaces,
-            micros=0 if last else 2,
+        got = list(
+            call(
+                "forward", functools.partial(forward_kernel, parts), args, outs, scratch, spaces,
+                micros=0 if last else 2,
+            )
         )
         if not last:
-            p[k + 1] = got[0]
-            p_halo = swap(*got[1:3])
+            p[k + 1] = got.pop(0)
+            if parts["sends"]:
+                p_halo = swap(got.pop(0), got.pop(0))
             if parts["stores"]:
-                laps[k] = got[3]
+                laps[k] = got.pop(0)
             else:
-                acc = got[3]
-        else:
+                acc = got.pop(0)
+        if k == 0:
+            at = 1 + len(blocks)
+            inject, q[steps + 1], q[steps], *sides = call(
+                "receivers",
+                functools.partial(scatter_kernel, len(blocks)),
+                [where_to, *blocks, adjoint_after[0], adjoint_now[0], p[1], zeros],
+                [tiles, field, field, edge, edge],
+                [dma((2,))],
+                {0: SMEM, at: HBM, at + 1: HBM},
+                aliases={at + 3: 0},
+            )
+            p_halo = swap(*sides)
+
+        t = steps - 1 - k
+        if last:
             send, kept = got
             arrived = lax.ppermute(send, "shot", [(i, i ^ 1) for i in range(shots)])
+            whole = plain(count, width_y, width_z)
+            opening, second = call(
+                "last_inner",
+                last_inner_kernel,
+                [q[1], q[2], speed, inject, right, left],
+                [whole, whole],
+                [vmem(count - 2 * reach, width_y, width_z), dma((2,))],
+                None,
+                {0: HBM, 1: HBM},
+                micros=30,
+            )
             piece = vmem(count, width_y // shots, width_z)
-            pieces = call("pair", pair_kernel, [kept, arrived], [piece] * (shots // 2), micros=0)
+            pieces = call(
+                "pair", pair_kernel, [kept, arrived, opening], [piece] * (shots // 2), (), {2: HBM}, micros=0
+            )
             terms = [pieces[0]] + [
                 lax.ppermute(pieces[m], "shot", [(i, i ^ (2 * m)) for i in range(shots)])
                 for m in range(1, shots // 2)
             ]
+            (opening,) = call(
+                "last_border",
+                last_border_kernel,
+                [q[1], q[2], speed, *q_halo, inject, right, left, opening],
+                [whole],
+                [halo, vmem(2 * reach, width_y, width_z), dma((2,))],
+                {8: HBM},
+                {0: HBM},
+                micros=30,
+                aliases={8: 0},
+            )
             (gradient,) = call("sum", sum_kernel, terms, [plain(count, width_y // shots, width_z)], micros=0)
-
-        t = steps - 1 - k
-        parts = dict(adds=k >= half and not last, last=last, time=t)
+            break
+        parts = dict(adds=k >= half, time=t)
         args = [q[t + 1], q[t + 2], speed, *q_halo, inject, right, left]
-        outs, scratch, out_spaces = [field, edge, edge], [halo], {}
-        if last:
-            outs = [plain(count, width_y, width_z)] * 2
-            scratch += [field, dma((count // 2,)), dma]
-            out_spaces = {0: HBM, 1: HBM}
+        outs = [field, edge, edge]
         if parts["adds"]:
             args += [laps[t], acc]
             outs += [field]
-        got = call(
-            "adjoint", functools.partial(adjoint_kernel, parts), args, outs, scratch, None, out_spaces,
-            micros=30 if last else 2,
-        )
+        got = call("adjoint", functools.partial(adjoint_kernel, parts), args, outs, [halo])
         q[t] = got[0]
-        if last:
-            opening, second = got
-        else:
-            q_halo = swap(*got[1:3])
+        q_halo = swap(*got[1:3])
         if parts["adds"]:
             acc = got[3]
 

time: 121 us -> 123 us (1.017)
  starting transfers between devices: 73.2 us -> 75.8 us
  local copies, waits for them, and re-layouts: 0.73 us -> 2.04 us
    ppermute x16, waiting for transfers between devices: 6.01 us -> 1.46 us  [swap(): lax.ppermute(even, 'slab', even_pairs)]
    ppermute x3, waiting for transfers between devices: 1.18 us -> 4.52 us  [body(): lax.ppermute(pieces[m], 'shot', [(i, i ^ 2 * m) for i in range(shots)])]
    ppermute x16, starting transfers between devices: 49.8 us -> 52.4 us  [swap(): lax.ppermute(even, 'slab', even_pairs)]
    unnamed x7 -> x9, local copies, waits for them, and re-layouts: 0.73 us -> 2.04 us
    pallas_call x21 -> x23, Pallas kernels: 36.6 us -> 35.9 us  [call(): pl.pallas_call(kernel, out_shape=outs, in_specs=[spec(spaces.get(i, VMEM)...]
where the time goes in v4:
time: 123 us; the launch traced here: 122 us
  starting transfers between devices  75.8 us (62%)
  Pallas kernels  35.9 us (29%)
  waiting for transfers between devices  7.29 us (6%)
  local copies, waits for them, and re-layouts  2.04 us (2%)
    ppermute x16, starting transfers between devices, swap(): lax.ppermute(even, 'slab', even_pairs)  52.4 us
    pallas_call x23, Pallas kernels, call(): pl.pallas_call(kernel, out_shape=outs, in_specs=[spec(spaces.get(i, VMEM)...  35.9 us
    ppermute x16, starting transfers between devices, swap(): lax.ppermute(odd, 'slab', odd_pairs)  10.7 us
    ppermute x2, starting transfers between devices, body(): lax.ppermute(held, 'slab', [(i, i ^ bit) for i in range(slabs)])  9.09 us
    ppermute x3, waiting for transfers between devices, body(): lax.ppermute(pieces[m], 'shot', [(i, i ^ 2 * m) for i in range(shots)])  4.52 us
    ppermute x3, starting transfers between devices, body(): lax.ppermute(pieces[m], 'shot', [(i, i ^ 2 * m) for i in range(shots)])  3.55 us
  transfers between devices with their start and end apart: 38, of which 8 were waited for; matrix products, arithmetic and copies ran while one was open for 1% of the time, Pallas kernels for 28%

profile of v4, /device:TPU:0, one launch (start us, length us, event | category | flops | bytes accessed | tf_op | source)
XLA Modules:
  0.0 122.2 jit_solution(2803763410219652146)
XLA Ops:
  2.0 3.1 %collective-permute-start.2 = (f32[4,128,128]{2,1,0:T(8,128)S(1)}, f32[4,128,128]{2,1,0:T(8,128)S(1)}, u32[]{:S(2)}, u32[]{:S(2)}) collective-permute-start(f32[4,128,128]{2,1,0:T(8,128)S(1)} %get-tuple-element.77), channel_id=1, source_target_pairs={{0,1},{1,0},{2,3},{3,2},{4,5},{5,4},{6,7},{7,6},{8,9},{9,8},{10,11... | collective-permute-start | bytes 786440 | tf_op jit(solution)/shard_map/ppermute | solution.py:399
  5.7 4.4 %collective-permute-start = (f32[1,8,256]{2,1,0:T(8,128)}, f32[1,8,256]{2,1,0:T(8,128)S(1)}, u32[]{:S(2)}, u32[]{:S(2)}) collective-permute-start(f32[1,8,256]{2,1,0:T(8,128)} %refs_0_.3), channel_id=1, source_target_pairs={{0,1},{1,0},{2,3},{3,2},{4,5},{5,4},{6,7},{7,6},{8,9},{9,8},{10,11... | collective-permute-start | bytes 24584 | tf_op jit(solution)/shard_map/ppermute | solution.py:410
  13.0 4.6 %collective-permute-start.1 = (f32[2,8,256]{2,1,0:T(8,128)S(1)}, f32[2,8,256]{2,1,0:T(8,128)S(1)}, u32[]{:S(2)}, u32[]{:S(2)}) collective-permute-start(f32[2,8,256]{2,1,0:T(8,128)S(1)} %stack.1.refs_3_), channel_id=1, source_target_pairs={{0,2},{1,3},{2,0},{3,1},{4,6},{5,7},{6,4},{7,5},{8,10},{9,11},{10,... | collective-permute-start | bytes 49160 | tf_op jit(solution)/shard_map/ppermute | solution.py:410
  17.6 1.9 %load.1 = (f32[16,128,128]{2,1,0:T(8,128)S(1)}, f32[16,128,128]{2,1,0:T(8,128)S(1)}, f32[16,128,128]{2,1,0:T(8,128)S(1)}, s32[1,1024]{1,0:T(1,128)S(1)}, f32[16392,128]{1,0:T(8,128)S(1)}) custom-call(s32[1,3,1024]{2,1,0:T(4,128)} %copy.16.listen_hbm, f32[16,128,128]{2,1,0:T(8,128)} %bitcast.10, f32[16,128,128]{2,1,0:T(8,128)} %bitcast.12, ...), custom_call_target="tpu_custom_call" | custom-call | flops 1000000000 | bytes 65536 | tf_op jit(solution)/shard_map/load/pallas_call | solution.py:353
  21.9 5.4 %receivers.1 = (f32[16392,128]{1,0:T(8,128)S(1)}, f32[16,128,128]{2,1,0:T(8,128)S(1)}, f32[16,128,128]{2,1,0:T(8,128)S(1)}, f32[4,128,128]{2,1,0:T(8,128)S(1)}, f32[4,128,128]{2,1,0:T(8,128)S(1)}) custom-call(s32[1,1024]{1,0:T(1,128)S(1)} %get-tuple-element.75.where_to, f32[1,8,256]{2,1,0:T(8,128)S(1)} %copy-done.3, ...), custom_call_target="tpu_custom_call", output_to_operand_aliasing={{0}: (7, {})} | custom-call | flops 2000000000 | bytes 131072 | tf_op jit(solution)/shard_map/receivers/pallas_call | solution.py:353
  28.1 1.6 %adjoint.7 = (f32[16,128,128]{2,1,0:T(8,128)S(1)}, f32[4,128,128]{2,1,0:T(8,128)S(1)}, f32[4,128,128]{2,1,0:T(8,128)S(1)}) custom-call(f32[16,128,128]{2,1,0:T(8,128)S(1)} %get-tuple-element.83.refs_0_.refs_1_.refs_5_, f32[16,128,128]{2,1,0:T(8,128)S(1)} %get-tuple-element.84.refs_1_, f32[16,128,128]{2,1,0:T(8,128)S(1)} %get-tuple-element.80.refs_6_.refs_2_.speed, ...), custom_call_target="tpu_custom_call" | custom-call | flops 2000000000 | bytes 131072 | tf_op jit(solution)/shard_map/adjoint/pallas_call | solution.py:353
  29.7 5.2 %collective-permute-start.6 = (f32[4,128,128]{2,1,0:T(8,128)S(1)}, f32[4,128,128]{2,1,0:T(8,128)S(1)}, u32[]{:S(2)}, u32[]{:S(2)}) collective-permute-start(f32[4,128,128]{2,1,0:T(8,128)S(1)} %get-tuple-element.89), channel_id=1, source_target_pairs={{0,1},{1,0},{2,3},{3,2},{4,5},{5,4},{6,7},{7,6},{8,9},{9,8},{10,11... | collective-permute-start | bytes 786440 | tf_op jit(solution)/shard_map/ppermute | solution.py:399
  35.5 1.6 %forward.9 = (f32[16,128,128]{2,1,0:T(8,128)S(1)}, f32[4,128,128]{2,1,0:T(8,128)S(1)}, f32[4,128,128]{2,1,0:T(8,128)S(1)}, f32[16,128,128]{2,1,0:T(8,128)S(1)}) custom-call(f32[16,128,128]{2,1,0:T(8,128)S(1)} %get-tuple-element.81.refs_5_.refs_0_, f32[4,128,128]{2,1,0:T(8,128)S(1)} %collective-permute-done.14.refs_1_, ...), custom_call_target="tpu_custom_call" | custom-call | flops 2000000000 | bytes 131072 | tf_op jit(solution)/shard_map/forward/pallas_call | solution.py:353
  37.1 3.9 %collective-permute-start.16 = (f32[4,128,128]{2,1,0:T(8,128)S(1)}, f32[4,128,128]{2,1,0:T(8,128)S(1)}, u32[]{:S(2)}, u32[]{:S(2)}) collective-permute-start(f32[4,128,128]{2,1,0:T(8,128)S(1)} %get-tuple-element.103), channel_id=1, source_target_pairs={{0,1},{1,0},{2,3},{3,2},{4,5},{5,4},{6,7},{7,6},{8,9},{9,8},{10,11... | collective-permute-start | bytes 786440 | tf_op jit(solution)/shard_map/ppermute | solution.py:399
  41.8 1.5 %adjoint.8 = (f32[16,128,128]{2,1,0:T(8,128)S(1)}, f32[4,128,128]{2,1,0:T(8,128)S(1)}, f32[4,128,128]{2,1,0:T(8,128)S(1)}) custom-call(f32[16,128,128]{2,1,0:T(8,128)S(1)} %get-tuple-element.88.refs_0_.refs_1_.refs_9_, f32[16,128,128]{2,1,0:T(8,128)S(1)} %get-tuple-element.83.refs_0_.refs_1_.refs_5_, ...), custom_call_target="tpu_custom_call" | custom-call | flops 2000000000 | bytes 131072 | tf_op jit(solution)/shard_map/adjoint/pallas_call | solution.py:353
  43.3 4.0 %collective-permute-start.8 = (f32[4,128,128]{2,1,0:T(8,128)S(1)}, f32[4,128,128]{2,1,0:T(8,128)S(1)}, u32[]{:S(2)}, u32[]{:S(2)}) collective-permute-start(f32[4,128,128]{2,1,0:T(8,128)S(1)} %get-tuple-element.92), channel_id=1, source_target_pairs={{0,1},{1,0},{2,3},{3,2},{4,5},{5,4},{6,7},{7,6},{8,9},{9,8},{10,11... | collective-permute-start | bytes 786440 | tf_op jit(solution)/shard_map/ppermute | solution.py:399
  49.5 4.3 %collective-permute-start.18 = (f32[4,128,128]{2,1,0:T(8,128)S(1)}, f32[4,128,128]{2,1,0:T(8,128)S(1)}, u32[]{:S(2)}, u32[]{:S(2)}) collective-permute-start(f32[4,128,128]{2,1,0:T(8,128)S(1)} %get-tuple-element.106), channel_id=1, source_target_pairs={{0,1},{1,0},{2,3},{3,2},{4,5},{5,4},{6,7},{7,6},{8,9},{9,8},{10,11... | collective-permute-start | bytes 786440 | tf_op jit(solution)/shard_map/ppermute | solution.py:399
  56.0 3.8 %collective-permute-start.10 = (f32[4,128,128]{2,1,0:T(8,128)S(1)}, f32[4,128,128]{2,1,0:T(8,128)S(1)}, u32[]{:S(2)}, u32[]{:S(2)}) collective-permute-start(f32[4,128,128]{2,1,0:T(8,128)S(1)} %get-tuple-element.95), channel_id=1, source_target_pairs={{0,1},{1,0},{2,3},{3,2},{4,5},{5,4},{6,7},{7,6},{8,9},{9,8},{10,11... | collective-permute-start | bytes 786440 | tf_op jit(solution)/shard_map/ppermute | solution.py:399
  61.0 1.5 %forward.11 = (f32[16,128,128]{2,1,0:T(8,128)S(1)}, f32[4,128,128]{2,1,0:T(8,128)S(1)}, f32[4,128,128]{2,1,0:T(8,128)S(1)}, f32[16,128,128]{2,1,0:T(8,128)S(1)}) custom-call(f32[16,128,128]{2,1,0:T(8,128)S(1)} %get-tuple-element.105.refs_0_.refs_5_, f32[4,128,128]{2,1,0:T(8,128)S(1)} %collective-permute-done.18.refs_1_, ...), custom_call_target="tpu_custom_call" | custom-call | flops 2000000000 | bytes 131072 | tf_op jit(solution)/shard_map/forward/pallas_call | solution.py:353
  62.5 3.8 %collective-permute-start.20 = (f32[4,128,128]{2,1,0:T(8,128)S(1)}, f32[4,128,128]{2,1,0:T(8,128)S(1)}, u32[]{:S(2)}, u32[]{:S(2)}) collective-permute-start(f32[4,128,128]{2,1,0:T(8,128)S(1)} %get-tuple-element.110), channel_id=1, source_target_pairs={{0,1},{1,0},{2,3},{3,2},{4,5},{5,4},{6,7},{7,6},{8,9},{9,8},{10,11... | collective-permute-start | bytes 786440 | tf_op jit(solution)/shard_map/ppermute | solution.py:399
  68.5 3.4 %collective-permute-start.12 = (f32[4,128,128]{2,1,0:T(8,128)S(1)}, f32[4,128,128]{2,1,0:T(8,128)S(1)}, u32[]{:S(2)}, u32[]{:S(2)}) collective-permute-start(f32[4,128,128]{2,1,0:T(8,128)S(1)} %get-tuple-element.98), channel_id=1, source_target_pairs={{0,1},{1,0},{2,3},{3,2},{4,5},{5,4},{6,7},{7,6},{8,9},{9,8},{10,11... | collective-permute-start | bytes 786440 | tf_op jit(solution)/shard_map/ppermute | solution.py:399
  72.6 1.5 %forward.12 = (f32[16,128,128]{2,1,0:T(8,128)S(1)}, f32[4,128,128]{2,1,0:T(8,128)S(1)}, f32[4,128,128]{2,1,0:T(8,128)S(1)}, f32[16,128,128]{2,1,0:T(8,128)S(1)}) custom-call(f32[16,128,128]{2,1,0:T(8,128)S(1)} %get-tuple-element.109.refs_0_.refs_5_, f32[4,128,128]{2,1,0:T(8,128)S(1)} %collective-permute-done.20.refs_1_, ...), custom_call_target="tpu_custom_call" | custom-call | flops 2000000000 | bytes 131072 | tf_op jit(solution)/shard_map/forward/pallas_call | solution.py:353
  74.1 3.5 %collective-permute-start.24 = (f32[4,128,128]{2,1,0:T(8,128)S(1)}, f32[4,128,128]{2,1,0:T(8,128)S(1)}, u32[]{:S(2)}, u32[]{:S(2)}) collective-permute-start(f32[4,128,128]{2,1,0:T(8,128)S(1)} %get-tuple-element.118), channel_id=1, source_target_pairs={{0,1},{1,0},{2,3},{3,2},{4,5},{5,4},{6,7},{7,6},{8,9},{9,8},{10,11... | collective-permute-start | bytes 786440 | tf_op jit(solution)/shard_map/ppermute | solution.py:399
  78.6 1.6 %adjoint.11 = (f32[16,128,128]{2,1,0:T(8,128)S(1)}, f32[4,128,128]{2,1,0:T(8,128)S(1)}, f32[4,128,128]{2,1,0:T(8,128)S(1)}, f32[16,128,128]{2,1,0:T(8,128)S(1)}) custom-call(f32[16,128,128]{2,1,0:T(8,128)S(1)} %get-tuple-element.97.refs_0_.refs_1_, f32[16,128,128]{2,1,0:T(8,128)S(1)} %get-tuple-element.94.refs_0_.refs_9_.refs_1_, ...), custom_call_target="tpu_custom_call" | custom-call | flops 2000000000 | bytes 131072 | tf_op jit(solution)/shard_map/adjoint/pallas_call | solution.py:353
  80.3 3.7 %collective-permute-start.22 = (f32[4,128,128]{2,1,0:T(8,128)S(1)}, f32[4,128,128]{2,1,0:T(8,128)S(1)}, u32[]{:S(2)}, u32[]{:S(2)}) collective-permute-start(f32[4,128,128]{2,1,0:T(8,128)S(1)} %get-tuple-element.114), channel_id=1, source_target_pairs={{0,1},{1,0},{2,3},{3,2},{4,5},{5,4},{6,7},{7,6},{8,9},{9,8},{10,11... | collective-permute-start | bytes 786440 | tf_op jit(solution)/shard_map/ppermute | solution.py:399
  84.7 1.5 %forward.13 = (f32[16,128,128]{2,1,0:T(8,128)S(1)}, f32[4,128,128]{2,1,0:T(8,128)S(1)}, f32[4,128,128]{2,1,0:T(8,128)S(1)}, f32[16,128,128]{2,1,0:T(8,128)S(1)}) custom-call(f32[16,128,128]{2,1,0:T(8,128)S(1)} %get-tuple-element.117.refs_0_.refs_5_, f32[4,128,128]{2,1,0:T(8,128)S(1)} %collective-permute-done.24.refs_1_, ...), custom_call_target="tpu_custom_call" | custom-call | flops 2000000000 | bytes 131072 | tf_op jit(solution)/shard_map/forward/pallas_call | solution.py:353
  86.2 3.4 %collective-permute-start.28 = (f32[4,128,128]{2,1,0:T(8,128)S(1)}, f32[4,128,128]{2,1,0:T(8,128)S(1)}, u32[]{:S(2)}, u32[]{:S(2)}) collective-permute-start(f32[4,128,128]{2,1,0:T(8,128)S(1)} %get-tuple-element.127), channel_id=1, source_target_pairs={{0,1},{1,0},{2,3},{3,2},{4,5},{5,4},{6,7},{7,6},{8,9},{9,8},{10,11... | collective-permute-start | bytes 786440 | tf_op jit(solution)/shard_map/ppermute | solution.py:399
  90.3 1.7 %adjoint.12 = (f32[16,128,128]{2,1,0:T(8,128)S(1)}, f32[4,128,128]{2,1,0:T(8,128)S(1)}, f32[4,128,128]{2,1,0:T(8,128)S(1)}, f32[16,128,128]{2,1,0:T(8,128)S(1)}) custom-call(f32[16,128,128]{2,1,0:T(8,128)S(1)} %get-tuple-element.113.refs_0_.refs_1_, f32[16,128,128]{2,1,0:T(8,128)S(1)} %get-tuple-element.97.refs_0_.refs_1_, ...), custom_call_target="tpu_custom_call" | custom-call | flops 2000000000 | bytes 131072 | tf_op jit(solution)/shard_map/adjoint/pallas_call | solution.py:353
  91.9 3.4 %collective-permute-start.26 = (f32[4,128,128]{2,1,0:T(8,128)S(1)}, f32[4,128,128]{2,1,0:T(8,128)S(1)}, u32[]{:S(2)}, u32[]{:S(2)}) collective-permute-start(f32[4,128,128]{2,1,0:T(8,128)S(1)} %get-tuple-element.123), channel_id=1, source_target_pairs={{0,1},{1,0},{2,3},{3,2},{4,5},{5,4},{6,7},{7,6},{8,9},{9,8},{10,11... | collective-permute-start | bytes 786440 | tf_op jit(solution)/shard_map/ppermute | solution.py:399
  98.0 3.7 %collective-permute-start.32 = (f32[4,128,128]{2,1,0:T(8,128)S(1)}, f32[4,128,128]{2,1,0:T(8,128)S(1)}, u32[]{:S(2)}, u32[]{:S(2)}) collective-permute-start(f32[4,128,128]{2,1,0:T(8,128)S(1)} %get-tuple-element.137), channel_id=1, source_target_pairs={{0,1},{1,0},{2,3},{3,2},{4,5},{5,4},{6,7},{7,6},{8,9},{9,8},{10,11... | collective-permute-start | bytes 786440 | tf_op jit(solution)/shard_map/ppermute | solution.py:399
  102.4 2.1 %adjoint.13 = (f32[16,128,128]{2,1,0:T(8,128)S(1)}, f32[4,128,128]{2,1,0:T(8,128)S(1)}, f32[4,128,128]{2,1,0:T(8,128)S(1)}, f32[16,128,128]{2,1,0:T(8,128)S(1)}) custom-call(f32[16,128,128]{2,1,0:T(8,128)S(1)} %get-tuple-element.122.refs_0_.later, f32[16,128,128]{2,1,0:T(8,128)S(1)} %get-tuple-element.113.refs_0_.refs_1_, ...), custom_call_target="tpu_custom_call" | custom-call | flops 2000000000 | bytes 131072 | tf_op jit(solution)/shard_map/adjoint/pallas_call | solution.py:353
  104.4 3.1 %collective-permute-start.30 = (f32[4,128,128]{2,1,0:T(8,128)S(1)}, f32[4,128,128]{2,1,0:T(8,128)S(1)}, u32[]{:S(2)}, u32[]{:S(2)}) collective-permute-start(f32[4,128,128]{2,1,0:T(8,128)S(1)} %get-tuple-element.132), channel_id=1, source_target_pairs={{0,1},{1,0},{2,3},{3,2},{4,5},{5,4},{6,7},{7,6},{8,9},{9,8},{10,11... | collective-permute-start | bytes 786440 | tf_op jit(solution)/shard_map/ppermute | solution.py:399
  108.2 1.6 %forward.15 = (f32[4,16,16,128]{3,2,1,0:T(8,128)S(1)}, f32[4,16,16,128]{3,2,1,0:T(8,128)S(1)}) custom-call(f32[16,128,128]{2,1,0:T(8,128)S(1)} %get-tuple-element.136.refs_0_, f32[4,128,128]{2,1,0:T(8,128)S(1)} %collective-permute-done.32.refs_1_, f32[4,128,128]{2,1,0:T(8,128)S(1)} %collective-permute-done.33.refs_2_, bf16[256,256]{1,0:T(8,128)(2,1)S(1)} %copy-done.1, ...), custom_call_target="tpu_custom_call" | custom-call | tf_op jit(solution)/shard_map/forward/pallas_call | solution.py:353
  109.9 1.6 %last_inner.1 = (f32[16,128,128]{2,1,0:T(8,128)}, f32[16,128,128]{2,1,0:T(8,128)}) custom-call(f32[16,128,128]{2,1,0:T(8,128)S(1)} %get-tuple-element.131.cur.refs_7_, f32[16,128,128]{2,1,0:T(8,128)S(1)} %get-tuple-element.122.refs_0_.later, f32[16,128,128]{2,1,0:T(8,128)S(1)} %get-tuple-element.80.refs_6_.refs_2_.speed, ...), custom_call_target="tpu_custom_call" | custom-call | flops 30000001024 | bytes 1966080 | tf_op jit(solution)/shard_map/last_inner/pallas_call | solution.py:353
  113.4 1.6 %collective-permute-start.36 = (f32[16,16,128]{2,1,0:T(8,128)S(1)}, f32[16,16,128]{2,1,0:T(8,128)S(1)}, u32[]{:S(2)}, u32[]{:S(2)}) collective-permute-start(f32[16,16,128]{2,1,0:T(8,128)S(1)} %get-tuple-element.145), channel_id=1, source_target_pairs={{0,16},{4,20},{8,24},{12,28},{16,0},{20,4},{24,8},{28,12},{1,17},{... | collective-permute-start | bytes 393224 | tf_op jit(solution)/shard_map/ppermute | solution.py:507
  115.5 1.5 %last_border.1 = f32[16,128,128]{2,1,0:T(8,128)} custom-call(f32[16,128,128]{2,1,0:T(8,128)S(1)} %get-tuple-element.131.cur.refs_7_, f32[16,128,128]{2,1,0:T(8,128)S(1)} %get-tuple-element.122.refs_0_.later, f32[16,128,128]{2,1,0:T(8,128)S(1)} %get-tuple-element.80.refs_6_.refs_2_.speed, ...), custom_call_target="tpu_custom_call", output_to_operand_aliasing={{}: (8, {})} | custom-call | flops 30000001024 | bytes 1966080 | tf_op jit(solution)/shard_map/last_border/pallas_call | solution.py:353
  118.1 3.5 %collective-permute-done.36.refs_2_ = f32[16,16,128]{2,1,0:T(8,128)S(1)} collective-permute-done((f32[16,16,128]{2,1,0:T(8,128)S(1)}, f32[16,16,128]{2,1,0:T(8,128)S(1)}, u32[]{:S(2)}, u32[]{:S(2)}) %collective-permute-start.36) | collective-permute-done | bytes 131104 | tf_op jit(solution)/shard_map/ppermute | solution.py:507
  (76 shorter events, 28.0 us)
Async XLA Ops:
  2.0 17.5 %collective-permute-start.2 = (f32[4,128,128]{2,1,0:T(8,128)S(1)}, f32[4,128,128]{2,1,0:T(8,128)S(1)}, u32[]{:S(2)}, u32[]{:S(2)}) collective-permute-start(f32[4,128,128]{2,1,0:T(8,128)S(1)} %get-tuple-element.77), channel_id=1, source_target_pairs={{0,1},{1,0},{2,3},{3,2},{4,5},{5,4},{6,7},{7,6},{8,9},{9,8},{10,11... | collective-permute-start | bytes 786440 | tf_op jit(solution)/shard_map/ppermute | solution.py:399
  5.1 14.5 %collective-permute-start.3 = (f32[4,128,128]{2,1,0:T(8,128)S(1)}, f32[4,128,128]{2,1,0:T(8,128)S(1)}, u32[]{:S(2)}, u32[]{:S(2)}) collective-permute-start(f32[4,128,128]{2,1,0:T(8,128)S(1)} %get-tuple-element.78), channel_id=1, source_target_pairs={{1,2},{2,1},{5,6},{6,5},{9,10},{10,9},{13,14},{14,13},{17,18},{18,... | collective-permute-start | bytes 786440 | tf_op jit(solution)/shard_map/ppermute | solution.py:399
  10.2 17.9 %collective-permute-start.4 = (f32[4,128,128]{2,1,0:T(8,128)S(1)}, f32[4,128,128]{2,1,0:T(8,128)S(1)}, u32[]{:S(2)}, u32[]{:S(2)}) collective-permute-start(f32[4,128,128]{2,1,0:T(8,128)S(1)} %get-tuple-element.85), channel_id=1, source_target_pairs={{0,1},{1,0},{2,3},{3,2},{4,5},{5,4},{6,7},{7,6},{8,9},{9,8},{10,11... | collective-permute-start | bytes 786440 | tf_op jit(solution)/shard_map/ppermute | solution.py:399
  10.3 17.8 %collective-permute-start.5 = (f32[4,128,128]{2,1,0:T(8,128)S(1)}, f32[4,128,128]{2,1,0:T(8,128)S(1)}, u32[]{:S(2)}, u32[]{:S(2)}) collective-permute-start(f32[4,128,128]{2,1,0:T(8,128)S(1)} %get-tuple-element.86), channel_id=1, source_target_pairs={{1,2},{2,1},{5,6},{6,5},{9,10},{10,9},{13,14},{14,13},{17,18},{18,... | collective-permute-start | bytes 786440 | tf_op jit(solution)/shard_map/ppermute | solution.py:399
  13.0 8.9 %collective-permute-start.1 = (f32[2,8,256]{2,1,0:T(8,128)S(1)}, f32[2,8,256]{2,1,0:T(8,128)S(1)}, u32[]{:S(2)}, u32[]{:S(2)}) collective-permute-start(f32[2,8,256]{2,1,0:T(8,128)S(1)} %stack.1.refs_3_), channel_id=1, source_target_pairs={{0,2},{1,3},{2,0},{3,1},{4,6},{5,7},{6,4},{7,5},{8,10},{9,11},{10,... | collective-permute-start | bytes 49160 | tf_op jit(solution)/shard_map/ppermute | solution.py:410
  27.3 8.2 %collective-permute-start.14 = (f32[4,128,128]{2,1,0:T(8,128)S(1)}, f32[4,128,128]{2,1,0:T(8,128)S(1)}, u32[]{:S(2)}, u32[]{:S(2)}) collective-permute-start(f32[4,128,128]{2,1,0:T(8,128)S(1)} %get-tuple-element.100), channel_id=1, source_target_pairs={{0,1},{1,0},{2,3},{3,2},{4,5},{5,4},{6,7},{7,6},{8,9},{9,8},{10,11... | collective-permute-start | bytes 786440 | tf_op jit(solution)/shard_map/ppermute | solution.py:399
  27.4 8.1 %collective-permute-start.15 = (f32[4,128,128]{2,1,0:T(8,128)S(1)}, f32[4,128,128]{2,1,0:T(8,128)S(1)}, u32[]{:S(2)}, u32[]{:S(2)}) collective-permute-start(f32[4,128,128]{2,1,0:T(8,128)S(1)} %get-tuple-element.101), channel_id=1, source_target_pairs={{1,2},{2,1},{5,6},{6,5},{9,10},{10,9},{13,14},{14,13},{17,18},{18,... | collective-permute-start | bytes 786440 | tf_op jit(solution)/shard_map/ppermute | solution.py:399
  29.7 12.1 %collective-permute-start.6 = (f32[4,128,128]{2,1,0:T(8,128)S(1)}, f32[4,128,128]{2,1,0:T(8,128)S(1)}, u32[]{:S(2)}, u32[]{:S(2)}) collective-permute-start(f32[4,128,128]{2,1,0:T(8,128)S(1)} %get-tuple-element.89), channel_id=1, source_target_pairs={{0,1},{1,0},{2,3},{3,2},{4,5},{5,4},{6,7},{7,6},{8,9},{9,8},{10,11... | collective-permute-start | bytes 786440 | tf_op jit(solution)/shard_map/ppermute | solution.py:399
  34.9 6.9 %collective-permute-start.7 = (f32[4,128,128]{2,1,0:T(8,128)S(1)}, f32[4,128,128]{2,1,0:T(8,128)S(1)}, u32[]{:S(2)}, u32[]{:S(2)}) collective-permute-start(f32[4,128,128]{2,1,0:T(8,128)S(1)} %get-tuple-element.90), channel_id=1, source_target_pairs={{1,2},{2,1},{5,6},{6,5},{9,10},{10,9},{13,14},{14,13},{17,18},{18,... | collective-permute-start | bytes 786440 | tf_op jit(solution)/shard_map/ppermute | solution.py:399
  37.1 10.9 %collective-permute-start.16 = (f32[4,128,128]{2,1,0:T(8,128)S(1)}, f32[4,128,128]{2,1,0:T(8,128)S(1)}, u32[]{:S(2)}, u32[]{:S(2)}) collective-permute-start(f32[4,128,128]{2,1,0:T(8,128)S(1)} %get-tuple-element.103), channel_id=1, source_target_pairs={{0,1},{1,0},{2,3},{3,2},{4,5},{5,4},{6,7},{7,6},{8,9},{9,8},{10,11... | collective-permute-start | bytes 786440 | tf_op jit(solution)/shard_map/ppermute | solution.py:399
  41.0 7.0 %collective-permute-start.17 = (f32[4,128,128]{2,1,0:T(8,128)S(1)}, f32[4,128,128]{2,1,0:T(8,128)S(1)}, u32[]{:S(2)}, u32[]{:S(2)}) collective-permute-start(f32[4,128,128]{2,1,0:T(8,128)S(1)} %get-tuple-element.104), channel_id=1, source_target_pairs={{1,2},{2,1},{5,6},{6,5},{9,10},{10,9},{13,14},{14,13},{17,18},{18,... | collective-permute-start | bytes 786440 | tf_op jit(solution)/shard_map/ppermute | solution.py:399
  43.3 11.2 %collective-permute-start.8 = (f32[4,128,128]{2,1,0:T(8,128)S(1)}, f32[4,128,128]{2,1,0:T(8,128)S(1)}, u32[]{:S(2)}, u32[]{:S(2)}) collective-permute-start(f32[4,128,128]{2,1,0:T(8,128)S(1)} %get-tuple-element.92), channel_id=1, source_target_pairs={{0,1},{1,0},{2,3},{3,2},{4,5},{5,4},{6,7},{7,6},{8,9},{9,8},{10,11... | collective-permute-start | bytes 786440 | tf_op jit(solution)/shard_map/ppermute | solution.py:399
  47.3 7.2 %collective-permute-start.9 = (f32[4,128,128]{2,1,0:T(8,128)S(1)}, f32[4,128,128]{2,1,0:T(8,128)S(1)}, u32[]{:S(2)}, u32[]{:S(2)}) collective-permute-start(f32[4,128,128]{2,1,0:T(8,128)S(1)} %get-tuple-element.93), channel_id=1, source_target_pairs={{1,2},{2,1},{5,6},{6,5},{9,10},{10,9},{13,14},{14,13},{17,18},{18,... | collective-permute-start | bytes 786440 | tf_op jit(solution)/shard_map/ppermute | solution.py:399
  49.5 11.5 %collective-permute-start.18 = (f32[4,128,128]{2,1,0:T(8,128)S(1)}, f32[4,128,128]{2,1,0:T(8,128)S(1)}, u32[]{:S(2)}, u32[]{:S(2)}) collective-permute-start(f32[4,128,128]{2,1,0:T(8,128)S(1)} %get-tuple-element.106), channel_id=1, source_target_pairs={{0,1},{1,0},{2,3},{3,2},{4,5},{5,4},{6,7},{7,6},{8,9},{9,8},{10,11... | collective-permute-start | bytes 786440 | tf_op jit(solution)/shard_map/ppermute | solution.py:399
  53.8 7.2 %collective-permute-start.19 = (f32[4,128,128]{2,1,0:T(8,128)S(1)}, f32[4,128,128]{2,1,0:T(8,128)S(1)}, u32[]{:S(2)}, u32[]{:S(2)}) collective-permute-start(f32[4,128,128]{2,1,0:T(8,128)S(1)} %get-tuple-element.107), channel_id=1, source_target_pairs={{1,2},{2,1},{5,6},{6,5},{9,10},{10,9},{13,14},{14,13},{17,18},{18,... | collective-permute-start | bytes 786440 | tf_op jit(solution)/shard_map/ppermute | solution.py:399
  56.0 11.0 %collective-permute-start.10 = (f32[4,128,128]{2,1,0:T(8,128)S(1)}, f32[4,128,128]{2,1,0:T(8,128)S(1)}, u32[]{:S(2)}, u32[]{:S(2)}) collective-permute-start(f32[4,128,128]{2,1,0:T(8,128)S(1)} %get-tuple-element.95), channel_id=1, source_target_pairs={{0,1},{1,0},{2,3},{3,2},{4,5},{5,4},{6,7},{7,6},{8,9},{9,8},{10,11... | collective-permute-start | bytes 786440 | tf_op jit(solution)/shard_map/ppermute | solution.py:399
  59.8 7.2 %collective-permute-start.11 = (f32[4,128,128]{2,1,0:T(8,128)S(1)}, f32[4,128,128]{2,1,0:T(8,128)S(1)}, u32[]{:S(2)}, u32[]{:S(2)}) collective-permute-start(f32[4,128,128]{2,1,0:T(8,128)S(1)} %get-tuple-element.96), channel_id=1, source_target_pairs={{1,2},{2,1},{5,6},{6,5},{9,10},{10,9},{13,14},{14,13},{17,18},{18,... | collective-permute-start | bytes 786440 | tf_op jit(solution)/shard_map/ppermute | solution.py:399
  62.5 10.0 %collective-permute-start.20 = (f32[4,128,128]{2,1,0:T(8,128)S(1)}, f32[4,128,128]{2,1,0:T(8,128)S(1)}, u32[]{:S(2)}, u32[]{:S(2)}) collective-permute-start(f32[4,128,128]{2,1,0:T(8,128)S(1)} %get-tuple-element.110), channel_id=1, source_target_pairs={{0,1},{1,0},{2,3},{3,2},{4,5},{5,4},{6,7},{7,6},{8,9},{9,8},{10,11... | collective-permute-start | bytes 786440 | tf_op jit(solution)/shard_map/ppermute | solution.py:399
  68.5 10.1 %collective-permute-start.12 = (f32[4,128,128]{2,1,0:T(8,128)S(1)}, f32[4,128,128]{2,1,0:T(8,128)S(1)}, u32[]{:S(2)}, u32[]{:S(2)}) collective-permute-start(f32[4,128,128]{2,1,0:T(8,128)S(1)} %get-tuple-element.98), channel_id=1, source_target_pairs={{0,1},{1,0},{2,3},{3,2},{4,5},{5,4},{6,7},{7,6},{8,9},{9,8},{10,11... | collective-permute-start | bytes 786440 | tf_op jit(solution)/shard_map/ppermute | solution.py:399
  71.9 6.7 %collective-permute-start.13 = (f32[4,128,128]{2,1,0:T(8,128)S(1)}, f32[4,128,128]{2,1,0:T(8,128)S(1)}, u32[]{:S(2)}, u32[]{:S(2)}) collective-permute-start(f32[4,128,128]{2,1,0:T(8,128)S(1)} %get-tuple-element.99), channel_id=1, source_target_pairs={{1,2},{2,1},{5,6},{6,5},{9,10},{10,9},{13,14},{14,13},{17,18},{18,... | collective-permute-start | bytes 786440 | tf_op jit(solution)/shard_map/ppermute | solution.py:399
  74.1 10.5 %collective-permute-start.24 = (f32[4,128,128]{2,1,0:T(8,128)S(1)}, f32[4,128,128]{2,1,0:T(8,128)S(1)}, u32[]{:S(2)}, u32[]{:S(2)}) collective-permute-start(f32[4,128,128]{2,1,0:T(8,128)S(1)} %get-tuple-element.118), channel_id=1, source_target_pairs={{0,1},{1,0},{2,3},{3,2},{4,5},{5,4},{6,7},{7,6},{8,9},{9,8},{10,11... | collective-permute-start | bytes 786440 | tf_op jit(solution)/shard_map/ppermute | solution.py:399
  77.6 7.0 %collective-permute-start.25 = (f32[4,128,128]{2,1,0:T(8,128)S(1)}, f32[4,128,128]{2,1,0:T(8,128)S(1)}, u32[]{:S(2)}, u32[]{:S(2)}) collective-permute-start(f32[4,128,128]{2,1,0:T(8,128)S(1)} %get-tuple-element.119), channel_id=1, source_target_pairs={{1,2},{2,1},{5,6},{6,5},{9,10},{10,9},{13,14},{14,13},{17,18},{18,... | collective-permute-start | bytes 786440 | tf_op jit(solution)/shard_map/ppermute | solution.py:399
  80.3 10.0 %collective-permute-start.22 = (f32[4,128,128]{2,1,0:T(8,128)S(1)}, f32[4,128,128]{2,1,0:T(8,128)S(1)}, u32[]{:S(2)}, u32[]{:S(2)}) collective-permute-start(f32[4,128,128]{2,1,0:T(8,128)S(1)} %get-tuple-element.114), channel_id=1, source_target_pairs={{0,1},{1,0},{2,3},{3,2},{4,5},{5,4},{6,7},{7,6},{8,9},{9,8},{10,11... | collective-permute-start | bytes 786440 | tf_op jit(solution)/shard_map/ppermute | solution.py:399
  86.2 10.3 %collective-permute-start.28 = (f32[4,128,128]{2,1,0:T(8,128)S(1)}, f32[4,128,128]{2,1,0:T(8,128)S(1)}, u32[]{:S(2)}, u32[]{:S(2)}) collective-permute-start(f32[4,128,128]{2,1,0:T(8,128)S(1)} %get-tuple-element.127), channel_id=1, source_target_pairs={{0,1},{1,0},{2,3},{3,2},{4,5},{5,4},{6,7},{7,6},{8,9},{9,8},{10,11... | collective-permute-start | bytes 786440 | tf_op jit(solution)/shard_map/ppermute | solution.py:399
  89.6 7.0 %collective-permute-start.29 = (f32[4,128,128]{2,1,0:T(8,128)S(1)}, f32[4,128,128]{2,1,0:T(8,128)S(1)}, u32[]{:S(2)}, u32[]{:S(2)}) collective-permute-start(f32[4,128,128]{2,1,0:T(8,128)S(1)} %get-tuple-element.128), channel_id=1, source_target_pairs={{1,2},{2,1},{5,6},{6,5},{9,10},{10,9},{13,14},{14,13},{17,18},{18,... | collective-permute-start | bytes 786440 | tf_op jit(solution)/shard_map/ppermute | solution.py:399
  91.9 10.4 %collective-permute-start.26 = (f32[4,128,128]{2,1,0:T(8,128)S(1)}, f32[4,128,128]{2,1,0:T(8,128)S(1)}, u32[]{:S(2)}, u32[]{:S(2)}) collective-permute-start(f32[4,128,128]{2,1,0:T(8,128)S(1)} %get-tuple-element.123), channel_id=1, source_target_pairs={{0,1},{1,0},{2,3},{3,2},{4,5},{5,4},{6,7},{7,6},{8,9},{9,8},{10,11... | collective-permute-start | bytes 786440 | tf_op jit(solution)/shard_map/ppermute | solution.py:399
  95.3 7.0 %collective-permute-start.27 = (f32[4,128,128]{2,1,0:T(8,128)S(1)}, f32[4,128,128]{2,1,0:T(8,128)S(1)}, u32[]{:S(2)}, u32[]{:S(2)}) collective-permute-start(f32[4,128,128]{2,1,0:T(8,128)S(1)} %get-tuple-element.124), channel_id=1, source_target_pairs={{1,2},{2,1},{5,6},{6,5},{9,10},{10,9},{13,14},{14,13},{17,18},{18,... | collective-permute-start | bytes 786440 | tf_op jit(solution)/shard_map/ppermute | solution.py:399
  98.0 10.3 %collective-permute-start.32 = (f32[4,128,128]{2,1,0:T(8,128)S(1)}, f32[4,128,128]{2,1,0:T(8,128)S(1)}, u32[]{:S(2)}, u32[]{:S(2)}) collective-permute-start(f32[4,128,128]{2,1,0:T(8,128)S(1)} %get-tuple-element.137), channel_id=1, source_target_pairs={{0,1},{1,0},{2,3},{3,2},{4,5},{5,4},{6,7},{7,6},{8,9},{9,8},{10,11... | collective-permute-start | bytes 786440 | tf_op jit(solution)/shard_map/ppermute | solution.py:399
  101.7 6.6 %collective-permute-start.33 = (f32[4,128,128]{2,1,0:T(8,128)S(1)}, f32[4,128,128]{2,1,0:T(8,128)S(1)}, u32[]{:S(2)}, u32[]{:S(2)}) collective-permute-start(f32[4,128,128]{2,1,0:T(8,128)S(1)} %get-tuple-element.138), channel_id=1, source_target_pairs={{1,2},{2,1},{5,6},{6,5},{9,10},{10,9},{13,14},{14,13},{17,18},{18,... | collective-permute-start | bytes 786440 | tf_op jit(solution)/shard_map/ppermute | solution.py:399
  104.4 11.0 %collective-permute-start.30 = (f32[4,128,128]{2,1,0:T(8,128)S(1)}, f32[4,128,128]{2,1,0:T(8,128)S(1)}, u32[]{:S(2)}, u32[]{:S(2)}) collective-permute-start(f32[4,128,128]{2,1,0:T(8,128)S(1)} %get-tuple-element.132), channel_id=1, source_target_pairs={{0,1},{1,0},{2,3},{3,2},{4,5},{5,4},{6,7},{7,6},{8,9},{9,8},{10,11... | collective-permute-start | bytes 786440 | tf_op jit(solution)/shard_map/ppermute | solution.py:399
  107.6 7.9 %collective-permute-start.31 = (f32[4,128,128]{2,1,0:T(8,128)S(1)}, f32[4,128,128]{2,1,0:T(8,128)S(1)}, u32[]{:S(2)}, u32[]{:S(2)}) collective-permute-start(f32[4,128,128]{2,1,0:T(8,128)S(1)} %get-tuple-element.133), channel_id=1, source_target_pairs={{1,2},{2,1},{5,6},{6,5},{9,10},{10,9},{13,14},{14,13},{17,18},{18,... | collective-permute-start | bytes 786440 | tf_op jit(solution)/shard_map/ppermute | solution.py:399
  113.4 8.2 %collective-permute-start.36 = (f32[16,16,128]{2,1,0:T(8,128)S(1)}, f32[16,16,128]{2,1,0:T(8,128)S(1)}, u32[]{:S(2)}, u32[]{:S(2)}) collective-permute-start(f32[16,16,128]{2,1,0:T(8,128)S(1)} %get-tuple-element.145), channel_id=1, source_target_pairs={{0,16},{4,20},{8,24},{12,28},{16,0},{20,4},{24,8},{28,12},{1,17},{... | collective-permute-start | bytes 393224 | tf_op jit(solution)/shard_map/ppermute | solution.py:507
  (10 other events, 93.5 us)

commit v5 on v4

--- a/solution.py
+++ b/solution.py
@@ -167,21 +167,30 @@
             keep[j] = total[:, pl.ds(here, chunk), :]
 
 
+def injected(tiles, x, time, width_y):
+    return tiles[pl.ds((x + reach) * width_y * 8 + time, width_y, stride=8), :]
+
+
 def adjoint_kernel(parts, *refs):
     it = iter(refs)
-    cur, later, speed, even, odd, inject, right, left = [next(it) for _ in range(8)]
-    adds = parts["adds"]
+    cur, later, speed, even, odd, right, left = [next(it) for _ in range(7)]
+    adds, injects = parts["adds"], parts["injects"]
+    inject = next(it) if injects else None
     lap_of, acc_in = (next(it), next(it)) if adds else (None, None)
     nxt, even_out, odd_out = [next(it) for _ in range(3)]
     acc_out = next(it) if adds else None
     halo = next(it)
     parity = lax.axis_index("slab") % 2
     fill_halo(parity, even, odd, halo)
-    width_y = cur.shape[1]
+    count, width_y = cur.shape[:2]
+    if parts["late"]:
+        for i in range(2 * reach):
+            x = i - reach if i < reach else count + i - reach
+            halo[i] = halo[i] + injected(inject, x, parts["time"] + 1, width_y)
 
     def put(x, v, lap):
-        added = inject[pl.ds(x * width_y * 8 + parts["time"], width_y, stride=8), :]
-        nxt[x] = 2.0 * v - later[x] + speed[x] * lap + added
+        value = 2.0 * v - later[x] + speed[x] * lap
+        nxt[x] = value + injected(inject, x, parts["time"], width_y) if injects else value
         if adds:
             acc_out[x] = acc_in[x] + v * lap_of[x]
 
@@ -195,7 +204,7 @@
     copies[0].start()
 
     def put(x, v, lap):
-        added = inject[pl.ds(x * width_y * 8, width_y, stride=8), :]
+        added = injected(inject, x, 0, width_y)
         field[x - reach] = 2.0 * v - later[x] + speed[x] * lap + added
 
     laplace_planes(cur, None, right, left, put, range(reach, count - reach, 2))
@@ -216,7 +225,7 @@
     for n, first in enumerate((0, top)):
 
         def put(x, v, lap):
-            added = inject[pl.ds(x * width_y * 8, width_y, stride=8), :]
+            added = injected(inject, x, 0, width_y)
             field[n * reach + x - first] = 2.0 * v - later[x] + speed[x] * lap + added
 
         laplace_planes(cur, halo, right, left, put, range(first, first + reach, 2))
@@ -268,23 +277,20 @@
         tiles[tiles.shape[0] - rest :, :] = jnp.zeros((rest, 128), jnp.float32)
     listen_copy.wait()
     count, width_y, width_z = fields[0].shape
-    depth = listen[0:1, :] - lax.axis_index("slab") * count
-    inside = (depth >= 0) & (depth < count)
+    held = count + 2 * reach
+    depth = listen[0:1, :] - lax.axis_index("slab") * count + reach
+    inside = (depth >= 0) & (depth < held)
     flat = depth * (width_y * width_z) + listen[1:2, :] * width_z + listen[2:3, :]
-    where_to[...] = jnp.where(inside, flat, count * width_y * width_z)
+    where_to[...] = jnp.where(inside, flat, held * width_y * width_z)
     for copy in copies:
         copy.wait()
 
 
 def scatter_kernel(levels, where_to, *refs):
     blocks, refs = refs[:levels], refs[levels:]
-    fields, stepped, _, out, outs, even_out, odd_out, sems = refs[:2], *refs[2:5], refs[5:7], *refs[7:]
-    copies = [pltpu.make_async_copy(fields[i], outs[i], sems.at[i]) for i in range(2)]
-    for copy in copies:
-        copy.start()
-    emit_edges(lax.axis_index("slab") % 2, stepped, even_out, odd_out)
+    field, _, out, field_out = refs
     per = blocks[0].shape[-1]
-    group, groups = 4, 8
+    group, groups = 8, 4
     slab = lax.axis_index("slab")
     lanes = lax.broadcasted_iota(jnp.int32, (8, 128), 1)
     d = 0
@@ -317,8 +323,9 @@
                             held[u] = value
                         for u in own:
                             out[slots[u], :] = held[u]
-    for copy in copies:
-        copy.wait()
+    count, width_y = field.shape[:2]
+    for x in range(count):
+        field_out[x] = field[x] + injected(out, x, blocks[0].shape[1] - 1, width_y)
 
 
 def pair_kernel(keep, arrived, _, *outs):
@@ -415,7 +422,7 @@
     )
     p_halo = swap(p0_even, p0_odd)
     q_halo = swap(q8_even, q8_odd)
-    tiles = vmem((count * width_y + 1) * 8, width_z)
+    tiles = vmem(((count + 2 * reach) * width_y + 1) * 8, width_z)
     before, now, speed, where_to, zeros = call(
         "load",
         load_kernel,
@@ -425,7 +432,8 @@
         {i: HBM for i in range(4)},
         micros=1,
     )
-    p, q = {-1: before, 0: now}, {}
+    p = {-1: before, 0: now}
+    q = {steps + 1: adjoint_after[0], steps: adjoint_now[0]}
     laps = {}
     acc = None
 
@@ -433,7 +441,7 @@
         last = k == steps - 1
         parts = dict(
             moves=not last, stores=k < half, adds=k >= half, opens=k == half, step=k, scale=scale,
-            sends=0 < k < steps - 1,
+            sends=not last,
         )
         args = [p[k], *p_halo, right, left]
         outs, scratch, spaces = [], [halo], {}
@@ -471,19 +479,6 @@
                 laps[k] = got.pop(0)
             else:
                 acc = got.pop(0)
-        if k == 0:
-            at = 1 + len(blocks)
-            inject, q[steps + 1], q[steps], *sides = call(
-                "receivers",
-                functools.partial(scatter_kernel, len(blocks)),
-                [where_to, *blocks, adjoint_after[0], adjoint_now[0], p[1], zeros],
-                [tiles, field, field, edge, edge],
-                [dma((2,))],
-                {0: SMEM, at: HBM, at + 1: HBM},
-                aliases={at + 3: 0},
-            )
-            p_halo = swap(*sides)
-
         t = steps - 1 - k
         if last:
             send, kept = got
@@ -520,8 +515,10 @@
             )
             (gradient,) = call("sum", sum_kernel, terms, [plain(count, width_y // shots, width_z)], micros=0)
             break
-        parts = dict(adds=k >= half, time=t)
-        args = [q[t + 1], q[t + 2], speed, *q_halo, inject, right, left]
+        parts = dict(adds=k >= half, time=t, injects=k > 0, late=k == 1)
+        args = [q[t + 1], q[t + 2], speed, *q_halo, right, left]
+        if k > 0:
+            args += [inject]
         outs = [field, edge, edge]
         if parts["adds"]:
             args += [laps[t], acc]
@@ -531,6 +528,17 @@
         q_halo = swap(*got[1:3])
         if parts["adds"]:
             acc = got[3]
+        if k == 0:
+            at = 1 + len(blocks)
+            inject, q[t] = call(
+                "receivers",
+                functools.partial(scatter_kernel, len(blocks)),
+                [where_to, *blocks, q[t], zeros],
+                [tiles, field],
+                (),
+                {0: SMEM},
+                aliases={at: 1, at + 1: 0},
+            )
 
     return (opening[None], second[None], gradient)
 

time: 123 us -> 119 us (0.967)
  starting transfers between devices: 75.8 us -> 71 us
  Pallas kernels: 35.9 us -> 33.6 us
  local copies, waits for them, and re-layouts: 2.04 us -> 3.85 us
  waiting for transfers between devices: 7.29 us -> 8.82 us
    ppermute x16, starting transfers between devices: 52.4 us -> 49.4 us  [swap(): lax.ppermute(even, 'slab', even_pairs)]
    ppermute x16, waiting for transfers between devices: 1.46 us -> 3.77 us  [swap(): lax.ppermute(even, 'slab', even_pairs)]
    pallas_call x23, Pallas kernels: 35.9 us -> 33.6 us  [call(): pl.pallas_call(kernel, out_shape=outs, in_specs=[spec(spaces.get(i, VMEM)...]
    unnamed x9 -> x17, local copies, waits for them, and re-layouts: 2.04 us -> 3.85 us
    ppermute x2, starting transfers between devices: 9.09 us -> 7.32 us  [body(): lax.ppermute(held, 'slab', [(i, i ^ bit) for i in range(slabs)])]
  transfers between devices with their start and end apart: 38 -> 38, of which waited for: 8 -> 8; matrix products, arithmetic and copies ran while one was open for 1% -> 1% of each run, Pallas kernels for 28% -> 27%
where the time goes in v5:
time: 119 us; the launch traced here: 118 us
  starting transfers between devices  71 us (60%)
  Pallas kernels  33.6 us (28%)
  waiting for transfers between devices  8.82 us (7%)
  local copies, waits for them, and re-layouts  3.85 us (3%)
    ppermute x16, starting transfers between devices, swap(): lax.ppermute(even, 'slab', even_pairs)  49.4 us
    pallas_call x23, Pallas kernels, call(): pl.pallas_call(kernel, out_shape=outs, in_specs=[spec(spaces.get(i, VMEM)...  33.6 us
    ppermute x16, starting transfers between devices, swap(): lax.ppermute(odd, 'slab', odd_pairs)  10.6 us
    ppermute x2, starting transfers between devices, body(): lax.ppermute(held, 'slab', [(i, i ^ bit) for i in range(slabs)])  7.32 us
    ppermute x3, waiting for transfers between devices, body(): lax.ppermute(pieces[m], 'shot', [(i, i ^ 2 * m) for i in range(shots)])  4.61 us
    unnamed x17, local copies, waits for them, and re-layouts  3.85 us
    ppermute x16, waiting for transfers between devices, swap(): lax.ppermute(even, 'slab', even_pairs)  3.77 us
    ppermute x3, starting transfers between devices, body(): lax.ppermute(pieces[m], 'shot', [(i, i ^ 2 * m) for i in range(shots)])  3.55 us
  transfers between devices with their start and end apart: 38, of which 8 were waited for; matrix products, arithmetic and copies ran while one was open for 1% of the time, Pallas kernels for 27%

profile of v5, /device:TPU:0, one launch (start us, length us, event | category | flops | bytes accessed | tf_op | source)
XLA Modules:
  0.0 118.5 jit_solution(9120156569586675119)
XLA Ops:
  0.7 1.4 %edges.1 = (f32[4,128,128]{2,1,0:T(8,128)S(1)}, f32[4,128,128]{2,1,0:T(8,128)S(1)}, f32[4,128,128]{2,1,0:T(8,128)S(1)}, f32[4,128,128]{2,1,0:T(8,128)S(1)}) custom-call(f32[16,128,128]{2,1,0:T(8,128)} %bitcast.13, f32[16,128,128]{2,1,0:T(8,128)} %bitcast.6), custom_call_target="tpu_custom_call" | custom-call | flops 2000000000 | bytes 131072 | tf_op jit(solution)/shard_map/edges/pallas_call | solution.py:360
  2.1 3.1 %collective-permute-start.12 = (f32[4,128,128]{2,1,0:T(8,128)S(1)}, f32[4,128,128]{2,1,0:T(8,128)S(1)}, u32[]{:S(2)}, u32[]{:S(2)}) collective-permute-start(f32[4,128,128]{2,1,0:T(8,128)S(1)} %get-tuple-element.94), channel_id=1, source_target_pairs={{0,1},{1,0},{2,3},{3,2},{4,5},{5,4},{6,7},{7,6},{8,9},{9,8},{10,11... | collective-permute-start | bytes 786440 | tf_op jit(solution)/shard_map/ppermute | solution.py:406
  5.8 4.4 %collective-permute-start = (f32[1,8,256]{2,1,0:T(8,128)}, f32[1,8,256]{2,1,0:T(8,128)S(1)}, u32[]{:S(2)}, u32[]{:S(2)}) collective-permute-start(f32[1,8,256]{2,1,0:T(8,128)} %refs_0_.3), channel_id=1, source_target_pairs={{0,1},{1,0},{2,3},{3,2},{4,5},{5,4},{6,7},{7,6},{8,9},{9,8},{10,11... | collective-permute-start | bytes 24584 | tf_op jit(solution)/shard_map/ppermute | solution.py:417
  13.1 1.9 %load.1 = (f32[16,128,128]{2,1,0:T(8,128)S(1)}, f32[16,128,128]{2,1,0:T(8,128)S(1)}, f32[16,128,128]{2,1,0:T(8,128)S(1)}, s32[1,1024]{1,0:T(1,128)S(1)}, f32[24584,128]{1,0:T(8,128)S(1)}) custom-call(s32[1,3,1024]{2,1,0:T(4,128)} %copy.17.listen_hbm, f32[16,128,128]{2,1,0:T(8,128)} %bitcast.12, f32[16,128,128]{2,1,0:T(8,128)} %bitcast.14, ...), custom_call_target="tpu_custom_call" | custom-call | flops 1000000000 | bytes 65536 | tf_op jit(solution)/shard_map/load/pallas_call | solution.py:360
  18.0 3.3 %collective-permute-start.14 = (f32[4,128,128]{2,1,0:T(8,128)S(1)}, f32[4,128,128]{2,1,0:T(8,128)S(1)}, u32[]{:S(2)}, u32[]{:S(2)}) collective-permute-start(f32[4,128,128]{2,1,0:T(8,128)S(1)} %get-tuple-element.98), channel_id=1, source_target_pairs={{0,1},{1,0},{2,3},{3,2},{4,5},{5,4},{6,7},{7,6},{8,9},{9,8},{10,11... | collective-permute-start | bytes 786440 | tf_op jit(solution)/shard_map/ppermute | solution.py:406
  21.9 2.9 %collective-permute-start.1 = (f32[2,8,256]{2,1,0:T(8,128)S(1)}, f32[2,8,256]{2,1,0:T(8,128)S(1)}, u32[]{:S(2)}, u32[]{:S(2)}) collective-permute-start(f32[2,8,256]{2,1,0:T(8,128)S(1)} %stack.1.refs_3_), channel_id=1, source_target_pairs={{0,2},{1,3},{2,0},{3,1},{4,6},{5,7},{6,4},{7,5},{8,10},{9,11},{10,... | collective-permute-start | bytes 49160 | tf_op jit(solution)/shard_map/ppermute | solution.py:417
  28.8 4.7 %collective-permute-start.16 = (f32[4,128,128]{2,1,0:T(8,128)S(1)}, f32[4,128,128]{2,1,0:T(8,128)S(1)}, u32[]{:S(2)}, u32[]{:S(2)}) collective-permute-start(f32[4,128,128]{2,1,0:T(8,128)S(1)} %get-tuple-element.101), channel_id=1, source_target_pairs={{0,1},{1,0},{2,3},{3,2},{4,5},{5,4},{6,7},{7,6},{8,9},{9,8},{10,11... | collective-permute-start | bytes 786440 | tf_op jit(solution)/shard_map/ppermute | solution.py:406
  34.1 6.1 %receivers.1 = (f32[24584,128]{1,0:T(8,128)S(1)}, f32[16,128,128]{2,1,0:T(8,128)S(1)}) custom-call(s32[1,1024]{1,0:T(1,128)S(1)} %get-tuple-element.74.where_to, f32[1,8,256]{2,1,0:T(8,128)S(1)} %copy-done.6, f32[1,8,256]{2,1,0:T(8,128)S(1)} %collective-permute-done.refs_1_, ...), custom_call_target="tpu_custom_call", output_to_operand_aliasing={{1}: (4, {}), {0}: (5, {})} | custom-call | flops 2000000000 | bytes 131072 | tf_op jit(solution)/shard_map/receivers/pallas_call | solution.py:360
  40.2 1.5 %adjoint.8 = (f32[16,128,128]{2,1,0:T(8,128)S(1)}, f32[4,128,128]{2,1,0:T(8,128)S(1)}, f32[4,128,128]{2,1,0:T(8,128)S(1)}) custom-call(f32[16,128,128]{2,1,0:T(8,128)S(1)} %get-tuple-element.80.refs_0_.refs_1_.refs_9_, f32[16,128,128]{2,1,0:T(8,128)S(1)} %bitcast.8, f32[16,128,128]{2,1,0:T(8,128)S(1)} %get-tuple-element.75.refs_2_.refs_6_.speed, ...), custom_call_target="tpu_custom_call" | custom-call | flops 2000000000 | bytes 131072 | tf_op jit(solution)/shard_map/adjoint/pallas_call | solution.py:360
  41.8 1.5 %collective-permute-start.6 = (f32[4,128,128]{2,1,0:T(8,128)S(1)}, f32[4,128,128]{2,1,0:T(8,128)S(1)}, u32[]{:S(2)}, u32[]{:S(2)}) collective-permute-start(f32[4,128,128]{2,1,0:T(8,128)S(1)} %get-tuple-element.85), channel_id=1, source_target_pairs={{0,1},{1,0},{2,3},{3,2},{4,5},{5,4},{6,7},{7,6},{8,9},{9,8},{10,11... | collective-permute-start | bytes 786440 | tf_op jit(solution)/shard_map/ppermute | solution.py:406
  45.2 3.2 %collective-permute-start.18 = (f32[4,128,128]{2,1,0:T(8,128)S(1)}, f32[4,128,128]{2,1,0:T(8,128)S(1)}, u32[]{:S(2)}, u32[]{:S(2)}) collective-permute-start(f32[4,128,128]{2,1,0:T(8,128)S(1)} %get-tuple-element.104), channel_id=1, source_target_pairs={{0,1},{1,0},{2,3},{3,2},{4,5},{5,4},{6,7},{7,6},{8,9},{9,8},{10,11... | collective-permute-start | bytes 786440 | tf_op jit(solution)/shard_map/ppermute | solution.py:406
  49.0 1.6 %collective-permute-done.6.refs_3_ = f32[4,128,128]{2,1,0:T(8,128)S(1)} collective-permute-done((f32[4,128,128]{2,1,0:T(8,128)S(1)}, f32[4,128,128]{2,1,0:T(8,128)S(1)}, u32[]{:S(2)}, u32[]{:S(2)}) %collective-permute-start.6) | collective-permute-done | bytes 262176 | tf_op jit(solution)/shard_map/ppermute | solution.py:406
  52.0 4.2 %collective-permute-start.8 = (f32[4,128,128]{2,1,0:T(8,128)S(1)}, f32[4,128,128]{2,1,0:T(8,128)S(1)}, u32[]{:S(2)}, u32[]{:S(2)}) collective-permute-start(f32[4,128,128]{2,1,0:T(8,128)S(1)} %get-tuple-element.88), channel_id=1, source_target_pairs={{0,1},{1,0},{2,3},{3,2},{4,5},{5,4},{6,7},{7,6},{8,9},{9,8},{10,11... | collective-permute-start | bytes 786440 | tf_op jit(solution)/shard_map/ppermute | solution.py:406
  56.8 1.4 %forward.11 = (f32[16,128,128]{2,1,0:T(8,128)S(1)}, f32[4,128,128]{2,1,0:T(8,128)S(1)}, f32[4,128,128]{2,1,0:T(8,128)S(1)}, f32[16,128,128]{2,1,0:T(8,128)S(1)}) custom-call(f32[16,128,128]{2,1,0:T(8,128)S(1)} %get-tuple-element.103.refs_0_.refs_5_, f32[4,128,128]{2,1,0:T(8,128)S(1)} %collective-permute-done.18.refs_1_, ...), custom_call_target="tpu_custom_call" | custom-call | flops 2000000000 | bytes 131072 | tf_op jit(solution)/shard_map/forward/pallas_call | solution.py:360
  58.2 3.6 %collective-permute-start.20 = (f32[4,128,128]{2,1,0:T(8,128)S(1)}, f32[4,128,128]{2,1,0:T(8,128)S(1)}, u32[]{:S(2)}, u32[]{:S(2)}) collective-permute-start(f32[4,128,128]{2,1,0:T(8,128)S(1)} %get-tuple-element.108), channel_id=1, source_target_pairs={{0,1},{1,0},{2,3},{3,2},{4,5},{5,4},{6,7},{7,6},{8,9},{9,8},{10,11... | collective-permute-start | bytes 786440 | tf_op jit(solution)/shard_map/ppermute | solution.py:406
  64.6 3.7 %collective-permute-start.10 = (f32[4,128,128]{2,1,0:T(8,128)S(1)}, f32[4,128,128]{2,1,0:T(8,128)S(1)}, u32[]{:S(2)}, u32[]{:S(2)}) collective-permute-start(f32[4,128,128]{2,1,0:T(8,128)S(1)} %get-tuple-element.91), channel_id=1, source_target_pairs={{0,1},{1,0},{2,3},{3,2},{4,5},{5,4},{6,7},{7,6},{8,9},{9,8},{10,11... | collective-permute-start | bytes 786440 | tf_op jit(solution)/shard_map/ppermute | solution.py:406
  70.3 3.4 %collective-permute-start.24 = (f32[4,128,128]{2,1,0:T(8,128)S(1)}, f32[4,128,128]{2,1,0:T(8,128)S(1)}, u32[]{:S(2)}, u32[]{:S(2)}) collective-permute-start(f32[4,128,128]{2,1,0:T(8,128)S(1)} %get-tuple-element.116), channel_id=1, source_target_pairs={{0,1},{1,0},{2,3},{3,2},{4,5},{5,4},{6,7},{7,6},{8,9},{9,8},{10,11... | collective-permute-start | bytes 786440 | tf_op jit(solution)/shard_map/ppermute | solution.py:406
  74.4 1.5 %adjoint.11 = (f32[16,128,128]{2,1,0:T(8,128)S(1)}, f32[4,128,128]{2,1,0:T(8,128)S(1)}, f32[4,128,128]{2,1,0:T(8,128)S(1)}, f32[16,128,128]{2,1,0:T(8,128)S(1)}) custom-call(f32[16,128,128]{2,1,0:T(8,128)S(1)} %get-tuple-element.90.refs_0_.refs_1_, f32[16,128,128]{2,1,0:T(8,128)S(1)} %get-tuple-element.87.refs_0_.refs_9_.refs_1_, ...), custom_call_target="tpu_custom_call" | custom-call | flops 2000000000 | bytes 131072 | tf_op jit(solution)/shard_map/adjoint/pallas_call | solution.py:360
  75.9 3.7 %collective-permute-start.22 = (f32[4,128,128]{2,1,0:T(8,128)S(1)}, f32[4,128,128]{2,1,0:T(8,128)S(1)}, u32[]{:S(2)}, u32[]{:S(2)}) collective-permute-start(f32[4,128,128]{2,1,0:T(8,128)S(1)} %get-tuple-element.112), channel_id=1, source_target_pairs={{0,1},{1,0},{2,3},{3,2},{4,5},{5,4},{6,7},{7,6},{8,9},{9,8},{10,11... | collective-permute-start | bytes 786440 | tf_op jit(solution)/shard_map/ppermute | solution.py:406
  80.8 1.4 %forward.13 = (f32[16,128,128]{2,1,0:T(8,128)S(1)}, f32[4,128,128]{2,1,0:T(8,128)S(1)}, f32[4,128,128]{2,1,0:T(8,128)S(1)}, f32[16,128,128]{2,1,0:T(8,128)S(1)}) custom-call(f32[16,128,128]{2,1,0:T(8,128)S(1)} %get-tuple-element.115.refs_0_.refs_5_, f32[4,128,128]{2,1,0:T(8,128)S(1)} %collective-permute-done.24.refs_1_, ...), custom_call_target="tpu_custom_call" | custom-call | flops 2000000000 | bytes 131072 | tf_op jit(solution)/shard_map/forward/pallas_call | solution.py:360
  82.2 4.0 %collective-permute-start.28 = (f32[4,128,128]{2,1,0:T(8,128)S(1)}, f32[4,128,128]{2,1,0:T(8,128)S(1)}, u32[]{:S(2)}, u32[]{:S(2)}) collective-permute-start(f32[4,128,128]{2,1,0:T(8,128)S(1)} %get-tuple-element.125), channel_id=1, source_target_pairs={{0,1},{1,0},{2,3},{3,2},{4,5},{5,4},{6,7},{7,6},{8,9},{9,8},{10,11... | collective-permute-start | bytes 786440 | tf_op jit(solution)/shard_map/ppermute | solution.py:406
  86.9 1.5 %adjoint.12 = (f32[16,128,128]{2,1,0:T(8,128)S(1)}, f32[4,128,128]{2,1,0:T(8,128)S(1)}, f32[4,128,128]{2,1,0:T(8,128)S(1)}, f32[16,128,128]{2,1,0:T(8,128)S(1)}) custom-call(f32[16,128,128]{2,1,0:T(8,128)S(1)} %get-tuple-element.111.refs_0_.refs_1_, f32[16,128,128]{2,1,0:T(8,128)S(1)} %get-tuple-element.90.refs_0_.refs_1_, ...), custom_call_target="tpu_custom_call" | custom-call | flops 2000000000 | bytes 131072 | tf_op jit(solution)/shard_map/adjoint/pallas_call | solution.py:360
  88.4 2.9 %collective-permute-start.26 = (f32[4,128,128]{2,1,0:T(8,128)S(1)}, f32[4,128,128]{2,1,0:T(8,128)S(1)}, u32[]{:S(2)}, u32[]{:S(2)}) collective-permute-start(f32[4,128,128]{2,1,0:T(8,128)S(1)} %get-tuple-element.121), channel_id=1, source_target_pairs={{0,1},{1,0},{2,3},{3,2},{4,5},{5,4},{6,7},{7,6},{8,9},{9,8},{10,11... | collective-permute-start | bytes 786440 | tf_op jit(solution)/shard_map/ppermute | solution.py:406
  93.5 3.7 %collective-permute-start.32 = (f32[4,128,128]{2,1,0:T(8,128)S(1)}, f32[4,128,128]{2,1,0:T(8,128)S(1)}, u32[]{:S(2)}, u32[]{:S(2)}) collective-permute-start(f32[4,128,128]{2,1,0:T(8,128)S(1)} %get-tuple-element.135), channel_id=1, source_target_pairs={{0,1},{1,0},{2,3},{3,2},{4,5},{5,4},{6,7},{7,6},{8,9},{9,8},{10,11... | collective-permute-start | bytes 786440 | tf_op jit(solution)/shard_map/ppermute | solution.py:406
  98.4 1.8 %adjoint.13 = (f32[16,128,128]{2,1,0:T(8,128)S(1)}, f32[4,128,128]{2,1,0:T(8,128)S(1)}, f32[4,128,128]{2,1,0:T(8,128)S(1)}, f32[16,128,128]{2,1,0:T(8,128)S(1)}) custom-call(f32[16,128,128]{2,1,0:T(8,128)S(1)} %get-tuple-element.120.refs_0_.later, f32[16,128,128]{2,1,0:T(8,128)S(1)} %get-tuple-element.111.refs_0_.refs_1_, ...), custom_call_target="tpu_custom_call" | custom-call | flops 2000000000 | bytes 131072 | tf_op jit(solution)/shard_map/adjoint/pallas_call | solution.py:360
  100.3 3.7 %collective-permute-start.30 = (f32[4,128,128]{2,1,0:T(8,128)S(1)}, f32[4,128,128]{2,1,0:T(8,128)S(1)}, u32[]{:S(2)}, u32[]{:S(2)}) collective-permute-start(f32[4,128,128]{2,1,0:T(8,128)S(1)} %get-tuple-element.130), channel_id=1, source_target_pairs={{0,1},{1,0},{2,3},{3,2},{4,5},{5,4},{6,7},{7,6},{8,9},{9,8},{10,11... | collective-permute-start | bytes 786440 | tf_op jit(solution)/shard_map/ppermute | solution.py:406
  104.7 1.5 %forward.15 = (f32[4,16,16,128]{3,2,1,0:T(8,128)S(1)}, f32[4,16,16,128]{3,2,1,0:T(8,128)S(1)}) custom-call(f32[16,128,128]{2,1,0:T(8,128)S(1)} %get-tuple-element.134.refs_0_, f32[4,128,128]{2,1,0:T(8,128)S(1)} %collective-permute-done.32.refs_1_, f32[4,128,128]{2,1,0:T(8,128)S(1)} %collective-permute-done.33.refs_2_, bf16[256,256]{1,0:T(8,128)(2,1)S(1)} %copy-done.3, ...), custom_call_target="tpu_custom_call" | custom-call | tf_op jit(solution)/shard_map/forward/pallas_call | solution.py:360
  106.2 1.5 %last_inner.1 = (f32[16,128,128]{2,1,0:T(8,128)}, f32[16,128,128]{2,1,0:T(8,128)}) custom-call(f32[16,128,128]{2,1,0:T(8,128)S(1)} %get-tuple-element.129.cur.refs_7_, f32[16,128,128]{2,1,0:T(8,128)S(1)} %get-tuple-element.120.refs_0_.later, f32[16,128,128]{2,1,0:T(8,128)S(1)} %get-tuple-element.75.refs_2_.refs_6_.speed, ...), custom_call_target="tpu_custom_call" | custom-call | flops 30000001024 | bytes 1966080 | tf_op jit(solution)/shard_map/last_inner/pallas_call | solution.py:360
  108.2 1.5 %collective-permute-start.35 = (f32[16,16,128]{2,1,0:T(8,128)S(1)}, f32[16,16,128]{2,1,0:T(8,128)S(1)}, u32[]{:S(2)}, u32[]{:S(2)}) collective-permute-start(f32[16,16,128]{2,1,0:T(8,128)S(1)} %get-tuple-element.142), channel_id=1, source_target_pairs={{0,8},{4,12},{8,0},{12,4},{16,24},{20,28},{24,16},{28,20},{1,9},{5... | collective-permute-start | bytes 393224 | tf_op jit(solution)/shard_map/ppermute | solution.py:502
  109.7 1.5 %collective-permute-start.36 = (f32[16,16,128]{2,1,0:T(8,128)S(1)}, f32[16,16,128]{2,1,0:T(8,128)S(1)}, u32[]{:S(2)}, u32[]{:S(2)}) collective-permute-start(f32[16,16,128]{2,1,0:T(8,128)S(1)} %get-tuple-element.143), channel_id=1, source_target_pairs={{0,16},{4,20},{8,24},{12,28},{16,0},{20,4},{24,8},{28,12},{1,17},{... | collective-permute-start | bytes 393224 | tf_op jit(solution)/shard_map/ppermute | solution.py:502
  111.7 1.4 %last_border.1 = f32[16,128,128]{2,1,0:T(8,128)} custom-call(f32[16,128,128]{2,1,0:T(8,128)S(1)} %get-tuple-element.129.cur.refs_7_, f32[16,128,128]{2,1,0:T(8,128)S(1)} %get-tuple-element.120.refs_0_.later, f32[16,128,128]{2,1,0:T(8,128)S(1)} %get-tuple-element.75.refs_2_.refs_6_.speed, ...), custom_call_target="tpu_custom_call", output_to_operand_aliasing={{}: (8, {})} | custom-call | flops 30000001024 | bytes 1966080 | tf_op jit(solution)/shard_map/last_border/pallas_call | solution.py:360
  114.1 3.7 %collective-permute-done.36.refs_2_ = f32[16,16,128]{2,1,0:T(8,128)S(1)} collective-permute-done((f32[16,16,128]{2,1,0:T(8,128)S(1)}, f32[16,16,128]{2,1,0:T(8,128)S(1)}, u32[]{:S(2)}, u32[]{:S(2)}) %collective-permute-start.36) | collective-permute-done | bytes 131104 | tf_op jit(solution)/shard_map/ppermute | solution.py:502
  (84 shorter events, 30.3 us)
Async XLA Ops:
  2.1 12.9 %collective-permute-start.12 = (f32[4,128,128]{2,1,0:T(8,128)S(1)}, f32[4,128,128]{2,1,0:T(8,128)S(1)}, u32[]{:S(2)}, u32[]{:S(2)}) collective-permute-start(f32[4,128,128]{2,1,0:T(8,128)S(1)} %get-tuple-element.94), channel_id=1, source_target_pairs={{0,1},{1,0},{2,3},{3,2},{4,5},{5,4},{6,7},{7,6},{8,9},{9,8},{10,11... | collective-permute-start | bytes 786440 | tf_op jit(solution)/shard_map/ppermute | solution.py:406
  5.2 9.8 %collective-permute-start.13 = (f32[4,128,128]{2,1,0:T(8,128)S(1)}, f32[4,128,128]{2,1,0:T(8,128)S(1)}, u32[]{:S(2)}, u32[]{:S(2)}) collective-permute-start(f32[4,128,128]{2,1,0:T(8,128)S(1)} %get-tuple-element.95), channel_id=1, source_target_pairs={{1,2},{2,1},{5,6},{6,5},{9,10},{10,9},{13,14},{14,13},{17,18},{18,... | collective-permute-start | bytes 786440 | tf_op jit(solution)/shard_map/ppermute | solution.py:406
  10.3 14.5 %collective-permute-start.2 = (f32[4,128,128]{2,1,0:T(8,128)S(1)}, f32[4,128,128]{2,1,0:T(8,128)S(1)}, u32[]{:S(2)}, u32[]{:S(2)}) collective-permute-start(f32[4,128,128]{2,1,0:T(8,128)S(1)} %get-tuple-element.76), channel_id=1, source_target_pairs={{0,1},{1,0},{2,3},{3,2},{4,5},{5,4},{6,7},{7,6},{8,9},{9,8},{10,11... | collective-permute-start | bytes 786440 | tf_op jit(solution)/shard_map/ppermute | solution.py:406
  10.4 14.4 %collective-permute-start.3 = (f32[4,128,128]{2,1,0:T(8,128)S(1)}, f32[4,128,128]{2,1,0:T(8,128)S(1)}, u32[]{:S(2)}, u32[]{:S(2)}) collective-permute-start(f32[4,128,128]{2,1,0:T(8,128)S(1)} %get-tuple-element.77), channel_id=1, source_target_pairs={{1,2},{2,1},{5,6},{6,5},{9,10},{10,9},{13,14},{14,13},{17,18},{18,... | collective-permute-start | bytes 786440 | tf_op jit(solution)/shard_map/ppermute | solution.py:406
  18.0 9.5 %collective-permute-start.14 = (f32[4,128,128]{2,1,0:T(8,128)S(1)}, f32[4,128,128]{2,1,0:T(8,128)S(1)}, u32[]{:S(2)}, u32[]{:S(2)}) collective-permute-start(f32[4,128,128]{2,1,0:T(8,128)S(1)} %get-tuple-element.98), channel_id=1, source_target_pairs={{0,1},{1,0},{2,3},{3,2},{4,5},{5,4},{6,7},{7,6},{8,9},{9,8},{10,11... | collective-permute-start | bytes 786440 | tf_op jit(solution)/shard_map/ppermute | solution.py:406
  21.9 12.2 %collective-permute-start.1 = (f32[2,8,256]{2,1,0:T(8,128)S(1)}, f32[2,8,256]{2,1,0:T(8,128)S(1)}, u32[]{:S(2)}, u32[]{:S(2)}) collective-permute-start(f32[2,8,256]{2,1,0:T(8,128)S(1)} %stack.1.refs_3_), channel_id=1, source_target_pairs={{0,2},{1,3},{2,0},{3,1},{4,6},{5,7},{6,4},{7,5},{8,10},{9,11},{10,... | collective-permute-start | bytes 49160 | tf_op jit(solution)/shard_map/ppermute | solution.py:417
  26.1 14.1 %collective-permute-start.4 = (f32[4,128,128]{2,1,0:T(8,128)S(1)}, f32[4,128,128]{2,1,0:T(8,128)S(1)}, u32[]{:S(2)}, u32[]{:S(2)}) collective-permute-start(f32[4,128,128]{2,1,0:T(8,128)S(1)} %get-tuple-element.81), channel_id=1, source_target_pairs={{0,1},{1,0},{2,3},{3,2},{4,5},{5,4},{6,7},{7,6},{8,9},{9,8},{10,11... | collective-permute-start | bytes 786440 | tf_op jit(solution)/shard_map/ppermute | solution.py:406
  26.9 13.4 %collective-permute-start.5 = (f32[4,128,128]{2,1,0:T(8,128)S(1)}, f32[4,128,128]{2,1,0:T(8,128)S(1)}, u32[]{:S(2)}, u32[]{:S(2)}) collective-permute-start(f32[4,128,128]{2,1,0:T(8,128)S(1)} %get-tuple-element.82), channel_id=1, source_target_pairs={{1,2},{2,1},{5,6},{6,5},{9,10},{10,9},{13,14},{14,13},{17,18},{18,... | collective-permute-start | bytes 786440 | tf_op jit(solution)/shard_map/ppermute | solution.py:406
  28.8 15.2 %collective-permute-start.16 = (f32[4,128,128]{2,1,0:T(8,128)S(1)}, f32[4,128,128]{2,1,0:T(8,128)S(1)}, u32[]{:S(2)}, u32[]{:S(2)}) collective-permute-start(f32[4,128,128]{2,1,0:T(8,128)S(1)} %get-tuple-element.101), channel_id=1, source_target_pairs={{0,1},{1,0},{2,3},{3,2},{4,5},{5,4},{6,7},{7,6},{8,9},{9,8},{10,11... | collective-permute-start | bytes 786440 | tf_op jit(solution)/shard_map/ppermute | solution.py:406
  33.4 10.5 %collective-permute-start.17 = (f32[4,128,128]{2,1,0:T(8,128)S(1)}, f32[4,128,128]{2,1,0:T(8,128)S(1)}, u32[]{:S(2)}, u32[]{:S(2)}) collective-permute-start(f32[4,128,128]{2,1,0:T(8,128)S(1)} %get-tuple-element.102), channel_id=1, source_target_pairs={{1,2},{2,1},{5,6},{6,5},{9,10},{10,9},{13,14},{14,13},{17,18},{18,... | collective-permute-start | bytes 786440 | tf_op jit(solution)/shard_map/ppermute | solution.py:406
  41.8 8.9 %collective-permute-start.6 = (f32[4,128,128]{2,1,0:T(8,128)S(1)}, f32[4,128,128]{2,1,0:T(8,128)S(1)}, u32[]{:S(2)}, u32[]{:S(2)}) collective-permute-start(f32[4,128,128]{2,1,0:T(8,128)S(1)} %get-tuple-element.85), channel_id=1, source_target_pairs={{0,1},{1,0},{2,3},{3,2},{4,5},{5,4},{6,7},{7,6},{8,9},{9,8},{10,11... | collective-permute-start | bytes 786440 | tf_op jit(solution)/shard_map/ppermute | solution.py:406
  43.3 7.3 %collective-permute-start.7 = (f32[4,128,128]{2,1,0:T(8,128)S(1)}, f32[4,128,128]{2,1,0:T(8,128)S(1)}, u32[]{:S(2)}, u32[]{:S(2)}) collective-permute-start(f32[4,128,128]{2,1,0:T(8,128)S(1)} %get-tuple-element.86), channel_id=1, source_target_pairs={{1,2},{2,1},{5,6},{6,5},{9,10},{10,9},{13,14},{14,13},{17,18},{18,... | collective-permute-start | bytes 786440 | tf_op jit(solution)/shard_map/ppermute | solution.py:406
  45.2 11.6 %collective-permute-start.18 = (f32[4,128,128]{2,1,0:T(8,128)S(1)}, f32[4,128,128]{2,1,0:T(8,128)S(1)}, u32[]{:S(2)}, u32[]{:S(2)}) collective-permute-start(f32[4,128,128]{2,1,0:T(8,128)S(1)} %get-tuple-element.104), channel_id=1, source_target_pairs={{0,1},{1,0},{2,3},{3,2},{4,5},{5,4},{6,7},{7,6},{8,9},{9,8},{10,11... | collective-permute-start | bytes 786440 | tf_op jit(solution)/shard_map/ppermute | solution.py:406
  48.3 8.5 %collective-permute-start.19 = (f32[4,128,128]{2,1,0:T(8,128)S(1)}, f32[4,128,128]{2,1,0:T(8,128)S(1)}, u32[]{:S(2)}, u32[]{:S(2)}) collective-permute-start(f32[4,128,128]{2,1,0:T(8,128)S(1)} %get-tuple-element.105), channel_id=1, source_target_pairs={{1,2},{2,1},{5,6},{6,5},{9,10},{10,9},{13,14},{14,13},{17,18},{18,... | collective-permute-start | bytes 786440 | tf_op jit(solution)/shard_map/ppermute | solution.py:406
  52.0 11.3 %collective-permute-start.8 = (f32[4,128,128]{2,1,0:T(8,128)S(1)}, f32[4,128,128]{2,1,0:T(8,128)S(1)}, u32[]{:S(2)}, u32[]{:S(2)}) collective-permute-start(f32[4,128,128]{2,1,0:T(8,128)S(1)} %get-tuple-element.88), channel_id=1, source_target_pairs={{0,1},{1,0},{2,3},{3,2},{4,5},{5,4},{6,7},{7,6},{8,9},{9,8},{10,11... | collective-permute-start | bytes 786440 | tf_op jit(solution)/shard_map/ppermute | solution.py:406
  56.1 7.2 %collective-permute-start.9 = (f32[4,128,128]{2,1,0:T(8,128)S(1)}, f32[4,128,128]{2,1,0:T(8,128)S(1)}, u32[]{:S(2)}, u32[]{:S(2)}) collective-permute-start(f32[4,128,128]{2,1,0:T(8,128)S(1)} %get-tuple-element.89), channel_id=1, source_target_pairs={{1,2},{2,1},{5,6},{6,5},{9,10},{10,9},{13,14},{14,13},{17,18},{18,... | collective-permute-start | bytes 786440 | tf_op jit(solution)/shard_map/ppermute | solution.py:406
  58.2 10.8 %collective-permute-start.20 = (f32[4,128,128]{2,1,0:T(8,128)S(1)}, f32[4,128,128]{2,1,0:T(8,128)S(1)}, u32[]{:S(2)}, u32[]{:S(2)}) collective-permute-start(f32[4,128,128]{2,1,0:T(8,128)S(1)} %get-tuple-element.108), channel_id=1, source_target_pairs={{0,1},{1,0},{2,3},{3,2},{4,5},{5,4},{6,7},{7,6},{8,9},{9,8},{10,11... | collective-permute-start | bytes 786440 | tf_op jit(solution)/shard_map/ppermute | solution.py:406
  61.8 7.3 %collective-permute-start.21 = (f32[4,128,128]{2,1,0:T(8,128)S(1)}, f32[4,128,128]{2,1,0:T(8,128)S(1)}, u32[]{:S(2)}, u32[]{:S(2)}) collective-permute-start(f32[4,128,128]{2,1,0:T(8,128)S(1)} %get-tuple-element.109), channel_id=1, source_target_pairs={{1,2},{2,1},{5,6},{6,5},{9,10},{10,9},{13,14},{14,13},{17,18},{18,... | collective-permute-start | bytes 786440 | tf_op jit(solution)/shard_map/ppermute | solution.py:406
  64.6 9.7 %collective-permute-start.10 = (f32[4,128,128]{2,1,0:T(8,128)S(1)}, f32[4,128,128]{2,1,0:T(8,128)S(1)}, u32[]{:S(2)}, u32[]{:S(2)}) collective-permute-start(f32[4,128,128]{2,1,0:T(8,128)S(1)} %get-tuple-element.91), channel_id=1, source_target_pairs={{0,1},{1,0},{2,3},{3,2},{4,5},{5,4},{6,7},{7,6},{8,9},{9,8},{10,11... | collective-permute-start | bytes 786440 | tf_op jit(solution)/shard_map/ppermute | solution.py:406
  70.3 10.6 %collective-permute-start.24 = (f32[4,128,128]{2,1,0:T(8,128)S(1)}, f32[4,128,128]{2,1,0:T(8,128)S(1)}, u32[]{:S(2)}, u32[]{:S(2)}) collective-permute-start(f32[4,128,128]{2,1,0:T(8,128)S(1)} %get-tuple-element.116), channel_id=1, source_target_pairs={{0,1},{1,0},{2,3},{3,2},{4,5},{5,4},{6,7},{7,6},{8,9},{9,8},{10,11... | collective-permute-start | bytes 786440 | tf_op jit(solution)/shard_map/ppermute | solution.py:406
  73.7 7.1 %collective-permute-start.25 = (f32[4,128,128]{2,1,0:T(8,128)S(1)}, f32[4,128,128]{2,1,0:T(8,128)S(1)}, u32[]{:S(2)}, u32[]{:S(2)}) collective-permute-start(f32[4,128,128]{2,1,0:T(8,128)S(1)} %get-tuple-element.117), channel_id=1, source_target_pairs={{1,2},{2,1},{5,6},{6,5},{9,10},{10,9},{13,14},{14,13},{17,18},{18,... | collective-permute-start | bytes 786440 | tf_op jit(solution)/shard_map/ppermute | solution.py:406
  75.9 11.1 %collective-permute-start.22 = (f32[4,128,128]{2,1,0:T(8,128)S(1)}, f32[4,128,128]{2,1,0:T(8,128)S(1)}, u32[]{:S(2)}, u32[]{:S(2)}) collective-permute-start(f32[4,128,128]{2,1,0:T(8,128)S(1)} %get-tuple-element.112), channel_id=1, source_target_pairs={{0,1},{1,0},{2,3},{3,2},{4,5},{5,4},{6,7},{7,6},{8,9},{9,8},{10,11... | collective-permute-start | bytes 786440 | tf_op jit(solution)/shard_map/ppermute | solution.py:406
  79.5 7.4 %collective-permute-start.23 = (f32[4,128,128]{2,1,0:T(8,128)S(1)}, f32[4,128,128]{2,1,0:T(8,128)S(1)}, u32[]{:S(2)}, u32[]{:S(2)}) collective-permute-start(f32[4,128,128]{2,1,0:T(8,128)S(1)} %get-tuple-element.113), channel_id=1, source_target_pairs={{1,2},{2,1},{5,6},{6,5},{9,10},{10,9},{13,14},{14,13},{17,18},{18,... | collective-permute-start | bytes 786440 | tf_op jit(solution)/shard_map/ppermute | solution.py:406
  82.2 10.0 %collective-permute-start.28 = (f32[4,128,128]{2,1,0:T(8,128)S(1)}, f32[4,128,128]{2,1,0:T(8,128)S(1)}, u32[]{:S(2)}, u32[]{:S(2)}) collective-permute-start(f32[4,128,128]{2,1,0:T(8,128)S(1)} %get-tuple-element.125), channel_id=1, source_target_pairs={{0,1},{1,0},{2,3},{3,2},{4,5},{5,4},{6,7},{7,6},{8,9},{9,8},{10,11... | collective-permute-start | bytes 786440 | tf_op jit(solution)/shard_map/ppermute | solution.py:406
  88.4 10.0 %collective-permute-start.26 = (f32[4,128,128]{2,1,0:T(8,128)S(1)}, f32[4,128,128]{2,1,0:T(8,128)S(1)}, u32[]{:S(2)}, u32[]{:S(2)}) collective-permute-start(f32[4,128,128]{2,1,0:T(8,128)S(1)} %get-tuple-element.121), channel_id=1, source_target_pairs={{0,1},{1,0},{2,3},{3,2},{4,5},{5,4},{6,7},{7,6},{8,9},{9,8},{10,11... | collective-permute-start | bytes 786440 | tf_op jit(solution)/shard_map/ppermute | solution.py:406
  91.3 7.1 %collective-permute-start.27 = (f32[4,128,128]{2,1,0:T(8,128)S(1)}, f32[4,128,128]{2,1,0:T(8,128)S(1)}, u32[]{:S(2)}, u32[]{:S(2)}) collective-permute-start(f32[4,128,128]{2,1,0:T(8,128)S(1)} %get-tuple-element.122), channel_id=1, source_target_pairs={{1,2},{2,1},{5,6},{6,5},{9,10},{10,9},{13,14},{14,13},{17,18},{18,... | collective-permute-start | bytes 786440 | tf_op jit(solution)/shard_map/ppermute | solution.py:406
  93.5 11.1 %collective-permute-start.32 = (f32[4,128,128]{2,1,0:T(8,128)S(1)}, f32[4,128,128]{2,1,0:T(8,128)S(1)}, u32[]{:S(2)}, u32[]{:S(2)}) collective-permute-start(f32[4,128,128]{2,1,0:T(8,128)S(1)} %get-tuple-element.135), channel_id=1, source_target_pairs={{0,1},{1,0},{2,3},{3,2},{4,5},{5,4},{6,7},{7,6},{8,9},{9,8},{10,11... | collective-permute-start | bytes 786440 | tf_op jit(solution)/shard_map/ppermute | solution.py:406
  97.2 7.4 %collective-permute-start.33 = (f32[4,128,128]{2,1,0:T(8,128)S(1)}, f32[4,128,128]{2,1,0:T(8,128)S(1)}, u32[]{:S(2)}, u32[]{:S(2)}) collective-permute-start(f32[4,128,128]{2,1,0:T(8,128)S(1)} %get-tuple-element.136), channel_id=1, source_target_pairs={{1,2},{2,1},{5,6},{6,5},{9,10},{10,9},{13,14},{14,13},{17,18},{18,... | collective-permute-start | bytes 786440 | tf_op jit(solution)/shard_map/ppermute | solution.py:406
  100.3 11.5 %collective-permute-start.30 = (f32[4,128,128]{2,1,0:T(8,128)S(1)}, f32[4,128,128]{2,1,0:T(8,128)S(1)}, u32[]{:S(2)}, u32[]{:S(2)}) collective-permute-start(f32[4,128,128]{2,1,0:T(8,128)S(1)} %get-tuple-element.130), channel_id=1, source_target_pairs={{0,1},{1,0},{2,3},{3,2},{4,5},{5,4},{6,7},{7,6},{8,9},{9,8},{10,11... | collective-permute-start | bytes 786440 | tf_op jit(solution)/shard_map/ppermute | solution.py:406
  104.0 7.8 %collective-permute-start.31 = (f32[4,128,128]{2,1,0:T(8,128)S(1)}, f32[4,128,128]{2,1,0:T(8,128)S(1)}, u32[]{:S(2)}, u32[]{:S(2)}) collective-permute-start(f32[4,128,128]{2,1,0:T(8,128)S(1)} %get-tuple-element.131), channel_id=1, source_target_pairs={{1,2},{2,1},{5,6},{6,5},{9,10},{10,9},{13,14},{14,13},{17,18},{18,... | collective-permute-start | bytes 786440 | tf_op jit(solution)/shard_map/ppermute | solution.py:406
  109.7 8.1 %collective-permute-start.36 = (f32[16,16,128]{2,1,0:T(8,128)S(1)}, f32[16,16,128]{2,1,0:T(8,128)S(1)}, u32[]{:S(2)}, u32[]{:S(2)}) collective-permute-start(f32[16,16,128]{2,1,0:T(8,128)S(1)} %get-tuple-element.143), channel_id=1, source_target_pairs={{0,16},{4,20},{8,24},{12,28},{16,0},{20,4},{24,8},{28,12},{1,17},{... | collective-permute-start | bytes 393224 | tf_op jit(solution)/shard_map/ppermute | solution.py:502
  111.2 6.6 %collective-permute-start.37 = (f32[16,16,128]{2,1,0:T(8,128)S(1)}, f32[16,16,128]{2,1,0:T(8,128)S(1)}, u32[]{:S(2)}, u32[]{:S(2)}) collective-permute-start(f32[16,16,128]{2,1,0:T(8,128)S(1)} %get-tuple-element.144), channel_id=1, source_target_pairs={{0,24},{4,28},{8,16},{12,20},{16,8},{20,12},{24,0},{28,4},{1,25},{... | collective-permute-start | bytes 393224 | tf_op jit(solution)/shard_map/ppermute | solution.py:502
  (14 other events, 153.0 us)

commit v6 on v5

--- a/solution.py
+++ b/solution.py
@@ -102,7 +102,7 @@
 
 def forward_kernel(parts, *refs):
     it = iter(refs)
-    cur, even, odd, right, left = [next(it) for _ in range(5)]
+    cur, odd, even, right, left = [next(it) for _ in range(5)]
     moves, stores, adds, opens = parts["moves"], parts["stores"], parts["adds"], parts["opens"]
     prev, speed, source, wave = [next(it) for _ in range(4)] if moves else (None,) * 4
     late = next(it) if adds else None
@@ -173,7 +173,7 @@
 
 def adjoint_kernel(parts, *refs):
     it = iter(refs)
-    cur, later, speed, even, odd, right, left = [next(it) for _ in range(7)]
+    cur, later, speed, odd, even, right, left = [next(it) for _ in range(7)]
     adds, injects = parts["adds"], parts["injects"]
     inject = next(it) if injects else None
     lap_of, acc_in = (next(it), next(it)) if adds else (None, None)
@@ -216,7 +216,7 @@
 
 
 def last_border_kernel(
-    cur, later, speed, even, odd, inject, right, left, opening_in, opening, halo, field, sems
+    cur, later, speed, odd, even, inject, right, left, opening_in, opening, halo, field, sems
 ):
     count, width_y = cur.shape[:2]
     fill_halo(lax.axis_index("slab") % 2, even, odd, halo)
@@ -403,7 +403,8 @@
     dma = pltpu.SemaphoreType.DMA
 
     def swap(even, odd):
-        return lax.ppermute(even, "slab", even_pairs), lax.ppermute(odd, "slab", odd_pairs)
+        odd = lax.ppermute(odd, "slab", odd_pairs)
+        return odd, lax.ppermute(even, "slab", even_pairs)
 
     right = jnp.asarray(band_right(width_z))
     left = jnp.asarray(band_left(width_y))

time: 119 us -> 126 us (1.059)
  starting transfers between devices: 71 us -> 77.1 us
  waiting for transfers between devices: 8.82 us -> 10.3 us
    ppermute x32, starting transfers between devices: 60 us -> 71.9 us  [the longest x16 61 us: swap(): return (odd, lax.ppermute(even, 'slab', even_pairs))]
    ppermute x2, starting transfers between devices: 7.32 us -> 1.61 us  [body(): lax.ppermute(held, 'slab', [(i, i ^ bit) for i in range(slabs)])]
    ppermute x2, waiting for transfers between devices: 0.01 us -> 1.59 us  [body(): lax.ppermute(held, 'slab', [(i, i ^ bit) for i in range(slabs)])]
  transfers between devices with their start and end apart: 38 -> 38, of which waited for: 8 -> 10; matrix products, arithmetic and copies ran while one was open for 1% -> 1% of each run, Pallas kernels for 27% -> 25%
where the time goes in v6:
time: 126 us
  starting transfers between devices  77.1 us (61%)
  Pallas kernels  33.5 us (27%)
  waiting for transfers between devices  10.3 us (8%)
  local copies, waits for them, and re-layouts  3.84 us (3%)
    ppermute x16, starting transfers between devices, swap(): return (odd, lax.ppermute(even, 'slab', even_pairs))  61 us
    pallas_call x23, Pallas kernels, call(): pl.pallas_call(kernel, out_shape=outs, in_specs=[spec(spaces.get(i, VMEM)...  33.5 us
    ppermute x16, starting transfers between devices, swap(): odd = lax.ppermute(odd, 'slab', odd_pairs)  10.8 us
    ppermute x3, waiting for transfers between devices, body(): lax.ppermute(pieces[m], 'shot', [(i, i ^ 2 * m) for i in range(shots)])  4.65 us
    unnamed x17, local copies, waits for them, and re-layouts  3.84 us
    ppermute x16, waiting for transfers between devices, swap(): return (odd, lax.ppermute(even, 'slab', even_pairs))  3.63 us
    ppermute x3, starting transfers between devices, body(): lax.ppermute(pieces[m], 'shot', [(i, i ^ 2 * m) for i in range(shots)])  3.55 us
  transfers between devices with their start and end apart: 38, of which 10 were waited for; matrix products, arithmetic and copies ran while one was open for 1% of the time, Pallas kernels for 25%

profile of v6, /device:TPU:0, one launch (start us, length us, event | category | flops | bytes accessed | tf_op | source)
XLA Modules:
  0.0 125.8 jit_solution(6935460057593338877)
XLA Ops:
  2.8 5.9 %collective-permute-start.13 = (f32[4,128,128]{2,1,0:T(8,128)S(1)}, f32[4,128,128]{2,1,0:T(8,128)S(1)}, u32[]{:S(2)}, u32[]{:S(2)}) collective-permute-start(f32[4,128,128]{2,1,0:T(8,128)S(1)} %get-tuple-element.95), channel_id=1, source_target_pairs={{0,1},{1,0},{2,3},{3,2},{4,5},{5,4},{6,7},{7,6},{8,9},{9,8},{10,11... | collective-permute-start | bytes 786440 | tf_op jit(solution)/shard_map/ppermute | solution.py:407
  9.4 3.7 %collective-permute-start.3 = (f32[4,128,128]{2,1,0:T(8,128)S(1)}, f32[4,128,128]{2,1,0:T(8,128)S(1)}, u32[]{:S(2)}, u32[]{:S(2)}) collective-permute-start(f32[4,128,128]{2,1,0:T(8,128)S(1)} %get-tuple-element.77), channel_id=1, source_target_pairs={{0,1},{1,0},{2,3},{3,2},{4,5},{5,4},{6,7},{7,6},{8,9},{9,8},{10,11... | collective-permute-start | bytes 786440 | tf_op jit(solution)/shard_map/ppermute | solution.py:407
  14.4 1.6 %collective-permute-done.refs_1_ = f32[1,8,256]{2,1,0:T(8,128)S(1)} collective-permute-done((f32[1,8,256]{2,1,0:T(8,128)}, f32[1,8,256]{2,1,0:T(8,128)S(1)}, u32[]{:S(2)}, u32[]{:S(2)}) %collective-permute-start) | collective-permute-done | bytes 8224 | tf_op jit(solution)/shard_map/ppermute | solution.py:418
  16.7 1.9 %load.1 = (f32[16,128,128]{2,1,0:T(8,128)S(1)}, f32[16,128,128]{2,1,0:T(8,128)S(1)}, f32[16,128,128]{2,1,0:T(8,128)S(1)}, s32[1,1024]{1,0:T(1,128)S(1)}, f32[24584,128]{1,0:T(8,128)S(1)}) custom-call(s32[1,3,1024]{2,1,0:T(4,128)} %copy.17.listen_hbm, f32[16,128,128]{2,1,0:T(8,128)} %bitcast.12, f32[16,128,128]{2,1,0:T(8,128)} %bitcast.14, ...), custom_call_target="tpu_custom_call" | custom-call | flops 1000000000 | bytes 65536 | tf_op jit(solution)/shard_map/load/pallas_call | solution.py:360
  22.3 3.4 %collective-permute-start.15 = (f32[4,128,128]{2,1,0:T(8,128)S(1)}, f32[4,128,128]{2,1,0:T(8,128)S(1)}, u32[]{:S(2)}, u32[]{:S(2)}) collective-permute-start(f32[4,128,128]{2,1,0:T(8,128)S(1)} %get-tuple-element.99), channel_id=1, source_target_pairs={{0,1},{1,0},{2,3},{3,2},{4,5},{5,4},{6,7},{7,6},{8,9},{9,8},{10,11... | collective-permute-start | bytes 786440 | tf_op jit(solution)/shard_map/ppermute | solution.py:407
  25.7 1.5 %collective-permute-start.1 = (f32[2,8,256]{2,1,0:T(8,128)S(1)}, f32[2,8,256]{2,1,0:T(8,128)S(1)}, u32[]{:S(2)}, u32[]{:S(2)}) collective-permute-start(f32[2,8,256]{2,1,0:T(8,128)S(1)} %stack.1.refs_3_), channel_id=1, source_target_pairs={{0,2},{1,3},{2,0},{3,1},{4,6},{5,7},{6,4},{7,5},{8,10},{9,11},{10,... | collective-permute-start | bytes 49160 | tf_op jit(solution)/shard_map/ppermute | solution.py:418
  29.2 3.3 %collective-permute-start.5 = (f32[4,128,128]{2,1,0:T(8,128)S(1)}, f32[4,128,128]{2,1,0:T(8,128)S(1)}, u32[]{:S(2)}, u32[]{:S(2)}) collective-permute-start(f32[4,128,128]{2,1,0:T(8,128)S(1)} %get-tuple-element.82), channel_id=1, source_target_pairs={{0,1},{1,0},{2,3},{3,2},{4,5},{5,4},{6,7},{7,6},{8,9},{9,8},{10,11... | collective-permute-start | bytes 786440 | tf_op jit(solution)/shard_map/ppermute | solution.py:407
  34.4 3.7 %collective-permute-start.17 = (f32[4,128,128]{2,1,0:T(8,128)S(1)}, f32[4,128,128]{2,1,0:T(8,128)S(1)}, u32[]{:S(2)}, u32[]{:S(2)}) collective-permute-start(f32[4,128,128]{2,1,0:T(8,128)S(1)} %get-tuple-element.102), channel_id=1, source_target_pairs={{0,1},{1,0},{2,3},{3,2},{4,5},{5,4},{6,7},{7,6},{8,9},{9,8},{10,11... | collective-permute-start | bytes 786440 | tf_op jit(solution)/shard_map/ppermute | solution.py:407
  38.1 6.1 %receivers.1 = (f32[24584,128]{1,0:T(8,128)S(1)}, f32[16,128,128]{2,1,0:T(8,128)S(1)}) custom-call(s32[1,1024]{1,0:T(1,128)S(1)} %get-tuple-element.74.where_to, f32[1,8,256]{2,1,0:T(8,128)S(1)} %copy-done.6, f32[1,8,256]{2,1,0:T(8,128)S(1)} %collective-permute-done.refs_1_, ...), custom_call_target="tpu_custom_call", output_to_operand_aliasing={{1}: (4, {}), {0}: (5, {})} | custom-call | flops 2000000000 | bytes 131072 | tf_op jit(solution)/shard_map/receivers/pallas_call | solution.py:360
  44.2 1.5 %adjoint.8 = (f32[16,128,128]{2,1,0:T(8,128)S(1)}, f32[4,128,128]{2,1,0:T(8,128)S(1)}, f32[4,128,128]{2,1,0:T(8,128)S(1)}) custom-call(f32[16,128,128]{2,1,0:T(8,128)S(1)} %get-tuple-element.80.refs_0_.refs_1_.refs_9_, f32[16,128,128]{2,1,0:T(8,128)S(1)} %bitcast.8, f32[16,128,128]{2,1,0:T(8,128)S(1)} %get-tuple-element.75.refs_2_.refs_6_.speed, ...), custom_call_target="tpu_custom_call" | custom-call | flops 2000000000 | bytes 131072 | tf_op jit(solution)/shard_map/adjoint/pallas_call | solution.py:360
  46.4 1.7 %collective-permute-start.7 = (f32[4,128,128]{2,1,0:T(8,128)S(1)}, f32[4,128,128]{2,1,0:T(8,128)S(1)}, u32[]{:S(2)}, u32[]{:S(2)}) collective-permute-start(f32[4,128,128]{2,1,0:T(8,128)S(1)} %get-tuple-element.86), channel_id=1, source_target_pairs={{0,1},{1,0},{2,3},{3,2},{4,5},{5,4},{6,7},{7,6},{8,9},{9,8},{10,11... | collective-permute-start | bytes 786440 | tf_op jit(solution)/shard_map/ppermute | solution.py:407
  50.0 3.0 %collective-permute-start.19 = (f32[4,128,128]{2,1,0:T(8,128)S(1)}, f32[4,128,128]{2,1,0:T(8,128)S(1)}, u32[]{:S(2)}, u32[]{:S(2)}) collective-permute-start(f32[4,128,128]{2,1,0:T(8,128)S(1)} %get-tuple-element.105), channel_id=1, source_target_pairs={{0,1},{1,0},{2,3},{3,2},{4,5},{5,4},{6,7},{7,6},{8,9},{9,8},{10,11... | collective-permute-start | bytes 786440 | tf_op jit(solution)/shard_map/ppermute | solution.py:407
  53.0 1.5 %collective-permute-done.7.refs_4_ = f32[4,128,128]{2,1,0:T(8,128)S(1)} collective-permute-done((f32[4,128,128]{2,1,0:T(8,128)S(1)}, f32[4,128,128]{2,1,0:T(8,128)S(1)}, u32[]{:S(2)}, u32[]{:S(2)}) %collective-permute-start.7) | collective-permute-done | bytes 262176 | tf_op jit(solution)/shard_map/ppermute | solution.py:407
  56.6 3.5 %collective-permute-start.9 = (f32[4,128,128]{2,1,0:T(8,128)S(1)}, f32[4,128,128]{2,1,0:T(8,128)S(1)}, u32[]{:S(2)}, u32[]{:S(2)}) collective-permute-start(f32[4,128,128]{2,1,0:T(8,128)S(1)} %get-tuple-element.89), channel_id=1, source_target_pairs={{0,1},{1,0},{2,3},{3,2},{4,5},{5,4},{6,7},{7,6},{8,9},{9,8},{10,11... | collective-permute-start | bytes 786440 | tf_op jit(solution)/shard_map/ppermute | solution.py:407
  62.2 3.3 %collective-permute-start.21 = (f32[4,128,128]{2,1,0:T(8,128)S(1)}, f32[4,128,128]{2,1,0:T(8,128)S(1)}, u32[]{:S(2)}, u32[]{:S(2)}) collective-permute-start(f32[4,128,128]{2,1,0:T(8,128)S(1)} %get-tuple-element.109), channel_id=1, source_target_pairs={{0,1},{1,0},{2,3},{3,2},{4,5},{5,4},{6,7},{7,6},{8,9},{9,8},{10,11... | collective-permute-start | bytes 786440 | tf_op jit(solution)/shard_map/ppermute | solution.py:407
  67.6 3.9 %collective-permute-start.11 = (f32[4,128,128]{2,1,0:T(8,128)S(1)}, f32[4,128,128]{2,1,0:T(8,128)S(1)}, u32[]{:S(2)}, u32[]{:S(2)}) collective-permute-start(f32[4,128,128]{2,1,0:T(8,128)S(1)} %get-tuple-element.92), channel_id=1, source_target_pairs={{0,1},{1,0},{2,3},{3,2},{4,5},{5,4},{6,7},{7,6},{8,9},{9,8},{10,11... | collective-permute-start | bytes 786440 | tf_op jit(solution)/shard_map/ppermute | solution.py:407
  74.2 5.2 %collective-permute-start.25 = (f32[4,128,128]{2,1,0:T(8,128)S(1)}, f32[4,128,128]{2,1,0:T(8,128)S(1)}, u32[]{:S(2)}, u32[]{:S(2)}) collective-permute-start(f32[4,128,128]{2,1,0:T(8,128)S(1)} %get-tuple-element.117), channel_id=1, source_target_pairs={{0,1},{1,0},{2,3},{3,2},{4,5},{5,4},{6,7},{7,6},{8,9},{9,8},{10,11... | collective-permute-start | bytes 786440 | tf_op jit(solution)/shard_map/ppermute | solution.py:407
  79.4 1.4 %adjoint.11 = (f32[16,128,128]{2,1,0:T(8,128)S(1)}, f32[4,128,128]{2,1,0:T(8,128)S(1)}, f32[4,128,128]{2,1,0:T(8,128)S(1)}, f32[16,128,128]{2,1,0:T(8,128)S(1)}) custom-call(f32[16,128,128]{2,1,0:T(8,128)S(1)} %get-tuple-element.90.refs_0_.refs_1_, f32[16,128,128]{2,1,0:T(8,128)S(1)} %get-tuple-element.87.refs_0_.refs_9_.refs_1_, ...), custom_call_target="tpu_custom_call" | custom-call | flops 2000000000 | bytes 131072 | tf_op jit(solution)/shard_map/adjoint/pallas_call | solution.py:360
  81.5 3.1 %collective-permute-start.23 = (f32[4,128,128]{2,1,0:T(8,128)S(1)}, f32[4,128,128]{2,1,0:T(8,128)S(1)}, u32[]{:S(2)}, u32[]{:S(2)}) collective-permute-start(f32[4,128,128]{2,1,0:T(8,128)S(1)} %get-tuple-element.113), channel_id=1, source_target_pairs={{0,1},{1,0},{2,3},{3,2},{4,5},{5,4},{6,7},{7,6},{8,9},{9,8},{10,11... | collective-permute-start | bytes 786440 | tf_op jit(solution)/shard_map/ppermute | solution.py:407
  84.8 1.4 %forward.13 = (f32[16,128,128]{2,1,0:T(8,128)S(1)}, f32[4,128,128]{2,1,0:T(8,128)S(1)}, f32[4,128,128]{2,1,0:T(8,128)S(1)}, f32[16,128,128]{2,1,0:T(8,128)S(1)}) custom-call(f32[16,128,128]{2,1,0:T(8,128)S(1)} %get-tuple-element.115.refs_0_.refs_5_, f32[4,128,128]{2,1,0:T(8,128)S(1)} %collective-permute-done.24.refs_1_, ...), custom_call_target="tpu_custom_call" | custom-call | flops 2000000000 | bytes 131072 | tf_op jit(solution)/shard_map/forward/pallas_call | solution.py:360
  86.8 3.7 %collective-permute-start.29 = (f32[4,128,128]{2,1,0:T(8,128)S(1)}, f32[4,128,128]{2,1,0:T(8,128)S(1)}, u32[]{:S(2)}, u32[]{:S(2)}) collective-permute-start(f32[4,128,128]{2,1,0:T(8,128)S(1)} %get-tuple-element.126), channel_id=1, source_target_pairs={{0,1},{1,0},{2,3},{3,2},{4,5},{5,4},{6,7},{7,6},{8,9},{9,8},{10,11... | collective-permute-start | bytes 786440 | tf_op jit(solution)/shard_map/ppermute | solution.py:407
  91.6 1.4 %adjoint.12 = (f32[16,128,128]{2,1,0:T(8,128)S(1)}, f32[4,128,128]{2,1,0:T(8,128)S(1)}, f32[4,128,128]{2,1,0:T(8,128)S(1)}, f32[16,128,128]{2,1,0:T(8,128)S(1)}) custom-call(f32[16,128,128]{2,1,0:T(8,128)S(1)} %get-tuple-element.111.refs_0_.refs_1_, f32[16,128,128]{2,1,0:T(8,128)S(1)} %get-tuple-element.90.refs_0_.refs_1_, ...), custom_call_target="tpu_custom_call" | custom-call | flops 2000000000 | bytes 131072 | tf_op jit(solution)/shard_map/adjoint/pallas_call | solution.py:360
  93.7 3.6 %collective-permute-start.27 = (f32[4,128,128]{2,1,0:T(8,128)S(1)}, f32[4,128,128]{2,1,0:T(8,128)S(1)}, u32[]{:S(2)}, u32[]{:S(2)}) collective-permute-start(f32[4,128,128]{2,1,0:T(8,128)S(1)} %get-tuple-element.122), channel_id=1, source_target_pairs={{0,1},{1,0},{2,3},{3,2},{4,5},{5,4},{6,7},{7,6},{8,9},{9,8},{10,11... | collective-permute-start | bytes 786440 | tf_op jit(solution)/shard_map/ppermute | solution.py:407
  99.3 5.1 %collective-permute-start.33 = (f32[4,128,128]{2,1,0:T(8,128)S(1)}, f32[4,128,128]{2,1,0:T(8,128)S(1)}, u32[]{:S(2)}, u32[]{:S(2)}) collective-permute-start(f32[4,128,128]{2,1,0:T(8,128)S(1)} %get-tuple-element.136), channel_id=1, source_target_pairs={{0,1},{1,0},{2,3},{3,2},{4,5},{5,4},{6,7},{7,6},{8,9},{9,8},{10,11... | collective-permute-start | bytes 786440 | tf_op jit(solution)/shard_map/ppermute | solution.py:407
  104.4 1.8 %adjoint.13 = (f32[16,128,128]{2,1,0:T(8,128)S(1)}, f32[4,128,128]{2,1,0:T(8,128)S(1)}, f32[4,128,128]{2,1,0:T(8,128)S(1)}, f32[16,128,128]{2,1,0:T(8,128)S(1)}) custom-call(f32[16,128,128]{2,1,0:T(8,128)S(1)} %get-tuple-element.120.refs_0_.later, f32[16,128,128]{2,1,0:T(8,128)S(1)} %get-tuple-element.111.refs_0_.refs_1_, ...), custom_call_target="tpu_custom_call" | custom-call | flops 2000000000 | bytes 131072 | tf_op jit(solution)/shard_map/adjoint/pallas_call | solution.py:360
  106.9 5.0 %collective-permute-start.31 = (f32[4,128,128]{2,1,0:T(8,128)S(1)}, f32[4,128,128]{2,1,0:T(8,128)S(1)}, u32[]{:S(2)}, u32[]{:S(2)}) collective-permute-start(f32[4,128,128]{2,1,0:T(8,128)S(1)} %get-tuple-element.131), channel_id=1, source_target_pairs={{0,1},{1,0},{2,3},{3,2},{4,5},{5,4},{6,7},{7,6},{8,9},{9,8},{10,11... | collective-permute-start | bytes 786440 | tf_op jit(solution)/shard_map/ppermute | solution.py:407
  112.0 1.4 %forward.15 = (f32[4,16,16,128]{3,2,1,0:T(8,128)S(1)}, f32[4,16,16,128]{3,2,1,0:T(8,128)S(1)}) custom-call(f32[16,128,128]{2,1,0:T(8,128)S(1)} %get-tuple-element.134.refs_0_, f32[4,128,128]{2,1,0:T(8,128)S(1)} %collective-permute-done.32.refs_1_, f32[4,128,128]{2,1,0:T(8,128)S(1)} %collective-permute-done.33.refs_2_, bf16[256,256]{1,0:T(8,128)(2,1)S(1)} %copy-done.3, ...), custom_call_target="tpu_custom_call" | custom-call | tf_op jit(solution)/shard_map/forward/pallas_call | solution.py:360
  113.5 1.5 %last_inner.1 = (f32[16,128,128]{2,1,0:T(8,128)}, f32[16,128,128]{2,1,0:T(8,128)}) custom-call(f32[16,128,128]{2,1,0:T(8,128)S(1)} %get-tuple-element.129.cur.refs_7_, f32[16,128,128]{2,1,0:T(8,128)S(1)} %get-tuple-element.120.refs_0_.later, f32[16,128,128]{2,1,0:T(8,128)S(1)} %get-tuple-element.75.refs_2_.refs_6_.speed, ...), custom_call_target="tpu_custom_call" | custom-call | flops 30000001024 | bytes 1966080 | tf_op jit(solution)/shard_map/last_inner/pallas_call | solution.py:360
  115.5 1.6 %collective-permute-start.35 = (f32[16,16,128]{2,1,0:T(8,128)S(1)}, f32[16,16,128]{2,1,0:T(8,128)S(1)}, u32[]{:S(2)}, u32[]{:S(2)}) collective-permute-start(f32[16,16,128]{2,1,0:T(8,128)S(1)} %get-tuple-element.142), channel_id=1, source_target_pairs={{0,8},{4,12},{8,0},{12,4},{16,24},{20,28},{24,16},{28,20},{1,9},{5... | collective-permute-start | bytes 393224 | tf_op jit(solution)/shard_map/ppermute | solution.py:503
  117.0 1.6 %collective-permute-start.36 = (f32[16,16,128]{2,1,0:T(8,128)S(1)}, f32[16,16,128]{2,1,0:T(8,128)S(1)}, u32[]{:S(2)}, u32[]{:S(2)}) collective-permute-start(f32[16,16,128]{2,1,0:T(8,128)S(1)} %get-tuple-element.143), channel_id=1, source_target_pairs={{0,16},{4,20},{8,24},{12,28},{16,0},{20,4},{24,8},{28,12},{1,17},{... | collective-permute-start | bytes 393224 | tf_op jit(solution)/shard_map/ppermute | solution.py:503
  119.0 1.4 %last_border.1 = f32[16,128,128]{2,1,0:T(8,128)} custom-call(f32[16,128,128]{2,1,0:T(8,128)S(1)} %get-tuple-element.129.cur.refs_7_, f32[16,128,128]{2,1,0:T(8,128)S(1)} %get-tuple-element.120.refs_0_.later, f32[16,128,128]{2,1,0:T(8,128)S(1)} %get-tuple-element.75.refs_2_.refs_6_.speed, ...), custom_call_target="tpu_custom_call", output_to_operand_aliasing={{}: (8, {})} | custom-call | flops 30000001024 | bytes 1966080 | tf_op jit(solution)/shard_map/last_border/pallas_call | solution.py:360
  121.4 3.7 %collective-permute-done.36.refs_2_ = f32[16,16,128]{2,1,0:T(8,128)S(1)} collective-permute-done((f32[16,16,128]{2,1,0:T(8,128)S(1)}, f32[16,16,128]{2,1,0:T(8,128)S(1)}, u32[]{:S(2)}, u32[]{:S(2)}) %collective-permute-start.36) | collective-permute-done | bytes 131104 | tf_op jit(solution)/shard_map/ppermute | solution.py:503
  (84 shorter events, 32.2 us)
Async XLA Ops:
  2.1 16.6 %collective-permute-start.12 = (f32[4,128,128]{2,1,0:T(8,128)S(1)}, f32[4,128,128]{2,1,0:T(8,128)S(1)}, u32[]{:S(2)}, u32[]{:S(2)}) collective-permute-start(f32[4,128,128]{2,1,0:T(8,128)S(1)} %get-tuple-element.94), channel_id=1, source_target_pairs={{1,2},{2,1},{5,6},{6,5},{9,10},{10,9},{13,14},{14,13},{17,18},{18,... | collective-permute-start | bytes 786440 | tf_op jit(solution)/shard_map/ppermute | solution.py:406
  2.8 15.9 %collective-permute-start.13 = (f32[4,128,128]{2,1,0:T(8,128)S(1)}, f32[4,128,128]{2,1,0:T(8,128)S(1)}, u32[]{:S(2)}, u32[]{:S(2)}) collective-permute-start(f32[4,128,128]{2,1,0:T(8,128)S(1)} %get-tuple-element.95), channel_id=1, source_target_pairs={{0,1},{1,0},{2,3},{3,2},{4,5},{5,4},{6,7},{7,6},{8,9},{9,8},{10,11... | collective-permute-start | bytes 786440 | tf_op jit(solution)/shard_map/ppermute | solution.py:407
  8.7 18.5 %collective-permute-start.2 = (f32[4,128,128]{2,1,0:T(8,128)S(1)}, f32[4,128,128]{2,1,0:T(8,128)S(1)}, u32[]{:S(2)}, u32[]{:S(2)}) collective-permute-start(f32[4,128,128]{2,1,0:T(8,128)S(1)} %get-tuple-element.76), channel_id=1, source_target_pairs={{1,2},{2,1},{5,6},{6,5},{9,10},{10,9},{13,14},{14,13},{17,18},{18,... | collective-permute-start | bytes 786440 | tf_op jit(solution)/shard_map/ppermute | solution.py:406
  9.4 17.8 %collective-permute-start.3 = (f32[4,128,128]{2,1,0:T(8,128)S(1)}, f32[4,128,128]{2,1,0:T(8,128)S(1)}, u32[]{:S(2)}, u32[]{:S(2)}) collective-permute-start(f32[4,128,128]{2,1,0:T(8,128)S(1)} %get-tuple-element.77), channel_id=1, source_target_pairs={{0,1},{1,0},{2,3},{3,2},{4,5},{5,4},{6,7},{7,6},{8,9},{9,8},{10,11... | collective-permute-start | bytes 786440 | tf_op jit(solution)/shard_map/ppermute | solution.py:407
  21.6 10.9 %collective-permute-start.14 = (f32[4,128,128]{2,1,0:T(8,128)S(1)}, f32[4,128,128]{2,1,0:T(8,128)S(1)}, u32[]{:S(2)}, u32[]{:S(2)}) collective-permute-start(f32[4,128,128]{2,1,0:T(8,128)S(1)} %get-tuple-element.98), channel_id=1, source_target_pairs={{1,2},{2,1},{5,6},{6,5},{9,10},{10,9},{13,14},{14,13},{17,18},{18,... | collective-permute-start | bytes 786440 | tf_op jit(solution)/shard_map/ppermute | solution.py:406
  22.3 10.2 %collective-permute-start.15 = (f32[4,128,128]{2,1,0:T(8,128)S(1)}, f32[4,128,128]{2,1,0:T(8,128)S(1)}, u32[]{:S(2)}, u32[]{:S(2)}) collective-permute-start(f32[4,128,128]{2,1,0:T(8,128)S(1)} %get-tuple-element.99), channel_id=1, source_target_pairs={{0,1},{1,0},{2,3},{3,2},{4,5},{5,4},{6,7},{7,6},{8,9},{9,8},{10,11... | collective-permute-start | bytes 786440 | tf_op jit(solution)/shard_map/ppermute | solution.py:407
  25.7 12.4 %collective-permute-start.1 = (f32[2,8,256]{2,1,0:T(8,128)S(1)}, f32[2,8,256]{2,1,0:T(8,128)S(1)}, u32[]{:S(2)}, u32[]{:S(2)}) collective-permute-start(f32[2,8,256]{2,1,0:T(8,128)S(1)} %stack.1.refs_3_), channel_id=1, source_target_pairs={{0,2},{1,3},{2,0},{3,1},{4,6},{5,7},{6,4},{7,5},{8,10},{9,11},{10,... | collective-permute-start | bytes 49160 | tf_op jit(solution)/shard_map/ppermute | solution.py:418
  28.6 15.6 %collective-permute-start.4 = (f32[4,128,128]{2,1,0:T(8,128)S(1)}, f32[4,128,128]{2,1,0:T(8,128)S(1)}, u32[]{:S(2)}, u32[]{:S(2)}) collective-permute-start(f32[4,128,128]{2,1,0:T(8,128)S(1)} %get-tuple-element.81), channel_id=1, source_target_pairs={{1,2},{2,1},{5,6},{6,5},{9,10},{10,9},{13,14},{14,13},{17,18},{18,... | collective-permute-start | bytes 786440 | tf_op jit(solution)/shard_map/ppermute | solution.py:406
  29.2 15.0 %collective-permute-start.5 = (f32[4,128,128]{2,1,0:T(8,128)S(1)}, f32[4,128,128]{2,1,0:T(8,128)S(1)}, u32[]{:S(2)}, u32[]{:S(2)}) collective-permute-start(f32[4,128,128]{2,1,0:T(8,128)S(1)} %get-tuple-element.82), channel_id=1, source_target_pairs={{0,1},{1,0},{2,3},{3,2},{4,5},{5,4},{6,7},{7,6},{8,9},{9,8},{10,11... | collective-permute-start | bytes 786440 | tf_op jit(solution)/shard_map/ppermute | solution.py:407
  33.7 14.4 %collective-permute-start.16 = (f32[4,128,128]{2,1,0:T(8,128)S(1)}, f32[4,128,128]{2,1,0:T(8,128)S(1)}, u32[]{:S(2)}, u32[]{:S(2)}) collective-permute-start(f32[4,128,128]{2,1,0:T(8,128)S(1)} %get-tuple-element.101), channel_id=1, source_target_pairs={{1,2},{2,1},{5,6},{6,5},{9,10},{10,9},{13,14},{14,13},{17,18},{18,... | collective-permute-start | bytes 786440 | tf_op jit(solution)/shard_map/ppermute | solution.py:406
  34.4 13.7 %collective-permute-start.17 = (f32[4,128,128]{2,1,0:T(8,128)S(1)}, f32[4,128,128]{2,1,0:T(8,128)S(1)}, u32[]{:S(2)}, u32[]{:S(2)}) collective-permute-start(f32[4,128,128]{2,1,0:T(8,128)S(1)} %get-tuple-element.102), channel_id=1, source_target_pairs={{0,1},{1,0},{2,3},{3,2},{4,5},{5,4},{6,7},{7,6},{8,9},{9,8},{10,11... | collective-permute-start | bytes 786440 | tf_op jit(solution)/shard_map/ppermute | solution.py:407
  46.4 8.1 %collective-permute-start.7 = (f32[4,128,128]{2,1,0:T(8,128)S(1)}, f32[4,128,128]{2,1,0:T(8,128)S(1)}, u32[]{:S(2)}, u32[]{:S(2)}) collective-permute-start(f32[4,128,128]{2,1,0:T(8,128)S(1)} %get-tuple-element.86), channel_id=1, source_target_pairs={{0,1},{1,0},{2,3},{3,2},{4,5},{5,4},{6,7},{7,6},{8,9},{9,8},{10,11... | collective-permute-start | bytes 786440 | tf_op jit(solution)/shard_map/ppermute | solution.py:407
  49.3 10.8 %collective-permute-start.18 = (f32[4,128,128]{2,1,0:T(8,128)S(1)}, f32[4,128,128]{2,1,0:T(8,128)S(1)}, u32[]{:S(2)}, u32[]{:S(2)}) collective-permute-start(f32[4,128,128]{2,1,0:T(8,128)S(1)} %get-tuple-element.104), channel_id=1, source_target_pairs={{1,2},{2,1},{5,6},{6,5},{9,10},{10,9},{13,14},{14,13},{17,18},{18,... | collective-permute-start | bytes 786440 | tf_op jit(solution)/shard_map/ppermute | solution.py:406
  50.0 10.2 %collective-permute-start.19 = (f32[4,128,128]{2,1,0:T(8,128)S(1)}, f32[4,128,128]{2,1,0:T(8,128)S(1)}, u32[]{:S(2)}, u32[]{:S(2)}) collective-permute-start(f32[4,128,128]{2,1,0:T(8,128)S(1)} %get-tuple-element.105), channel_id=1, source_target_pairs={{0,1},{1,0},{2,3},{3,2},{4,5},{5,4},{6,7},{7,6},{8,9},{9,8},{10,11... | collective-permute-start | bytes 786440 | tf_op jit(solution)/shard_map/ppermute | solution.py:407
  55.9 9.6 %collective-permute-start.8 = (f32[4,128,128]{2,1,0:T(8,128)S(1)}, f32[4,128,128]{2,1,0:T(8,128)S(1)}, u32[]{:S(2)}, u32[]{:S(2)}) collective-permute-start(f32[4,128,128]{2,1,0:T(8,128)S(1)} %get-tuple-element.88), channel_id=1, source_target_pairs={{1,2},{2,1},{5,6},{6,5},{9,10},{10,9},{13,14},{14,13},{17,18},{18,... | collective-permute-start | bytes 786440 | tf_op jit(solution)/shard_map/ppermute | solution.py:406
  56.6 9.0 %collective-permute-start.9 = (f32[4,128,128]{2,1,0:T(8,128)S(1)}, f32[4,128,128]{2,1,0:T(8,128)S(1)}, u32[]{:S(2)}, u32[]{:S(2)}) collective-permute-start(f32[4,128,128]{2,1,0:T(8,128)S(1)} %get-tuple-element.89), channel_id=1, source_target_pairs={{0,1},{1,0},{2,3},{3,2},{4,5},{5,4},{6,7},{7,6},{8,9},{9,8},{10,11... | collective-permute-start | bytes 786440 | tf_op jit(solution)/shard_map/ppermute | solution.py:407
  61.5 10.0 %collective-permute-start.20 = (f32[4,128,128]{2,1,0:T(8,128)S(1)}, f32[4,128,128]{2,1,0:T(8,128)S(1)}, u32[]{:S(2)}, u32[]{:S(2)}) collective-permute-start(f32[4,128,128]{2,1,0:T(8,128)S(1)} %get-tuple-element.108), channel_id=1, source_target_pairs={{1,2},{2,1},{5,6},{6,5},{9,10},{10,9},{13,14},{14,13},{17,18},{18,... | collective-permute-start | bytes 786440 | tf_op jit(solution)/shard_map/ppermute | solution.py:406
  62.2 10.1 %collective-permute-start.21 = (f32[4,128,128]{2,1,0:T(8,128)S(1)}, f32[4,128,128]{2,1,0:T(8,128)S(1)}, u32[]{:S(2)}, u32[]{:S(2)}) collective-permute-start(f32[4,128,128]{2,1,0:T(8,128)S(1)} %get-tuple-element.109), channel_id=1, source_target_pairs={{0,1},{1,0},{2,3},{3,2},{4,5},{5,4},{6,7},{7,6},{8,9},{9,8},{10,11... | collective-permute-start | bytes 786440 | tf_op jit(solution)/shard_map/ppermute | solution.py:407
  66.9 12.5 %collective-permute-start.10 = (f32[4,128,128]{2,1,0:T(8,128)S(1)}, f32[4,128,128]{2,1,0:T(8,128)S(1)}, u32[]{:S(2)}, u32[]{:S(2)}) collective-permute-start(f32[4,128,128]{2,1,0:T(8,128)S(1)} %get-tuple-element.91), channel_id=1, source_target_pairs={{1,2},{2,1},{5,6},{6,5},{9,10},{10,9},{13,14},{14,13},{17,18},{18,... | collective-permute-start | bytes 786440 | tf_op jit(solution)/shard_map/ppermute | solution.py:406
  67.6 11.8 %collective-permute-start.11 = (f32[4,128,128]{2,1,0:T(8,128)S(1)}, f32[4,128,128]{2,1,0:T(8,128)S(1)}, u32[]{:S(2)}, u32[]{:S(2)}) collective-permute-start(f32[4,128,128]{2,1,0:T(8,128)S(1)} %get-tuple-element.92), channel_id=1, source_target_pairs={{0,1},{1,0},{2,3},{3,2},{4,5},{5,4},{6,7},{7,6},{8,9},{9,8},{10,11... | collective-permute-start | bytes 786440 | tf_op jit(solution)/shard_map/ppermute | solution.py:407
  73.5 11.1 %collective-permute-start.24 = (f32[4,128,128]{2,1,0:T(8,128)S(1)}, f32[4,128,128]{2,1,0:T(8,128)S(1)}, u32[]{:S(2)}, u32[]{:S(2)}) collective-permute-start(f32[4,128,128]{2,1,0:T(8,128)S(1)} %get-tuple-element.116), channel_id=1, source_target_pairs={{1,2},{2,1},{5,6},{6,5},{9,10},{10,9},{13,14},{14,13},{17,18},{18,... | collective-permute-start | bytes 786440 | tf_op jit(solution)/shard_map/ppermute | solution.py:406
  74.2 10.6 %collective-permute-start.25 = (f32[4,128,128]{2,1,0:T(8,128)S(1)}, f32[4,128,128]{2,1,0:T(8,128)S(1)}, u32[]{:S(2)}, u32[]{:S(2)}) collective-permute-start(f32[4,128,128]{2,1,0:T(8,128)S(1)} %get-tuple-element.117), channel_id=1, source_target_pairs={{0,1},{1,0},{2,3},{3,2},{4,5},{5,4},{6,7},{7,6},{8,9},{9,8},{10,11... | collective-permute-start | bytes 786440 | tf_op jit(solution)/shard_map/ppermute | solution.py:407
  80.8 9.7 %collective-permute-start.22 = (f32[4,128,128]{2,1,0:T(8,128)S(1)}, f32[4,128,128]{2,1,0:T(8,128)S(1)}, u32[]{:S(2)}, u32[]{:S(2)}) collective-permute-start(f32[4,128,128]{2,1,0:T(8,128)S(1)} %get-tuple-element.112), channel_id=1, source_target_pairs={{1,2},{2,1},{5,6},{6,5},{9,10},{10,9},{13,14},{14,13},{17,18},{18,... | collective-permute-start | bytes 786440 | tf_op jit(solution)/shard_map/ppermute | solution.py:406
  81.5 10.1 %collective-permute-start.23 = (f32[4,128,128]{2,1,0:T(8,128)S(1)}, f32[4,128,128]{2,1,0:T(8,128)S(1)}, u32[]{:S(2)}, u32[]{:S(2)}) collective-permute-start(f32[4,128,128]{2,1,0:T(8,128)S(1)} %get-tuple-element.113), channel_id=1, source_target_pairs={{0,1},{1,0},{2,3},{3,2},{4,5},{5,4},{6,7},{7,6},{8,9},{9,8},{10,11... | collective-permute-start | bytes 786440 | tf_op jit(solution)/shard_map/ppermute | solution.py:407
  86.2 11.1 %collective-permute-start.28 = (f32[4,128,128]{2,1,0:T(8,128)S(1)}, f32[4,128,128]{2,1,0:T(8,128)S(1)}, u32[]{:S(2)}, u32[]{:S(2)}) collective-permute-start(f32[4,128,128]{2,1,0:T(8,128)S(1)} %get-tuple-element.125), channel_id=1, source_target_pairs={{1,2},{2,1},{5,6},{6,5},{9,10},{10,9},{13,14},{14,13},{17,18},{18,... | collective-permute-start | bytes 786440 | tf_op jit(solution)/shard_map/ppermute | solution.py:406
  86.8 10.5 %collective-permute-start.29 = (f32[4,128,128]{2,1,0:T(8,128)S(1)}, f32[4,128,128]{2,1,0:T(8,128)S(1)}, u32[]{:S(2)}, u32[]{:S(2)}) collective-permute-start(f32[4,128,128]{2,1,0:T(8,128)S(1)} %get-tuple-element.126), channel_id=1, source_target_pairs={{0,1},{1,0},{2,3},{3,2},{4,5},{5,4},{6,7},{7,6},{8,9},{9,8},{10,11... | collective-permute-start | bytes 786440 | tf_op jit(solution)/shard_map/ppermute | solution.py:407
  93.0 11.4 %collective-permute-start.26 = (f32[4,128,128]{2,1,0:T(8,128)S(1)}, f32[4,128,128]{2,1,0:T(8,128)S(1)}, u32[]{:S(2)}, u32[]{:S(2)}) collective-permute-start(f32[4,128,128]{2,1,0:T(8,128)S(1)} %get-tuple-element.121), channel_id=1, source_target_pairs={{1,2},{2,1},{5,6},{6,5},{9,10},{10,9},{13,14},{14,13},{17,18},{18,... | collective-permute-start | bytes 786440 | tf_op jit(solution)/shard_map/ppermute | solution.py:406
  93.7 10.7 %collective-permute-start.27 = (f32[4,128,128]{2,1,0:T(8,128)S(1)}, f32[4,128,128]{2,1,0:T(8,128)S(1)}, u32[]{:S(2)}, u32[]{:S(2)}) collective-permute-start(f32[4,128,128]{2,1,0:T(8,128)S(1)} %get-tuple-element.122), channel_id=1, source_target_pairs={{0,1},{1,0},{2,3},{3,2},{4,5},{5,4},{6,7},{7,6},{8,9},{9,8},{10,11... | collective-permute-start | bytes 786440 | tf_op jit(solution)/shard_map/ppermute | solution.py:407
  98.6 13.3 %collective-permute-start.32 = (f32[4,128,128]{2,1,0:T(8,128)S(1)}, f32[4,128,128]{2,1,0:T(8,128)S(1)}, u32[]{:S(2)}, u32[]{:S(2)}) collective-permute-start(f32[4,128,128]{2,1,0:T(8,128)S(1)} %get-tuple-element.135), channel_id=1, source_target_pairs={{1,2},{2,1},{5,6},{6,5},{9,10},{10,9},{13,14},{14,13},{17,18},{18,... | collective-permute-start | bytes 786440 | tf_op jit(solution)/shard_map/ppermute | solution.py:406
  99.3 12.6 %collective-permute-start.33 = (f32[4,128,128]{2,1,0:T(8,128)S(1)}, f32[4,128,128]{2,1,0:T(8,128)S(1)}, u32[]{:S(2)}, u32[]{:S(2)}) collective-permute-start(f32[4,128,128]{2,1,0:T(8,128)S(1)} %get-tuple-element.136), channel_id=1, source_target_pairs={{0,1},{1,0},{2,3},{3,2},{4,5},{5,4},{6,7},{7,6},{8,9},{9,8},{10,11... | collective-permute-start | bytes 786440 | tf_op jit(solution)/shard_map/ppermute | solution.py:407
  106.2 12.8 %collective-permute-start.30 = (f32[4,128,128]{2,1,0:T(8,128)S(1)}, f32[4,128,128]{2,1,0:T(8,128)S(1)}, u32[]{:S(2)}, u32[]{:S(2)}) collective-permute-start(f32[4,128,128]{2,1,0:T(8,128)S(1)} %get-tuple-element.130), channel_id=1, source_target_pairs={{1,2},{2,1},{5,6},{6,5},{9,10},{10,9},{13,14},{14,13},{17,18},{18,... | collective-permute-start | bytes 786440 | tf_op jit(solution)/shard_map/ppermute | solution.py:406
  106.9 12.1 %collective-permute-start.31 = (f32[4,128,128]{2,1,0:T(8,128)S(1)}, f32[4,128,128]{2,1,0:T(8,128)S(1)}, u32[]{:S(2)}, u32[]{:S(2)}) collective-permute-start(f32[4,128,128]{2,1,0:T(8,128)S(1)} %get-tuple-element.131), channel_id=1, source_target_pairs={{0,1},{1,0},{2,3},{3,2},{4,5},{5,4},{6,7},{7,6},{8,9},{9,8},{10,11... | collective-permute-start | bytes 786440 | tf_op jit(solution)/shard_map/ppermute | solution.py:407
  (14 other events, 167.4 us)

commit v7 on v3

--- a/solution.py
+++ b/solution.py
@@ -55,14 +55,16 @@
         halo[reach:] = odd[...]
 
 
-def emit_edge(upper, outer, out):
-    @pl.when(upper)
+def emit_edges(parity, outer, even, odd):
+    @pl.when(parity == 0)
     def _():
-        out[...] = outer[reach:]
-
-    @pl.when(jnp.logical_not(upper))
+        even[...] = outer[reach:]
+        odd[...] = outer[:reach]
+
+    @pl.when(parity != 0)
     def _():
-        out[...] = outer[:reach]
+        even[...] = outer[:reach]
+        odd[...] = outer[reach:]
 
 
 def rows_of(count, border):
@@ -119,11 +121,14 @@
     late = next(it) if adds else None
     acc_in = next(it) if adds and not opens else None
     first, lap_first = (next(it), next(it)) if not moves else (None, None)
+    total_inner = next(it) if border and not moves else None
+    if parts["after"]:
+        next(it)
     nxt = next(it) if moves else None
-    edge_out = next(it) if moves or not border else None
+    even_out, odd_out = (next(it), next(it)) if moves and border else (None, None)
     lap_out = next(it) if stores else None
     acc_out = next(it) if adds and moves else None
-    send, keep = (next(it), next(it)) if not moves else (None, None)
+    send, keep = (next(it), next(it)) if border and not moves else (None, None)
     halo = next(it) if border else None
     if moves:
         spot_smem, wave_smem, spot_sem, wave_sem = [next(it) for _ in range(4)]
@@ -137,8 +142,6 @@
     count = inner.shape[0] + 2 * reach
     if border:
         fill_halo(parity, even, odd, halo)
-    else:
-        emit_edge(parity != 0, outer, edge_out)
 
     def put(i, x, v, lap):
         if moves:
@@ -177,15 +180,18 @@
             nxt[place, tile, :] = nxt[place, tile, :] + added
 
         if border:
-            emit_edge(parity == 0, nxt, edge_out)
-    else:
+            emit_edges(parity, nxt, even_out, odd_out)
+    elif border:
         chunk = send.shape[2]
         mine = lax.axis_index("shot") % 2
         for j in range(send.shape[0]):
             away = pl.multiple_of((2 * j + 1 - mine) * chunk, 8)
             here = pl.multiple_of((2 * j + mine) * chunk, 8)
-            send[j] = total[:, pl.ds(away, chunk), :]
-            keep[j] = total[:, pl.ds(here, chunk), :]
+            for out, first_row in ((send, away), (keep, here)):
+                rows = pl.ds(first_row, chunk)
+                out[j, :reach] = total[:reach, rows, :]
+                out[j, reach : count - reach] = total_inner[:, rows, :]
+                out[j, count - reach :] = total[reach:, rows, :]
 
 
 def part_copies(border, part, whole, sems, to_whole):
@@ -202,39 +208,47 @@
     return copies
 
 
+def injected(tiles, x, time, width_y):
+    return tiles[pl.ds((x + reach) * width_y * 8 + time, width_y, stride=8), :]
+
+
 def adjoint_kernel(parts, *refs):
     it = iter(refs)
     border, adds, last = parts["border"], parts["adds"], parts["last"]
     inner, outer = next(it), next(it)
     even, odd = (next(it), next(it)) if border else (None, None)
-    right, left, later, speed, inject = [next(it) for _ in range(5)]
+    right, left, later, speed = [next(it) for _ in range(4)]
+    inject = next(it) if parts["injects"] else None
     lap_of, acc_in = (next(it), next(it)) if adds else (None, None)
     if last and border:
         next(it)
+    if parts["after"]:
+        next(it)
     nxt = next(it)
     second = next(it) if last and not border else None
-    edge_out = next(it) if parts["sends"] else None
+    even_out, odd_out = (next(it), next(it)) if border and not last else (None, None)
     acc_out = next(it) if adds else None
     halo = next(it) if border else None
     part, copies = nxt, []
     if last:
         part, sems = next(it), next(it)
     parity = lax.axis_index("slab") % 2
-    width_y = inner.shape[1]
+    count, width_y = inner.shape[0] + 2 * reach, inner.shape[1]
     if border:
         fill_halo(parity, even, odd, halo)
-    else:
-        if parts["sends"]:
-            emit_edge(parity != 0, outer, edge_out)
-        if last:
-            copies += part_copies(True, outer, second, sems.at[pl.ds(2, 2)], True)
-            copies += part_copies(False, inner, second, sems.at[pl.ds(4, 1)], True)
-            for copy in copies:
-                copy.start()
+        if parts["late"]:
+            for i in range(2 * reach):
+                x = i - reach if i < reach else count + i - reach
+                halo[i] = halo[i] + injected(inject, x, parts["time"] + 1, width_y)
+    elif last:
+        copies += part_copies(True, outer, second, sems.at[pl.ds(2, 2)], True)
+        copies += part_copies(False, inner, second, sems.at[pl.ds(4, 1)], True)
+        for copy in copies:
+            copy.start()
 
     def put(i, x, v, lap):
-        added = inject[pl.ds(x * width_y * 8 + parts["time"], width_y, stride=8), :]
-        part[i] = 2.0 * v - later[i] + speed[x] * lap + added
+        value = 2.0 * v - later[i] + speed[x] * lap
+        part[i] = value + injected(inject, x, parts["time"], width_y) if parts["injects"] else value
         if adds:
             acc_out[i] = acc_in[i] + v * lap_of[i]
 
@@ -244,42 +258,41 @@
             copy.start()
             copies.append(copy)
     elif border:
-        emit_edge(parity == 0, part, edge_out)
+        emit_edges(parity, part, even_out, odd_out)
     for copy in copies:
         copy.wait()
 
 
 def edges_kernel(*refs):
-    fields, outs, sems = refs[:2], refs[2:4], refs[4]
+    fields, outs, sems = refs[:2], refs[2:6], refs[6]
     parity = lax.axis_index("slab") % 2
     top = fields[0].shape[0] - reach
-    rows = pl.ds(top * (1 - parity), reach)
-    copies = [pltpu.make_async_copy(fields[i].at[rows], outs[i], sems.at[i]) for i in range(2)]
-    for copy in copies:
-        copy.start()
+    starts = (top * (1 - parity), top * parity)
+    copies = []
+    for i in range(4):
+        rows = pl.ds(starts[i % 2], reach)
+        copies.append(pltpu.make_async_copy(fields[i // 2].at[rows], outs[i], sems.at[i]))
+        copies[-1].start()
     for copy in copies:
         copy.wait()
 
 
-def load_kernel(listen, *refs):
-    fields, speed, refs = refs[:4], refs[4], refs[5:]
-    parts, speed_out, where_to, tiles, edge, sems = refs[:8], *refs[8:13]
-    top = fields[3].shape[0] - reach
-    rows = pl.ds(top * (lax.axis_index("slab") % 2), reach)
-    copies = [
-        pltpu.make_async_copy(speed, speed_out, sems.at[12]),
-        pltpu.make_async_copy(fields[3].at[rows], edge, sems.at[13]),
-    ]
-    for i in range(4):
+def stack_kernel(*refs):
+    first = 0
+    for ref in refs[:-1]:
+        refs[-1][first : first + ref.shape[0]] = ref[...]
+        first += ref.shape[0]
+
+
+def load_kernel(listen_hbm, *refs):
+    fields, parts, speed, where_to, tiles, listen, sems = refs[:3], refs[4:8], *refs[8:]
+    listen_copy = pltpu.make_async_copy(listen_hbm.at[0], listen, sems.at[7])
+    copies = [listen_copy, pltpu.make_async_copy(fields[2], speed, sems.at[6])]
+    for i in range(2):
         copies += part_copies(False, parts[2 * i], fields[i], sems.at[pl.ds(3 * i, 1)], False)
         copies += part_copies(True, parts[2 * i + 1], fields[i], sems.at[pl.ds(3 * i + 1, 2)], False)
     for copy in copies:
         copy.start()
-    count, width_y, width_z = fields[0].shape
-    depth = listen[0:1, :] - lax.axis_index("slab") * count
-    inside = (depth >= 0) & (depth < count)
-    flat = depth * (width_y * width_z) + listen[1:2, :] * width_z + listen[2:3, :]
-    where_to[...] = jnp.where(inside, flat, count * width_y * width_z)
     zero_rows = 64 * 8
 
     @pl.loop(0, tiles.shape[0] // zero_rows)
@@ -293,12 +306,31 @@
         tiles[tiles.shape[0] - rest :, :] = jnp.zeros((rest, 128), jnp.float32)
     for copy in copies:
         copy.wait()
-
-
-def scatter_kernel(where_to, *refs):
-    blocks, out = refs[:-3], refs[-1]
-    steps, per = blocks[0].shape[-2:]
-    group, groups = 4, 8
+    count, width_y, width_z = fields[0].shape
+    held = count + 2 * reach
+    depth = listen[0:1, :] - lax.axis_index("slab") * count + reach
+    inside = (depth >= 0) & (depth < held)
+    flat = depth * (width_y * width_z) + listen[1:2, :] * width_z + listen[2:3, :]
+    where_to[...] = jnp.where(inside, flat, held * width_y * width_z)
+
+
+def load_adjoint_kernel(*refs):
+    fields, parts, sems = refs[:2], refs[3:7], refs[7]
+    copies = []
+    for i in range(2):
+        copies += part_copies(False, parts[2 * i], fields[i], sems.at[pl.ds(3 * i, 1)], False)
+        copies += part_copies(True, parts[2 * i + 1], fields[i], sems.at[pl.ds(3 * i + 1, 2)], False)
+    for copy in copies:
+        copy.start()
+    for copy in copies:
+        copy.wait()
+
+
+def scatter_kernel(levels, where_to, *refs):
+    blocks, refs = refs[:levels], refs[levels:]
+    inner, outer, _, _, out, inner_out, outer_out = refs
+    per = blocks[0].shape[-1]
+    group, groups = 8, 4
     slab = lax.axis_index("slab")
     lanes = lax.broadcasted_iota(jnp.int32, (8, 128), 1)
     d = 0
@@ -318,7 +350,7 @@
                         lane = flat & 127
                         tile = flat >> 7
                         moved = pltpu.roll(block, (lane - j) & 127, 1)
-                        tiles.append(tile)
+                        tiles.append(jnp.full((8, 128), tile, jnp.int32))
                         terms.append(jnp.where(lanes == lane, moved, 0.0))
                         slots.append(pl.ds(pl.multiple_of(tile * 8, 8), 8))
                     for g in range(groups):
@@ -327,31 +359,27 @@
                         for u in own:
                             value = held[u] + terms[u]
                             for w in range(g * group, u):
-                                same = (tiles[w] == tiles[u]).astype(jnp.float32)
-                                value = value + terms[w] * same
+                                value = value + jnp.where(tiles[w] == tiles[u], terms[w], 0.0)
                             held[u] = value
                         for u in own:
                             out[slots[u], :] = held[u]
-
-
-def pair_kernel(keep, arrived, *outs):
+    count, width_y = inner.shape[0] + 2 * reach, inner.shape[1]
+    for part, part_out, border in ((inner, inner_out, False), (outer, outer_out, True)):
+        for i, x in enumerate(rows_of(count, border)):
+            part_out[i] = part[i] + injected(out, x, blocks[0].shape[1] - 1, width_y)
+
+
+def pair_kernel(keep, arrived, _, *outs):
     mine = lax.axis_index("shot") // 2
     for m in range(len(outs)):
         outs[m][...] = keep[mine ^ m] + arrived[mine ^ m]
 
 
 def sum_kernel(*refs):
-    out = refs[-1]
-    half = len(refs) // 2
-    for border, terms in ((False, refs[:half]), (True, refs[half:-1])):
-        total = terms[0][...]
-        for term in terms[1:]:
-            total = total + term[...]
-        if border:
-            out[:reach] = total[:reach]
-            out[out.shape[0] - reach :] = total[reach:]
-        else:
-            out[reach : out.shape[0] - reach] = total
+    total = refs[0][...]
+    for ref in refs[1:-1]:
+        total = total + ref[...]
+    refs[-1][...] = total
 
 
 def vmem(*shape):
@@ -362,7 +390,7 @@
     return jax.ShapeDtypeStruct(shape, jnp.float32)
 
 
-def call(name, kernel, args, outs, scratch=(), spaces=None, out_spaces=None, micros=1, aliases=None):
+def call(name, kernel, args, outs, scratch=(), spaces=None, out_spaces=None, micros=2, aliases=None):
     spec = lambda space: pl.BlockSpec(memory_space=space)
     spaces = spaces or {}
     args = [
@@ -416,45 +444,47 @@
     edge = vmem(reach, width_y, width_z)
     dma = pltpu.SemaphoreType.DMA
 
-    def by_even(edges):
-        return lax.ppermute(edges, "slab", even_pairs)
-
-    def by_odd(edges):
-        return lax.ppermute(edges, "slab", odd_pairs)
+    def swap(even, odd):
+        return lax.ppermute(even, "slab", even_pairs), lax.ppermute(odd, "slab", odd_pairs)
 
     right = jnp.asarray(band_right(width_z))
     left = jnp.asarray(band_left(width_y))
-    listen = receivers[0]
 
     blocks = [traces]
     bit = 1
     while bit < slabs:
-        held = blocks[0] if len(blocks) == 1 else jnp.concatenate(blocks, axis=0)
+        held = blocks[0]
+        if len(blocks) > 1:
+            (held,) = call("stack", stack_kernel, blocks, [vmem(bit, *traces.shape[1:])], micros=0)
         blocks.append(lax.ppermute(held, "slab", [(i, i ^ bit) for i in range(slabs)]))
         bit *= 2
 
-    p_even, q_even = call(
-        "edges", edges_kernel, [state_now[0], adjoint_now[0]], [edge] * 2, [dma((2,))], {0: HBM, 1: HBM}
+    p0_even, p0_odd, q8_even, q8_odd = call(
+        "edges", edges_kernel, [state_now[0], adjoint_now[0]], [edge] * 4, [dma((4,))], {0: HBM, 1: HBM}
     )
-    p_even, q_even = by_even(p_even), by_even(q_even)
-    fields = [state_before[0], state_now[0], adjoint_after[0], adjoint_now[0], speed_term]
-    tiles = vmem((count * width_y + 1) * 8, width_z)
-    *loaded, speed, where_to, zeros, q_odd = call(
+    p_halo = swap(p0_even, p0_odd)
+    q_halo = swap(q8_even, q8_odd)
+    tiles = vmem(((count + 2 * reach) * width_y + 1) * 8, width_z)
+    pair_of_parts = [part[False], part[True]]
+    *loaded, speed, where_to, zeros = call(
         "load",
         load_kernel,
-        [listen, *fields],
-        [part[False], part[True]] * 4 + [field, VMEM((1, listen.shape[1]), jnp.int32), tiles, edge],
-        [dma((14,))],
-        {1 + i: HBM for i in range(5)},
+        [receivers, state_before[0], state_now[0], speed_term, held],
+        pair_of_parts * 2 + [field, VMEM((1, receivers.shape[2]), jnp.int32), tiles],
+        [VMEM(receivers.shape[1:], jnp.int32), dma((8,))],
+        {i: HBM for i in range(4)},
+        micros=1,
     )
     p = {-1: loaded[0:2], 0: loaded[2:4]}
-    q = {steps + 1: loaded[4:6], steps: loaded[6:8]}
+    q = {}
     laps, acc = {}, {False: None, True: None}
-
-    def forward(k, border, halos):
+    inject = None
+
+    def forward(k, border, halos=(), after=()):
         last = k == steps - 1
         parts = dict(
-            border=border, moves=not last, stores=k < half, adds=k >= half, opens=k == half, step=k, scale=scale
+            border=border, moves=not last, stores=k < half, adds=k >= half, opens=k == half, step=k,
+            scale=scale, after=len(after) > 0,
         )
         args = [*p[k], *halos, right, left]
         outs, scratch, spaces = [], [part[True]] if border else [], {}
@@ -463,8 +493,8 @@
             args += [p[k - 1][border], speed, source, wavelet]
             outs += [part[border]]
             scratch += [SMEM(source.shape, jnp.int32), SMEM(wavelet.shape, jnp.float32), dma, dma]
-        if not last or not border:
-            outs += [edge]
+            if border:
+                outs += [edge, edge]
         if parts["stores"]:
             outs += [part[border]]
         if parts["adds"]:
@@ -475,30 +505,44 @@
                 outs += [part[border]]
         if last:
             args += [q[1][border], laps[0][border]]
-            piece = vmem(shots // 2, part[border].shape[0], width_y // shots, width_z)
-            outs += [piece, piece]
-            scratch += [part[border]]
+            if border:
+                args += [acc[False]]
+                outs += [vmem(shots // 2, count, width_y // shots, width_z)] * 2
+                scratch += [part[True]]
+            else:
+                outs += [part[False]]
+        args += after
         name = "forward_border" if border else "forward_inner"
-        got = list(call(name, functools.partial(forward_kernel, parts), args, outs, scratch, spaces))
-        nxt = None if last else got.pop(0)
-        sides = None if last and border else got.pop(0)
+        got = list(
+            call(
+                name, functools.partial(forward_kernel, parts), args, outs, scratch, spaces,
+                micros=0 if last and border else 1,
+            )
+        )
+        if last and not border:
+            acc[False] = got[0]
         if last:
-            return sides, got
+            return got
+        p.setdefault(k + 1, [None, None])[border] = got.pop(0)
+        sides = [got.pop(0), got.pop(0)] if border else None
         if parts["stores"]:
             laps.setdefault(k, [None, None])[border] = got[0]
         else:
             acc[border] = got[0]
-        p.setdefault(k + 1, [None, None])[border] = nxt
         return sides
 
-    def adjoint(k, border, halos, opening=None):
+    def adjoint(k, border, halos=(), opening=None, after=()):
         last = k == steps - 1
         t = steps - 1 - k
-        sends = not last if border else k > 0
-        parts = dict(border=border, adds=k >= half and not last, last=last, time=t, sends=sends)
-        args = [*q[t + 1], *halos, right, left, q[t + 2][border], speed, inject]
+        parts = dict(
+            border=border, adds=k >= half and not last, last=last, time=t, injects=k > 0, late=k == 1,
+            after=len(after) > 0,
+        )
+        args = [*q[t + 1], *halos, right, left, q[t + 2][border], speed]
         outs, scratch, out_spaces, aliases = [part[border]], [part[True]] if border else [], {}, {}
         spaces = {}
+        if k > 0:
+            args += [inject]
         if parts["adds"]:
             args += [laps[t][border], acc[border]]
         if last:
@@ -509,61 +553,69 @@
             if border:
                 spaces, aliases = {len(args): HBM}, {len(args): 0}
                 args += [opening]
-        if sends:
-            outs += [edge]
+        elif border:
+            outs += [edge, edge]
         if parts["adds"]:
             outs += [part[border]]
+        args += after
         name = "adjoint_border" if border else "adjoint_inner"
         got = call(
             name, functools.partial(adjoint_kernel, parts), args, outs, scratch, spaces, out_spaces,
-            micros=30 if last and border else 1, aliases=aliases,
+            micros=30 if last else 1, aliases=aliases,
         )
         if last:
             return got
         q.setdefault(t, [None, None])[border] = got[0]
         if parts["adds"]:
-            acc[border] = got[2]
-        return got[1] if sends else None
-
-    def spread(send, kept):
-        arrived = lax.ppermute(send, "shot", [(i, i ^ 1) for i in range(shots)])
-        piece = vmem(*send.shape[1:])
-        pieces = call("pair", pair_kernel, [kept, arrived], [piece] * (shots // 2), micros=0)
-        return [pieces[0]] + [
-            lax.ppermute(pieces[m], "shot", [(i, i ^ (2 * m)) for i in range(shots)])
-            for m in range(1, shots // 2)
-        ]
-
-    p_odd = by_odd(forward(0, False, ()))
-    q_odd = by_odd(q_odd)
+            acc[border] = got[-1]
+        return got[1:3] if border else None
+
+    forward(0, False)
     for k in range(steps - 1):
-        p_even = by_even(forward(k, True, (p_even, p_odd)))
+        first = [q[steps - 1 - k][False]] if k > 1 else []
+        p_halo = swap(*forward(k, True, p_halo, first))
         if k == 0:
-            (inject,) = call(
+            loaded = call(
+                "load_adjoint",
+                load_adjoint_kernel,
+                [adjoint_after[0], adjoint_now[0], p[1][True]],
+                pair_of_parts * 2,
+                [dma((6,))],
+                {0: HBM, 1: HBM},
+                micros=1,
+            )
+            q.update({steps + 1: loaded[0:2], steps: loaded[2:4]})
+            adjoint(0, False)
+        if k == 1:
+            at = 1 + len(blocks)
+            inject, *q[steps - 1] = call(
                 "receivers",
-                scatter_kernel,
-                [where_to, *blocks, p[1][True], zeros],
-                [tiles],
+                functools.partial(scatter_kernel, len(blocks)),
+                [where_to, *blocks, *q[steps - 1], p[2][True], zeros],
+                [tiles, *pair_of_parts],
                 (),
                 {0: SMEM},
-                aliases={2 + len(blocks): 0},
+                micros=0,
+                aliases={at: 1, at + 1: 2, at + 3: 0},
             )
-            adjoint(0, False, ())
-        if k + 1 < steps - 1:
-            p_odd = by_odd(forward(k + 1, False, ()))
-        else:
-            sides, halves = forward(k + 1, False, ())
-            p_odd = by_odd(sides)
-            terms = spread(*halves)
-        q_even = by_even(adjoint(k, True, (q_even, q_odd)))
-        if k + 1 < steps - 1:
-            q_odd = by_odd(adjoint(k + 1, False, ()))
-        else:
-            opening, second, sides = adjoint(k + 1, False, ())
-            q_odd = by_odd(sides)
-    _, halves = forward(steps - 1, True, (p_even, p_odd))
-    terms += spread(*halves)
-    (opening,) = adjoint(steps - 1, True, (q_even, q_odd), opening)
+            adjoint(1, False)
+        forward(k + 1, False)
+        first = [acc[False] if k + 1 == steps - 1 else p[k + 2][False]]
+        q_halo = swap(*adjoint(k, True, q_halo, after=first))
+        if 0 < k < steps - 2:
+            adjoint(k + 1, False)
+    send, kept = forward(steps - 1, True, p_halo)
+    arrived = lax.ppermute(send, "shot", [(i, i ^ 1) for i in range(shots)])
+    opening, second = adjoint(steps - 1, False)
+    piece = vmem(count, width_y // shots, width_z)
+    pieces = call(
+        "pair", pair_kernel, [kept, arrived, opening], [piece] * (shots // 2), (), {2: HBM}, micros=0
+    )
+    terms = [pieces[0]] + [
+        lax.ppermute(pieces[m], "shot", [(i, i ^ (2 * m)) for i in range(shots)])
+        for m in range(1, shots // 2)
+    ]
+    (opening,) = adjoint(steps - 1, True, q_halo, opening)
     (gradient,) = call("sum", sum_kernel, terms, [plain(count, width_y // shots, width_z)], micros=0)
     return (opening[None], second[None], gradient)
 

time: 132 us -> 119 us (0.902)
  the two profiles are of different devices: /device:TPU:10 before, /device:TPU:0 now
where the time goes in v7:
time: 119 us; the launch traced here: 118 us
  starting transfers between devices  70.3 us (59%)
  Pallas kernels  36.9 us (31%)
  waiting for transfers between devices  5.62 us (5%)
  local copies, waits for them, and re-layouts  3.84 us (3%)
  between operations  1.34 us (1%)
    ppermute x16, starting transfers between devices, swap(): lax.ppermute(even, 'slab', even_pairs)  47 us
    pallas_call x39, Pallas kernels, call(): pl.pallas_call(kernel, out_shape=outs, in_specs=[spec(spaces.get(i, VMEM)...  36.9 us
    ppermute x16, starting transfers between devices, swap(): lax.ppermute(odd, 'slab', odd_pairs)  10.6 us
    ppermute x2, starting transfers between devices, body(): lax.ppermute(held, 'slab', [(i, i ^ bit) for i in range(slabs)])  9.09 us
    ppermute x3, waiting for transfers between devices, body(): lax.ppermute(pieces[m], 'shot', [(i, i ^ 2 * m) for i in range(shots)])  4.59 us
    unnamed x13, local copies, waits for them, and re-layouts  3.84 us
    ppermute x3, starting transfers between devices, body(): lax.ppermute(pieces[m], 'shot', [(i, i ^ 2 * m) for i in range(shots)])  3.55 us
  transfers between devices with their start and end apart: 38, of which 4 were waited for; matrix products, arithmetic and copies ran while one was open for 1% of the time, Pallas kernels for 30%

profile of v7, /device:TPU:0, one launch (start us, length us, event | category | flops | bytes accessed | tf_op | source)
XLA Modules:
  0.0 118.0 jit_solution(7320678596137753121)
XLA Ops:
  0.7 1.3 %edges.1 = (f32[4,128,128]{2,1,0:T(8,128)S(1)}, f32[4,128,128]{2,1,0:T(8,128)S(1)}, f32[4,128,128]{2,1,0:T(8,128)S(1)}, f32[4,128,128]{2,1,0:T(8,128)S(1)}) custom-call(f32[16,128,128]{2,1,0:T(8,128)} %bitcast.8, f32[16,128,128]{2,1,0:T(8,128)} %bitcast.10), custom_call_target="tpu_custom_call" | custom-call | flops 2000000000 | bytes 131072 | tf_op jit(solution)/shard_map/edges/pallas_call | solution.py:401
  1.9 3.1 %collective-permute-start.2 = (f32[4,128,128]{2,1,0:T(8,128)S(1)}, f32[4,128,128]{2,1,0:T(8,128)S(1)}, u32[]{:S(2)}, u32[]{:S(2)}) collective-permute-start(f32[4,128,128]{2,1,0:T(8,128)S(1)} %get-tuple-element.104), channel_id=1, source_target_pairs={{0,1},{1,0},{2,3},{3,2},{4,5},{5,4},{6,7},{7,6},{8,9},{9,8},{10,11... | collective-permute-start | bytes 786440 | tf_op jit(solution)/shard_map/ppermute | solution.py:448
  5.7 4.4 %collective-permute-start = (f32[1,8,256]{2,1,0:T(8,128)}, f32[1,8,256]{2,1,0:T(8,128)S(1)}, u32[]{:S(2)}, u32[]{:S(2)}) collective-permute-start(f32[1,8,256]{2,1,0:T(8,128)} %refs_0_.3), channel_id=1, source_target_pairs={{0,1},{1,0},{2,3},{3,2},{4,5},{5,4},{6,7},{7,6},{8,9},{9,8},{10,11... | collective-permute-start | bytes 24584 | tf_op jit(solution)/shard_map/ppermute | solution.py:459
  10.9 1.3 %copy.18.listen_hbm = s32[1,3,1024]{2,1,0:T(4,128)} copy(s32[1,3,1024]{2,0,1:T(1,128)} %param.18) | data formatting | bytes 24576 | tf_op args[7]
  12.9 4.6 %collective-permute-start.1 = (f32[2,8,256]{2,1,0:T(8,128)S(1)}, f32[2,8,256]{2,1,0:T(8,128)S(1)}, u32[]{:S(2)}, u32[]{:S(2)}) collective-permute-start(f32[2,8,256]{2,1,0:T(8,128)S(1)} %stack.1.refs_3_), channel_id=1, source_target_pairs={{0,2},{1,3},{2,0},{3,1},{4,6},{5,7},{6,4},{7,5},{8,10},{9,11},{10,... | collective-permute-start | bytes 49160 | tf_op jit(solution)/shard_map/ppermute | solution.py:459
  17.6 1.9 %load.1 = (f32[8,128,128]{2,1,0:T(8,128)S(1)}, f32[8,128,128]{2,1,0:T(8,128)S(1)}, f32[8,128,128]{2,1,0:T(8,128)S(1)}, f32[8,128,128]{2,1,0:T(8,128)S(1)}, f32[1...) custom-call(s32[1,3,1024]{2,1,0:T(4,128)} %copy.18.listen_hbm, f32[16,128,128]{2,1,0:T(8,128)} %bitcast.7, ...), custom_call_target="tpu_custom_call" | custom-call | flops 1000000000 | bytes 65536 | tf_op jit(solution)/shard_map/load/pallas_call | solution.py:401
  19.5 0.9 copy-done
  20.4 0.9 copy-done.2
  21.3 0.8 forward_inner.8
  24.5 1.6 %load_adjoint.1 = (f32[8,128,128]{2,1,0:T(8,128)S(1)}, f32[8,128,128]{2,1,0:T(8,128)S(1)}, f32[8,128,128]{2,1,0:T(8,128)S(1)}, f32[8,128,128]{2,1,0:T(8,128)S(1)}) custom-call(f32[16,128,128]{2,1,0:T(8,128)} %bitcast.12, f32[16,128,128]{2,1,0:T(8,128)} %bitcast.11, f32[8,128,128]{2,1,0:T(8,128)S(1)} %get-tuple-element.108.refs_2_.refs_1_.refs_6_), custom_call_target="tpu_custom_call" | custom-call | flops 1000000000 | bytes 65536 | tf_op jit(solution)/shard_map/load_adjoint/pallas_call | solution.py:401
  26.8 3.2 %collective-permute-start.8 = (f32[4,128,128]{2,1,0:T(8,128)S(1)}, f32[4,128,128]{2,1,0:T(8,128)S(1)}, u32[]{:S(2)}, u32[]{:S(2)}) collective-permute-start(f32[4,128,128]{2,1,0:T(8,128)S(1)} %get-tuple-element.126), channel_id=1, source_target_pairs={{0,1},{1,0},{2,3},{3,2},{4,5},{5,4},{6,7},{7,6},{8,9},{9,8},{10,11... | collective-permute-start | bytes 786440 | tf_op jit(solution)/shard_map/ppermute | solution.py:448
  32.0 3.3 %collective-permute-start.12 = (f32[4,128,128]{2,1,0:T(8,128)S(1)}, f32[4,128,128]{2,1,0:T(8,128)S(1)}, u32[]{:S(2)}, u32[]{:S(2)}) collective-permute-start(f32[4,128,128]{2,1,0:T(8,128)S(1)} %get-tuple-element.132), channel_id=1, source_target_pairs={{0,1},{1,0},{2,3},{3,2},{4,5},{5,4},{6,7},{7,6},{8,9},{9,8},{10,11... | collective-permute-start | bytes 786440 | tf_op jit(solution)/shard_map/ppermute | solution.py:448
  36.1 6.1 %receivers.1 = (f32[24584,128]{1,0:T(8,128)S(1)}, f32[8,128,128]{2,1,0:T(8,128)S(1)}, f32[8,128,128]{2,1,0:T(8,128)S(1)}) custom-call(s32[1,1024]{1,0:T(1,128)S(1)} %get-tuple-element.101.where_to, f32[1,8,256]{2,1,0:T(8,128)S(1)} %copy-done.5, ...), custom_call_target="tpu_custom_call", output_to_operand_aliasing={{1}: (4, {}), {2}: (5, {}), {0}: (7, {})} | custom-call | tf_op jit(solution)/shard_map/receivers/pallas_call | solution.py:401
  43.7 2.1 %collective-permute-start.10 = (f32[4,128,128]{2,1,0:T(8,128)S(1)}, f32[4,128,128]{2,1,0:T(8,128)S(1)}, u32[]{:S(2)}, u32[]{:S(2)}) collective-permute-start(f32[4,128,128]{2,1,0:T(8,128)S(1)} %get-tuple-element.130), channel_id=1, source_target_pairs={{0,1},{1,0},{2,3},{3,2},{4,5},{5,4},{6,7},{7,6},{8,9},{9,8},{10,11... | collective-permute-start | bytes 786440 | tf_op jit(solution)/shard_map/ppermute | solution.py:448
  48.7 2.6 %collective-permute-start.16 = (f32[4,128,128]{2,1,0:T(8,128)S(1)}, f32[4,128,128]{2,1,0:T(8,128)S(1)}, u32[]{:S(2)}, u32[]{:S(2)}) collective-permute-start(f32[4,128,128]{2,1,0:T(8,128)S(1)} %get-tuple-element.139), channel_id=1, source_target_pairs={{0,1},{1,0},{2,3},{3,2},{4,5},{5,4},{6,7},{7,6},{8,9},{9,8},{10,11... | collective-permute-start | bytes 786440 | tf_op jit(solution)/shard_map/ppermute | solution.py:448
  52.7 0.9 adjoint_border.10
  53.6 2.9 %collective-permute-start.14 = (f32[4,128,128]{2,1,0:T(8,128)S(1)}, f32[4,128,128]{2,1,0:T(8,128)S(1)}, u32[]{:S(2)}, u32[]{:S(2)}) collective-permute-start(f32[4,128,128]{2,1,0:T(8,128)S(1)} %get-tuple-element.137), channel_id=1, source_target_pairs={{0,1},{1,0},{2,3},{3,2},{4,5},{5,4},{6,7},{7,6},{8,9},{9,8},{10,11... | collective-permute-start | bytes 786440 | tf_op jit(solution)/shard_map/ppermute | solution.py:448
  59.3 4.0 %collective-permute-start.20 = (f32[4,128,128]{2,1,0:T(8,128)S(1)}, f32[4,128,128]{2,1,0:T(8,128)S(1)}, u32[]{:S(2)}, u32[]{:S(2)}) collective-permute-start(f32[4,128,128]{2,1,0:T(8,128)S(1)} %get-tuple-element.150), channel_id=1, source_target_pairs={{0,1},{1,0},{2,3},{3,2},{4,5},{5,4},{6,7},{7,6},{8,9},{9,8},{10,11... | collective-permute-start | bytes 786440 | tf_op jit(solution)/shard_map/ppermute | solution.py:448
  65.4 3.4 %collective-permute-start.18 = (f32[4,128,128]{2,1,0:T(8,128)S(1)}, f32[4,128,128]{2,1,0:T(8,128)S(1)}, u32[]{:S(2)}, u32[]{:S(2)}) collective-permute-start(f32[4,128,128]{2,1,0:T(8,128)S(1)} %get-tuple-element.147), channel_id=1, source_target_pairs={{0,1},{1,0},{2,3},{3,2},{4,5},{5,4},{6,7},{7,6},{8,9},{9,8},{10,11... | collective-permute-start | bytes 786440 | tf_op jit(solution)/shard_map/ppermute | solution.py:448
  71.0 3.6 %collective-permute-start.24 = (f32[4,128,128]{2,1,0:T(8,128)S(1)}, f32[4,128,128]{2,1,0:T(8,128)S(1)}, u32[]{:S(2)}, u32[]{:S(2)}) collective-permute-start(f32[4,128,128]{2,1,0:T(8,128)S(1)} %get-tuple-element.163), channel_id=1, source_target_pairs={{0,1},{1,0},{2,3},{3,2},{4,5},{5,4},{6,7},{7,6},{8,9},{9,8},{10,11... | collective-permute-start | bytes 786440 | tf_op jit(solution)/shard_map/ppermute | solution.py:448
  76.9 3.9 %collective-permute-start.22 = (f32[4,128,128]{2,1,0:T(8,128)S(1)}, f32[4,128,128]{2,1,0:T(8,128)S(1)}, u32[]{:S(2)}, u32[]{:S(2)}) collective-permute-start(f32[4,128,128]{2,1,0:T(8,128)S(1)} %get-tuple-element.160), channel_id=1, source_target_pairs={{0,1},{1,0},{2,3},{3,2},{4,5},{5,4},{6,7},{7,6},{8,9},{9,8},{10,11... | collective-permute-start | bytes 786440 | tf_op jit(solution)/shard_map/ppermute | solution.py:448
  82.9 3.6 %collective-permute-start.28 = (f32[4,128,128]{2,1,0:T(8,128)S(1)}, f32[4,128,128]{2,1,0:T(8,128)S(1)}, u32[]{:S(2)}, u32[]{:S(2)}) collective-permute-start(f32[4,128,128]{2,1,0:T(8,128)S(1)} %get-tuple-element.177), channel_id=1, source_target_pairs={{0,1},{1,0},{2,3},{3,2},{4,5},{5,4},{6,7},{7,6},{8,9},{9,8},{10,11... | collective-permute-start | bytes 786440 | tf_op jit(solution)/shard_map/ppermute | solution.py:448
  88.6 3.8 %collective-permute-start.26 = (f32[4,128,128]{2,1,0:T(8,128)S(1)}, f32[4,128,128]{2,1,0:T(8,128)S(1)}, u32[]{:S(2)}, u32[]{:S(2)}) collective-permute-start(f32[4,128,128]{2,1,0:T(8,128)S(1)} %get-tuple-element.174), channel_id=1, source_target_pairs={{0,1},{1,0},{2,3},{3,2},{4,5},{5,4},{6,7},{7,6},{8,9},{9,8},{10,11... | collective-permute-start | bytes 786440 | tf_op jit(solution)/shard_map/ppermute | solution.py:448
  93.8 1.0 forward_border.14
  94.8 3.7 %collective-permute-start.32 = (f32[4,128,128]{2,1,0:T(8,128)S(1)}, f32[4,128,128]{2,1,0:T(8,128)S(1)}, u32[]{:S(2)}, u32[]{:S(2)}) collective-permute-start(f32[4,128,128]{2,1,0:T(8,128)S(1)} %get-tuple-element.189), channel_id=1, source_target_pairs={{0,1},{1,0},{2,3},{3,2},{4,5},{5,4},{6,7},{7,6},{8,9},{9,8},{10,11... | collective-permute-start | bytes 786440 | tf_op jit(solution)/shard_map/ppermute | solution.py:448
  100.5 3.6 %collective-permute-start.30 = (f32[4,128,128]{2,1,0:T(8,128)S(1)}, f32[4,128,128]{2,1,0:T(8,128)S(1)}, u32[]{:S(2)}, u32[]{:S(2)}) collective-permute-start(f32[4,128,128]{2,1,0:T(8,128)S(1)} %get-tuple-element.185), channel_id=1, source_target_pairs={{0,1},{1,0},{2,3},{3,2},{4,5},{5,4},{6,7},{7,6},{8,9},{9,8},{10,11... | collective-permute-start | bytes 786440 | tf_op jit(solution)/shard_map/ppermute | solution.py:448
  105.7 1.5 %adjoint_inner.15 = (f32[16,128,128]{2,1,0:T(8,128)}, f32[16,128,128]{2,1,0:T(8,128)}) custom-call(f32[8,128,128]{2,1,0:T(8,128)S(1)} %get-tuple-element.173.refs_12_.refs_6_.refs_0_, f32[8,128,128]{2,1,0:T(8,128)S(1)} %get-tuple-element.184.refs_1_.refs_8_, bf16[256,256]{1,0:T(8,128)(2,1)S(1)} %copy-done.1, bf16[256,256]{1,0:T(8,128)(2,1)S(1)} %copy-done.3, ...), custom_call_target="tpu_custom_call" | custom-call | flops 30000001024 | bytes 1966080 | tf_op jit(solution)/shard_map/adjoint_inner/pallas_call | solution.py:401
  107.7 1.6 %collective-permute-start.35 = (f32[16,16,128]{2,1,0:T(8,128)S(1)}, f32[16,16,128]{2,1,0:T(8,128)S(1)}, u32[]{:S(2)}, u32[]{:S(2)}) collective-permute-start(f32[16,16,128]{2,1,0:T(8,128)S(1)} %get-tuple-element.196), channel_id=1, source_target_pairs={{0,8},{4,12},{8,0},{12,4},{16,24},{20,28},{24,16},{28,20},{1,9},{5... | collective-permute-start | bytes 393224 | tf_op jit(solution)/shard_map/ppermute | solution.py:615
  109.2 1.5 %collective-permute-start.36 = (f32[16,16,128]{2,1,0:T(8,128)S(1)}, f32[16,16,128]{2,1,0:T(8,128)S(1)}, u32[]{:S(2)}, u32[]{:S(2)}) collective-permute-start(f32[16,16,128]{2,1,0:T(8,128)S(1)} %get-tuple-element.197), channel_id=1, source_target_pairs={{0,16},{4,20},{8,24},{12,28},{16,0},{20,4},{24,8},{28,12},{1,17},{... | collective-permute-start | bytes 393224 | tf_op jit(solution)/shard_map/ppermute | solution.py:615
  111.2 1.5 %adjoint_border.15 = f32[16,128,128]{2,1,0:T(8,128)} custom-call(f32[8,128,128]{2,1,0:T(8,128)S(1)} %get-tuple-element.173.refs_12_.refs_6_.refs_0_, f32[8,128,128]{2,1,0:T(8,128)S(1)} %get-tuple-element.184.refs_1_.refs_8_, f32[4,128,128]{2,1,0:T(8,128)S(1)} %collective-permute-done.30.refs_2_, ...), custom_call_target="tpu_custom_call", output_to_operand_aliasing={{}: (9, {})} | custom-call | flops 30000001024 | bytes 1966080 | tf_op jit(solution)/shard_map/adjoint_border/pallas_call | solution.py:401
  112.8 0.9 collective-permute-done.35.refs_1_
  113.6 3.7 %collective-permute-done.36.refs_2_ = f32[16,16,128]{2,1,0:T(8,128)S(1)} collective-permute-done((f32[16,16,128]{2,1,0:T(8,128)S(1)}, f32[16,16,128]{2,1,0:T(8,128)S(1)}, u32[]{:S(2)}, u32[]{:S(2)}) %collective-permute-start.36) | collective-permute-done | bytes 131104 | tf_op jit(solution)/shard_map/ppermute | solution.py:615
  (96 shorter events, 33.5 us)
Async XLA Ops:
  1.9 20.2 %collective-permute-start.2 = (f32[4,128,128]{2,1,0:T(8,128)S(1)}, f32[4,128,128]{2,1,0:T(8,128)S(1)}, u32[]{:S(2)}, u32[]{:S(2)}) collective-permute-start(f32[4,128,128]{2,1,0:T(8,128)S(1)} %get-tuple-element.104), channel_id=1, source_target_pairs={{0,1},{1,0},{2,3},{3,2},{4,5},{5,4},{6,7},{7,6},{8,9},{9,8},{10,11... | collective-permute-start | bytes 786440 | tf_op jit(solution)/shard_map/ppermute | solution.py:448
  5.0 17.1 %collective-permute-start.3 = (f32[4,128,128]{2,1,0:T(8,128)S(1)}, f32[4,128,128]{2,1,0:T(8,128)S(1)}, u32[]{:S(2)}, u32[]{:S(2)}) collective-permute-start(f32[4,128,128]{2,1,0:T(8,128)S(1)} %get-tuple-element.105), channel_id=1, source_target_pairs={{1,2},{2,1},{5,6},{6,5},{9,10},{10,9},{13,14},{14,13},{17,18},{18,... | collective-permute-start | bytes 786440 | tf_op jit(solution)/shard_map/ppermute | solution.py:448
  10.2 15.9 %collective-permute-start.4 = (f32[4,128,128]{2,1,0:T(8,128)S(1)}, f32[4,128,128]{2,1,0:T(8,128)S(1)}, u32[]{:S(2)}, u32[]{:S(2)}) collective-permute-start(f32[4,128,128]{2,1,0:T(8,128)S(1)} %get-tuple-element.112), channel_id=1, source_target_pairs={{0,1},{1,0},{2,3},{3,2},{4,5},{5,4},{6,7},{7,6},{8,9},{9,8},{10,11... | collective-permute-start | bytes 786440 | tf_op jit(solution)/shard_map/ppermute | solution.py:448
  10.2 15.9 %collective-permute-start.5 = (f32[4,128,128]{2,1,0:T(8,128)S(1)}, f32[4,128,128]{2,1,0:T(8,128)S(1)}, u32[]{:S(2)}, u32[]{:S(2)}) collective-permute-start(f32[4,128,128]{2,1,0:T(8,128)S(1)} %get-tuple-element.113), channel_id=1, source_target_pairs={{1,2},{2,1},{5,6},{6,5},{9,10},{10,9},{13,14},{14,13},{17,18},{18,... | collective-permute-start | bytes 786440 | tf_op jit(solution)/shard_map/ppermute | solution.py:448
  12.9 23.1 %collective-permute-start.1 = (f32[2,8,256]{2,1,0:T(8,128)S(1)}, f32[2,8,256]{2,1,0:T(8,128)S(1)}, u32[]{:S(2)}, u32[]{:S(2)}) collective-permute-start(f32[2,8,256]{2,1,0:T(8,128)S(1)} %stack.1.refs_3_), channel_id=1, source_target_pairs={{0,2},{1,3},{2,0},{3,1},{4,6},{5,7},{6,4},{7,5},{8,10},{9,11},{10,... | collective-permute-start | bytes 49160 | tf_op jit(solution)/shard_map/ppermute | solution.py:459
  22.9 8.3 %collective-permute-start.6 = (f32[4,128,128]{2,1,0:T(8,128)S(1)}, f32[4,128,128]{2,1,0:T(8,128)S(1)}, u32[]{:S(2)}, u32[]{:S(2)}) collective-permute-start(f32[4,128,128]{2,1,0:T(8,128)S(1)} %get-tuple-element.119), channel_id=1, source_target_pairs={{0,1},{1,0},{2,3},{3,2},{4,5},{5,4},{6,7},{7,6},{8,9},{9,8},{10,11... | collective-permute-start | bytes 786440 | tf_op jit(solution)/shard_map/ppermute | solution.py:448
  23.1 8.2 %collective-permute-start.7 = (f32[4,128,128]{2,1,0:T(8,128)S(1)}, f32[4,128,128]{2,1,0:T(8,128)S(1)}, u32[]{:S(2)}, u32[]{:S(2)}) collective-permute-start(f32[4,128,128]{2,1,0:T(8,128)S(1)} %get-tuple-element.120), channel_id=1, source_target_pairs={{1,2},{2,1},{5,6},{6,5},{9,10},{10,9},{13,14},{14,13},{17,18},{18,... | collective-permute-start | bytes 786440 | tf_op jit(solution)/shard_map/ppermute | solution.py:448
  26.8 16.1 %collective-permute-start.8 = (f32[4,128,128]{2,1,0:T(8,128)S(1)}, f32[4,128,128]{2,1,0:T(8,128)S(1)}, u32[]{:S(2)}, u32[]{:S(2)}) collective-permute-start(f32[4,128,128]{2,1,0:T(8,128)S(1)} %get-tuple-element.126), channel_id=1, source_target_pairs={{0,1},{1,0},{2,3},{3,2},{4,5},{5,4},{6,7},{7,6},{8,9},{9,8},{10,11... | collective-permute-start | bytes 786440 | tf_op jit(solution)/shard_map/ppermute | solution.py:448
  30.0 12.9 %collective-permute-start.9 = (f32[4,128,128]{2,1,0:T(8,128)S(1)}, f32[4,128,128]{2,1,0:T(8,128)S(1)}, u32[]{:S(2)}, u32[]{:S(2)}) collective-permute-start(f32[4,128,128]{2,1,0:T(8,128)S(1)} %get-tuple-element.127), channel_id=1, source_target_pairs={{1,2},{2,1},{5,6},{6,5},{9,10},{10,9},{13,14},{14,13},{17,18},{18,... | collective-permute-start | bytes 786440 | tf_op jit(solution)/shard_map/ppermute | solution.py:448
  32.0 15.9 %collective-permute-start.12 = (f32[4,128,128]{2,1,0:T(8,128)S(1)}, f32[4,128,128]{2,1,0:T(8,128)S(1)}, u32[]{:S(2)}, u32[]{:S(2)}) collective-permute-start(f32[4,128,128]{2,1,0:T(8,128)S(1)} %get-tuple-element.132), channel_id=1, source_target_pairs={{0,1},{1,0},{2,3},{3,2},{4,5},{5,4},{6,7},{7,6},{8,9},{9,8},{10,11... | collective-permute-start | bytes 786440 | tf_op jit(solution)/shard_map/ppermute | solution.py:448
  35.4 12.6 %collective-permute-start.13 = (f32[4,128,128]{2,1,0:T(8,128)S(1)}, f32[4,128,128]{2,1,0:T(8,128)S(1)}, u32[]{:S(2)}, u32[]{:S(2)}) collective-permute-start(f32[4,128,128]{2,1,0:T(8,128)S(1)} %get-tuple-element.133), channel_id=1, source_target_pairs={{1,2},{2,1},{5,6},{6,5},{9,10},{10,9},{13,14},{14,13},{17,18},{18,... | collective-permute-start | bytes 786440 | tf_op jit(solution)/shard_map/ppermute | solution.py:448
  43.7 8.9 %collective-permute-start.10 = (f32[4,128,128]{2,1,0:T(8,128)S(1)}, f32[4,128,128]{2,1,0:T(8,128)S(1)}, u32[]{:S(2)}, u32[]{:S(2)}) collective-permute-start(f32[4,128,128]{2,1,0:T(8,128)S(1)} %get-tuple-element.130), channel_id=1, source_target_pairs={{0,1},{1,0},{2,3},{3,2},{4,5},{5,4},{6,7},{7,6},{8,9},{9,8},{10,11... | collective-permute-start | bytes 786440 | tf_op jit(solution)/shard_map/ppermute | solution.py:448
  48.7 9.8 %collective-permute-start.16 = (f32[4,128,128]{2,1,0:T(8,128)S(1)}, f32[4,128,128]{2,1,0:T(8,128)S(1)}, u32[]{:S(2)}, u32[]{:S(2)}) collective-permute-start(f32[4,128,128]{2,1,0:T(8,128)S(1)} %get-tuple-element.139), channel_id=1, source_target_pairs={{0,1},{1,0},{2,3},{3,2},{4,5},{5,4},{6,7},{7,6},{8,9},{9,8},{10,11... | collective-permute-start | bytes 786440 | tf_op jit(solution)/shard_map/ppermute | solution.py:448
  51.3 7.2 %collective-permute-start.17 = (f32[4,128,128]{2,1,0:T(8,128)S(1)}, f32[4,128,128]{2,1,0:T(8,128)S(1)}, u32[]{:S(2)}, u32[]{:S(2)}) collective-permute-start(f32[4,128,128]{2,1,0:T(8,128)S(1)} %get-tuple-element.140), channel_id=1, source_target_pairs={{1,2},{2,1},{5,6},{6,5},{9,10},{10,9},{13,14},{14,13},{17,18},{18,... | collective-permute-start | bytes 786440 | tf_op jit(solution)/shard_map/ppermute | solution.py:448
  53.6 11.0 %collective-permute-start.14 = (f32[4,128,128]{2,1,0:T(8,128)S(1)}, f32[4,128,128]{2,1,0:T(8,128)S(1)}, u32[]{:S(2)}, u32[]{:S(2)}) collective-permute-start(f32[4,128,128]{2,1,0:T(8,128)S(1)} %get-tuple-element.137), channel_id=1, source_target_pairs={{0,1},{1,0},{2,3},{3,2},{4,5},{5,4},{6,7},{7,6},{8,9},{9,8},{10,11... | collective-permute-start | bytes 786440 | tf_op jit(solution)/shard_map/ppermute | solution.py:448
  56.6 8.1 %collective-permute-start.15 = (f32[4,128,128]{2,1,0:T(8,128)S(1)}, f32[4,128,128]{2,1,0:T(8,128)S(1)}, u32[]{:S(2)}, u32[]{:S(2)}) collective-permute-start(f32[4,128,128]{2,1,0:T(8,128)S(1)} %get-tuple-element.138), channel_id=1, source_target_pairs={{1,2},{2,1},{5,6},{6,5},{9,10},{10,9},{13,14},{14,13},{17,18},{18,... | collective-permute-start | bytes 786440 | tf_op jit(solution)/shard_map/ppermute | solution.py:448
  59.3 10.9 %collective-permute-start.20 = (f32[4,128,128]{2,1,0:T(8,128)S(1)}, f32[4,128,128]{2,1,0:T(8,128)S(1)}, u32[]{:S(2)}, u32[]{:S(2)}) collective-permute-start(f32[4,128,128]{2,1,0:T(8,128)S(1)} %get-tuple-element.150), channel_id=1, source_target_pairs={{0,1},{1,0},{2,3},{3,2},{4,5},{5,4},{6,7},{7,6},{8,9},{9,8},{10,11... | collective-permute-start | bytes 786440 | tf_op jit(solution)/shard_map/ppermute | solution.py:448
  63.3 6.9 %collective-permute-start.21 = (f32[4,128,128]{2,1,0:T(8,128)S(1)}, f32[4,128,128]{2,1,0:T(8,128)S(1)}, u32[]{:S(2)}, u32[]{:S(2)}) collective-permute-start(f32[4,128,128]{2,1,0:T(8,128)S(1)} %get-tuple-element.151), channel_id=1, source_target_pairs={{1,2},{2,1},{5,6},{6,5},{9,10},{10,9},{13,14},{14,13},{17,18},{18,... | collective-permute-start | bytes 786440 | tf_op jit(solution)/shard_map/ppermute | solution.py:448
  65.4 10.6 %collective-permute-start.18 = (f32[4,128,128]{2,1,0:T(8,128)S(1)}, f32[4,128,128]{2,1,0:T(8,128)S(1)}, u32[]{:S(2)}, u32[]{:S(2)}) collective-permute-start(f32[4,128,128]{2,1,0:T(8,128)S(1)} %get-tuple-element.147), channel_id=1, source_target_pairs={{0,1},{1,0},{2,3},{3,2},{4,5},{5,4},{6,7},{7,6},{8,9},{9,8},{10,11... | collective-permute-start | bytes 786440 | tf_op jit(solution)/shard_map/ppermute | solution.py:448
  68.9 7.2 %collective-permute-start.19 = (f32[4,128,128]{2,1,0:T(8,128)S(1)}, f32[4,128,128]{2,1,0:T(8,128)S(1)}, u32[]{:S(2)}, u32[]{:S(2)}) collective-permute-start(f32[4,128,128]{2,1,0:T(8,128)S(1)} %get-tuple-element.148), channel_id=1, source_target_pairs={{1,2},{2,1},{5,6},{6,5},{9,10},{10,9},{13,14},{14,13},{17,18},{18,... | collective-permute-start | bytes 786440 | tf_op jit(solution)/shard_map/ppermute | solution.py:448
  71.0 11.1 %collective-permute-start.24 = (f32[4,128,128]{2,1,0:T(8,128)S(1)}, f32[4,128,128]{2,1,0:T(8,128)S(1)}, u32[]{:S(2)}, u32[]{:S(2)}) collective-permute-start(f32[4,128,128]{2,1,0:T(8,128)S(1)} %get-tuple-element.163), channel_id=1, source_target_pairs={{0,1},{1,0},{2,3},{3,2},{4,5},{5,4},{6,7},{7,6},{8,9},{9,8},{10,11... | collective-permute-start | bytes 786440 | tf_op jit(solution)/shard_map/ppermute | solution.py:448
  74.7 7.4 %collective-permute-start.25 = (f32[4,128,128]{2,1,0:T(8,128)S(1)}, f32[4,128,128]{2,1,0:T(8,128)S(1)}, u32[]{:S(2)}, u32[]{:S(2)}) collective-permute-start(f32[4,128,128]{2,1,0:T(8,128)S(1)} %get-tuple-element.164), channel_id=1, source_target_pairs={{1,2},{2,1},{5,6},{6,5},{9,10},{10,9},{13,14},{14,13},{17,18},{18,... | collective-permute-start | bytes 786440 | tf_op jit(solution)/shard_map/ppermute | solution.py:448
  76.9 11.0 %collective-permute-start.22 = (f32[4,128,128]{2,1,0:T(8,128)S(1)}, f32[4,128,128]{2,1,0:T(8,128)S(1)}, u32[]{:S(2)}, u32[]{:S(2)}) collective-permute-start(f32[4,128,128]{2,1,0:T(8,128)S(1)} %get-tuple-element.160), channel_id=1, source_target_pairs={{0,1},{1,0},{2,3},{3,2},{4,5},{5,4},{6,7},{7,6},{8,9},{9,8},{10,11... | collective-permute-start | bytes 786440 | tf_op jit(solution)/shard_map/ppermute | solution.py:448
  80.7 7.1 %collective-permute-start.23 = (f32[4,128,128]{2,1,0:T(8,128)S(1)}, f32[4,128,128]{2,1,0:T(8,128)S(1)}, u32[]{:S(2)}, u32[]{:S(2)}) collective-permute-start(f32[4,128,128]{2,1,0:T(8,128)S(1)} %get-tuple-element.161), channel_id=1, source_target_pairs={{1,2},{2,1},{5,6},{6,5},{9,10},{10,9},{13,14},{14,13},{17,18},{18,... | collective-permute-start | bytes 786440 | tf_op jit(solution)/shard_map/ppermute | solution.py:448
  82.9 10.9 %collective-permute-start.28 = (f32[4,128,128]{2,1,0:T(8,128)S(1)}, f32[4,128,128]{2,1,0:T(8,128)S(1)}, u32[]{:S(2)}, u32[]{:S(2)}) collective-permute-start(f32[4,128,128]{2,1,0:T(8,128)S(1)} %get-tuple-element.177), channel_id=1, source_target_pairs={{0,1},{1,0},{2,3},{3,2},{4,5},{5,4},{6,7},{7,6},{8,9},{9,8},{10,11... | collective-permute-start | bytes 786440 | tf_op jit(solution)/shard_map/ppermute | solution.py:448
  86.4 7.3 %collective-permute-start.29 = (f32[4,128,128]{2,1,0:T(8,128)S(1)}, f32[4,128,128]{2,1,0:T(8,128)S(1)}, u32[]{:S(2)}, u32[]{:S(2)}) collective-permute-start(f32[4,128,128]{2,1,0:T(8,128)S(1)} %get-tuple-element.178), channel_id=1, source_target_pairs={{1,2},{2,1},{5,6},{6,5},{9,10},{10,9},{13,14},{14,13},{17,18},{18,... | collective-permute-start | bytes 786440 | tf_op jit(solution)/shard_map/ppermute | solution.py:448
  88.6 11.1 %collective-permute-start.26 = (f32[4,128,128]{2,1,0:T(8,128)S(1)}, f32[4,128,128]{2,1,0:T(8,128)S(1)}, u32[]{:S(2)}, u32[]{:S(2)}) collective-permute-start(f32[4,128,128]{2,1,0:T(8,128)S(1)} %get-tuple-element.174), channel_id=1, source_target_pairs={{0,1},{1,0},{2,3},{3,2},{4,5},{5,4},{6,7},{7,6},{8,9},{9,8},{10,11... | collective-permute-start | bytes 786440 | tf_op jit(solution)/shard_map/ppermute | solution.py:448
  92.4 7.4 %collective-permute-start.27 = (f32[4,128,128]{2,1,0:T(8,128)S(1)}, f32[4,128,128]{2,1,0:T(8,128)S(1)}, u32[]{:S(2)}, u32[]{:S(2)}) collective-permute-start(f32[4,128,128]{2,1,0:T(8,128)S(1)} %get-tuple-element.175), channel_id=1, source_target_pairs={{1,2},{2,1},{5,6},{6,5},{9,10},{10,9},{13,14},{14,13},{17,18},{18,... | collective-permute-start | bytes 786440 | tf_op jit(solution)/shard_map/ppermute | solution.py:448
  94.8 10.1 %collective-permute-start.32 = (f32[4,128,128]{2,1,0:T(8,128)S(1)}, f32[4,128,128]{2,1,0:T(8,128)S(1)}, u32[]{:S(2)}, u32[]{:S(2)}) collective-permute-start(f32[4,128,128]{2,1,0:T(8,128)S(1)} %get-tuple-element.189), channel_id=1, source_target_pairs={{0,1},{1,0},{2,3},{3,2},{4,5},{5,4},{6,7},{7,6},{8,9},{9,8},{10,11... | collective-permute-start | bytes 786440 | tf_op jit(solution)/shard_map/ppermute | solution.py:448
  100.5 10.7 %collective-permute-start.30 = (f32[4,128,128]{2,1,0:T(8,128)S(1)}, f32[4,128,128]{2,1,0:T(8,128)S(1)}, u32[]{:S(2)}, u32[]{:S(2)}) collective-permute-start(f32[4,128,128]{2,1,0:T(8,128)S(1)} %get-tuple-element.185), channel_id=1, source_target_pairs={{0,1},{1,0},{2,3},{3,2},{4,5},{5,4},{6,7},{7,6},{8,9},{9,8},{10,11... | collective-permute-start | bytes 786440 | tf_op jit(solution)/shard_map/ppermute | solution.py:448
  104.1 7.1 %collective-permute-start.31 = (f32[4,128,128]{2,1,0:T(8,128)S(1)}, f32[4,128,128]{2,1,0:T(8,128)S(1)}, u32[]{:S(2)}, u32[]{:S(2)}) collective-permute-start(f32[4,128,128]{2,1,0:T(8,128)S(1)} %get-tuple-element.186), channel_id=1, source_target_pairs={{1,2},{2,1},{5,6},{6,5},{9,10},{10,9},{13,14},{14,13},{17,18},{18,... | collective-permute-start | bytes 786440 | tf_op jit(solution)/shard_map/ppermute | solution.py:448
  109.2 8.1 %collective-permute-start.36 = (f32[16,16,128]{2,1,0:T(8,128)S(1)}, f32[16,16,128]{2,1,0:T(8,128)S(1)}, u32[]{:S(2)}, u32[]{:S(2)}) collective-permute-start(f32[16,16,128]{2,1,0:T(8,128)S(1)} %get-tuple-element.197), channel_id=1, source_target_pairs={{0,16},{4,20},{8,24},{12,28},{16,0},{20,4},{24,8},{28,12},{1,17},{... | collective-permute-start | bytes 393224 | tf_op jit(solution)/shard_map/ppermute | solution.py:615
  (12 other events, 102.6 us)

commit v8 on v7

--- a/solution.py
+++ b/solution.py
@@ -122,10 +122,11 @@
     acc_in = next(it) if adds and not opens else None
     first, lap_first = (next(it), next(it)) if not moves else (None, None)
     total_inner = next(it) if border and not moves else None
-    if parts["after"]:
+    for _ in range(parts["after"]):
         next(it)
     nxt = next(it) if moves else None
     even_out, odd_out = (next(it), next(it)) if moves and border else (None, None)
+    token = next(it) if parts["token"] else None
     lap_out = next(it) if stores else None
     acc_out = next(it) if adds and moves else None
     send, keep = (next(it), next(it)) if border and not moves else (None, None)
@@ -181,6 +182,8 @@
 
         if border:
             emit_edges(parity, nxt, even_out, odd_out)
+        if parts["token"]:
+            token[...] = nxt[0, :8, :]
     elif border:
         chunk = send.shape[2]
         mine = lax.axis_index("shot") % 2
@@ -222,7 +225,7 @@
     lap_of, acc_in = (next(it), next(it)) if adds else (None, None)
     if last and border:
         next(it)
-    if parts["after"]:
+    for _ in range(parts["after"]):
         next(it)
     nxt = next(it)
     second = next(it) if last and not border else None
@@ -264,7 +267,7 @@
 
 
 def edges_kernel(*refs):
-    fields, outs, sems = refs[:2], refs[2:6], refs[6]
+    fields, traces, outs, traces_out, sems = refs[:2], refs[2], refs[3:7], *refs[7:]
     parity = lax.axis_index("slab") % 2
     top = fields[0].shape[0] - reach
     starts = (top * (1 - parity), top * parity)
@@ -272,7 +275,9 @@
     for i in range(4):
         rows = pl.ds(starts[i % 2], reach)
         copies.append(pltpu.make_async_copy(fields[i // 2].at[rows], outs[i], sems.at[i]))
-        copies[-1].start()
+    copies.append(pltpu.make_async_copy(traces, traces_out, sems.at[4]))
+    for copy in copies:
+        copy.start()
     for copy in copies:
         copy.wait()
 
@@ -284,10 +289,11 @@
         first += ref.shape[0]
 
 
-def load_kernel(listen_hbm, *refs):
-    fields, parts, speed, where_to, tiles, listen, sems = refs[:3], refs[4:8], *refs[8:]
-    listen_copy = pltpu.make_async_copy(listen_hbm.at[0], listen, sems.at[7])
-    copies = [listen_copy, pltpu.make_async_copy(fields[2], speed, sems.at[6])]
+def load_kernel(listen, *refs):
+    fields, bands, parts, speed, refs = refs[:3], refs[4:6], refs[6:10], refs[10], refs[11:]
+    bands_out, where_to, tiles, sems = refs[:2], *refs[2:]
+    copies = [pltpu.make_async_copy(bands[i], bands_out[i], sems.at[7 + i]) for i in range(2)]
+    copies.append(pltpu.make_async_copy(fields[2], speed, sems.at[6]))
     for i in range(2):
         copies += part_copies(False, parts[2 * i], fields[i], sems.at[pl.ds(3 * i, 1)], False)
         copies += part_copies(True, parts[2 * i + 1], fields[i], sems.at[pl.ds(3 * i + 1, 2)], False)
@@ -447,44 +453,50 @@
     def swap(even, odd):
         return lax.ppermute(even, "slab", even_pairs), lax.ppermute(odd, "slab", odd_pairs)
 
-    right = jnp.asarray(band_right(width_z))
-    left = jnp.asarray(band_left(width_y))
-
-    blocks = [traces]
+    p0_even, p0_odd, q8_even, q8_odd, own = call(
+        "edges",
+        edges_kernel,
+        [state_now[0], adjoint_now[0], traces],
+        [edge] * 4 + [vmem(*traces.shape)],
+        [dma((5,))],
+        {0: HBM, 1: HBM, 2: HBM},
+    )
+    p_halo = swap(p0_even, p0_odd)
+    q_halo = swap(q8_even, q8_odd)
+    blocks = [own]
     bit = 1
     while bit < slabs:
-        held = blocks[0]
+        held = traces
         if len(blocks) > 1:
             (held,) = call("stack", stack_kernel, blocks, [vmem(bit, *traces.shape[1:])], micros=0)
         blocks.append(lax.ppermute(held, "slab", [(i, i ^ bit) for i in range(slabs)]))
         bit *= 2
-
-    p0_even, p0_odd, q8_even, q8_odd = call(
-        "edges", edges_kernel, [state_now[0], adjoint_now[0]], [edge] * 4, [dma((4,))], {0: HBM, 1: HBM}
-    )
-    p_halo = swap(p0_even, p0_odd)
-    q_halo = swap(q8_even, q8_odd)
     tiles = vmem(((count + 2 * reach) * width_y + 1) * 8, width_z)
     pair_of_parts = [part[False], part[True]]
-    *loaded, speed, where_to, zeros = call(
+    bands = [jnp.asarray(band_right(width_z)), jnp.asarray(band_left(width_y))]
+    *loaded, speed, right, left, where_to, zeros = call(
         "load",
         load_kernel,
-        [receivers, state_before[0], state_now[0], speed_term, held],
-        pair_of_parts * 2 + [field, VMEM((1, receivers.shape[2]), jnp.int32), tiles],
-        [VMEM(receivers.shape[1:], jnp.int32), dma((8,))],
-        {i: HBM for i in range(4)},
+        [receivers[0], state_before[0], state_now[0], speed_term, held, *bands],
+        pair_of_parts * 2
+        + [field, *(VMEM(band.shape, band.dtype) for band in bands)]
+        + [VMEM((1, receivers.shape[2]), jnp.int32), tiles],
+        [dma((9,))],
+        {i: HBM for i in (1, 2, 3, 5, 6)},
         micros=1,
     )
     p = {-1: loaded[0:2], 0: loaded[2:4]}
     q = {}
     laps, acc = {}, {False: None, True: None}
     inject = None
+    meets, met = (1, 3, 5), {}
 
     def forward(k, border, halos=(), after=()):
         last = k == steps - 1
+        token = border and k in meets
         parts = dict(
             border=border, moves=not last, stores=k < half, adds=k >= half, opens=k == half, step=k,
-            scale=scale, after=len(after) > 0,
+            scale=scale, after=len(after), token=token,
         )
         args = [*p[k], *halos, right, left]
         outs, scratch, spaces = [], [part[True]] if border else [], {}
@@ -495,6 +507,8 @@
             scratch += [SMEM(source.shape, jnp.int32), SMEM(wavelet.shape, jnp.float32), dma, dma]
             if border:
                 outs += [edge, edge]
+            if token:
+                outs += [vmem(8, width_z)]
         if parts["stores"]:
             outs += [part[border]]
         if parts["adds"]:
@@ -525,6 +539,8 @@
             return got
         p.setdefault(k + 1, [None, None])[border] = got.pop(0)
         sides = [got.pop(0), got.pop(0)] if border else None
+        if token:
+            met[k] = lax.ppermute(got.pop(0), "shot", [(i, i ^ 1) for i in range(shots)])
         if parts["stores"]:
             laps.setdefault(k, [None, None])[border] = got[0]
         else:
@@ -536,7 +552,7 @@
         t = steps - 1 - k
         parts = dict(
             border=border, adds=k >= half and not last, last=last, time=t, injects=k > 0, late=k == 1,
-            after=len(after) > 0,
+            after=len(after),
         )
         args = [*q[t + 1], *halos, right, left, q[t + 2][border], speed]
         outs, scratch, out_spaces, aliases = [part[border]], [part[True]] if border else [], {}, {}
@@ -601,6 +617,8 @@
             adjoint(1, False)
         forward(k + 1, False)
         first = [acc[False] if k + 1 == steps - 1 else p[k + 2][False]]
+        if k in meets:
+            first += [met[k]]
         q_halo = swap(*adjoint(k, True, q_halo, after=first))
         if 0 < k < steps - 2:
             adjoint(k + 1, False)

time: 119 us -> 118 us (level)
  local copies, waits for them, and re-layouts: 3.84 us -> 0.71 us
  starting transfers between devices: 70.3 us -> 67.6 us
  Pallas kernels: 36.9 us -> 39.1 us
  waiting for transfers between devices: 5.62 us -> 7.6 us
    unnamed x13 -> x1, local copies, waits for them, and re-layouts: 3.84 us -> 0.71 us
    ppermute x16, starting transfers between devices: 47 us -> 44.4 us  [swap(): lax.ppermute(even, 'slab', even_pairs)]
    pallas_call x39, Pallas kernels: 36.9 us -> 39.1 us  [call(): pl.pallas_call(kernel, out_shape=outs, in_specs=[spec(spaces.get(i, VMEM)...]
    ppermute x16, waiting for transfers between devices: 0.64 us -> 2.28 us  [swap(): lax.ppermute(even, 'slab', even_pairs)]
  transfers between devices with their start and end apart: 38 -> 41, of which waited for: 4 -> 8; matrix products, arithmetic and copies ran while one was open for 1% -> 1% of each run, Pallas kernels for 30% -> 32%
where the time goes in v8:
time: 118 us; the launch traced here: 116 us
  starting transfers between devices  67.6 us (57%)
  Pallas kernels  39.1 us (33%)
  waiting for transfers between devices  7.6 us (6%)
  between operations  1.28 us (1%)
    ppermute x16, starting transfers between devices, swap(): lax.ppermute(even, 'slab', even_pairs)  44.4 us
    pallas_call x39, Pallas kernels, call(): pl.pallas_call(kernel, out_shape=outs, in_specs=[spec(spaces.get(i, VMEM)...  39.1 us
    ppermute x16, starting transfers between devices, swap(): lax.ppermute(odd, 'slab', odd_pairs)  10.6 us
    ppermute x2, starting transfers between devices, body(): lax.ppermute(held, 'slab', [(i, i ^ bit) for i in range(slabs)])  8.7 us
    ppermute x3, waiting for transfers between devices, body(): lax.ppermute(pieces[m], 'shot', [(i, i ^ 2 * m) for i in range(shots)])  4.51 us
    ppermute x3, starting transfers between devices, body(): lax.ppermute(pieces[m], 'shot', [(i, i ^ 2 * m) for i in range(shots)])  3.55 us
  transfers between devices with their start and end apart: 41, of which 8 were waited for; matrix products, arithmetic and copies ran while one was open for 1% of the time, Pallas kernels for 32%

profile of v8, /device:TPU:0, one launch (start us, length us, event | category | flops | bytes accessed | tf_op | source)
XLA Modules:
  0.0 116.3 jit_solution(15699472020864496707)
XLA Ops:
  0.6 1.2 %edges.1 = (f32[4,128,128]{2,1,0:T(8,128)S(1)}, f32[4,128,128]{2,1,0:T(8,128)S(1)}, f32[4,128,128]{2,1,0:T(8,128)S(1)}, f32[4,128,128]{2,1,0:T(8,128)S(1)}, f32[1,8,256]{2,1,0:T(8,128)S(1)}) custom-call(f32[16,128,128]{2,1,0:T(8,128)} %bitcast.12, f32[16,128,128]{2,1,0:T(8,128)} %bitcast.14, f32[1,8,256]{2,1,0:T(8,128)} %refs_2_.2), custom_call_target="tpu_custom_call" | custom-call | flops 2000000000 | bytes 131072 | tf_op jit(solution)/shard_map/edges/pallas_call | solution.py:407
  1.9 3.1 %collective-permute-start.2 = (f32[4,128,128]{2,1,0:T(8,128)S(1)}, f32[4,128,128]{2,1,0:T(8,128)S(1)}, u32[]{:S(2)}, u32[]{:S(2)}) collective-permute-start(f32[4,128,128]{2,1,0:T(8,128)S(1)} %get-tuple-element.111), channel_id=1, source_target_pairs={{0,1},{1,0},{2,3},{3,2},{4,5},{5,4},{6,7},{7,6},{8,9},{9,8},{10,11... | collective-permute-start | bytes 786440 | tf_op jit(solution)/shard_map/ppermute | solution.py:454
  5.6 4.4 %collective-permute-start = (f32[1,8,256]{2,1,0:T(8,128)}, f32[1,8,256]{2,1,0:T(8,128)S(1)}, u32[]{:S(2)}, u32[]{:S(2)}) collective-permute-start(f32[1,8,256]{2,1,0:T(8,128)} %refs_2_.2), channel_id=1, source_target_pairs={{0,1},{1,0},{2,3},{3,2},{4,5},{5,4},{6,7},{7,6},{8,9},{9,8},{10,11... | collective-permute-start | bytes 24584 | tf_op jit(solution)/shard_map/ppermute | solution.py:472
  12.0 4.2 %collective-permute-start.1 = (f32[2,8,256]{2,1,0:T(8,128)S(1)}, f32[2,8,256]{2,1,0:T(8,128)S(1)}, u32[]{:S(2)}, u32[]{:S(2)}) collective-permute-start(f32[2,8,256]{2,1,0:T(8,128)S(1)} %stack.1.refs_3_), channel_id=1, source_target_pairs={{0,2},{1,3},{2,0},{3,1},{4,6},{5,7},{6,4},{7,5},{8,10},{9,11},{10,... | collective-permute-start | bytes 49160 | tf_op jit(solution)/shard_map/ppermute | solution.py:472
  16.3 2.0 %load.1 = (f32[8,128,128]{2,1,0:T(8,128)S(1)}, f32[8,128,128]{2,1,0:T(8,128)S(1)}, f32[8,128,128]{2,1,0:T(8,128)S(1)}, f32[8,128,128]{2,1,0:T(8,128)S(1)}, f32[1...) custom-call(s32[3,1024]{1,0:T(4,128)S(1)} %bitcast.9, ...), custom_call_target="tpu_custom_call" | custom-call | flops 1000000000 | bytes 65536 | tf_op jit(solution)/shard_map/load/pallas_call | solution.py:407
  22.0 1.6 %load_adjoint.1 = (f32[8,128,128]{2,1,0:T(8,128)S(1)}, f32[8,128,128]{2,1,0:T(8,128)S(1)}, f32[8,128,128]{2,1,0:T(8,128)S(1)}, f32[8,128,128]{2,1,0:T(8,128)S(1)}) custom-call(f32[16,128,128]{2,1,0:T(8,128)} %bitcast.16, f32[16,128,128]{2,1,0:T(8,128)} %bitcast.15, f32[8,128,128]{2,1,0:T(8,128)S(1)} %get-tuple-element.117.refs_2_.refs_1_.refs_6_), custom_call_target="tpu_custom_call" | custom-call | flops 1000000000 | bytes 65536 | tf_op jit(solution)/shard_map/load_adjoint/pallas_call | solution.py:407
  24.3 2.7 %collective-permute-start.8 = (f32[4,128,128]{2,1,0:T(8,128)S(1)}, f32[4,128,128]{2,1,0:T(8,128)S(1)}, u32[]{:S(2)}, u32[]{:S(2)}) collective-permute-start(f32[4,128,128]{2,1,0:T(8,128)S(1)} %get-tuple-element.135), channel_id=1, source_target_pairs={{0,1},{1,0},{2,3},{3,2},{4,5},{5,4},{6,7},{7,6},{8,9},{9,8},{10,11... | collective-permute-start | bytes 786440 | tf_op jit(solution)/shard_map/ppermute | solution.py:454
  29.3 3.3 %collective-permute-start.13 = (f32[4,128,128]{2,1,0:T(8,128)S(1)}, f32[4,128,128]{2,1,0:T(8,128)S(1)}, u32[]{:S(2)}, u32[]{:S(2)}) collective-permute-start(f32[4,128,128]{2,1,0:T(8,128)S(1)} %get-tuple-element.142), channel_id=1, source_target_pairs={{0,1},{1,0},{2,3},{3,2},{4,5},{5,4},{6,7},{7,6},{8,9},{9,8},{10,11... | collective-permute-start | bytes 786440 | tf_op jit(solution)/shard_map/ppermute | solution.py:454
  33.3 6.1 %receivers.1 = (f32[24584,128]{1,0:T(8,128)S(1)}, f32[8,128,128]{2,1,0:T(8,128)S(1)}, f32[8,128,128]{2,1,0:T(8,128)S(1)}) custom-call(s32[1,1024]{1,0:T(1,128)S(1)} %get-tuple-element.108.where_to, f32[1,8,256]{2,1,0:T(8,128)S(1)} %get-tuple-element.107.refs_0_, ...), custom_call_target="tpu_custom_call", output_to_operand_aliasing={{1}: (4, {}), {2}: (5, {}), {0}: (7, {})} | custom-call | tf_op jit(solution)/shard_map/receivers/pallas_call | solution.py:407
  40.9 0.9 adjoint_border.9
  41.9 2.1 %collective-permute-start.11 = (f32[4,128,128]{2,1,0:T(8,128)S(1)}, f32[4,128,128]{2,1,0:T(8,128)S(1)}, u32[]{:S(2)}, u32[]{:S(2)}) collective-permute-start(f32[4,128,128]{2,1,0:T(8,128)S(1)} %get-tuple-element.140), channel_id=1, source_target_pairs={{0,1},{1,0},{2,3},{3,2},{4,5},{5,4},{6,7},{7,6},{8,9},{9,8},{10,11... | collective-permute-start | bytes 786440 | tf_op jit(solution)/shard_map/ppermute | solution.py:454
  46.2 2.6 %collective-permute-start.17 = (f32[4,128,128]{2,1,0:T(8,128)S(1)}, f32[4,128,128]{2,1,0:T(8,128)S(1)}, u32[]{:S(2)}, u32[]{:S(2)}) collective-permute-start(f32[4,128,128]{2,1,0:T(8,128)S(1)} %get-tuple-element.149), channel_id=1, source_target_pairs={{0,1},{1,0},{2,3},{3,2},{4,5},{5,4},{6,7},{7,6},{8,9},{9,8},{10,11... | collective-permute-start | bytes 786440 | tf_op jit(solution)/shard_map/ppermute | solution.py:454
  51.0 1.0 adjoint_border.10
  52.0 3.7 %collective-permute-start.15 = (f32[4,128,128]{2,1,0:T(8,128)S(1)}, f32[4,128,128]{2,1,0:T(8,128)S(1)}, u32[]{:S(2)}, u32[]{:S(2)}) collective-permute-start(f32[4,128,128]{2,1,0:T(8,128)S(1)} %get-tuple-element.147), channel_id=1, source_target_pairs={{0,1},{1,0},{2,3},{3,2},{4,5},{5,4},{6,7},{7,6},{8,9},{9,8},{10,11... | collective-permute-start | bytes 786440 | tf_op jit(solution)/shard_map/ppermute | solution.py:454
  58.1 3.1 %collective-permute-start.22 = (f32[4,128,128]{2,1,0:T(8,128)S(1)}, f32[4,128,128]{2,1,0:T(8,128)S(1)}, u32[]{:S(2)}, u32[]{:S(2)}) collective-permute-start(f32[4,128,128]{2,1,0:T(8,128)S(1)} %get-tuple-element.161), channel_id=1, source_target_pairs={{0,1},{1,0},{2,3},{3,2},{4,5},{5,4},{6,7},{7,6},{8,9},{9,8},{10,11... | collective-permute-start | bytes 786440 | tf_op jit(solution)/shard_map/ppermute | solution.py:454
  63.5 2.9 %collective-permute-start.20 = (f32[4,128,128]{2,1,0:T(8,128)S(1)}, f32[4,128,128]{2,1,0:T(8,128)S(1)}, u32[]{:S(2)}, u32[]{:S(2)}) collective-permute-start(f32[4,128,128]{2,1,0:T(8,128)S(1)} %get-tuple-element.158), channel_id=1, source_target_pairs={{0,1},{1,0},{2,3},{3,2},{4,5},{5,4},{6,7},{7,6},{8,9},{9,8},{10,11... | collective-permute-start | bytes 786440 | tf_op jit(solution)/shard_map/ppermute | solution.py:454
  69.2 3.9 %collective-permute-start.26 = (f32[4,128,128]{2,1,0:T(8,128)S(1)}, f32[4,128,128]{2,1,0:T(8,128)S(1)}, u32[]{:S(2)}, u32[]{:S(2)}) collective-permute-start(f32[4,128,128]{2,1,0:T(8,128)S(1)} %get-tuple-element.174), channel_id=1, source_target_pairs={{0,1},{1,0},{2,3},{3,2},{4,5},{5,4},{6,7},{7,6},{8,9},{9,8},{10,11... | collective-permute-start | bytes 786440 | tf_op jit(solution)/shard_map/ppermute | solution.py:454
  74.5 0.9 adjoint_border.12
  75.4 3.3 %collective-permute-start.24 = (f32[4,128,128]{2,1,0:T(8,128)S(1)}, f32[4,128,128]{2,1,0:T(8,128)S(1)}, u32[]{:S(2)}, u32[]{:S(2)}) collective-permute-start(f32[4,128,128]{2,1,0:T(8,128)S(1)} %get-tuple-element.171), channel_id=1, source_target_pairs={{0,1},{1,0},{2,3},{3,2},{4,5},{5,4},{6,7},{7,6},{8,9},{9,8},{10,11... | collective-permute-start | bytes 786440 | tf_op jit(solution)/shard_map/ppermute | solution.py:454
  80.2 0.9 forward_border.13
  81.2 3.2 %collective-permute-start.31 = (f32[4,128,128]{2,1,0:T(8,128)S(1)}, f32[4,128,128]{2,1,0:T(8,128)S(1)}, u32[]{:S(2)}, u32[]{:S(2)}) collective-permute-start(f32[4,128,128]{2,1,0:T(8,128)S(1)} %get-tuple-element.189), channel_id=1, source_target_pairs={{0,1},{1,0},{2,3},{3,2},{4,5},{5,4},{6,7},{7,6},{8,9},{9,8},{10,11... | collective-permute-start | bytes 786440 | tf_op jit(solution)/shard_map/ppermute | solution.py:454
  85.9 0.9 adjoint_border.13
  86.8 2.9 %collective-permute-start.29 = (f32[4,128,128]{2,1,0:T(8,128)S(1)}, f32[4,128,128]{2,1,0:T(8,128)S(1)}, u32[]{:S(2)}, u32[]{:S(2)}) collective-permute-start(f32[4,128,128]{2,1,0:T(8,128)S(1)} %get-tuple-element.186), channel_id=1, source_target_pairs={{0,1},{1,0},{2,3},{3,2},{4,5},{5,4},{6,7},{7,6},{8,9},{9,8},{10,11... | collective-permute-start | bytes 786440 | tf_op jit(solution)/shard_map/ppermute | solution.py:454
  91.6 1.1 forward_border.14
  92.6 3.9 %collective-permute-start.35 = (f32[4,128,128]{2,1,0:T(8,128)S(1)}, f32[4,128,128]{2,1,0:T(8,128)S(1)}, u32[]{:S(2)}, u32[]{:S(2)}) collective-permute-start(f32[4,128,128]{2,1,0:T(8,128)S(1)} %get-tuple-element.201), channel_id=1, source_target_pairs={{0,1},{1,0},{2,3},{3,2},{4,5},{5,4},{6,7},{7,6},{8,9},{9,8},{10,11... | collective-permute-start | bytes 786440 | tf_op jit(solution)/shard_map/ppermute | solution.py:454
  97.9 0.9 adjoint_border.14
  98.8 3.0 %collective-permute-start.33 = (f32[4,128,128]{2,1,0:T(8,128)S(1)}, f32[4,128,128]{2,1,0:T(8,128)S(1)}, u32[]{:S(2)}, u32[]{:S(2)}) collective-permute-start(f32[4,128,128]{2,1,0:T(8,128)S(1)} %get-tuple-element.197), channel_id=1, source_target_pairs={{0,1},{1,0},{2,3},{3,2},{4,5},{5,4},{6,7},{7,6},{8,9},{9,8},{10,11... | collective-permute-start | bytes 786440 | tf_op jit(solution)/shard_map/ppermute | solution.py:454
  103.9 1.6 %adjoint_inner.15 = (f32[16,128,128]{2,1,0:T(8,128)}, f32[16,128,128]{2,1,0:T(8,128)}) custom-call(f32[8,128,128]{2,1,0:T(8,128)S(1)} %get-tuple-element.185.refs_12_.refs_6_.refs_0_, f32[8,128,128]{2,1,0:T(8,128)S(1)} %get-tuple-element.196.refs_1_.refs_8_, bf16[256,256]{1,0:T(8,128)(2,1)S(1)} %get-tuple-element.113.refs_4_.refs_2_, ...), custom_call_target="tpu_custom_call" | custom-call | flops 30000001024 | bytes 1966080 | tf_op jit(solution)/shard_map/adjoint_inner/pallas_call | solution.py:407
  105.9 1.5 %collective-permute-start.38 = (f32[16,16,128]{2,1,0:T(8,128)S(1)}, f32[16,16,128]{2,1,0:T(8,128)S(1)}, u32[]{:S(2)}, u32[]{:S(2)}) collective-permute-start(f32[16,16,128]{2,1,0:T(8,128)S(1)} %get-tuple-element.208), channel_id=1, source_target_pairs={{0,8},{4,12},{8,0},{12,4},{16,24},{20,28},{24,16},{28,20},{1,9},{5... | collective-permute-start | bytes 393224 | tf_op jit(solution)/shard_map/ppermute | solution.py:633
  107.4 1.5 %collective-permute-start.39 = (f32[16,16,128]{2,1,0:T(8,128)S(1)}, f32[16,16,128]{2,1,0:T(8,128)S(1)}, u32[]{:S(2)}, u32[]{:S(2)}) collective-permute-start(f32[16,16,128]{2,1,0:T(8,128)S(1)} %get-tuple-element.209), channel_id=1, source_target_pairs={{0,16},{4,20},{8,24},{12,28},{16,0},{20,4},{24,8},{28,12},{1,17},{... | collective-permute-start | bytes 393224 | tf_op jit(solution)/shard_map/ppermute | solution.py:633
  109.4 1.6 %adjoint_border.15 = f32[16,128,128]{2,1,0:T(8,128)} custom-call(f32[8,128,128]{2,1,0:T(8,128)S(1)} %get-tuple-element.185.refs_12_.refs_6_.refs_0_, f32[8,128,128]{2,1,0:T(8,128)S(1)} %get-tuple-element.196.refs_1_.refs_8_, f32[4,128,128]{2,1,0:T(8,128)S(1)} %collective-permute-done.33.refs_2_, ...), custom_call_target="tpu_custom_call", output_to_operand_aliasing={{}: (9, {})} | custom-call | flops 30000001024 | bytes 1966080 | tf_op jit(solution)/shard_map/adjoint_border/pallas_call | solution.py:407
  111.9 3.7 %collective-permute-done.39.refs_2_ = f32[16,16,128]{2,1,0:T(8,128)S(1)} collective-permute-done((f32[16,16,128]{2,1,0:T(8,128)S(1)}, f32[16,16,128]{2,1,0:T(8,128)S(1)}, u32[]{:S(2)}, u32[]{:S(2)}) %collective-permute-start.39) | collective-permute-done | bytes 131104 | tf_op jit(solution)/shard_map/ppermute | solution.py:633
  (90 shorter events, 35.2 us)
Async XLA Ops:
  1.9 17.2 %collective-permute-start.2 = (f32[4,128,128]{2,1,0:T(8,128)S(1)}, f32[4,128,128]{2,1,0:T(8,128)S(1)}, u32[]{:S(2)}, u32[]{:S(2)}) collective-permute-start(f32[4,128,128]{2,1,0:T(8,128)S(1)} %get-tuple-element.111), channel_id=1, source_target_pairs={{0,1},{1,0},{2,3},{3,2},{4,5},{5,4},{6,7},{7,6},{8,9},{9,8},{10,11... | collective-permute-start | bytes 786440 | tf_op jit(solution)/shard_map/ppermute | solution.py:454
  5.0 14.1 %collective-permute-start.3 = (f32[4,128,128]{2,1,0:T(8,128)S(1)}, f32[4,128,128]{2,1,0:T(8,128)S(1)}, u32[]{:S(2)}, u32[]{:S(2)}) collective-permute-start(f32[4,128,128]{2,1,0:T(8,128)S(1)} %get-tuple-element.112), channel_id=1, source_target_pairs={{1,2},{2,1},{5,6},{6,5},{9,10},{10,9},{13,14},{14,13},{17,18},{18,... | collective-permute-start | bytes 786440 | tf_op jit(solution)/shard_map/ppermute | solution.py:454
  10.1 13.5 %collective-permute-start.4 = (f32[4,128,128]{2,1,0:T(8,128)S(1)}, f32[4,128,128]{2,1,0:T(8,128)S(1)}, u32[]{:S(2)}, u32[]{:S(2)}) collective-permute-start(f32[4,128,128]{2,1,0:T(8,128)S(1)} %get-tuple-element.121), channel_id=1, source_target_pairs={{0,1},{1,0},{2,3},{3,2},{4,5},{5,4},{6,7},{7,6},{8,9},{9,8},{10,11... | collective-permute-start | bytes 786440 | tf_op jit(solution)/shard_map/ppermute | solution.py:454
  10.2 13.4 %collective-permute-start.5 = (f32[4,128,128]{2,1,0:T(8,128)S(1)}, f32[4,128,128]{2,1,0:T(8,128)S(1)}, u32[]{:S(2)}, u32[]{:S(2)}) collective-permute-start(f32[4,128,128]{2,1,0:T(8,128)S(1)} %get-tuple-element.122), channel_id=1, source_target_pairs={{1,2},{2,1},{5,6},{6,5},{9,10},{10,9},{13,14},{14,13},{17,18},{18,... | collective-permute-start | bytes 786440 | tf_op jit(solution)/shard_map/ppermute | solution.py:454
  12.0 20.6 %collective-permute-start.1 = (f32[2,8,256]{2,1,0:T(8,128)S(1)}, f32[2,8,256]{2,1,0:T(8,128)S(1)}, u32[]{:S(2)}, u32[]{:S(2)}) collective-permute-start(f32[2,8,256]{2,1,0:T(8,128)S(1)} %stack.1.refs_3_), channel_id=1, source_target_pairs={{0,2},{1,3},{2,0},{3,1},{4,6},{5,7},{6,4},{7,5},{8,10},{9,11},{10,... | collective-permute-start | bytes 49160 | tf_op jit(solution)/shard_map/ppermute | solution.py:472
  19.9 8.5 %collective-permute-start.6 = (f32[4,128,128]{2,1,0:T(8,128)S(1)}, f32[4,128,128]{2,1,0:T(8,128)S(1)}, u32[]{:S(2)}, u32[]{:S(2)}) collective-permute-start(f32[4,128,128]{2,1,0:T(8,128)S(1)} %get-tuple-element.128), channel_id=1, source_target_pairs={{0,1},{1,0},{2,3},{3,2},{4,5},{5,4},{6,7},{7,6},{8,9},{9,8},{10,11... | collective-permute-start | bytes 786440 | tf_op jit(solution)/shard_map/ppermute | solution.py:454
  20.6 7.8 %collective-permute-start.7 = (f32[4,128,128]{2,1,0:T(8,128)S(1)}, f32[4,128,128]{2,1,0:T(8,128)S(1)}, u32[]{:S(2)}, u32[]{:S(2)}) collective-permute-start(f32[4,128,128]{2,1,0:T(8,128)S(1)} %get-tuple-element.129), channel_id=1, source_target_pairs={{1,2},{2,1},{5,6},{6,5},{9,10},{10,9},{13,14},{14,13},{17,18},{18,... | collective-permute-start | bytes 786440 | tf_op jit(solution)/shard_map/ppermute | solution.py:454
  24.3 16.6 %collective-permute-start.8 = (f32[4,128,128]{2,1,0:T(8,128)S(1)}, f32[4,128,128]{2,1,0:T(8,128)S(1)}, u32[]{:S(2)}, u32[]{:S(2)}) collective-permute-start(f32[4,128,128]{2,1,0:T(8,128)S(1)} %get-tuple-element.135), channel_id=1, source_target_pairs={{0,1},{1,0},{2,3},{3,2},{4,5},{5,4},{6,7},{7,6},{8,9},{9,8},{10,11... | collective-permute-start | bytes 786440 | tf_op jit(solution)/shard_map/ppermute | solution.py:454
  27.0 13.9 %collective-permute-start.9 = (f32[4,128,128]{2,1,0:T(8,128)S(1)}, f32[4,128,128]{2,1,0:T(8,128)S(1)}, u32[]{:S(2)}, u32[]{:S(2)}) collective-permute-start(f32[4,128,128]{2,1,0:T(8,128)S(1)} %get-tuple-element.136), channel_id=1, source_target_pairs={{1,2},{2,1},{5,6},{6,5},{9,10},{10,9},{13,14},{14,13},{17,18},{18,... | collective-permute-start | bytes 786440 | tf_op jit(solution)/shard_map/ppermute | solution.py:454
  29.2 11.7 %collective-permute-start.10 = (f32[8,128]{1,0:T(8,128)S(1)}, f32[8,128]{1,0:T(8,128)S(1)}, u32[]{:S(2)}, u32[]{:S(2)}) collective-permute-start(f32[8,128]{1,0:T(8,128)S(1)} %get-tuple-element.138), channel_id=1, source_target_pairs={{0,4},{4,0},{8,12},{12,8},{16,20},{20,16},{24,28},{28,24},{1,5},{5... | collective-permute-start | bytes 12296 | tf_op jit(solution)/shard_map/ppermute | solution.py:543
  29.3 16.1 %collective-permute-start.13 = (f32[4,128,128]{2,1,0:T(8,128)S(1)}, f32[4,128,128]{2,1,0:T(8,128)S(1)}, u32[]{:S(2)}, u32[]{:S(2)}) collective-permute-start(f32[4,128,128]{2,1,0:T(8,128)S(1)} %get-tuple-element.142), channel_id=1, source_target_pairs={{0,1},{1,0},{2,3},{3,2},{4,5},{5,4},{6,7},{7,6},{8,9},{9,8},{10,11... | collective-permute-start | bytes 786440 | tf_op jit(solution)/shard_map/ppermute | solution.py:454
  32.6 12.8 %collective-permute-start.14 = (f32[4,128,128]{2,1,0:T(8,128)S(1)}, f32[4,128,128]{2,1,0:T(8,128)S(1)}, u32[]{:S(2)}, u32[]{:S(2)}) collective-permute-start(f32[4,128,128]{2,1,0:T(8,128)S(1)} %get-tuple-element.143), channel_id=1, source_target_pairs={{1,2},{2,1},{5,6},{6,5},{9,10},{10,9},{13,14},{14,13},{17,18},{18,... | collective-permute-start | bytes 786440 | tf_op jit(solution)/shard_map/ppermute | solution.py:454
  41.9 9.1 %collective-permute-start.11 = (f32[4,128,128]{2,1,0:T(8,128)S(1)}, f32[4,128,128]{2,1,0:T(8,128)S(1)}, u32[]{:S(2)}, u32[]{:S(2)}) collective-permute-start(f32[4,128,128]{2,1,0:T(8,128)S(1)} %get-tuple-element.140), channel_id=1, source_target_pairs={{0,1},{1,0},{2,3},{3,2},{4,5},{5,4},{6,7},{7,6},{8,9},{9,8},{10,11... | collective-permute-start | bytes 786440 | tf_op jit(solution)/shard_map/ppermute | solution.py:454
  46.2 10.9 %collective-permute-start.17 = (f32[4,128,128]{2,1,0:T(8,128)S(1)}, f32[4,128,128]{2,1,0:T(8,128)S(1)}, u32[]{:S(2)}, u32[]{:S(2)}) collective-permute-start(f32[4,128,128]{2,1,0:T(8,128)S(1)} %get-tuple-element.149), channel_id=1, source_target_pairs={{0,1},{1,0},{2,3},{3,2},{4,5},{5,4},{6,7},{7,6},{8,9},{9,8},{10,11... | collective-permute-start | bytes 786440 | tf_op jit(solution)/shard_map/ppermute | solution.py:454
  48.9 8.3 %collective-permute-start.18 = (f32[4,128,128]{2,1,0:T(8,128)S(1)}, f32[4,128,128]{2,1,0:T(8,128)S(1)}, u32[]{:S(2)}, u32[]{:S(2)}) collective-permute-start(f32[4,128,128]{2,1,0:T(8,128)S(1)} %get-tuple-element.150), channel_id=1, source_target_pairs={{1,2},{2,1},{5,6},{6,5},{9,10},{10,9},{13,14},{14,13},{17,18},{18,... | collective-permute-start | bytes 786440 | tf_op jit(solution)/shard_map/ppermute | solution.py:454
  52.0 10.5 %collective-permute-start.15 = (f32[4,128,128]{2,1,0:T(8,128)S(1)}, f32[4,128,128]{2,1,0:T(8,128)S(1)}, u32[]{:S(2)}, u32[]{:S(2)}) collective-permute-start(f32[4,128,128]{2,1,0:T(8,128)S(1)} %get-tuple-element.147), channel_id=1, source_target_pairs={{0,1},{1,0},{2,3},{3,2},{4,5},{5,4},{6,7},{7,6},{8,9},{9,8},{10,11... | collective-permute-start | bytes 786440 | tf_op jit(solution)/shard_map/ppermute | solution.py:454
  58.1 10.2 %collective-permute-start.22 = (f32[4,128,128]{2,1,0:T(8,128)S(1)}, f32[4,128,128]{2,1,0:T(8,128)S(1)}, u32[]{:S(2)}, u32[]{:S(2)}) collective-permute-start(f32[4,128,128]{2,1,0:T(8,128)S(1)} %get-tuple-element.161), channel_id=1, source_target_pairs={{0,1},{1,0},{2,3},{3,2},{4,5},{5,4},{6,7},{7,6},{8,9},{9,8},{10,11... | collective-permute-start | bytes 786440 | tf_op jit(solution)/shard_map/ppermute | solution.py:454
  61.2 7.2 %collective-permute-start.23 = (f32[4,128,128]{2,1,0:T(8,128)S(1)}, f32[4,128,128]{2,1,0:T(8,128)S(1)}, u32[]{:S(2)}, u32[]{:S(2)}) collective-permute-start(f32[4,128,128]{2,1,0:T(8,128)S(1)} %get-tuple-element.162), channel_id=1, source_target_pairs={{1,2},{2,1},{5,6},{6,5},{9,10},{10,9},{13,14},{14,13},{17,18},{18,... | collective-permute-start | bytes 786440 | tf_op jit(solution)/shard_map/ppermute | solution.py:454
  63.5 11.0 %collective-permute-start.20 = (f32[4,128,128]{2,1,0:T(8,128)S(1)}, f32[4,128,128]{2,1,0:T(8,128)S(1)}, u32[]{:S(2)}, u32[]{:S(2)}) collective-permute-start(f32[4,128,128]{2,1,0:T(8,128)S(1)} %get-tuple-element.158), channel_id=1, source_target_pairs={{0,1},{1,0},{2,3},{3,2},{4,5},{5,4},{6,7},{7,6},{8,9},{9,8},{10,11... | collective-permute-start | bytes 786440 | tf_op jit(solution)/shard_map/ppermute | solution.py:454
  66.3 8.2 %collective-permute-start.21 = (f32[4,128,128]{2,1,0:T(8,128)S(1)}, f32[4,128,128]{2,1,0:T(8,128)S(1)}, u32[]{:S(2)}, u32[]{:S(2)}) collective-permute-start(f32[4,128,128]{2,1,0:T(8,128)S(1)} %get-tuple-element.159), channel_id=1, source_target_pairs={{1,2},{2,1},{5,6},{6,5},{9,10},{10,9},{13,14},{14,13},{17,18},{18,... | collective-permute-start | bytes 786440 | tf_op jit(solution)/shard_map/ppermute | solution.py:454
  69.2 11.1 %collective-permute-start.26 = (f32[4,128,128]{2,1,0:T(8,128)S(1)}, f32[4,128,128]{2,1,0:T(8,128)S(1)}, u32[]{:S(2)}, u32[]{:S(2)}) collective-permute-start(f32[4,128,128]{2,1,0:T(8,128)S(1)} %get-tuple-element.174), channel_id=1, source_target_pairs={{0,1},{1,0},{2,3},{3,2},{4,5},{5,4},{6,7},{7,6},{8,9},{9,8},{10,11... | collective-permute-start | bytes 786440 | tf_op jit(solution)/shard_map/ppermute | solution.py:454
  73.1 7.2 %collective-permute-start.27 = (f32[4,128,128]{2,1,0:T(8,128)S(1)}, f32[4,128,128]{2,1,0:T(8,128)S(1)}, u32[]{:S(2)}, u32[]{:S(2)}) collective-permute-start(f32[4,128,128]{2,1,0:T(8,128)S(1)} %get-tuple-element.175), channel_id=1, source_target_pairs={{1,2},{2,1},{5,6},{6,5},{9,10},{10,9},{13,14},{14,13},{17,18},{18,... | collective-permute-start | bytes 786440 | tf_op jit(solution)/shard_map/ppermute | solution.py:454
  75.4 10.4 %collective-permute-start.24 = (f32[4,128,128]{2,1,0:T(8,128)S(1)}, f32[4,128,128]{2,1,0:T(8,128)S(1)}, u32[]{:S(2)}, u32[]{:S(2)}) collective-permute-start(f32[4,128,128]{2,1,0:T(8,128)S(1)} %get-tuple-element.171), channel_id=1, source_target_pairs={{0,1},{1,0},{2,3},{3,2},{4,5},{5,4},{6,7},{7,6},{8,9},{9,8},{10,11... | collective-permute-start | bytes 786440 | tf_op jit(solution)/shard_map/ppermute | solution.py:454
  78.8 7.1 %collective-permute-start.25 = (f32[4,128,128]{2,1,0:T(8,128)S(1)}, f32[4,128,128]{2,1,0:T(8,128)S(1)}, u32[]{:S(2)}, u32[]{:S(2)}) collective-permute-start(f32[4,128,128]{2,1,0:T(8,128)S(1)} %get-tuple-element.172), channel_id=1, source_target_pairs={{1,2},{2,1},{5,6},{6,5},{9,10},{10,9},{13,14},{14,13},{17,18},{18,... | collective-permute-start | bytes 786440 | tf_op jit(solution)/shard_map/ppermute | solution.py:454
  81.2 10.3 %collective-permute-start.31 = (f32[4,128,128]{2,1,0:T(8,128)S(1)}, f32[4,128,128]{2,1,0:T(8,128)S(1)}, u32[]{:S(2)}, u32[]{:S(2)}) collective-permute-start(f32[4,128,128]{2,1,0:T(8,128)S(1)} %get-tuple-element.189), channel_id=1, source_target_pairs={{0,1},{1,0},{2,3},{3,2},{4,5},{5,4},{6,7},{7,6},{8,9},{9,8},{10,11... | collective-permute-start | bytes 786440 | tf_op jit(solution)/shard_map/ppermute | solution.py:454
  84.4 7.2 %collective-permute-start.32 = (f32[4,128,128]{2,1,0:T(8,128)S(1)}, f32[4,128,128]{2,1,0:T(8,128)S(1)}, u32[]{:S(2)}, u32[]{:S(2)}) collective-permute-start(f32[4,128,128]{2,1,0:T(8,128)S(1)} %get-tuple-element.190), channel_id=1, source_target_pairs={{1,2},{2,1},{5,6},{6,5},{9,10},{10,9},{13,14},{14,13},{17,18},{18,... | collective-permute-start | bytes 786440 | tf_op jit(solution)/shard_map/ppermute | solution.py:454
  86.8 11.1 %collective-permute-start.29 = (f32[4,128,128]{2,1,0:T(8,128)S(1)}, f32[4,128,128]{2,1,0:T(8,128)S(1)}, u32[]{:S(2)}, u32[]{:S(2)}) collective-permute-start(f32[4,128,128]{2,1,0:T(8,128)S(1)} %get-tuple-element.186), channel_id=1, source_target_pairs={{0,1},{1,0},{2,3},{3,2},{4,5},{5,4},{6,7},{7,6},{8,9},{9,8},{10,11... | collective-permute-start | bytes 786440 | tf_op jit(solution)/shard_map/ppermute | solution.py:454
  89.7 8.2 %collective-permute-start.30 = (f32[4,128,128]{2,1,0:T(8,128)S(1)}, f32[4,128,128]{2,1,0:T(8,128)S(1)}, u32[]{:S(2)}, u32[]{:S(2)}) collective-permute-start(f32[4,128,128]{2,1,0:T(8,128)S(1)} %get-tuple-element.187), channel_id=1, source_target_pairs={{1,2},{2,1},{5,6},{6,5},{9,10},{10,9},{13,14},{14,13},{17,18},{18,... | collective-permute-start | bytes 786440 | tf_op jit(solution)/shard_map/ppermute | solution.py:454
  92.6 10.4 %collective-permute-start.35 = (f32[4,128,128]{2,1,0:T(8,128)S(1)}, f32[4,128,128]{2,1,0:T(8,128)S(1)}, u32[]{:S(2)}, u32[]{:S(2)}) collective-permute-start(f32[4,128,128]{2,1,0:T(8,128)S(1)} %get-tuple-element.201), channel_id=1, source_target_pairs={{0,1},{1,0},{2,3},{3,2},{4,5},{5,4},{6,7},{7,6},{8,9},{9,8},{10,11... | collective-permute-start | bytes 786440 | tf_op jit(solution)/shard_map/ppermute | solution.py:454
  98.8 10.7 %collective-permute-start.33 = (f32[4,128,128]{2,1,0:T(8,128)S(1)}, f32[4,128,128]{2,1,0:T(8,128)S(1)}, u32[]{:S(2)}, u32[]{:S(2)}) collective-permute-start(f32[4,128,128]{2,1,0:T(8,128)S(1)} %get-tuple-element.197), channel_id=1, source_target_pairs={{0,1},{1,0},{2,3},{3,2},{4,5},{5,4},{6,7},{7,6},{8,9},{9,8},{10,11... | collective-permute-start | bytes 786440 | tf_op jit(solution)/shard_map/ppermute | solution.py:454
  101.8 7.7 %collective-permute-start.34 = (f32[4,128,128]{2,1,0:T(8,128)S(1)}, f32[4,128,128]{2,1,0:T(8,128)S(1)}, u32[]{:S(2)}, u32[]{:S(2)}) collective-permute-start(f32[4,128,128]{2,1,0:T(8,128)S(1)} %get-tuple-element.198), channel_id=1, source_target_pairs={{1,2},{2,1},{5,6},{6,5},{9,10},{10,9},{13,14},{14,13},{17,18},{18,... | collective-permute-start | bytes 786440 | tf_op jit(solution)/shard_map/ppermute | solution.py:454
  107.4 8.2 %collective-permute-start.39 = (f32[16,16,128]{2,1,0:T(8,128)S(1)}, f32[16,16,128]{2,1,0:T(8,128)S(1)}, u32[]{:S(2)}, u32[]{:S(2)}) collective-permute-start(f32[16,16,128]{2,1,0:T(8,128)S(1)} %get-tuple-element.209), channel_id=1, source_target_pairs={{0,16},{4,20},{8,24},{12,28},{16,0},{20,4},{24,8},{28,12},{1,17},{... | collective-permute-start | bytes 393224 | tf_op jit(solution)/shard_map/ppermute | solution.py:633
  (9 other events, 50.7 us)

commit v9 on v8

--- a/solution.py
+++ b/solution.py
@@ -126,7 +126,6 @@
         next(it)
     nxt = next(it) if moves else None
     even_out, odd_out = (next(it), next(it)) if moves and border else (None, None)
-    token = next(it) if parts["token"] else None
     lap_out = next(it) if stores else None
     acc_out = next(it) if adds and moves else None
     send, keep = (next(it), next(it)) if border and not moves else (None, None)
@@ -182,8 +181,6 @@
 
         if border:
             emit_edges(parity, nxt, even_out, odd_out)
-        if parts["token"]:
-            token[...] = nxt[0, :8, :]
     elif border:
         chunk = send.shape[2]
         mine = lax.axis_index("shot") % 2
@@ -336,7 +333,7 @@
     blocks, refs = refs[:levels], refs[levels:]
     inner, outer, _, _, out, inner_out, outer_out = refs
     per = blocks[0].shape[-1]
-    group, groups = 8, 4
+    group, groups = 8, 8
     slab = lax.axis_index("slab")
     lanes = lax.broadcasted_iota(jnp.int32, (8, 128), 1)
     d = 0
@@ -349,26 +346,33 @@
 
                 @pl.loop(0, 128 // (group * groups))
                 def _(i):
-                    tiles, terms, slots = [], [], []
-                    for u in range(group * groups):
-                        j = i * (group * groups) + u
-                        flat = where_to[0, base + part * 128 + j]
-                        lane = flat & 127
-                        tile = flat >> 7
-                        moved = pltpu.roll(block, (lane - j) & 127, 1)
-                        tiles.append(jnp.full((8, 128), tile, jnp.int32))
-                        terms.append(jnp.where(lanes == lane, moved, 0.0))
-                        slots.append(pl.ds(pl.multiple_of(tile * 8, 8), 8))
+                    def gather(g):
+                        tiles, terms, slots = [], [], []
+                        for u in range(g * group, (g + 1) * group):
+                            j = i * (group * groups) + u
+                            flat = where_to[0, base + part * 128 + j]
+                            lane = flat & 127
+                            tile = flat >> 7
+                            moved = pltpu.roll(block, (lane - j) & 127, 1)
+                            tiles.append(jnp.full((8, 128), tile, jnp.int32))
+                            terms.append(jnp.where(lanes == lane, moved, 0.0))
+                            slots.append(pl.ds(pl.multiple_of(tile * 8, 8), 8))
+                        return tiles, terms, slots
+
+                    ahead = [gather(0), gather(1)]
                     for g in range(groups):
-                        own = range(g * group, (g + 1) * group)
-                        held = {u: out[slots[u], :] for u in own}
-                        for u in own:
+                        tiles, terms, slots = ahead.pop(0)
+                        if g + 2 < groups:
+                            ahead.append(gather(g + 2))
+                        held = [out[slot, :] for slot in slots]
+                        for u in range(group):
                             value = held[u] + terms[u]
-                            for w in range(g * group, u):
+                            for w in range(u):
                                 value = value + jnp.where(tiles[w] == tiles[u], terms[w], 0.0)
                             held[u] = value
-                        for u in own:
+                        for u in range(group):
                             out[slots[u], :] = held[u]
+
     count, width_y = inner.shape[0] + 2 * reach, inner.shape[1]
     for part, part_out, border in ((inner, inner_out, False), (outer, outer_out, True)):
         for i, x in enumerate(rows_of(count, border)):
@@ -489,14 +493,12 @@
     q = {}
     laps, acc = {}, {False: None, True: None}
     inject = None
-    meets, met = (1, 3, 5), {}
 
     def forward(k, border, halos=(), after=()):
         last = k == steps - 1
-        token = border and k in meets
         parts = dict(
             border=border, moves=not last, stores=k < half, adds=k >= half, opens=k == half, step=k,
-            scale=scale, after=len(after), token=token,
+            scale=scale, after=len(after),
         )
         args = [*p[k], *halos, right, left]
         outs, scratch, spaces = [], [part[True]] if border else [], {}
@@ -507,8 +509,6 @@
             scratch += [SMEM(source.shape, jnp.int32), SMEM(wavelet.shape, jnp.float32), dma, dma]
             if border:
                 outs += [edge, edge]
-            if token:
-                outs += [vmem(8, width_z)]
         if parts["stores"]:
             outs += [part[border]]
         if parts["adds"]:
@@ -539,8 +539,6 @@
             return got
         p.setdefault(k + 1, [None, None])[border] = got.pop(0)
         sides = [got.pop(0), got.pop(0)] if border else None
-        if token:
-            met[k] = lax.ppermute(got.pop(0), "shot", [(i, i ^ 1) for i in range(shots)])
         if parts["stores"]:
             laps.setdefault(k, [None, None])[border] = got[0]
         else:
@@ -617,8 +615,6 @@
             adjoint(1, False)
         forward(k + 1, False)
         first = [acc[False] if k + 1 == steps - 1 else p[k + 2][False]]
-        if k in meets:
-            first += [met[k]]
         q_halo = swap(*adjoint(k, True, q_halo, after=first))
         if 0 < k < steps - 2:
             adjoint(k + 1, False)

time: 118 us -> 115 us (0.975); the launches traced: 116 us -> 115 us
  Pallas kernels: 39.1 us -> 36.2 us
  starting transfers between devices: 67.6 us -> 69.9 us
    pallas_call x39, Pallas kernels: 39.1 us -> 36.2 us  [call(): pl.pallas_call(kernel, out_shape=outs, in_specs=[spec(spaces.get(i, VMEM)...]
    ppermute x16, starting transfers between devices: 44.4 us -> 46.7 us  [swap(): lax.ppermute(even, 'slab', even_pairs)]
  transfers between devices with their start and end apart: 41 -> 38, of which waited for: 8 -> 5; matrix products, arithmetic and copies ran while one was open for 1% -> 1% of each run, Pallas kernels for 32% -> 30%
where the time goes in v9:
time: 115 us
  starting transfers between devices  69.9 us (61%)
  Pallas kernels  36.2 us (31%)
  waiting for transfers between devices  6.58 us (6%)
  between operations  1.29 us (1%)
    ppermute x16, starting transfers between devices, swap(): lax.ppermute(even, 'slab', even_pairs)  46.7 us
    pallas_call x39, Pallas kernels, call(): pl.pallas_call(kernel, out_shape=outs, in_specs=[spec(spaces.get(i, VMEM)...  36.2 us
    ppermute x16, starting transfers between devices, swap(): lax.ppermute(odd, 'slab', odd_pairs)  10.9 us
    ppermute x2, starting transfers between devices, body(): lax.ppermute(held, 'slab', [(i, i ^ bit) for i in range(slabs)])  8.7 us
    ppermute x3, waiting for transfers between devices, body(): lax.ppermute(pieces[m], 'shot', [(i, i ^ 2 * m) for i in range(shots)])  4.58 us
    ppermute x3, starting transfers between devices, body(): lax.ppermute(pieces[m], 'shot', [(i, i ^ 2 * m) for i in range(shots)])  3.55 us
  transfers between devices with their start and end apart: 38, of which 5 were waited for; matrix products, arithmetic and copies ran while one was open for 1% of the time, Pallas kernels for 30%

profile of v9, /device:TPU:0, one launch (start us, length us, event | category | flops | bytes accessed | tf_op | source)
XLA Modules:
  0.0 114.7 jit_solution(8979900991803280489)
XLA Ops:
  0.6 1.2 %edges.1 = (f32[4,128,128]{2,1,0:T(8,128)S(1)}, f32[4,128,128]{2,1,0:T(8,128)S(1)}, f32[4,128,128]{2,1,0:T(8,128)S(1)}, f32[4,128,128]{2,1,0:T(8,128)S(1)}, f32[1,8,256]{2,1,0:T(8,128)S(1)}) custom-call(f32[16,128,128]{2,1,0:T(8,128)} %bitcast.12, f32[16,128,128]{2,1,0:T(8,128)} %bitcast.14, f32[1,8,256]{2,1,0:T(8,128)} %refs_2_.2), custom_call_target="tpu_custom_call" | custom-call | flops 2000000000 | bytes 131072 | tf_op jit(solution)/shard_map/edges/pallas_call | solution.py:411
  1.9 3.1 %collective-permute-start.2 = (f32[4,128,128]{2,1,0:T(8,128)S(1)}, f32[4,128,128]{2,1,0:T(8,128)S(1)}, u32[]{:S(2)}, u32[]{:S(2)}) collective-permute-start(f32[4,128,128]{2,1,0:T(8,128)S(1)} %get-tuple-element.108), channel_id=1, source_target_pairs={{0,1},{1,0},{2,3},{3,2},{4,5},{5,4},{6,7},{7,6},{8,9},{9,8},{10,11... | collective-permute-start | bytes 786440 | tf_op jit(solution)/shard_map/ppermute | solution.py:458
  5.6 4.4 %collective-permute-start = (f32[1,8,256]{2,1,0:T(8,128)}, f32[1,8,256]{2,1,0:T(8,128)S(1)}, u32[]{:S(2)}, u32[]{:S(2)}) collective-permute-start(f32[1,8,256]{2,1,0:T(8,128)} %refs_2_.2), channel_id=1, source_target_pairs={{0,1},{1,0},{2,3},{3,2},{4,5},{5,4},{6,7},{7,6},{8,9},{9,8},{10,11... | collective-permute-start | bytes 24584 | tf_op jit(solution)/shard_map/ppermute | solution.py:476
  12.0 4.2 %collective-permute-start.1 = (f32[2,8,256]{2,1,0:T(8,128)S(1)}, f32[2,8,256]{2,1,0:T(8,128)S(1)}, u32[]{:S(2)}, u32[]{:S(2)}) collective-permute-start(f32[2,8,256]{2,1,0:T(8,128)S(1)} %stack.1.refs_3_), channel_id=1, source_target_pairs={{0,2},{1,3},{2,0},{3,1},{4,6},{5,7},{6,4},{7,5},{8,10},{9,11},{10,... | collective-permute-start | bytes 49160 | tf_op jit(solution)/shard_map/ppermute | solution.py:476
  16.3 2.0 %load.1 = (f32[8,128,128]{2,1,0:T(8,128)S(1)}, f32[8,128,128]{2,1,0:T(8,128)S(1)}, f32[8,128,128]{2,1,0:T(8,128)S(1)}, f32[8,128,128]{2,1,0:T(8,128)S(1)}, f32[1...) custom-call(s32[3,1024]{1,0:T(4,128)S(1)} %bitcast.9, ...), custom_call_target="tpu_custom_call" | custom-call | flops 1000000000 | bytes 65536 | tf_op jit(solution)/shard_map/load/pallas_call | solution.py:411
  21.9 1.6 %load_adjoint.1 = (f32[8,128,128]{2,1,0:T(8,128)S(1)}, f32[8,128,128]{2,1,0:T(8,128)S(1)}, f32[8,128,128]{2,1,0:T(8,128)S(1)}, f32[8,128,128]{2,1,0:T(8,128)S(1)}) custom-call(f32[16,128,128]{2,1,0:T(8,128)} %bitcast.16, f32[16,128,128]{2,1,0:T(8,128)} %bitcast.15, f32[8,128,128]{2,1,0:T(8,128)S(1)} %get-tuple-element.114.refs_2_.refs_1_.refs_6_), custom_call_target="tpu_custom_call" | custom-call | flops 1000000000 | bytes 65536 | tf_op jit(solution)/shard_map/load_adjoint/pallas_call | solution.py:411
  24.2 2.7 %collective-permute-start.8 = (f32[4,128,128]{2,1,0:T(8,128)S(1)}, f32[4,128,128]{2,1,0:T(8,128)S(1)}, u32[]{:S(2)}, u32[]{:S(2)}) collective-permute-start(f32[4,128,128]{2,1,0:T(8,128)S(1)} %get-tuple-element.132), channel_id=1, source_target_pairs={{0,1},{1,0},{2,3},{3,2},{4,5},{5,4},{6,7},{7,6},{8,9},{9,8},{10,11... | collective-permute-start | bytes 786440 | tf_op jit(solution)/shard_map/ppermute | solution.py:458
  28.9 3.3 %collective-permute-start.12 = (f32[4,128,128]{2,1,0:T(8,128)S(1)}, f32[4,128,128]{2,1,0:T(8,128)S(1)}, u32[]{:S(2)}, u32[]{:S(2)}) collective-permute-start(f32[4,128,128]{2,1,0:T(8,128)S(1)} %get-tuple-element.138), channel_id=1, source_target_pairs={{0,1},{1,0},{2,3},{3,2},{4,5},{5,4},{6,7},{7,6},{8,9},{9,8},{10,11... | collective-permute-start | bytes 786440 | tf_op jit(solution)/shard_map/ppermute | solution.py:458
  32.9 5.7 %receivers.1 = (f32[24584,128]{1,0:T(8,128)S(1)}, f32[8,128,128]{2,1,0:T(8,128)S(1)}, f32[8,128,128]{2,1,0:T(8,128)S(1)}) custom-call(s32[1,1024]{1,0:T(1,128)S(1)} %get-tuple-element.105.where_to, f32[1,8,256]{2,1,0:T(8,128)S(1)} %get-tuple-element.104.refs_0_, ...), custom_call_target="tpu_custom_call", output_to_operand_aliasing={{1}: (4, {}), {2}: (5, {}), {0}: (7, {})} | custom-call | tf_op jit(solution)/shard_map/receivers/pallas_call | solution.py:411
  39.3 0.8 adjoint_border.9
  40.2 2.1 %collective-permute-start.10 = (f32[4,128,128]{2,1,0:T(8,128)S(1)}, f32[4,128,128]{2,1,0:T(8,128)S(1)}, u32[]{:S(2)}, u32[]{:S(2)}) collective-permute-start(f32[4,128,128]{2,1,0:T(8,128)S(1)} %get-tuple-element.136), channel_id=1, source_target_pairs={{0,1},{1,0},{2,3},{3,2},{4,5},{5,4},{6,7},{7,6},{8,9},{9,8},{10,11... | collective-permute-start | bytes 786440 | tf_op jit(solution)/shard_map/ppermute | solution.py:458
  44.4 0.9 forward_border.10
  45.3 2.6 %collective-permute-start.16 = (f32[4,128,128]{2,1,0:T(8,128)S(1)}, f32[4,128,128]{2,1,0:T(8,128)S(1)}, u32[]{:S(2)}, u32[]{:S(2)}) collective-permute-start(f32[4,128,128]{2,1,0:T(8,128)S(1)} %get-tuple-element.145), channel_id=1, source_target_pairs={{0,1},{1,0},{2,3},{3,2},{4,5},{5,4},{6,7},{7,6},{8,9},{9,8},{10,11... | collective-permute-start | bytes 786440 | tf_op jit(solution)/shard_map/ppermute | solution.py:458
  50.1 2.5 %collective-permute-start.14 = (f32[4,128,128]{2,1,0:T(8,128)S(1)}, f32[4,128,128]{2,1,0:T(8,128)S(1)}, u32[]{:S(2)}, u32[]{:S(2)}) collective-permute-start(f32[4,128,128]{2,1,0:T(8,128)S(1)} %get-tuple-element.143), channel_id=1, source_target_pairs={{0,1},{1,0},{2,3},{3,2},{4,5},{5,4},{6,7},{7,6},{8,9},{9,8},{10,11... | collective-permute-start | bytes 786440 | tf_op jit(solution)/shard_map/ppermute | solution.py:458
  53.9 1.1 collective-permute-done.16.refs_2_
  55.8 4.1 %collective-permute-start.20 = (f32[4,128,128]{2,1,0:T(8,128)S(1)}, f32[4,128,128]{2,1,0:T(8,128)S(1)}, u32[]{:S(2)}, u32[]{:S(2)}) collective-permute-start(f32[4,128,128]{2,1,0:T(8,128)S(1)} %get-tuple-element.156), channel_id=1, source_target_pairs={{0,1},{1,0},{2,3},{3,2},{4,5},{5,4},{6,7},{7,6},{8,9},{9,8},{10,11... | collective-permute-start | bytes 786440 | tf_op jit(solution)/shard_map/ppermute | solution.py:458
  62.1 3.4 %collective-permute-start.18 = (f32[4,128,128]{2,1,0:T(8,128)S(1)}, f32[4,128,128]{2,1,0:T(8,128)S(1)}, u32[]{:S(2)}, u32[]{:S(2)}) collective-permute-start(f32[4,128,128]{2,1,0:T(8,128)S(1)} %get-tuple-element.153), channel_id=1, source_target_pairs={{0,1},{1,0},{2,3},{3,2},{4,5},{5,4},{6,7},{7,6},{8,9},{9,8},{10,11... | collective-permute-start | bytes 786440 | tf_op jit(solution)/shard_map/ppermute | solution.py:458
  66.8 0.8 forward_border.12
  67.7 3.6 %collective-permute-start.24 = (f32[4,128,128]{2,1,0:T(8,128)S(1)}, f32[4,128,128]{2,1,0:T(8,128)S(1)}, u32[]{:S(2)}, u32[]{:S(2)}) collective-permute-start(f32[4,128,128]{2,1,0:T(8,128)S(1)} %get-tuple-element.169), channel_id=1, source_target_pairs={{0,1},{1,0},{2,3},{3,2},{4,5},{5,4},{6,7},{7,6},{8,9},{9,8},{10,11... | collective-permute-start | bytes 786440 | tf_op jit(solution)/shard_map/ppermute | solution.py:458
  73.4 4.0 %collective-permute-start.22 = (f32[4,128,128]{2,1,0:T(8,128)S(1)}, f32[4,128,128]{2,1,0:T(8,128)S(1)}, u32[]{:S(2)}, u32[]{:S(2)}) collective-permute-start(f32[4,128,128]{2,1,0:T(8,128)S(1)} %get-tuple-element.166), channel_id=1, source_target_pairs={{0,1},{1,0},{2,3},{3,2},{4,5},{5,4},{6,7},{7,6},{8,9},{9,8},{10,11... | collective-permute-start | bytes 786440 | tf_op jit(solution)/shard_map/ppermute | solution.py:458
  79.6 3.6 %collective-permute-start.28 = (f32[4,128,128]{2,1,0:T(8,128)S(1)}, f32[4,128,128]{2,1,0:T(8,128)S(1)}, u32[]{:S(2)}, u32[]{:S(2)}) collective-permute-start(f32[4,128,128]{2,1,0:T(8,128)S(1)} %get-tuple-element.183), channel_id=1, source_target_pairs={{0,1},{1,0},{2,3},{3,2},{4,5},{5,4},{6,7},{7,6},{8,9},{9,8},{10,11... | collective-permute-start | bytes 786440 | tf_op jit(solution)/shard_map/ppermute | solution.py:458
  85.3 3.7 %collective-permute-start.26 = (f32[4,128,128]{2,1,0:T(8,128)S(1)}, f32[4,128,128]{2,1,0:T(8,128)S(1)}, u32[]{:S(2)}, u32[]{:S(2)}) collective-permute-start(f32[4,128,128]{2,1,0:T(8,128)S(1)} %get-tuple-element.180), channel_id=1, source_target_pairs={{0,1},{1,0},{2,3},{3,2},{4,5},{5,4},{6,7},{7,6},{8,9},{9,8},{10,11... | collective-permute-start | bytes 786440 | tf_op jit(solution)/shard_map/ppermute | solution.py:458
  88.9 0.9 collective-permute-start.27
  91.3 3.8 %collective-permute-start.32 = (f32[4,128,128]{2,1,0:T(8,128)S(1)}, f32[4,128,128]{2,1,0:T(8,128)S(1)}, u32[]{:S(2)}, u32[]{:S(2)}) collective-permute-start(f32[4,128,128]{2,1,0:T(8,128)S(1)} %get-tuple-element.195), channel_id=1, source_target_pairs={{0,1},{1,0},{2,3},{3,2},{4,5},{5,4},{6,7},{7,6},{8,9},{9,8},{10,11... | collective-permute-start | bytes 786440 | tf_op jit(solution)/shard_map/ppermute | solution.py:458
  97.2 3.6 %collective-permute-start.30 = (f32[4,128,128]{2,1,0:T(8,128)S(1)}, f32[4,128,128]{2,1,0:T(8,128)S(1)}, u32[]{:S(2)}, u32[]{:S(2)}) collective-permute-start(f32[4,128,128]{2,1,0:T(8,128)S(1)} %get-tuple-element.191), channel_id=1, source_target_pairs={{0,1},{1,0},{2,3},{3,2},{4,5},{5,4},{6,7},{7,6},{8,9},{9,8},{10,11... | collective-permute-start | bytes 786440 | tf_op jit(solution)/shard_map/ppermute | solution.py:458
  101.5 0.8 forward_border.15
  102.4 1.5 %adjoint_inner.15 = (f32[16,128,128]{2,1,0:T(8,128)}, f32[16,128,128]{2,1,0:T(8,128)}) custom-call(f32[8,128,128]{2,1,0:T(8,128)S(1)} %get-tuple-element.179.refs_12_.refs_6_.refs_0_, f32[8,128,128]{2,1,0:T(8,128)S(1)} %get-tuple-element.190.refs_1_.refs_8_, bf16[256,256]{1,0:T(8,128)(2,1)S(1)} %get-tuple-element.110.refs_4_.refs_2_, ...), custom_call_target="tpu_custom_call" | custom-call | flops 30000001024 | bytes 1966080 | tf_op jit(solution)/shard_map/adjoint_inner/pallas_call | solution.py:411
  104.3 1.6 %collective-permute-start.35 = (f32[16,16,128]{2,1,0:T(8,128)S(1)}, f32[16,16,128]{2,1,0:T(8,128)S(1)}, u32[]{:S(2)}, u32[]{:S(2)}) collective-permute-start(f32[16,16,128]{2,1,0:T(8,128)S(1)} %get-tuple-element.202), channel_id=1, source_target_pairs={{0,8},{4,12},{8,0},{12,4},{16,24},{20,28},{24,16},{28,20},{1,9},{5... | collective-permute-start | bytes 393224 | tf_op jit(solution)/shard_map/ppermute | solution.py:629
  105.9 1.5 %collective-permute-start.36 = (f32[16,16,128]{2,1,0:T(8,128)S(1)}, f32[16,16,128]{2,1,0:T(8,128)S(1)}, u32[]{:S(2)}, u32[]{:S(2)}) collective-permute-start(f32[16,16,128]{2,1,0:T(8,128)S(1)} %get-tuple-element.203), channel_id=1, source_target_pairs={{0,16},{4,20},{8,24},{12,28},{16,0},{20,4},{24,8},{28,12},{1,17},{... | collective-permute-start | bytes 393224 | tf_op jit(solution)/shard_map/ppermute | solution.py:629
  107.9 1.5 %adjoint_border.15 = f32[16,128,128]{2,1,0:T(8,128)} custom-call(f32[8,128,128]{2,1,0:T(8,128)S(1)} %get-tuple-element.179.refs_12_.refs_6_.refs_0_, f32[8,128,128]{2,1,0:T(8,128)S(1)} %get-tuple-element.190.refs_1_.refs_8_, f32[4,128,128]{2,1,0:T(8,128)S(1)} %collective-permute-done.30.refs_2_, ...), custom_call_target="tpu_custom_call", output_to_operand_aliasing={{}: (9, {})} | custom-call | flops 30000001024 | bytes 1966080 | tf_op jit(solution)/shard_map/adjoint_border/pallas_call | solution.py:411
  109.4 0.9 collective-permute-done.35.refs_1_
  110.3 3.7 %collective-permute-done.36.refs_2_ = f32[16,16,128]{2,1,0:T(8,128)S(1)} collective-permute-done((f32[16,16,128]{2,1,0:T(8,128)S(1)}, f32[16,16,128]{2,1,0:T(8,128)S(1)}, u32[]{:S(2)}, u32[]{:S(2)}) %collective-permute-start.36) | collective-permute-done | bytes 131104 | tf_op jit(solution)/shard_map/ppermute | solution.py:629
  (84 shorter events, 32.2 us)
Async XLA Ops:
  1.9 17.2 %collective-permute-start.2 = (f32[4,128,128]{2,1,0:T(8,128)S(1)}, f32[4,128,128]{2,1,0:T(8,128)S(1)}, u32[]{:S(2)}, u32[]{:S(2)}) collective-permute-start(f32[4,128,128]{2,1,0:T(8,128)S(1)} %get-tuple-element.108), channel_id=1, source_target_pairs={{0,1},{1,0},{2,3},{3,2},{4,5},{5,4},{6,7},{7,6},{8,9},{9,8},{10,11... | collective-permute-start | bytes 786440 | tf_op jit(solution)/shard_map/ppermute | solution.py:458
  5.0 14.1 %collective-permute-start.3 = (f32[4,128,128]{2,1,0:T(8,128)S(1)}, f32[4,128,128]{2,1,0:T(8,128)S(1)}, u32[]{:S(2)}, u32[]{:S(2)}) collective-permute-start(f32[4,128,128]{2,1,0:T(8,128)S(1)} %get-tuple-element.109), channel_id=1, source_target_pairs={{1,2},{2,1},{5,6},{6,5},{9,10},{10,9},{13,14},{14,13},{17,18},{18,... | collective-permute-start | bytes 786440 | tf_op jit(solution)/shard_map/ppermute | solution.py:458
  10.1 13.4 %collective-permute-start.4 = (f32[4,128,128]{2,1,0:T(8,128)S(1)}, f32[4,128,128]{2,1,0:T(8,128)S(1)}, u32[]{:S(2)}, u32[]{:S(2)}) collective-permute-start(f32[4,128,128]{2,1,0:T(8,128)S(1)} %get-tuple-element.118), channel_id=1, source_target_pairs={{0,1},{1,0},{2,3},{3,2},{4,5},{5,4},{6,7},{7,6},{8,9},{9,8},{10,11... | collective-permute-start | bytes 786440 | tf_op jit(solution)/shard_map/ppermute | solution.py:458
  10.2 13.3 %collective-permute-start.5 = (f32[4,128,128]{2,1,0:T(8,128)S(1)}, f32[4,128,128]{2,1,0:T(8,128)S(1)}, u32[]{:S(2)}, u32[]{:S(2)}) collective-permute-start(f32[4,128,128]{2,1,0:T(8,128)S(1)} %get-tuple-element.119), channel_id=1, source_target_pairs={{1,2},{2,1},{5,6},{6,5},{9,10},{10,9},{13,14},{14,13},{17,18},{18,... | collective-permute-start | bytes 786440 | tf_op jit(solution)/shard_map/ppermute | solution.py:458
  12.0 20.9 %collective-permute-start.1 = (f32[2,8,256]{2,1,0:T(8,128)S(1)}, f32[2,8,256]{2,1,0:T(8,128)S(1)}, u32[]{:S(2)}, u32[]{:S(2)}) collective-permute-start(f32[2,8,256]{2,1,0:T(8,128)S(1)} %stack.1.refs_3_), channel_id=1, source_target_pairs={{0,2},{1,3},{2,0},{3,1},{4,6},{5,7},{6,4},{7,5},{8,10},{9,11},{10,... | collective-permute-start | bytes 49160 | tf_op jit(solution)/shard_map/ppermute | solution.py:476
  19.8 8.3 %collective-permute-start.6 = (f32[4,128,128]{2,1,0:T(8,128)S(1)}, f32[4,128,128]{2,1,0:T(8,128)S(1)}, u32[]{:S(2)}, u32[]{:S(2)}) collective-permute-start(f32[4,128,128]{2,1,0:T(8,128)S(1)} %get-tuple-element.125), channel_id=1, source_target_pairs={{0,1},{1,0},{2,3},{3,2},{4,5},{5,4},{6,7},{7,6},{8,9},{9,8},{10,11... | collective-permute-start | bytes 786440 | tf_op jit(solution)/shard_map/ppermute | solution.py:458
  20.5 7.6 %collective-permute-start.7 = (f32[4,128,128]{2,1,0:T(8,128)S(1)}, f32[4,128,128]{2,1,0:T(8,128)S(1)}, u32[]{:S(2)}, u32[]{:S(2)}) collective-permute-start(f32[4,128,128]{2,1,0:T(8,128)S(1)} %get-tuple-element.126), channel_id=1, source_target_pairs={{1,2},{2,1},{5,6},{6,5},{9,10},{10,9},{13,14},{14,13},{17,18},{18,... | collective-permute-start | bytes 786440 | tf_op jit(solution)/shard_map/ppermute | solution.py:458
  24.2 15.1 %collective-permute-start.8 = (f32[4,128,128]{2,1,0:T(8,128)S(1)}, f32[4,128,128]{2,1,0:T(8,128)S(1)}, u32[]{:S(2)}, u32[]{:S(2)}) collective-permute-start(f32[4,128,128]{2,1,0:T(8,128)S(1)} %get-tuple-element.132), channel_id=1, source_target_pairs={{0,1},{1,0},{2,3},{3,2},{4,5},{5,4},{6,7},{7,6},{8,9},{9,8},{10,11... | collective-permute-start | bytes 786440 | tf_op jit(solution)/shard_map/ppermute | solution.py:458
  26.9 12.5 %collective-permute-start.9 = (f32[4,128,128]{2,1,0:T(8,128)S(1)}, f32[4,128,128]{2,1,0:T(8,128)S(1)}, u32[]{:S(2)}, u32[]{:S(2)}) collective-permute-start(f32[4,128,128]{2,1,0:T(8,128)S(1)} %get-tuple-element.133), channel_id=1, source_target_pairs={{1,2},{2,1},{5,6},{6,5},{9,10},{10,9},{13,14},{14,13},{17,18},{18,... | collective-permute-start | bytes 786440 | tf_op jit(solution)/shard_map/ppermute | solution.py:458
  28.9 15.4 %collective-permute-start.12 = (f32[4,128,128]{2,1,0:T(8,128)S(1)}, f32[4,128,128]{2,1,0:T(8,128)S(1)}, u32[]{:S(2)}, u32[]{:S(2)}) collective-permute-start(f32[4,128,128]{2,1,0:T(8,128)S(1)} %get-tuple-element.138), channel_id=1, source_target_pairs={{0,1},{1,0},{2,3},{3,2},{4,5},{5,4},{6,7},{7,6},{8,9},{9,8},{10,11... | collective-permute-start | bytes 786440 | tf_op jit(solution)/shard_map/ppermute | solution.py:458
  32.2 12.1 %collective-permute-start.13 = (f32[4,128,128]{2,1,0:T(8,128)S(1)}, f32[4,128,128]{2,1,0:T(8,128)S(1)}, u32[]{:S(2)}, u32[]{:S(2)}) collective-permute-start(f32[4,128,128]{2,1,0:T(8,128)S(1)} %get-tuple-element.139), channel_id=1, source_target_pairs={{1,2},{2,1},{5,6},{6,5},{9,10},{10,9},{13,14},{14,13},{17,18},{18,... | collective-permute-start | bytes 786440 | tf_op jit(solution)/shard_map/ppermute | solution.py:458
  40.2 9.1 %collective-permute-start.10 = (f32[4,128,128]{2,1,0:T(8,128)S(1)}, f32[4,128,128]{2,1,0:T(8,128)S(1)}, u32[]{:S(2)}, u32[]{:S(2)}) collective-permute-start(f32[4,128,128]{2,1,0:T(8,128)S(1)} %get-tuple-element.136), channel_id=1, source_target_pairs={{0,1},{1,0},{2,3},{3,2},{4,5},{5,4},{6,7},{7,6},{8,9},{9,8},{10,11... | collective-permute-start | bytes 786440 | tf_op jit(solution)/shard_map/ppermute | solution.py:458
  42.2 7.1 %collective-permute-start.11 = (f32[4,128,128]{2,1,0:T(8,128)S(1)}, f32[4,128,128]{2,1,0:T(8,128)S(1)}, u32[]{:S(2)}, u32[]{:S(2)}) collective-permute-start(f32[4,128,128]{2,1,0:T(8,128)S(1)} %get-tuple-element.137), channel_id=1, source_target_pairs={{1,2},{2,1},{5,6},{6,5},{9,10},{10,9},{13,14},{14,13},{17,18},{18,... | collective-permute-start | bytes 786440 | tf_op jit(solution)/shard_map/ppermute | solution.py:458
  45.3 9.7 %collective-permute-start.16 = (f32[4,128,128]{2,1,0:T(8,128)S(1)}, f32[4,128,128]{2,1,0:T(8,128)S(1)}, u32[]{:S(2)}, u32[]{:S(2)}) collective-permute-start(f32[4,128,128]{2,1,0:T(8,128)S(1)} %get-tuple-element.145), channel_id=1, source_target_pairs={{0,1},{1,0},{2,3},{3,2},{4,5},{5,4},{6,7},{7,6},{8,9},{9,8},{10,11... | collective-permute-start | bytes 786440 | tf_op jit(solution)/shard_map/ppermute | solution.py:458
  47.9 7.1 %collective-permute-start.17 = (f32[4,128,128]{2,1,0:T(8,128)S(1)}, f32[4,128,128]{2,1,0:T(8,128)S(1)}, u32[]{:S(2)}, u32[]{:S(2)}) collective-permute-start(f32[4,128,128]{2,1,0:T(8,128)S(1)} %get-tuple-element.146), channel_id=1, source_target_pairs={{1,2},{2,1},{5,6},{6,5},{9,10},{10,9},{13,14},{14,13},{17,18},{18,... | collective-permute-start | bytes 786440 | tf_op jit(solution)/shard_map/ppermute | solution.py:458
  50.1 11.2 %collective-permute-start.14 = (f32[4,128,128]{2,1,0:T(8,128)S(1)}, f32[4,128,128]{2,1,0:T(8,128)S(1)}, u32[]{:S(2)}, u32[]{:S(2)}) collective-permute-start(f32[4,128,128]{2,1,0:T(8,128)S(1)} %get-tuple-element.143), channel_id=1, source_target_pairs={{0,1},{1,0},{2,3},{3,2},{4,5},{5,4},{6,7},{7,6},{8,9},{9,8},{10,11... | collective-permute-start | bytes 786440 | tf_op jit(solution)/shard_map/ppermute | solution.py:458
  52.6 8.7 %collective-permute-start.15 = (f32[4,128,128]{2,1,0:T(8,128)S(1)}, f32[4,128,128]{2,1,0:T(8,128)S(1)}, u32[]{:S(2)}, u32[]{:S(2)}) collective-permute-start(f32[4,128,128]{2,1,0:T(8,128)S(1)} %get-tuple-element.144), channel_id=1, source_target_pairs={{1,2},{2,1},{5,6},{6,5},{9,10},{10,9},{13,14},{14,13},{17,18},{18,... | collective-permute-start | bytes 786440 | tf_op jit(solution)/shard_map/ppermute | solution.py:458
  55.8 11.0 %collective-permute-start.20 = (f32[4,128,128]{2,1,0:T(8,128)S(1)}, f32[4,128,128]{2,1,0:T(8,128)S(1)}, u32[]{:S(2)}, u32[]{:S(2)}) collective-permute-start(f32[4,128,128]{2,1,0:T(8,128)S(1)} %get-tuple-element.156), channel_id=1, source_target_pairs={{0,1},{1,0},{2,3},{3,2},{4,5},{5,4},{6,7},{7,6},{8,9},{9,8},{10,11... | collective-permute-start | bytes 786440 | tf_op jit(solution)/shard_map/ppermute | solution.py:458
  62.1 10.6 %collective-permute-start.18 = (f32[4,128,128]{2,1,0:T(8,128)S(1)}, f32[4,128,128]{2,1,0:T(8,128)S(1)}, u32[]{:S(2)}, u32[]{:S(2)}) collective-permute-start(f32[4,128,128]{2,1,0:T(8,128)S(1)} %get-tuple-element.153), channel_id=1, source_target_pairs={{0,1},{1,0},{2,3},{3,2},{4,5},{5,4},{6,7},{7,6},{8,9},{9,8},{10,11... | collective-permute-start | bytes 786440 | tf_op jit(solution)/shard_map/ppermute | solution.py:458
  65.5 7.2 %collective-permute-start.19 = (f32[4,128,128]{2,1,0:T(8,128)S(1)}, f32[4,128,128]{2,1,0:T(8,128)S(1)}, u32[]{:S(2)}, u32[]{:S(2)}) collective-permute-start(f32[4,128,128]{2,1,0:T(8,128)S(1)} %get-tuple-element.154), channel_id=1, source_target_pairs={{1,2},{2,1},{5,6},{6,5},{9,10},{10,9},{13,14},{14,13},{17,18},{18,... | collective-permute-start | bytes 786440 | tf_op jit(solution)/shard_map/ppermute | solution.py:458
  67.7 11.1 %collective-permute-start.24 = (f32[4,128,128]{2,1,0:T(8,128)S(1)}, f32[4,128,128]{2,1,0:T(8,128)S(1)}, u32[]{:S(2)}, u32[]{:S(2)}) collective-permute-start(f32[4,128,128]{2,1,0:T(8,128)S(1)} %get-tuple-element.169), channel_id=1, source_target_pairs={{0,1},{1,0},{2,3},{3,2},{4,5},{5,4},{6,7},{7,6},{8,9},{9,8},{10,11... | collective-permute-start | bytes 786440 | tf_op jit(solution)/shard_map/ppermute | solution.py:458
  71.2 7.5 %collective-permute-start.25 = (f32[4,128,128]{2,1,0:T(8,128)S(1)}, f32[4,128,128]{2,1,0:T(8,128)S(1)}, u32[]{:S(2)}, u32[]{:S(2)}) collective-permute-start(f32[4,128,128]{2,1,0:T(8,128)S(1)} %get-tuple-element.170), channel_id=1, source_target_pairs={{1,2},{2,1},{5,6},{6,5},{9,10},{10,9},{13,14},{14,13},{17,18},{18,... | collective-permute-start | bytes 786440 | tf_op jit(solution)/shard_map/ppermute | solution.py:458
  73.4 11.1 %collective-permute-start.22 = (f32[4,128,128]{2,1,0:T(8,128)S(1)}, f32[4,128,128]{2,1,0:T(8,128)S(1)}, u32[]{:S(2)}, u32[]{:S(2)}) collective-permute-start(f32[4,128,128]{2,1,0:T(8,128)S(1)} %get-tuple-element.166), channel_id=1, source_target_pairs={{0,1},{1,0},{2,3},{3,2},{4,5},{5,4},{6,7},{7,6},{8,9},{9,8},{10,11... | collective-permute-start | bytes 786440 | tf_op jit(solution)/shard_map/ppermute | solution.py:458
  77.4 7.1 %collective-permute-start.23 = (f32[4,128,128]{2,1,0:T(8,128)S(1)}, f32[4,128,128]{2,1,0:T(8,128)S(1)}, u32[]{:S(2)}, u32[]{:S(2)}) collective-permute-start(f32[4,128,128]{2,1,0:T(8,128)S(1)} %get-tuple-element.167), channel_id=1, source_target_pairs={{1,2},{2,1},{5,6},{6,5},{9,10},{10,9},{13,14},{14,13},{17,18},{18,... | collective-permute-start | bytes 786440 | tf_op jit(solution)/shard_map/ppermute | solution.py:458
  79.6 11.0 %collective-permute-start.28 = (f32[4,128,128]{2,1,0:T(8,128)S(1)}, f32[4,128,128]{2,1,0:T(8,128)S(1)}, u32[]{:S(2)}, u32[]{:S(2)}) collective-permute-start(f32[4,128,128]{2,1,0:T(8,128)S(1)} %get-tuple-element.183), channel_id=1, source_target_pairs={{0,1},{1,0},{2,3},{3,2},{4,5},{5,4},{6,7},{7,6},{8,9},{9,8},{10,11... | collective-permute-start | bytes 786440 | tf_op jit(solution)/shard_map/ppermute | solution.py:458
  83.1 7.4 %collective-permute-start.29 = (f32[4,128,128]{2,1,0:T(8,128)S(1)}, f32[4,128,128]{2,1,0:T(8,128)S(1)}, u32[]{:S(2)}, u32[]{:S(2)}) collective-permute-start(f32[4,128,128]{2,1,0:T(8,128)S(1)} %get-tuple-element.184), channel_id=1, source_target_pairs={{1,2},{2,1},{5,6},{6,5},{9,10},{10,9},{13,14},{14,13},{17,18},{18,... | collective-permute-start | bytes 786440 | tf_op jit(solution)/shard_map/ppermute | solution.py:458
  85.3 11.1 %collective-permute-start.26 = (f32[4,128,128]{2,1,0:T(8,128)S(1)}, f32[4,128,128]{2,1,0:T(8,128)S(1)}, u32[]{:S(2)}, u32[]{:S(2)}) collective-permute-start(f32[4,128,128]{2,1,0:T(8,128)S(1)} %get-tuple-element.180), channel_id=1, source_target_pairs={{0,1},{1,0},{2,3},{3,2},{4,5},{5,4},{6,7},{7,6},{8,9},{9,8},{10,11... | collective-permute-start | bytes 786440 | tf_op jit(solution)/shard_map/ppermute | solution.py:458
  88.9 7.5 %collective-permute-start.27 = (f32[4,128,128]{2,1,0:T(8,128)S(1)}, f32[4,128,128]{2,1,0:T(8,128)S(1)}, u32[]{:S(2)}, u32[]{:S(2)}) collective-permute-start(f32[4,128,128]{2,1,0:T(8,128)S(1)} %get-tuple-element.181), channel_id=1, source_target_pairs={{1,2},{2,1},{5,6},{6,5},{9,10},{10,9},{13,14},{14,13},{17,18},{18,... | collective-permute-start | bytes 786440 | tf_op jit(solution)/shard_map/ppermute | solution.py:458
  91.3 10.2 %collective-permute-start.32 = (f32[4,128,128]{2,1,0:T(8,128)S(1)}, f32[4,128,128]{2,1,0:T(8,128)S(1)}, u32[]{:S(2)}, u32[]{:S(2)}) collective-permute-start(f32[4,128,128]{2,1,0:T(8,128)S(1)} %get-tuple-element.195), channel_id=1, source_target_pairs={{0,1},{1,0},{2,3},{3,2},{4,5},{5,4},{6,7},{7,6},{8,9},{9,8},{10,11... | collective-permute-start | bytes 786440 | tf_op jit(solution)/shard_map/ppermute | solution.py:458
  97.2 10.7 %collective-permute-start.30 = (f32[4,128,128]{2,1,0:T(8,128)S(1)}, f32[4,128,128]{2,1,0:T(8,128)S(1)}, u32[]{:S(2)}, u32[]{:S(2)}) collective-permute-start(f32[4,128,128]{2,1,0:T(8,128)S(1)} %get-tuple-element.191), channel_id=1, source_target_pairs={{0,1},{1,0},{2,3},{3,2},{4,5},{5,4},{6,7},{7,6},{8,9},{9,8},{10,11... | collective-permute-start | bytes 786440 | tf_op jit(solution)/shard_map/ppermute | solution.py:458
  100.8 7.1 %collective-permute-start.31 = (f32[4,128,128]{2,1,0:T(8,128)S(1)}, f32[4,128,128]{2,1,0:T(8,128)S(1)}, u32[]{:S(2)}, u32[]{:S(2)}) collective-permute-start(f32[4,128,128]{2,1,0:T(8,128)S(1)} %get-tuple-element.192), channel_id=1, source_target_pairs={{1,2},{2,1},{5,6},{6,5},{9,10},{10,9},{13,14},{14,13},{17,18},{18,... | collective-permute-start | bytes 786440 | tf_op jit(solution)/shard_map/ppermute | solution.py:458
  105.9 8.1 %collective-permute-start.36 = (f32[16,16,128]{2,1,0:T(8,128)S(1)}, f32[16,16,128]{2,1,0:T(8,128)S(1)}, u32[]{:S(2)}, u32[]{:S(2)}) collective-permute-start(f32[16,16,128]{2,1,0:T(8,128)S(1)} %get-tuple-element.203), channel_id=1, source_target_pairs={{0,16},{4,20},{8,24},{12,28},{16,0},{20,4},{24,8},{28,12},{1,17},{... | collective-permute-start | bytes 393224 | tf_op jit(solution)/shard_map/ppermute | solution.py:629
  (6 other events, 34.3 us)

commit v10 on v9

--- a/solution.py
+++ b/solution.py
@@ -586,7 +586,7 @@
 
     forward(0, False)
     for k in range(steps - 1):
-        first = [q[steps - 1 - k][False]] if k > 1 else []
+        first = [q[steps - 1 - k][False]] if k > 2 else []
         p_halo = swap(*forward(k, True, p_halo, first))
         if k == 0:
             loaded = call(
@@ -614,7 +614,7 @@
             )
             adjoint(1, False)
         forward(k + 1, False)
-        first = [acc[False] if k + 1 == steps - 1 else p[k + 2][False]]
+        first = [acc[False] if k + 1 == steps - 1 else p[k + 2][False]] if k > 0 else []
         q_halo = swap(*adjoint(k, True, q_halo, after=first))
         if 0 < k < steps - 2:
             adjoint(k + 1, False)

time: 115 us -> 116 us (level)
  no operation moved by 1% of the time
where the time goes in v10:
time: 116 us; the launch traced here: 115 us
  starting transfers between devices  70.7 us (61%)
  Pallas kernels  36.2 us (31%)
  waiting for transfers between devices  6.18 us (5%)
  between operations  1.28 us (1%)
    ppermute x16, starting transfers between devices, swap(): lax.ppermute(even, 'slab', even_pairs)  47.5 us
    pallas_call x39, Pallas kernels, call(): pl.pallas_call(kernel, out_shape=outs, in_specs=[spec(spaces.get(i, VMEM)...  36.2 us
    ppermute x16, starting transfers between devices, swap(): lax.ppermute(odd, 'slab', odd_pairs)  10.9 us
    ppermute x2, starting transfers between devices, body(): lax.ppermute(held, 'slab', [(i, i ^ bit) for i in range(slabs)])  8.7 us
    ppermute x3, waiting for transfers between devices, body(): lax.ppermute(pieces[m], 'shot', [(i, i ^ 2 * m) for i in range(shots)])  4.61 us
    ppermute x3, starting transfers between devices, body(): lax.ppermute(pieces[m], 'shot', [(i, i ^ 2 * m) for i in range(shots)])  3.55 us
  transfers between devices with their start and end apart: 38, of which 5 were waited for; matrix products, arithmetic and copies ran while one was open for 1% of the time, Pallas kernels for 30%

profile of v10, /device:TPU:0, one launch (start us, length us, event | category | flops | bytes accessed | tf_op | source)
XLA Modules:
  0.0 115.1 jit_solution(13295268834087802174)
XLA Ops:
  0.6 1.2 %edges.1 = (f32[4,128,128]{2,1,0:T(8,128)S(1)}, f32[4,128,128]{2,1,0:T(8,128)S(1)}, f32[4,128,128]{2,1,0:T(8,128)S(1)}, f32[4,128,128]{2,1,0:T(8,128)S(1)}, f32[1,8,256]{2,1,0:T(8,128)S(1)}) custom-call(f32[16,128,128]{2,1,0:T(8,128)} %bitcast.12, f32[16,128,128]{2,1,0:T(8,128)} %bitcast.14, f32[1,8,256]{2,1,0:T(8,128)} %refs_2_.2), custom_call_target="tpu_custom_call" | custom-call | flops 2000000000 | bytes 131072 | tf_op jit(solution)/shard_map/edges/pallas_call | solution.py:411
  1.9 3.1 %collective-permute-start.2 = (f32[4,128,128]{2,1,0:T(8,128)S(1)}, f32[4,128,128]{2,1,0:T(8,128)S(1)}, u32[]{:S(2)}, u32[]{:S(2)}) collective-permute-start(f32[4,128,128]{2,1,0:T(8,128)S(1)} %get-tuple-element.108), channel_id=1, source_target_pairs={{0,1},{1,0},{2,3},{3,2},{4,5},{5,4},{6,7},{7,6},{8,9},{9,8},{10,11... | collective-permute-start | bytes 786440 | tf_op jit(solution)/shard_map/ppermute | solution.py:458
  5.6 4.4 %collective-permute-start = (f32[1,8,256]{2,1,0:T(8,128)}, f32[1,8,256]{2,1,0:T(8,128)S(1)}, u32[]{:S(2)}, u32[]{:S(2)}) collective-permute-start(f32[1,8,256]{2,1,0:T(8,128)} %refs_2_.2), channel_id=1, source_target_pairs={{0,1},{1,0},{2,3},{3,2},{4,5},{5,4},{6,7},{7,6},{8,9},{9,8},{10,11... | collective-permute-start | bytes 24584 | tf_op jit(solution)/shard_map/ppermute | solution.py:476
  12.0 4.2 %collective-permute-start.1 = (f32[2,8,256]{2,1,0:T(8,128)S(1)}, f32[2,8,256]{2,1,0:T(8,128)S(1)}, u32[]{:S(2)}, u32[]{:S(2)}) collective-permute-start(f32[2,8,256]{2,1,0:T(8,128)S(1)} %stack.1.refs_3_), channel_id=1, source_target_pairs={{0,2},{1,3},{2,0},{3,1},{4,6},{5,7},{6,4},{7,5},{8,10},{9,11},{10,... | collective-permute-start | bytes 49160 | tf_op jit(solution)/shard_map/ppermute | solution.py:476
  16.3 2.0 %load.1 = (f32[8,128,128]{2,1,0:T(8,128)S(1)}, f32[8,128,128]{2,1,0:T(8,128)S(1)}, f32[8,128,128]{2,1,0:T(8,128)S(1)}, f32[8,128,128]{2,1,0:T(8,128)S(1)}, f32[1...) custom-call(s32[3,1024]{1,0:T(4,128)S(1)} %bitcast.9, ...), custom_call_target="tpu_custom_call" | custom-call | flops 1000000000 | bytes 65536 | tf_op jit(solution)/shard_map/load/pallas_call | solution.py:411
  21.2 1.6 %load_adjoint.1 = (f32[8,128,128]{2,1,0:T(8,128)S(1)}, f32[8,128,128]{2,1,0:T(8,128)S(1)}, f32[8,128,128]{2,1,0:T(8,128)S(1)}, f32[8,128,128]{2,1,0:T(8,128)S(1)}) custom-call(f32[16,128,128]{2,1,0:T(8,128)} %bitcast.16, f32[16,128,128]{2,1,0:T(8,128)} %bitcast.15, f32[8,128,128]{2,1,0:T(8,128)S(1)} %get-tuple-element.114.refs_2_.refs_1_.refs_6_), custom_call_target="tpu_custom_call" | custom-call | flops 1000000000 | bytes 65536 | tf_op jit(solution)/shard_map/load_adjoint/pallas_call | solution.py:411
  23.5 2.7 %collective-permute-start.8 = (f32[4,128,128]{2,1,0:T(8,128)S(1)}, f32[4,128,128]{2,1,0:T(8,128)S(1)}, u32[]{:S(2)}, u32[]{:S(2)}) collective-permute-start(f32[4,128,128]{2,1,0:T(8,128)S(1)} %get-tuple-element.131), channel_id=1, source_target_pairs={{0,1},{1,0},{2,3},{3,2},{4,5},{5,4},{6,7},{7,6},{8,9},{9,8},{10,11... | collective-permute-start | bytes 786440 | tf_op jit(solution)/shard_map/ppermute | solution.py:458
  28.9 3.7 %collective-permute-start.12 = (f32[4,128,128]{2,1,0:T(8,128)S(1)}, f32[4,128,128]{2,1,0:T(8,128)S(1)}, u32[]{:S(2)}, u32[]{:S(2)}) collective-permute-start(f32[4,128,128]{2,1,0:T(8,128)S(1)} %get-tuple-element.138), channel_id=1, source_target_pairs={{0,1},{1,0},{2,3},{3,2},{4,5},{5,4},{6,7},{7,6},{8,9},{9,8},{10,11... | collective-permute-start | bytes 786440 | tf_op jit(solution)/shard_map/ppermute | solution.py:458
  33.3 5.7 %receivers.1 = (f32[24584,128]{1,0:T(8,128)S(1)}, f32[8,128,128]{2,1,0:T(8,128)S(1)}, f32[8,128,128]{2,1,0:T(8,128)S(1)}) custom-call(s32[1,1024]{1,0:T(1,128)S(1)} %get-tuple-element.105.where_to, f32[1,8,256]{2,1,0:T(8,128)S(1)} %get-tuple-element.104.refs_0_, ...), custom_call_target="tpu_custom_call", output_to_operand_aliasing={{1}: (4, {}), {2}: (5, {}), {0}: (7, {})} | custom-call | tf_op jit(solution)/shard_map/receivers/pallas_call | solution.py:411
  39.7 0.8 adjoint_border.9
  40.5 1.7 %collective-permute-start.10 = (f32[4,128,128]{2,1,0:T(8,128)S(1)}, f32[4,128,128]{2,1,0:T(8,128)S(1)}, u32[]{:S(2)}, u32[]{:S(2)}) collective-permute-start(f32[4,128,128]{2,1,0:T(8,128)S(1)} %get-tuple-element.136), channel_id=1, source_target_pairs={{0,1},{1,0},{2,3},{3,2},{4,5},{5,4},{6,7},{7,6},{8,9},{9,8},{10,11... | collective-permute-start | bytes 786440 | tf_op jit(solution)/shard_map/ppermute | solution.py:458
  44.3 0.9 forward_border.10
  45.3 3.0 %collective-permute-start.16 = (f32[4,128,128]{2,1,0:T(8,128)S(1)}, f32[4,128,128]{2,1,0:T(8,128)S(1)}, u32[]{:S(2)}, u32[]{:S(2)}) collective-permute-start(f32[4,128,128]{2,1,0:T(8,128)S(1)} %get-tuple-element.145), channel_id=1, source_target_pairs={{0,1},{1,0},{2,3},{3,2},{4,5},{5,4},{6,7},{7,6},{8,9},{9,8},{10,11... | collective-permute-start | bytes 786440 | tf_op jit(solution)/shard_map/ppermute | solution.py:458
  50.4 3.0 %collective-permute-start.14 = (f32[4,128,128]{2,1,0:T(8,128)S(1)}, f32[4,128,128]{2,1,0:T(8,128)S(1)}, u32[]{:S(2)}, u32[]{:S(2)}) collective-permute-start(f32[4,128,128]{2,1,0:T(8,128)S(1)} %get-tuple-element.143), channel_id=1, source_target_pairs={{0,1},{1,0},{2,3},{3,2},{4,5},{5,4},{6,7},{7,6},{8,9},{9,8},{10,11... | collective-permute-start | bytes 786440 | tf_op jit(solution)/shard_map/ppermute | solution.py:458
  56.1 4.1 %collective-permute-start.20 = (f32[4,128,128]{2,1,0:T(8,128)S(1)}, f32[4,128,128]{2,1,0:T(8,128)S(1)}, u32[]{:S(2)}, u32[]{:S(2)}) collective-permute-start(f32[4,128,128]{2,1,0:T(8,128)S(1)} %get-tuple-element.156), channel_id=1, source_target_pairs={{0,1},{1,0},{2,3},{3,2},{4,5},{5,4},{6,7},{7,6},{8,9},{9,8},{10,11... | collective-permute-start | bytes 786440 | tf_op jit(solution)/shard_map/ppermute | solution.py:458
  62.4 3.4 %collective-permute-start.18 = (f32[4,128,128]{2,1,0:T(8,128)S(1)}, f32[4,128,128]{2,1,0:T(8,128)S(1)}, u32[]{:S(2)}, u32[]{:S(2)}) collective-permute-start(f32[4,128,128]{2,1,0:T(8,128)S(1)} %get-tuple-element.153), channel_id=1, source_target_pairs={{0,1},{1,0},{2,3},{3,2},{4,5},{5,4},{6,7},{7,6},{8,9},{9,8},{10,11... | collective-permute-start | bytes 786440 | tf_op jit(solution)/shard_map/ppermute | solution.py:458
  67.2 0.8 forward_border.12
  68.0 3.6 %collective-permute-start.24 = (f32[4,128,128]{2,1,0:T(8,128)S(1)}, f32[4,128,128]{2,1,0:T(8,128)S(1)}, u32[]{:S(2)}, u32[]{:S(2)}) collective-permute-start(f32[4,128,128]{2,1,0:T(8,128)S(1)} %get-tuple-element.169), channel_id=1, source_target_pairs={{0,1},{1,0},{2,3},{3,2},{4,5},{5,4},{6,7},{7,6},{8,9},{9,8},{10,11... | collective-permute-start | bytes 786440 | tf_op jit(solution)/shard_map/ppermute | solution.py:458
  73.8 4.0 %collective-permute-start.22 = (f32[4,128,128]{2,1,0:T(8,128)S(1)}, f32[4,128,128]{2,1,0:T(8,128)S(1)}, u32[]{:S(2)}, u32[]{:S(2)}) collective-permute-start(f32[4,128,128]{2,1,0:T(8,128)S(1)} %get-tuple-element.166), channel_id=1, source_target_pairs={{0,1},{1,0},{2,3},{3,2},{4,5},{5,4},{6,7},{7,6},{8,9},{9,8},{10,11... | collective-permute-start | bytes 786440 | tf_op jit(solution)/shard_map/ppermute | solution.py:458
  79.1 0.8 forward_border.13
  79.9 3.5 %collective-permute-start.28 = (f32[4,128,128]{2,1,0:T(8,128)S(1)}, f32[4,128,128]{2,1,0:T(8,128)S(1)}, u32[]{:S(2)}, u32[]{:S(2)}) collective-permute-start(f32[4,128,128]{2,1,0:T(8,128)S(1)} %get-tuple-element.183), channel_id=1, source_target_pairs={{0,1},{1,0},{2,3},{3,2},{4,5},{5,4},{6,7},{7,6},{8,9},{9,8},{10,11... | collective-permute-start | bytes 786440 | tf_op jit(solution)/shard_map/ppermute | solution.py:458
  85.6 3.6 %collective-permute-start.26 = (f32[4,128,128]{2,1,0:T(8,128)S(1)}, f32[4,128,128]{2,1,0:T(8,128)S(1)}, u32[]{:S(2)}, u32[]{:S(2)}) collective-permute-start(f32[4,128,128]{2,1,0:T(8,128)S(1)} %get-tuple-element.180), channel_id=1, source_target_pairs={{0,1},{1,0},{2,3},{3,2},{4,5},{5,4},{6,7},{7,6},{8,9},{9,8},{10,11... | collective-permute-start | bytes 786440 | tf_op jit(solution)/shard_map/ppermute | solution.py:458
  89.3 0.9 collective-permute-start.27
  91.6 3.8 %collective-permute-start.32 = (f32[4,128,128]{2,1,0:T(8,128)S(1)}, f32[4,128,128]{2,1,0:T(8,128)S(1)}, u32[]{:S(2)}, u32[]{:S(2)}) collective-permute-start(f32[4,128,128]{2,1,0:T(8,128)S(1)} %get-tuple-element.195), channel_id=1, source_target_pairs={{0,1},{1,0},{2,3},{3,2},{4,5},{5,4},{6,7},{7,6},{8,9},{9,8},{10,11... | collective-permute-start | bytes 786440 | tf_op jit(solution)/shard_map/ppermute | solution.py:458
  97.5 3.7 %collective-permute-start.30 = (f32[4,128,128]{2,1,0:T(8,128)S(1)}, f32[4,128,128]{2,1,0:T(8,128)S(1)}, u32[]{:S(2)}, u32[]{:S(2)}) collective-permute-start(f32[4,128,128]{2,1,0:T(8,128)S(1)} %get-tuple-element.191), channel_id=1, source_target_pairs={{0,1},{1,0},{2,3},{3,2},{4,5},{5,4},{6,7},{7,6},{8,9},{9,8},{10,11... | collective-permute-start | bytes 786440 | tf_op jit(solution)/shard_map/ppermute | solution.py:458
  101.9 0.8 forward_border.15
  102.7 1.5 %adjoint_inner.15 = (f32[16,128,128]{2,1,0:T(8,128)}, f32[16,128,128]{2,1,0:T(8,128)}) custom-call(f32[8,128,128]{2,1,0:T(8,128)S(1)} %get-tuple-element.179.refs_12_.refs_6_.refs_0_, f32[8,128,128]{2,1,0:T(8,128)S(1)} %get-tuple-element.190.refs_1_.refs_8_, bf16[256,256]{1,0:T(8,128)(2,1)S(1)} %get-tuple-element.110.refs_4_.refs_2_, ...), custom_call_target="tpu_custom_call" | custom-call | flops 30000001024 | bytes 1966080 | tf_op jit(solution)/shard_map/adjoint_inner/pallas_call | solution.py:411
  104.7 1.6 %collective-permute-start.35 = (f32[16,16,128]{2,1,0:T(8,128)S(1)}, f32[16,16,128]{2,1,0:T(8,128)S(1)}, u32[]{:S(2)}, u32[]{:S(2)}) collective-permute-start(f32[16,16,128]{2,1,0:T(8,128)S(1)} %get-tuple-element.202), channel_id=1, source_target_pairs={{0,8},{4,12},{8,0},{12,4},{16,24},{20,28},{24,16},{28,20},{1,9},{5... | collective-permute-start | bytes 393224 | tf_op jit(solution)/shard_map/ppermute | solution.py:629
  106.3 1.5 %collective-permute-start.36 = (f32[16,16,128]{2,1,0:T(8,128)S(1)}, f32[16,16,128]{2,1,0:T(8,128)S(1)}, u32[]{:S(2)}, u32[]{:S(2)}) collective-permute-start(f32[16,16,128]{2,1,0:T(8,128)S(1)} %get-tuple-element.203), channel_id=1, source_target_pairs={{0,16},{4,20},{8,24},{12,28},{16,0},{20,4},{24,8},{28,12},{1,17},{... | collective-permute-start | bytes 393224 | tf_op jit(solution)/shard_map/ppermute | solution.py:629
  108.2 1.5 %adjoint_border.15 = f32[16,128,128]{2,1,0:T(8,128)} custom-call(f32[8,128,128]{2,1,0:T(8,128)S(1)} %get-tuple-element.179.refs_12_.refs_6_.refs_0_, f32[8,128,128]{2,1,0:T(8,128)S(1)} %get-tuple-element.190.refs_1_.refs_8_, f32[4,128,128]{2,1,0:T(8,128)S(1)} %collective-permute-done.30.refs_2_, ...), custom_call_target="tpu_custom_call", output_to_operand_aliasing={{}: (9, {})} | custom-call | flops 30000001024 | bytes 1966080 | tf_op jit(solution)/shard_map/adjoint_border/pallas_call | solution.py:411
  109.8 0.9 collective-permute-done.35.refs_1_
  110.6 3.7 %collective-permute-done.36.refs_2_ = f32[16,16,128]{2,1,0:T(8,128)S(1)} collective-permute-done((f32[16,16,128]{2,1,0:T(8,128)S(1)}, f32[16,16,128]{2,1,0:T(8,128)S(1)}, u32[]{:S(2)}, u32[]{:S(2)}) %collective-permute-start.36) | collective-permute-done | bytes 131104 | tf_op jit(solution)/shard_map/ppermute | solution.py:629
  (84 shorter events, 32.1 us)
Async XLA Ops:
  1.9 17.2 %collective-permute-start.2 = (f32[4,128,128]{2,1,0:T(8,128)S(1)}, f32[4,128,128]{2,1,0:T(8,128)S(1)}, u32[]{:S(2)}, u32[]{:S(2)}) collective-permute-start(f32[4,128,128]{2,1,0:T(8,128)S(1)} %get-tuple-element.108), channel_id=1, source_target_pairs={{0,1},{1,0},{2,3},{3,2},{4,5},{5,4},{6,7},{7,6},{8,9},{9,8},{10,11... | collective-permute-start | bytes 786440 | tf_op jit(solution)/shard_map/ppermute | solution.py:458
  5.0 14.1 %collective-permute-start.3 = (f32[4,128,128]{2,1,0:T(8,128)S(1)}, f32[4,128,128]{2,1,0:T(8,128)S(1)}, u32[]{:S(2)}, u32[]{:S(2)}) collective-permute-start(f32[4,128,128]{2,1,0:T(8,128)S(1)} %get-tuple-element.109), channel_id=1, source_target_pairs={{1,2},{2,1},{5,6},{6,5},{9,10},{10,9},{13,14},{14,13},{17,18},{18,... | collective-permute-start | bytes 786440 | tf_op jit(solution)/shard_map/ppermute | solution.py:458
  10.1 12.7 %collective-permute-start.4 = (f32[4,128,128]{2,1,0:T(8,128)S(1)}, f32[4,128,128]{2,1,0:T(8,128)S(1)}, u32[]{:S(2)}, u32[]{:S(2)}) collective-permute-start(f32[4,128,128]{2,1,0:T(8,128)S(1)} %get-tuple-element.118), channel_id=1, source_target_pairs={{0,1},{1,0},{2,3},{3,2},{4,5},{5,4},{6,7},{7,6},{8,9},{9,8},{10,11... | collective-permute-start | bytes 786440 | tf_op jit(solution)/shard_map/ppermute | solution.py:458
  10.2 12.6 %collective-permute-start.5 = (f32[4,128,128]{2,1,0:T(8,128)S(1)}, f32[4,128,128]{2,1,0:T(8,128)S(1)}, u32[]{:S(2)}, u32[]{:S(2)}) collective-permute-start(f32[4,128,128]{2,1,0:T(8,128)S(1)} %get-tuple-element.119), channel_id=1, source_target_pairs={{1,2},{2,1},{5,6},{6,5},{9,10},{10,9},{13,14},{14,13},{17,18},{18,... | collective-permute-start | bytes 786440 | tf_op jit(solution)/shard_map/ppermute | solution.py:458
  12.0 21.2 %collective-permute-start.1 = (f32[2,8,256]{2,1,0:T(8,128)S(1)}, f32[2,8,256]{2,1,0:T(8,128)S(1)}, u32[]{:S(2)}, u32[]{:S(2)}) collective-permute-start(f32[2,8,256]{2,1,0:T(8,128)S(1)} %stack.1.refs_3_), channel_id=1, source_target_pairs={{0,2},{1,3},{2,0},{3,1},{4,6},{5,7},{6,4},{7,5},{8,10},{9,11},{10,... | collective-permute-start | bytes 49160 | tf_op jit(solution)/shard_map/ppermute | solution.py:476
  19.8 8.3 %collective-permute-start.6 = (f32[4,128,128]{2,1,0:T(8,128)S(1)}, f32[4,128,128]{2,1,0:T(8,128)S(1)}, u32[]{:S(2)}, u32[]{:S(2)}) collective-permute-start(f32[4,128,128]{2,1,0:T(8,128)S(1)} %get-tuple-element.124), channel_id=1, source_target_pairs={{0,1},{1,0},{2,3},{3,2},{4,5},{5,4},{6,7},{7,6},{8,9},{9,8},{10,11... | collective-permute-start | bytes 786440 | tf_op jit(solution)/shard_map/ppermute | solution.py:458
  20.5 7.6 %collective-permute-start.7 = (f32[4,128,128]{2,1,0:T(8,128)S(1)}, f32[4,128,128]{2,1,0:T(8,128)S(1)}, u32[]{:S(2)}, u32[]{:S(2)}) collective-permute-start(f32[4,128,128]{2,1,0:T(8,128)S(1)} %get-tuple-element.125), channel_id=1, source_target_pairs={{1,2},{2,1},{5,6},{6,5},{9,10},{10,9},{13,14},{14,13},{17,18},{18,... | collective-permute-start | bytes 786440 | tf_op jit(solution)/shard_map/ppermute | solution.py:458
  23.5 16.2 %collective-permute-start.8 = (f32[4,128,128]{2,1,0:T(8,128)S(1)}, f32[4,128,128]{2,1,0:T(8,128)S(1)}, u32[]{:S(2)}, u32[]{:S(2)}) collective-permute-start(f32[4,128,128]{2,1,0:T(8,128)S(1)} %get-tuple-element.131), channel_id=1, source_target_pairs={{0,1},{1,0},{2,3},{3,2},{4,5},{5,4},{6,7},{7,6},{8,9},{9,8},{10,11... | collective-permute-start | bytes 786440 | tf_op jit(solution)/shard_map/ppermute | solution.py:458
  26.1 13.5 %collective-permute-start.9 = (f32[4,128,128]{2,1,0:T(8,128)S(1)}, f32[4,128,128]{2,1,0:T(8,128)S(1)}, u32[]{:S(2)}, u32[]{:S(2)}) collective-permute-start(f32[4,128,128]{2,1,0:T(8,128)S(1)} %get-tuple-element.132), channel_id=1, source_target_pairs={{1,2},{2,1},{5,6},{6,5},{9,10},{10,9},{13,14},{14,13},{17,18},{18,... | collective-permute-start | bytes 786440 | tf_op jit(solution)/shard_map/ppermute | solution.py:458
  28.9 15.4 %collective-permute-start.12 = (f32[4,128,128]{2,1,0:T(8,128)S(1)}, f32[4,128,128]{2,1,0:T(8,128)S(1)}, u32[]{:S(2)}, u32[]{:S(2)}) collective-permute-start(f32[4,128,128]{2,1,0:T(8,128)S(1)} %get-tuple-element.138), channel_id=1, source_target_pairs={{0,1},{1,0},{2,3},{3,2},{4,5},{5,4},{6,7},{7,6},{8,9},{9,8},{10,11... | collective-permute-start | bytes 786440 | tf_op jit(solution)/shard_map/ppermute | solution.py:458
  32.6 11.7 %collective-permute-start.13 = (f32[4,128,128]{2,1,0:T(8,128)S(1)}, f32[4,128,128]{2,1,0:T(8,128)S(1)}, u32[]{:S(2)}, u32[]{:S(2)}) collective-permute-start(f32[4,128,128]{2,1,0:T(8,128)S(1)} %get-tuple-element.139), channel_id=1, source_target_pairs={{1,2},{2,1},{5,6},{6,5},{9,10},{10,9},{13,14},{14,13},{17,18},{18,... | collective-permute-start | bytes 786440 | tf_op jit(solution)/shard_map/ppermute | solution.py:458
  40.5 9.1 %collective-permute-start.10 = (f32[4,128,128]{2,1,0:T(8,128)S(1)}, f32[4,128,128]{2,1,0:T(8,128)S(1)}, u32[]{:S(2)}, u32[]{:S(2)}) collective-permute-start(f32[4,128,128]{2,1,0:T(8,128)S(1)} %get-tuple-element.136), channel_id=1, source_target_pairs={{0,1},{1,0},{2,3},{3,2},{4,5},{5,4},{6,7},{7,6},{8,9},{9,8},{10,11... | collective-permute-start | bytes 786440 | tf_op jit(solution)/shard_map/ppermute | solution.py:458
  42.2 7.4 %collective-permute-start.11 = (f32[4,128,128]{2,1,0:T(8,128)S(1)}, f32[4,128,128]{2,1,0:T(8,128)S(1)}, u32[]{:S(2)}, u32[]{:S(2)}) collective-permute-start(f32[4,128,128]{2,1,0:T(8,128)S(1)} %get-tuple-element.137), channel_id=1, source_target_pairs={{1,2},{2,1},{5,6},{6,5},{9,10},{10,9},{13,14},{14,13},{17,18},{18,... | collective-permute-start | bytes 786440 | tf_op jit(solution)/shard_map/ppermute | solution.py:458
  45.3 10.1 %collective-permute-start.16 = (f32[4,128,128]{2,1,0:T(8,128)S(1)}, f32[4,128,128]{2,1,0:T(8,128)S(1)}, u32[]{:S(2)}, u32[]{:S(2)}) collective-permute-start(f32[4,128,128]{2,1,0:T(8,128)S(1)} %get-tuple-element.145), channel_id=1, source_target_pairs={{0,1},{1,0},{2,3},{3,2},{4,5},{5,4},{6,7},{7,6},{8,9},{9,8},{10,11... | collective-permute-start | bytes 786440 | tf_op jit(solution)/shard_map/ppermute | solution.py:458
  48.2 7.1 %collective-permute-start.17 = (f32[4,128,128]{2,1,0:T(8,128)S(1)}, f32[4,128,128]{2,1,0:T(8,128)S(1)}, u32[]{:S(2)}, u32[]{:S(2)}) collective-permute-start(f32[4,128,128]{2,1,0:T(8,128)S(1)} %get-tuple-element.146), channel_id=1, source_target_pairs={{1,2},{2,1},{5,6},{6,5},{9,10},{10,9},{13,14},{14,13},{17,18},{18,... | collective-permute-start | bytes 786440 | tf_op jit(solution)/shard_map/ppermute | solution.py:458
  50.4 11.2 %collective-permute-start.14 = (f32[4,128,128]{2,1,0:T(8,128)S(1)}, f32[4,128,128]{2,1,0:T(8,128)S(1)}, u32[]{:S(2)}, u32[]{:S(2)}) collective-permute-start(f32[4,128,128]{2,1,0:T(8,128)S(1)} %get-tuple-element.143), channel_id=1, source_target_pairs={{0,1},{1,0},{2,3},{3,2},{4,5},{5,4},{6,7},{7,6},{8,9},{9,8},{10,11... | collective-permute-start | bytes 786440 | tf_op jit(solution)/shard_map/ppermute | solution.py:458
  53.4 8.3 %collective-permute-start.15 = (f32[4,128,128]{2,1,0:T(8,128)S(1)}, f32[4,128,128]{2,1,0:T(8,128)S(1)}, u32[]{:S(2)}, u32[]{:S(2)}) collective-permute-start(f32[4,128,128]{2,1,0:T(8,128)S(1)} %get-tuple-element.144), channel_id=1, source_target_pairs={{1,2},{2,1},{5,6},{6,5},{9,10},{10,9},{13,14},{14,13},{17,18},{18,... | collective-permute-start | bytes 786440 | tf_op jit(solution)/shard_map/ppermute | solution.py:458
  56.1 11.1 %collective-permute-start.20 = (f32[4,128,128]{2,1,0:T(8,128)S(1)}, f32[4,128,128]{2,1,0:T(8,128)S(1)}, u32[]{:S(2)}, u32[]{:S(2)}) collective-permute-start(f32[4,128,128]{2,1,0:T(8,128)S(1)} %get-tuple-element.156), channel_id=1, source_target_pairs={{0,1},{1,0},{2,3},{3,2},{4,5},{5,4},{6,7},{7,6},{8,9},{9,8},{10,11... | collective-permute-start | bytes 786440 | tf_op jit(solution)/shard_map/ppermute | solution.py:458
  62.4 10.6 %collective-permute-start.18 = (f32[4,128,128]{2,1,0:T(8,128)S(1)}, f32[4,128,128]{2,1,0:T(8,128)S(1)}, u32[]{:S(2)}, u32[]{:S(2)}) collective-permute-start(f32[4,128,128]{2,1,0:T(8,128)S(1)} %get-tuple-element.153), channel_id=1, source_target_pairs={{0,1},{1,0},{2,3},{3,2},{4,5},{5,4},{6,7},{7,6},{8,9},{9,8},{10,11... | collective-permute-start | bytes 786440 | tf_op jit(solution)/shard_map/ppermute | solution.py:458
  65.8 7.2 %collective-permute-start.19 = (f32[4,128,128]{2,1,0:T(8,128)S(1)}, f32[4,128,128]{2,1,0:T(8,128)S(1)}, u32[]{:S(2)}, u32[]{:S(2)}) collective-permute-start(f32[4,128,128]{2,1,0:T(8,128)S(1)} %get-tuple-element.154), channel_id=1, source_target_pairs={{1,2},{2,1},{5,6},{6,5},{9,10},{10,9},{13,14},{14,13},{17,18},{18,... | collective-permute-start | bytes 786440 | tf_op jit(solution)/shard_map/ppermute | solution.py:458
  68.0 11.1 %collective-permute-start.24 = (f32[4,128,128]{2,1,0:T(8,128)S(1)}, f32[4,128,128]{2,1,0:T(8,128)S(1)}, u32[]{:S(2)}, u32[]{:S(2)}) collective-permute-start(f32[4,128,128]{2,1,0:T(8,128)S(1)} %get-tuple-element.169), channel_id=1, source_target_pairs={{0,1},{1,0},{2,3},{3,2},{4,5},{5,4},{6,7},{7,6},{8,9},{9,8},{10,11... | collective-permute-start | bytes 786440 | tf_op jit(solution)/shard_map/ppermute | solution.py:458
  71.6 7.6 %collective-permute-start.25 = (f32[4,128,128]{2,1,0:T(8,128)S(1)}, f32[4,128,128]{2,1,0:T(8,128)S(1)}, u32[]{:S(2)}, u32[]{:S(2)}) collective-permute-start(f32[4,128,128]{2,1,0:T(8,128)S(1)} %get-tuple-element.170), channel_id=1, source_target_pairs={{1,2},{2,1},{5,6},{6,5},{9,10},{10,9},{13,14},{14,13},{17,18},{18,... | collective-permute-start | bytes 786440 | tf_op jit(solution)/shard_map/ppermute | solution.py:458
  73.8 11.1 %collective-permute-start.22 = (f32[4,128,128]{2,1,0:T(8,128)S(1)}, f32[4,128,128]{2,1,0:T(8,128)S(1)}, u32[]{:S(2)}, u32[]{:S(2)}) collective-permute-start(f32[4,128,128]{2,1,0:T(8,128)S(1)} %get-tuple-element.166), channel_id=1, source_target_pairs={{0,1},{1,0},{2,3},{3,2},{4,5},{5,4},{6,7},{7,6},{8,9},{9,8},{10,11... | collective-permute-start | bytes 786440 | tf_op jit(solution)/shard_map/ppermute | solution.py:458
  77.7 7.1 %collective-permute-start.23 = (f32[4,128,128]{2,1,0:T(8,128)S(1)}, f32[4,128,128]{2,1,0:T(8,128)S(1)}, u32[]{:S(2)}, u32[]{:S(2)}) collective-permute-start(f32[4,128,128]{2,1,0:T(8,128)S(1)} %get-tuple-element.167), channel_id=1, source_target_pairs={{1,2},{2,1},{5,6},{6,5},{9,10},{10,9},{13,14},{14,13},{17,18},{18,... | collective-permute-start | bytes 786440 | tf_op jit(solution)/shard_map/ppermute | solution.py:458
  79.9 10.9 %collective-permute-start.28 = (f32[4,128,128]{2,1,0:T(8,128)S(1)}, f32[4,128,128]{2,1,0:T(8,128)S(1)}, u32[]{:S(2)}, u32[]{:S(2)}) collective-permute-start(f32[4,128,128]{2,1,0:T(8,128)S(1)} %get-tuple-element.183), channel_id=1, source_target_pairs={{0,1},{1,0},{2,3},{3,2},{4,5},{5,4},{6,7},{7,6},{8,9},{9,8},{10,11... | collective-permute-start | bytes 786440 | tf_op jit(solution)/shard_map/ppermute | solution.py:458
  83.5 7.4 %collective-permute-start.29 = (f32[4,128,128]{2,1,0:T(8,128)S(1)}, f32[4,128,128]{2,1,0:T(8,128)S(1)}, u32[]{:S(2)}, u32[]{:S(2)}) collective-permute-start(f32[4,128,128]{2,1,0:T(8,128)S(1)} %get-tuple-element.184), channel_id=1, source_target_pairs={{1,2},{2,1},{5,6},{6,5},{9,10},{10,9},{13,14},{14,13},{17,18},{18,... | collective-permute-start | bytes 786440 | tf_op jit(solution)/shard_map/ppermute | solution.py:458
  85.6 11.1 %collective-permute-start.26 = (f32[4,128,128]{2,1,0:T(8,128)S(1)}, f32[4,128,128]{2,1,0:T(8,128)S(1)}, u32[]{:S(2)}, u32[]{:S(2)}) collective-permute-start(f32[4,128,128]{2,1,0:T(8,128)S(1)} %get-tuple-element.180), channel_id=1, source_target_pairs={{0,1},{1,0},{2,3},{3,2},{4,5},{5,4},{6,7},{7,6},{8,9},{9,8},{10,11... | collective-permute-start | bytes 786440 | tf_op jit(solution)/shard_map/ppermute | solution.py:458
  89.3 7.5 %collective-permute-start.27 = (f32[4,128,128]{2,1,0:T(8,128)S(1)}, f32[4,128,128]{2,1,0:T(8,128)S(1)}, u32[]{:S(2)}, u32[]{:S(2)}) collective-permute-start(f32[4,128,128]{2,1,0:T(8,128)S(1)} %get-tuple-element.181), channel_id=1, source_target_pairs={{1,2},{2,1},{5,6},{6,5},{9,10},{10,9},{13,14},{14,13},{17,18},{18,... | collective-permute-start | bytes 786440 | tf_op jit(solution)/shard_map/ppermute | solution.py:458
  91.6 10.2 %collective-permute-start.32 = (f32[4,128,128]{2,1,0:T(8,128)S(1)}, f32[4,128,128]{2,1,0:T(8,128)S(1)}, u32[]{:S(2)}, u32[]{:S(2)}) collective-permute-start(f32[4,128,128]{2,1,0:T(8,128)S(1)} %get-tuple-element.195), channel_id=1, source_target_pairs={{0,1},{1,0},{2,3},{3,2},{4,5},{5,4},{6,7},{7,6},{8,9},{9,8},{10,11... | collective-permute-start | bytes 786440 | tf_op jit(solution)/shard_map/ppermute | solution.py:458
  97.5 10.7 %collective-permute-start.30 = (f32[4,128,128]{2,1,0:T(8,128)S(1)}, f32[4,128,128]{2,1,0:T(8,128)S(1)}, u32[]{:S(2)}, u32[]{:S(2)}) collective-permute-start(f32[4,128,128]{2,1,0:T(8,128)S(1)} %get-tuple-element.191), channel_id=1, source_target_pairs={{0,1},{1,0},{2,3},{3,2},{4,5},{5,4},{6,7},{7,6},{8,9},{9,8},{10,11... | collective-permute-start | bytes 786440 | tf_op jit(solution)/shard_map/ppermute | solution.py:458
  101.2 7.1 %collective-permute-start.31 = (f32[4,128,128]{2,1,0:T(8,128)S(1)}, f32[4,128,128]{2,1,0:T(8,128)S(1)}, u32[]{:S(2)}, u32[]{:S(2)}) collective-permute-start(f32[4,128,128]{2,1,0:T(8,128)S(1)} %get-tuple-element.192), channel_id=1, source_target_pairs={{1,2},{2,1},{5,6},{6,5},{9,10},{10,9},{13,14},{14,13},{17,18},{18,... | collective-permute-start | bytes 786440 | tf_op jit(solution)/shard_map/ppermute | solution.py:458
  106.3 8.1 %collective-permute-start.36 = (f32[16,16,128]{2,1,0:T(8,128)S(1)}, f32[16,16,128]{2,1,0:T(8,128)S(1)}, u32[]{:S(2)}, u32[]{:S(2)}) collective-permute-start(f32[16,16,128]{2,1,0:T(8,128)S(1)} %get-tuple-element.203), channel_id=1, source_target_pairs={{0,16},{4,20},{8,24},{12,28},{16,0},{20,4},{24,8},{28,12},{1,17},{... | collective-permute-start | bytes 393224 | tf_op jit(solution)/shard_map/ppermute | solution.py:629
  (6 other events, 34.3 us)
